TPU v7x, 32 devices: a whole 2x2x4 slice. The times are simulated.
32 devices in a mesh: dp: 8 (over z, y), tp: 4 (over x, core).
Axes of the slice: x: 2, y: 2, z: 4, core: 2. Of those that a mesh axis runs over, the one named last changes fastest.
Arguments:
- cell_inputs: bfloat16 [512, 64, 1120], P('dp', 'tp'), may hold values from -6 to 6
- out_grad: bfloat16 [512, 64, 1120], P('dp', 'tp'), may hold values from -6 to 6
- lengths: int32 [512], P('dp'), may hold values from 0 to 64, as said below
- datasets: int32 [512], P('dp'), may hold values from 0 to 31
- norm_gain: bfloat16 [2, 1120], replicated, may hold values from 0.5 to 1.5
- norm_bias: bfloat16 [2, 1120], replicated, may hold values from -1.5 to 1.5
- qkv_weight: bfloat16 [1120, 3, 1120], P(None, None, 'tp'), may hold values from -0.1875 to 0.1875
- qv_bias: bfloat16 [2, 1120], P(None, 'tp'), may hold values from -3 to 3
- out_weight: bfloat16 [1120, 1120], P('tp'), may hold values from -0.75 to 0.75
- out_bias: bfloat16 [2, 1120], replicated, may hold values from -1.5 to 1.5
- up_weight: bfloat16 [1120, 4480], P(None, 'tp'), may hold values from -0.1875 to 0.1875
- up_bias: bfloat16 [4480], P('tp'), may hold values from -3 to 3
- down_weight: bfloat16 [4480, 1120], P('tp'), may hold values from -0.09375 to 0.09375
- dataset_table: bfloat16 [32, 1120], replicated, may hold values from -3 to 3
Outputs:
- cell_outputs: bfloat16 [512, 64, 1120], P('dp', 'tp')
- input_grad: bfloat16 [512, 64, 1120], P('dp', 'tp')
- norm_gain_grad: float32 [2, 1120], replicated
- norm_bias_grad: float32 [2, 1120], replicated
- qkv_weight_grad: float32 [1120, 3, 1120], P(None, None, 'tp')
- qv_bias_grad: float32 [2, 1120], P(None, 'tp')
- out_weight_grad: float32 [1120, 1120], P('tp')
- out_bias_grad: float32 [2, 1120], replicated
- up_weight_grad: float32 [1120, 4480], P(None, 'tp')
- up_bias_grad: float32 [4480], P('tp')
- down_weight_grad: float32 [4480, 1120], P('tp')
- table_grad: float32 [32, 1120], replicated
Inputs may be any that keep to these rules, and one draw needn't show every extreme that they name: `lengths`: the 64 consecutive entries of one dp group hold its cells; the cells with tokens occupy the group's first slots and have 64 // 4 to 64 tokens, slot 0 of every group exactly 64; the other slots have length 0. Each group has 4 to 60 cells with tokens, one group exactly 60, and all groups together have exactly 256.
All inputs are finite; a program needn't handle non-finite values.
Results may differ from a plain program's by a relative error of at most 0.012.
Values may be sent and summed in bfloat16 or wider, within the bound.
No kernel may reach another device: no remote copies, remote signals or barrier semaphores. Data moves between devices by JAX's collectives and lax.ppermute only.
A program may use at most 192 MiB of HBM per device.

v0:
```python
import math

import jax
import jax.numpy as jnp
from jax import lax
from jax.sharding import PartitionSpec as P

HEAD_DIM = 56


EPSILON = 1e-05


def layer_norm(inputs, scale_row, shift_row):
    center = inputs - jnp.mean(inputs, axis=-1, keepdims=True)
    spread = jnp.mean(center * center, axis=-1, keepdims=True)
    return center * lax.rsqrt(spread + EPSILON) * scale_row + shift_row


def gelu_exact(values):
    return jax.nn.gelu(values, approximate=False)


def on_device(
    cell_inputs,
    out_grad,
    lengths,
    datasets,
    norm_gain,
    norm_bias,
    qkv_weight,
    qv_bias,
    out_weight,
    out_bias,
    up_weight,
    up_bias,
    down_weight,
    dataset_table,
):
    groups = lax.axis_size("dp")
    my_group = lax.axis_index("dp")
    slot_count = lengths.shape[0]
    per_peer = slot_count // groups
    kept_cells = slot_count // 2
    quarter = cell_inputs.shape[1]
    cell_width = quarter * lax.axis_size("tp")
    width_local = qkv_weight.shape[2]
    head_count = width_local // HEAD_DIM
    score_scale = 1.0 / math.sqrt(HEAD_DIM)
    all_lengths, all_datasets = (
        lax.all_gather(lengths, "dp", axis=0, tiled=True),
        lax.all_gather(datasets, "dp", axis=0, tiled=True),
    )
    live_counts = jnp.sum((all_lengths > 0).reshape(groups, slot_count).astype(jnp.int32), axis=1)
    offsets = jnp.cumsum(live_counts) - live_counts
    my_offset = offsets[my_group]
    my_count = live_counts[my_group]
    buffer_index = jnp.arange(groups * per_peer, dtype=jnp.int32)
    peer_index = buffer_index // per_peer
    turn_index = buffer_index % per_peer
    local_cell = turn_index * groups + jnp.mod(peer_index - my_offset, groups)
    send_valid = local_cell < my_count
    local_cell = jnp.where(send_valid, local_cell, 0)
    send_mask = send_valid[:, None, None]
    send_inputs = jnp.where(
        send_mask, cell_inputs[local_cell], jnp.zeros_like(cell_inputs[local_cell])
    )
    send_grads = jnp.where(send_mask, out_grad[local_cell], jnp.zeros_like(out_grad[local_cell]))
    recv_inputs, recv_grads = (
        lax.all_to_all(send_inputs, "dp", split_axis=0, concat_axis=0, tiled=True),
        lax.all_to_all(send_grads, "dp", split_axis=0, concat_axis=0, tiled=True),
    )
    cell_rank = jnp.arange(kept_cells, dtype=jnp.int32) * groups + my_group
    source = jnp.sum((offsets[None, :] <= cell_rank[:, None]).astype(jnp.int32), axis=1) - 1
    within = cell_rank - offsets[source]
    pick_row = source * per_peer + within // groups
    cells_in = recv_inputs[pick_row]
    grads_in = recv_grads[pick_row]
    cell_ids = source * slot_count + within
    cell_lengths = all_lengths[cell_ids]
    cell_sets = all_datasets[cell_ids]
    positions = lax.axis_index("tp") * quarter + jnp.arange(quarter, dtype=jnp.int32)
    row_valid = (positions[None, :] < cell_lengths[:, None]).astype(jnp.float32)
    table_ids = jnp.arange(dataset_table.shape[0], dtype=jnp.int32)
    onehot_low = (cell_sets[:, None] == table_ids[None, :]).astype(jnp.bfloat16)
    embedded = jnp.dot(onehot_low, dataset_table, preferred_element_type=jnp.float32)
    start_rows = cells_in.astype(jnp.float32) + embedded[:, None, :]
    gain_first = norm_gain[0].astype(jnp.float32)
    gain_second = norm_gain[1].astype(jnp.float32)
    shift_first = norm_bias[0].astype(jnp.float32)
    shift_second = norm_bias[1].astype(jnp.float32)
    qkv_shift = jnp.stack(
        [
            qv_bias[0].astype(jnp.float32),
            jnp.zeros((width_local,), jnp.float32),
            qv_bias[1].astype(jnp.float32),
        ]
    )
    causal = lax.broadcasted_iota(jnp.int32, (cell_width, cell_width), 0) >= lax.broadcasted_iota(
        jnp.int32, (cell_width, cell_width), 1
    )
    head_shape = (kept_cells, cell_width, head_count, HEAD_DIM)

    def forward_pass(first_rows):
        normed = layer_norm(first_rows, gain_first, shift_first).astype(jnp.bfloat16)
        normed_full = lax.all_gather(normed, "tp", axis=1, tiled=True)
        projected = jnp.einsum(
            "ocd,dke->ocke", normed_full, qkv_weight, preferred_element_type=jnp.float32
        )
        projected = (projected + qkv_shift).astype(jnp.bfloat16)
        queries = projected[:, :, 0].reshape(head_shape)
        key_rows = projected[:, :, 1].reshape(head_shape)
        value_rows = projected[:, :, 2].reshape(head_shape)
        raw_scores = (
            jnp.einsum("bqhe,bkhe->bhqk", queries, key_rows, preferred_element_type=jnp.float32)
            * score_scale
        )
        masked = jnp.where(causal, raw_scores, -1e30)
        attend = jax.nn.softmax(masked, axis=-1)
        attend_low = attend.astype(jnp.bfloat16)
        context = jnp.einsum(
            "bhqk,bkhe->bqhe", attend_low, value_rows, preferred_element_type=jnp.float32
        )
        context_low = context.astype(jnp.bfloat16).reshape(kept_cells, cell_width, width_local)
        attn_part = jnp.einsum(
            "oce,ed->ocd", context_low, out_weight, preferred_element_type=jnp.float32
        )
        attn_rows = lax.psum_scatter(attn_part, "tp", scatter_dimension=1, tiled=True)
        middle = first_rows + attn_rows + out_bias[0].astype(jnp.float32)
        normed_second = layer_norm(middle, gain_second, shift_second).astype(jnp.bfloat16)
        second_full = lax.all_gather(normed_second, "tp", axis=1, tiled=True)
        hidden = jnp.einsum(
            "ocd,df->ocf", second_full, up_weight, preferred_element_type=jnp.float32
        )
        hidden = hidden + up_bias.astype(jnp.float32)
        active = gelu_exact(hidden).astype(jnp.bfloat16)
        mlp_part = jnp.einsum(
            "ocf,fd->ocd", active, down_weight, preferred_element_type=jnp.float32
        )
        branch = lax.psum_scatter(
            mlp_part.astype(jnp.bfloat16), "tp", scatter_dimension=1, tiled=True
        ).astype(jnp.float32)
        final_rows = (middle + branch + out_bias[1].astype(jnp.float32)) * row_valid[:, :, None]
        return (
            final_rows,
            normed_full,
            queries,
            key_rows,
            value_rows,
            attend,
            attend_low,
            context_low,
            middle,
            second_full,
            hidden,
            active,
        )

    saved = forward_pass(start_rows)
    final_rows = saved[0]
    grad_rows = grads_in.astype(jnp.float32) * row_valid[:, :, None]
    grad_full = lax.all_gather(grad_rows.astype(jnp.bfloat16), "tp", axis=1, tiled=True)
    start_again, grad_full = lax.optimization_barrier((start_rows, grad_full))
    saved = forward_pass(start_again)
    (
        unused_final,
        normed_full,
        queries,
        key_rows,
        value_rows,
        attend,
        attend_low,
        context_low,
        middle,
        second_full,
        hidden,
        active,
    ) = saved
    down_grad = jnp.einsum("ocf,ocd->fd", active, grad_full, preferred_element_type=jnp.float32)
    active_grad = jnp.einsum(
        "ocd,fd->ocf", grad_full, down_weight, preferred_element_type=jnp.float32
    )
    hidden_grad = jax.vjp(gelu_exact, hidden)[1](active_grad)[0].astype(jnp.bfloat16)
    up_bias_grad = jnp.sum(hidden_grad.astype(jnp.float32), axis=(0, 1))
    up_grad = jnp.einsum(
        "ocd,ocf->df", second_full, hidden_grad, preferred_element_type=jnp.float32
    )
    second_part = jnp.einsum(
        "ocf,df->ocd", hidden_grad, up_weight, preferred_element_type=jnp.float32
    )
    second_grad = lax.psum_scatter(second_part, "tp", scatter_dimension=1, tiled=True)
    second_pull = jax.vjp(layer_norm, middle, gain_second, shift_second)[1]
    middle_part, gain_second_grad, shift_second_grad = second_pull(second_grad)
    middle_grad = grad_rows + middle_part
    attn_full = lax.all_gather(middle_grad.astype(jnp.bfloat16), "tp", axis=1, tiled=True)
    out_weight_grad = jnp.einsum(
        "oce,ocd->ed", context_low, attn_full, preferred_element_type=jnp.float32
    )
    context_grad = jnp.einsum(
        "ocd,ed->oce", attn_full, out_weight, preferred_element_type=jnp.float32
    )
    context_grad = context_grad.astype(jnp.bfloat16).reshape(head_shape)
    attend_grad = jnp.einsum(
        "bqhe,bkhe->bhqk", context_grad, value_rows, preferred_element_type=jnp.float32
    )
    value_grad = jnp.einsum(
        "bhqk,bqhe->bkhe", attend_low, context_grad, preferred_element_type=jnp.float32
    )
    score_grad = attend * (attend_grad - jnp.sum(attend * attend_grad, axis=-1, keepdims=True))
    score_grad = score_grad.astype(jnp.bfloat16)
    query_grad = (
        jnp.einsum("bhqk,bkhe->bqhe", score_grad, key_rows, preferred_element_type=jnp.float32)
        * score_scale
    )
    key_grad = (
        jnp.einsum("bhqk,bqhe->bkhe", score_grad, queries, preferred_element_type=jnp.float32)
        * score_scale
    )
    stacked = jnp.stack(
        [
            query_grad.reshape(kept_cells, cell_width, width_local),
            key_grad.reshape(kept_cells, cell_width, width_local),
            value_grad.reshape(kept_cells, cell_width, width_local),
        ],
        axis=2,
    )
    projected_grad = stacked.astype(jnp.bfloat16)
    part_sums = jnp.sum(projected_grad.astype(jnp.float32), axis=(0, 1))
    qv_bias_grad = jnp.stack([part_sums[0], part_sums[2]])
    qkv_grad = jnp.einsum(
        "ocd,ocke->dke", normed_full, projected_grad, preferred_element_type=jnp.float32
    )
    first_part = jnp.einsum(
        "ocke,dke->ocd", projected_grad, qkv_weight, preferred_element_type=jnp.float32
    )
    first_grad = lax.psum_scatter(first_part, "tp", scatter_dimension=1, tiled=True)
    first_pull = jax.vjp(layer_norm, start_rows, gain_first, shift_first)[1]
    start_part, gain_first_grad, shift_first_grad = first_pull(first_grad)
    start_grad = middle_grad + start_part
    onehot_full = onehot_low.astype(jnp.float32)
    table_local = jnp.dot(
        onehot_full.T, jnp.sum(start_grad, axis=1), precision=lax.Precision.HIGHEST
    )
    gain_local = jnp.stack([gain_first_grad, gain_second_grad])
    shift_local = jnp.stack([shift_first_grad, shift_second_grad])
    bias_local = jnp.stack([jnp.sum(middle_grad, axis=(0, 1)), jnp.sum(grad_rows, axis=(0, 1))])
    qkv_sum, qv_sum, out_sum, up_sum, up_bias_sum, down_sum = lax.psum(
        (qkv_grad, qv_bias_grad, out_weight_grad, up_grad, up_bias_grad, down_grad), "dp"
    )
    gain_sum, shift_sum, bias_sum, table_sum = lax.psum(
        (gain_local, shift_local, bias_local, table_local), ("dp", "tp")
    )
    back_peer = buffer_index // per_peer
    back_turn = buffer_index % per_peer
    anchor_cell = back_turn * groups + jnp.mod(my_group - offsets[back_peer], groups)
    back_valid = anchor_cell < live_counts[back_peer]
    slot_back = jnp.where(back_valid, (offsets[back_peer] + anchor_cell) // groups, 0)
    back_mask = back_valid[:, None, None]
    final_low = final_rows.astype(jnp.bfloat16)[slot_back]
    start_low = start_grad.astype(jnp.bfloat16)[slot_back]
    send_final = jnp.where(back_mask, final_low, jnp.zeros_like(final_low))
    send_start = jnp.where(back_mask, start_low, jnp.zeros_like(start_low))
    recv_final, recv_start = (
        lax.all_to_all(send_final, "dp", split_axis=0, concat_axis=0, tiled=True),
        lax.all_to_all(send_start, "dp", split_axis=0, concat_axis=0, tiled=True),
    )
    cell_slot = jnp.arange(slot_count, dtype=jnp.int32)
    home_peer = jnp.mod(my_offset + cell_slot, groups)
    home_row = home_peer * per_peer + cell_slot // groups
    home_valid = (cell_slot < my_count)[:, None, None]
    home_final = recv_final[home_row]
    home_start = recv_start[home_row]
    cell_outputs = jnp.where(home_valid, home_final, jnp.zeros_like(home_final))
    input_grad = jnp.where(home_valid, home_start, jnp.zeros_like(home_start))
    return (
        cell_outputs,
        input_grad,
        gain_sum,
        shift_sum,
        qkv_sum,
        qv_sum,
        out_sum,
        bias_sum,
        up_sum,
        up_bias_sum,
        down_sum,
        table_sum,
    )


def solution(mesh):
    in_specs = (
        P("dp", "tp", None),
        P("dp", "tp", None),
        P("dp"),
        P("dp"),
        P(),
        P(),
        P(None, None, "tp"),
        P(None, "tp"),
        P("tp", None),
        P(),
        P(None, "tp"),
        P("tp"),
        P("tp", None),
        P(),
    )
    out_specs = (
        P("dp", "tp", None),
        P("dp", "tp", None),
        P(),
        P(),
        P(None, None, "tp"),
        P(None, "tp"),
        P("tp", None),
        P(),
        P(None, "tp"),
        P("tp"),
        P("tp", None),
        P(),
    )
    return jax.shard_map(
        on_device, mesh=mesh, in_specs=in_specs, out_specs=out_specs, check_vma=False
    )
```

profile of v0, /device:TPU:0, one launch (start us, length us, event | category | flops | bytes accessed | tf_op | source)
XLA Modules:
  0.0 1719.3 jit_solution(10423775088112516640)
XLA Ops:
  11.0 13.1 all-reduce.2
  27.6 3.9 gather_fusion.7
  31.5 3.9 gather_fusion
  35.3 5.0 broadcast_select_fusion
  40.4 4.4 all-to-all-start.2
  46.5 49.7 %all-to-all-done.2 = bf16[64,16,1120]{2,1,0:T(8,128)(2,1)} async-done(((bf16[64,16,1120]{2,1,0:T(8,128)(2,1)}), bf16[64,16,1120]{2,1,0:T(8,128)(2,1)}, u32[]{:S(2)}, u32[]{:S(2)}) %all-to-all-start.2) | async-done | bytes 2293792 | tf_op jit(solution)/shard_map/all_to_all | solution.py:71
  102.2 4.5 all-to-all-start
  107.8 52.1 %all-to-all-done = bf16[64,16,1120]{2,1,0:T(8,128)(2,1)} async-done(((bf16[64,16,1120]{2,1,0:T(8,128)(2,1)}), bf16[64,16,1120]{2,1,0:T(8,128)(2,1)}, u32[]{:S(2)}, u32[]{:S(2)}) %all-to-all-start) | async-done | bytes 2293792 | tf_op jit(solution)/shard_map/all_to_all | solution.py:70
  163.2 3.5 fusion.56
  172.9 36.2 %all-gather.13.cloned.1.call-done = bf16[32,64,1120]{2,1,0:T(8,128)(2,1)} async-done(((bf16[32,16,1120]{2,1,0:T(8,128)(2,1)}), bf16[32,64,1120]{2,1,0:T(8,128)(2,1)}) %all-gather.13.cloned.1.call-update) | async-done | bytes 4587536 | tf_op jit(solution)/shard_map/all_gather | solution.py:106
  209.2 9.3 add_convert_fusion.1
  220.9 3.9 copy.75
  224.8 3.9 copy.74
  228.7 3.9 copy.73
  232.6 7.5 fusion.145
  240.1 4.6 convolution_convert_fusion.2
  246.2 5.4 fusion.62
  253.0 77.3 %reduce-scatter.10.cloned.1.call-done = f32[32,16,1120]{2,1,0:T(8,128)} async-done(((f32[32,64,1120]{2,1,0:T(8,128)}), f32[32,16,1120]{2,1,0:T(8,128)}) %reduce-scatter.10.cloned.1.call-update) | async-done | bytes 2293776 | tf_op jit(solution)/shard_map/reduce_scatter | solution.py:128
  336.2 37.3 %all-gather.15.cloned.1.call-done = bf16[32,64,1120]{2,1,0:T(8,128)(2,1)} async-done(((bf16[32,16,1120]{2,1,0:T(8,128)(2,1)}), bf16[32,64,1120]{2,1,0:T(8,128)(2,1)}) %all-gather.15.cloned.1.call-update) | async-done | bytes 4587536 | tf_op jit(solution)/shard_map/all_gather | solution.py:131
  373.5 9.5 convert_reduce_fusion.1
  383.0 3.6 copy-done.15
  386.7 21.3 %fusion.5 = f32[32,64,1120]{2,1,0:T(8,128)} fusion(f32[32,64,1120]{2,1,0:T(8,128)S(1)} %get-tuple-element.101, u32[64,1120]{1,0:T(8,128)S(1)} %get-tuple-element.17, u32[64,1120]{1,0:T(8,128)S(1)} %get-tuple-element.16, f32[1120]{0:T(1024)S(1)} %convert_element_type.195), kind=kLoop, calls=%fused_computation.18 | loop fusion | flops 151388160 | bytes 18928000 | tf_op jit(solution)/shard_map/jvp()/erfc | solution.py:21
  408.0 17.0 convert_reduce_fusion.4
  427.1 9.6 fusion.40
  436.8 78.5 %reduce-scatter.12.cloned.1.call-done = f32[32,16,1120]{2,1,0:T(8,128)} async-done(((f32[32,64,1120]{2,1,0:T(8,128)}), f32[32,16,1120]{2,1,0:T(8,128)}) %reduce-scatter.12.cloned.1.call-update) | async-done | bytes 2293776 | tf_op jit(solution)/shard_map/reduce_scatter | solution.py:191
  515.4 3.6 fusion.137
  523.8 37.6 %all-gather.17.cloned.1.call-done = bf16[32,64,1120]{2,1,0:T(8,128)(2,1)} async-done(((bf16[32,16,1120]{2,1,0:T(8,128)(2,1)}), bf16[32,64,1120]{2,1,0:T(8,128)(2,1)}) %all-gather.17.cloned.1.call-update) | async-done | bytes 4587536 | tf_op jit(solution)/shard_map/all_gather | solution.py:195
  561.4 6.2 convolution_convert_fusion.3
  567.6 4.1 copy.78
  571.7 6.2 convolution_convert_fusion.1
  578.0 4.2 multiply_reduce_fusion
  589.6 4.0 copy.84
  593.6 4.0 copy.82
  597.7 4.0 copy.83
  601.7 10.5 convolution_bitcast_fusion.2
  612.9 77.9 %reduce-scatter.14.cloned.1.call-done = f32[32,16,1120]{2,1,0:T(8,128)} async-done(((f32[32,64,1120]{2,1,0:T(8,128)}), f32[32,16,1120]{2,1,0:T(8,128)}) %reduce-scatter.14.cloned.1.call-update) | async-done | bytes 2293776 | tf_op jit(solution)/shard_map/reduce_scatter | solution.py:236
  695.5 37.6 %all-gather.7.cloned.1.call-done = bf16[32,64,1120]{2,1,0:T(8,128)(2,1)} async-done(((bf16[32,16,1120]{2,1,0:T(8,128)(2,1)}), bf16[32,64,1120]{2,1,0:T(8,128)(2,1)}) %all-gather.7.cloned.1.call-update) | async-done | bytes 4587536 | tf_op jit(solution)/shard_map/all_gather | solution.py:106
  733.1 9.3 add_convert_fusion.2
  744.8 3.9 copy.70
  748.7 3.9 copy.69
  752.6 3.9 copy.68
  756.5 7.6 fusion.146
  764.1 4.6 fusion.52
  768.7 5.5 fusion.64
  774.7 78.2 %reduce-scatter.6.cloned.1.call-done = f32[32,16,1120]{2,1,0:T(8,128)} async-done(((f32[32,64,1120]{2,1,0:T(8,128)}), f32[32,16,1120]{2,1,0:T(8,128)}) %reduce-scatter.6.cloned.1.call-update) | async-done | bytes 2293776 | tf_op jit(solution)/shard_map/reduce_scatter | solution.py:128
  852.9 4.1 fusion.136
  857.4 5.3 fusion.59
  864.5 37.6 %all-gather.9.cloned.1.call-done = bf16[32,64,1120]{2,1,0:T(8,128)(2,1)} async-done(((bf16[32,16,1120]{2,1,0:T(8,128)(2,1)}), bf16[32,64,1120]{2,1,0:T(8,128)(2,1)}) %all-gather.9.cloned.1.call-update) | async-done | bytes 4587536 | tf_op jit(solution)/shard_map/all_gather | solution.py:131
  902.1 9.6 convert_reduce_fusion.3
  911.7 28.2 %convolution_convert_fusion = bf16[32,64,1120]{2,1,0:T(8,128)(2,1)} fusion(f32[32,64,1120]{2,1,0:T(8,128)S(1)} %get-tuple-element.106, u32[64,1120]{1,0:T(8,128)S(1)} %get-tuple-element.19, u32[64,1120]{1,0:T(8,128)S(1)} %get-tuple-element.18, f32[1120]{0:T(1024)S(1)} %copy-done.44, bf16[1120,1120]{1,0:T(8,128)(2,1)S(1)} %copy-done.61), kind=kOutput, calls=%fused_computation.62 | convolution fusion | flops 5298585600 | bytes 16849280 | tf_op jit(solution)/shard_map/ocf,fd->ocd/dot_general | solution.py:137
  940.1 12.4 convolution_bitcast_fusion.1
  952.5 17.4 %convolution_bitcast_fusion = f32[1120,1120]{1,0:T(8,128)} fusion(bf16[32,64,1120]{2,1,0:T(8,128)(2,1)} %all-gather.11.cloned.1.call-done, f32[32,64,1120]{2,1,0:T(8,128)} %fusion.5, f32[32,64,1120]{2,1,0:T(8,128)} %copy-done.15, f32[1120]{0:T(1024)S(1)} %copy-done.44), kind=kOutput, calls=%fused_computation.59 | convolution fusion | flops 5147197440 | bytes 27959680 | tf_op jit(solution)/shard_map/ocf,ocd->fd/dot_general | solution.py:179
  972.9 9.0 fusion.28
  981.9 10.2 fusion.78
  999.3 5.2 broadcast_select_fusion.2
  1004.5 117.2 %all_to_all.20 = bf16[64,16,1120]{2,1,0:T(8,128)(2,1)} all-to-all(bf16[64,16,1120]{2,1,0:T(8,128)(2,1)S(1)} %get-tuple-element.77), channel_id=1, replica_groups=mesh['dp'=8,'tp'=4] {'dp'}, dimensions={0} | all-to-all | bytes 4587520 | tf_op jit(solution)/shard_map/all_to_all | solution.py:265
  1121.7 3.7 all-to-all-start.1
  1129.8 128.1 %all-reduce.4 = (f32[2,280]{1,0:T(2,128)}, f32[1120]{0:T(1024)}) all-reduce(f32[2,280]{1,0:T(2,128)S(1)} %pad_maximum_fusion.5, f32[1120]{0:T(1024)S(1)} %copy-done.51), channel_id=1, replica_groups=mesh['dp'=8,'tp'=4] {'dp'}, use_global_device_ids=true, to_apply=%region_33.34 | all-reduce | flops 1680 | bytes 13440 | tf_op jit(solution)/shard_map/psum | solution.py:247
  1259.1 42.9 %all-reduce.3 = (f32[2,1120]{1,0:T(2,128)}, f32[2,1120]{1,0:T(2,128)}, f32[2,1120]{1,0:T(2,128)}) all-reduce(f32[2,1120]{1,0:T(2,128)S(1)} %pad_maximum_fusion.1, f32[2,1120]{1,0:T(2,128)S(1)} %pad_maximum_fusion.2, f32[2,1120]{1,0:T(2,128)S(1)} %pad_maximum_fusion.3), channel_id=1, replica_groups=mesh['dp'=8,'tp'=4] {'dp','tp'}, use_global_device_ids=true, to_apply=%region_27.28 | all-reduce | flops 6720 | bytes 53760 | tf_op jit(solution)/shard_map/psum | solution.py:250
  1301.9 3.9 gather_fusion.10
  1308.0 5.0 broadcast_select_fusion.4
  1313.1 260.6 %all-reduce.11.cloned.1.call-done = (f32[1120,3,280]{0,2,1:T(8,128)}, f32[280,1120]{1,0:T(8,128)}, f32[1120,1120]{1,0:T(8,128)}, f32[1120,1120]{1,0:T(8,128)}) async-done(((f32[1120,3,280]{0,2,1:T(8,128)}, f32[280,1120]{1,0:T(8,128)}, f32[1120,1120]{1,0:T(8,128)}, f32[1120,1120]{1,0:T(8,128)}), (f32[1120,3,280]{0,2,1:T(8,128)}, f32[280,1120]{1,0:T(8,128)}, f32[1120,1120]{1,0:T(8,128)}, ...) | async-done | bytes 15052816 | tf_op jit(solution)/shard_map/psum | solution.py:247
  1573.7 125.9 %all-reduce.9.cloned.1.call-done = f32[32,1120]{1,0:T(8,128)} async-done(((f32[32,1120]{1,0:T(8,128)}), f32[32,1120]{1,0:T(8,128)}) %all-reduce.9.cloned.1.call-update) | async-done | bytes 143376 | tf_op jit(solution)/shard_map/psum | solution.py:250
  1699.5 4.4 copy.109
  (261 shorter events, 86.9 us)
Async XLA Ops:
  7.2 366.3 %copy-start = (bf16[1120,1120]{1,0:T(8,128)(2,1)S(1)}, bf16[1120,1120]{1,0:T(8,128)(2,1)}, u32[]{:S(2)}) copy-start(bf16[1120,1120]{1,0:T(8,128)(2,1)} %param.24) | copy-start | bytes 7526404
  40.4 55.8 %all-to-all-start.2 = ((bf16[64,16,1120]{2,1,0:T(8,128)(2,1)}), bf16[64,16,1120]{2,1,0:T(8,128)(2,1)}, u32[]{:S(2)}, u32[]{:S(2)}) async-start(bf16[64,16,1120]{2,1,0:T(8,128)(2,1)} %get-tuple-element.97), calls=%async_computation.4 | async-start | bytes 4718592 | tf_op jit(solution)/shard_map/all_to_all | solution.py:71
  44.8 122.0 %all-gather.11.cloned.1.call-start = ((), (), s32[]{:S(2)}) async-start(), calls=%async_computation.13 | async-start | bytes 5898240 | tf_op jit(solution)/shard_map/all_gather | solution.py:162
  46.5 474.3 %copy-start.31 = (f32[32,16]{1,0:T(8,128)}, f32[32,16]{1,0:T(8,128)S(1)}, u32[]{:S(2)}) copy-start(f32[32,16]{1,0:T(8,128)S(1)} %compare_convert_fusion) | copy-start | bytes 6148
  102.1 5.3 copy-start.48
  102.1 5.3 copy-start.49
  102.2 5.4 copy-start.37
  102.2 57.7 %all-to-all-start = ((bf16[64,16,1120]{2,1,0:T(8,128)(2,1)}), bf16[64,16,1120]{2,1,0:T(8,128)(2,1)}, u32[]{:S(2)}, u32[]{:S(2)}) async-start(bf16[64,16,1120]{2,1,0:T(8,128)(2,1)} %get-tuple-element.98), calls=%async_computation | async-start | bytes 4718592 | tf_op jit(solution)/shard_map/all_to_all | solution.py:70
  106.7 102.5 %all-gather.13.cloned.1.call-start = ((), (), s32[]{:S(2)}) async-start(), calls=%async_computation.14 | async-start | bytes 5898240 | tf_op jit(solution)/shard_map/all_gather | solution.py:106
  107.4 59.3 %copy-start.57 = (s32[32]{0:T(128)}, s32[32]{0:T(128)S(1)}, u32[]{:S(2)}) copy-start(s32[32]{0:T(128)S(1)} %gather_fusion.3) | copy-start | bytes 388
  107.5 63.3 %copy-start.35 = (f32[1120]{0:T(1024)}, f32[1120]{0:T(1024)S(1)}, u32[]{:S(2)}) copy-start(f32[1120]{0:T(1024)S(1)} %get-tuple-element.37) | copy-start | bytes 13444
  107.8 754.9 %copy-start.13 = (f32[32,1120]{1,0:T(8,128)}, f32[32,1120]{1,0:T(8,128)S(1)}, u32[]{:S(2)}) copy-start(f32[32,1120]{1,0:T(8,128)S(1)} %fusion.68) | copy-start | bytes 430084
  172.5 157.8 %reduce-scatter.10.cloned.1.call-start = ((), (), s32[]{:S(2)}) async-start(), calls=%async_computation.15 | async-start | bytes 11796480 | tf_op jit(solution)/shard_map/reduce_scatter | solution.py:128
  172.8 59.8 %copy-start.52 = (pred[64,64]{0,1:T(8,128)(4,1)}, pred[64,64]{0,1:T(8,128)(4,1)S(1)}, u32[]{:S(2)}) copy-start(pred[64,64]{0,1:T(8,128)(4,1)S(1)} %iota_compare_fusion) | copy-start | bytes 12292
  172.9 45.6 %copy-start.54 = (f32[3,280]{1,0:T(4,128)}, f32[3,280]{1,0:T(4,128)S(1)}, u32[]{:S(2)}) copy-start(f32[3,280]{1,0:T(4,128)S(1)} %pad_maximum_fusion.4) | copy-start | bytes 10084
  240.1 6.1 copy-start.22
  251.7 121.8 %all-gather.15.cloned.1.call-start = ((), (), s32[]{:S(2)}) async-start(), calls=%async_computation.16 | async-start | bytes 5898240 | tf_op jit(solution)/shard_map/all_gather | solution.py:131
  253.0 609.7 %copy-start.29 = (f32[1120]{0:T(1024)}, f32[1120]{0:T(1024)S(1)}, u32[]{:S(2)}) copy-start(f32[1120]{0:T(1024)S(1)} %get-tuple-element.34) | copy-start | bytes 13444
  335.9 179.5 %reduce-scatter.12.cloned.1.call-start = ((), (), s32[]{:S(2)}) async-start(), calls=%async_computation.17 | async-start | bytes 11796480 | tf_op jit(solution)/shard_map/reduce_scatter | solution.py:191
  336.2 71.8 %copy-start.43 = (f32[1120]{0:T(1024)}, f32[1120]{0:T(1024)S(1)}, u32[]{:S(2)}) copy-start(f32[1120]{0:T(1024)S(1)} %convert_element_type.195) | copy-start | bytes 13444
  386.7 21.3 %copy-start.60 = (bf16[1120,1120]{1,0:T(8,128)(2,1)S(1)}, bf16[1120,1120]{1,0:T(8,128)(2,1)}, u32[]{:S(2)}) copy-start(bf16[1120,1120]{1,0:T(8,128)(2,1)} %param.26) | copy-start | bytes 7526404
  436.8 124.6 %all-gather.17.cloned.1.call-start = ((), (), s32[]{:S(2)}) async-start(), calls=%async_computation.18 | async-start | bytes 5898240 | tf_op jit(solution)/shard_map/all_gather | solution.py:195
  523.7 167.1 %reduce-scatter.14.cloned.1.call-start = ((), (), s32[]{:S(2)}) async-start(), calls=%async_computation.19 | async-start | bytes 11796480 | tf_op jit(solution)/shard_map/reduce_scatter | solution.py:236
  567.6 4.1 copy-start.34
  571.7 6.2 copy-start.23
  571.7 6.2 copy-start.24
  571.7 10.4 slice-start
  578.0 4.2 slice-start.1
  612.2 81.6 %copy-start.36 = (f32[1120]{0:T(1024)S(1)}, f32[1120]{0:T(1024)}, u32[]{:S(2)}) copy-start(f32[1120]{0:T(1024)} %copy-done.35) | copy-start | bytes 13444
  612.2 120.9 %all-gather.7.cloned.1.call-start = ((), (), s32[]{:S(2)}) async-start(), calls=%async_computation.9 | async-start | bytes 5898240 | tf_op jit(solution)/shard_map/all_gather | solution.py:106
  693.8 39.3 %copy-start.55 = (f32[3,280]{1,0:T(4,128)S(1)}, f32[3,280]{1,0:T(4,128)}, u32[]{:S(2)}) copy-start(f32[3,280]{1,0:T(4,128)} %copy-done.54) | copy-start | bytes 10084
  695.5 157.4 %reduce-scatter.6.cloned.1.call-start = ((), (), s32[]{:S(2)}) async-start(), calls=%async_computation.10 | async-start | bytes 11796480 | tf_op jit(solution)/shard_map/reduce_scatter | solution.py:128
  752.6 3.9 copy-start.53
  774.3 127.8 %all-gather.9.cloned.1.call-start = ((), (), s32[]{:S(2)}) async-start(), calls=%async_computation.11 | async-start | bytes 5898240 | tf_op jit(solution)/shard_map/all_gather | solution.py:131
  852.9 4.1 copy-start.5
  852.9 4.1 copy-start.8
  852.9 4.5 copy-start.9
  862.7 39.4 %copy-start.44 = (f32[1120]{0:T(1024)S(1)}, f32[1120]{0:T(1024)}, u32[]{:S(2)}) copy-start(f32[1120]{0:T(1024)} %copy-done.43) | copy-start | bytes 13444
  864.5 129.9 %reduce-scatter.8.cloned.1.call-start = ((), (), s32[]{:S(2)}) async-start(), calls=%async_computation.12 | async-start | bytes 5898240 | tf_op jit(solution)/shard_map/reduce_scatter | solution.py:140
  902.1 9.6 copy-start.61
  939.9 633.8 %all-reduce.11.cloned.1.call-start = ((), (), s32[]{:S(2)}) async-start(), calls=%async_computation.21 | async-start | bytes 30965760 | tf_op jit(solution)/shard_map/psum | solution.py:247
  940.1 29.8 %slice-start.4 = ((s8[4718592]{0:T(1024)(128)(4,1)}), s8[4194304]{0:T(1024)(128)(4,1)S(1)}, s32[]{:S(2)}) async-start(s8[4718592]{0:T(1024)(128)(4,1)} %bitcast.226), calls=%async_computation.26 | async-start | bytes 8388608
  952.5 17.4 %copy-start.26 = (bf16[32,5,56,64]{3,2,1,0:T(8,128)(2,1)S(1)}, bf16[32,5,56,64]{3,2,1,0:T(8,128)(2,1)}, u32[]{:S(2)}) copy-start(bf16[32,5,56,64]{3,2,1,0:T(8,128)(2,1)} %copy-done.25) | copy-start | bytes 3440644
  952.5 17.4 %slice-start.5 = ((s8[4718592]{0:T(1024)(128)(4,1)}), s8[524288]{0:T(1024)(128)(4,1)S(1)}, s32[]{:S(2)}) async-start(s8[4718592]{0:T(1024)(128)(4,1)} %bitcast.226), calls=%async_computation.27 | async-start | bytes 1048576
  981.8 10.3 copy-start.12
  981.9 12.5 copy-start.6
  981.9 12.5 copy-start.14
  981.9 12.5 copy-start.30
  981.9 12.5 copy-start.32
  981.9 12.5 copy-start.39
  1121.7 5.2 copy-start.40
  1121.7 5.2 copy-start.41
  1121.7 5.2 copy-start.42
  1121.7 184.1 %all-to-all-start.1 = ((bf16[64,16,1120]{2,1,0:T(8,128)(2,1)}), bf16[64,16,1120]{2,1,0:T(8,128)(2,1)S(1)}, u32[]{:S(2)}, u32[]{:S(2)}) async-start(bf16[64,16,1120]{2,1,0:T(8,128)(2,1)} %get-tuple-element.78), calls=%async_computation.3 | async-start | bytes 4718592 | tf_op jit(solution)/shard_map/all_to_all | solution.py:264
  1125.5 4.4 copy-start.51
  1125.5 132.5 %copy-start.47 = (f32[1120]{0:T(1024)S(1)}, f32[1120]{0:T(1024)}, u32[]{:S(2)}) copy-start(f32[1120]{0:T(1024)} %get-tuple-element.23) | copy-start | bytes 13444
  1125.5 132.5 %copy-start.46 = (f32[1120]{0:T(1024)S(1)}, f32[1120]{0:T(1024)}, u32[]{:S(2)}) copy-start(f32[1120]{0:T(1024)} %get-tuple-element.24) | copy-start | bytes 13444
  1125.5 132.5 %copy-start.45 = (f32[1120]{0:T(1024)S(1)}, f32[1120]{0:T(1024)}, u32[]{:S(2)}) copy-start(f32[1120]{0:T(1024)} %get-tuple-element.25) | copy-start | bytes 13444
  1125.5 132.5 %copy-start.28 = (f32[32,1120]{1,0:T(8,128)S(1)}, f32[32,1120]{1,0:T(8,128)}, u32[]{:S(2)}) copy-start(f32[32,1120]{1,0:T(8,128)} %get-tuple-element.22) | copy-start | bytes 430084
  1125.5 132.5 %copy-start.58 = (s32[32]{0:T(128)S(1)}, s32[32]{0:T(128)}, u32[]{:S(2)}) copy-start(s32[32]{0:T(128)} %copy-done.57) | copy-start | bytes 388
  1125.5 574.0 %all-reduce.9.cloned.1.call-start = ((), (), s32[]{:S(2)}) async-start(), calls=%async_computation.20 | async-start | bytes 294912 | tf_op jit(solution)/shard_map/psum | solution.py:250
  1699.5 4.4 copy-start.27
  1699.5 5.5 copy-start.21
  1704.0 4.3 slice-start.2
  (21 other events, 52.9 us)
Sparse Core Ops, SparseCore 0:
  102.2 36.2 all-gather.10
  172.6 36.4 all-gather.12
  251.8 78.4 reduce-scatter.9
  336.0 37.4 all-gather.14
  436.9 78.4 reduce-scatter.11
  523.8 37.4 all-gather.16
  612.3 78.4 reduce-scatter.13
  695.6 37.4 all-gather.6
  774.4 78.4 reduce-scatter.5
  864.6 37.4 all-gather.8
  940.0 47.8 reduce-scatter.7
  994.4 579.2 all-reduce.10
  1579.8 119.7 all-reduce.8
where the time goes:
time: 1730 us; the launch traced here: 1720 us
  waiting for transfers between devices  987 us (57%)
  blocking collectives  301 us (17%)
  matrix products  203 us (12%)
  other arithmetic  99.3 us (6%)
  local copies, waits for them, and re-layouts  98.6 us (6%)
    psum x1, waiting for transfers between devices, on_device(): lax.psum((qkv_grad, qv_bias_grad, out_weight_grad, up_grad, up_bias_grad,...  261 us
    reduce_scatter x2, waiting for transfers between devices, forward_pass(): lax.psum_scatter(attn_part, 'tp', scatter_dimension=1, tiled=True)  155 us
    psum x1, blocking collectives, on_device(): lax.psum((qkv_grad, qv_bias_grad, out_weight_grad, up_grad, up_bias_grad,...  128 us
    psum x1, waiting for transfers between devices, on_device(): lax.psum((gain_local, shift_local, bias_local, table_local), ('dp', 'tp'))  126 us
    all_to_all x1, blocking collectives, on_device(): lax.all_to_all(send_start, 'dp', split_axis=0, concat_axis=0, tiled=True)  117 us
    reduce_scatter x1, waiting for transfers between devices, on_device(): lax.psum_scatter(second_part, 'tp', scatter_dimension=1, tiled=True)  78.5 us
    reduce_scatter x1, waiting for transfers between devices, on_device(): lax.psum_scatter(first_part, 'tp', scatter_dimension=1, tiled=True)  77.9 us
    all_gather x2, waiting for transfers between devices, forward_pass(): second_full = lax.all_gather(normed_second, 'tp', axis=1, tiled=True)  74.9 us
  transfers between devices with their start and end apart: 16, of which 13 were waited for; matrix products, arithmetic and copies ran while one was open for 5% of the time, Pallas kernels for 0%

commit v1 on v0

v1 whole, which is shorter than its diff:
```python
import functools
import math

import jax
import jax.numpy as jnp
from jax import lax
from jax.experimental import pallas as pl
from jax.experimental.pallas import tpu as pltpu
from jax.sharding import PartitionSpec as P

HEAD_DIM = 56
EPSILON = 1e-05
BLOCK = 256
META_BLOCKS = 8
TILE = 16
F32 = jnp.float32
LOW = jnp.bfloat16
VMEM_BYTES = 56 * 1024 * 1024
BYTES_PER_US = 3_690_000

NBLK, NCELL, HALF, QUARTER, TILE_SRC, TILE_SET, TILE_LEN, TILE_DST, CELL_OFF, CELL_ROWS, META = 0, 1, 2, 3, 8, 136, 264, 392, 520, 552, 584


def swap(value, axis, bit):
    count = lax.axis_size(axis)
    if value.ndim == 2 and value.shape[0] % TILE == 0:
        chunk = TILE if value.shape[0] // TILE % 128 else 2 * TILE
        tiled = value.reshape(value.shape[0] // chunk, chunk, value.shape[1])
        return swap(tiled, axis, bit).reshape(value.shape)
    return lax.ppermute(value, axis, [(i, i ^ bit) for i in range(count)])


CHUNKS = 4


def swap_cores(parts):
    return tuple(swap(part, "tp", 1) for part in parts)


class Sequence:
    def __init__(self):
        self.last = ()

    def then(self, *values):
        if not self.last:
            return values
        return lax.optimization_barrier((*values, *self.last))[: len(values)]

    def done(self, *values):
        self.last = (values[-1],)

    def step(self, *values):
        values = self.then(*values)
        self.last = (values[-1],)
        return values


def dot(a, b):
    return jnp.dot(a, b, preferred_element_type=F32)


def dot_nt(a, b):
    return lax.dot_general(a, b, (((1,), (1,)), ((), ())), preferred_element_type=F32)


def dot_tn(a, b):
    return lax.dot_general(a, b, (((0,), (0,)), ((), ())), preferred_element_type=F32)


def row_norm(rows):
    center = rows - jnp.mean(rows, axis=-1, keepdims=True)
    spread = jnp.mean(center * center, axis=-1, keepdims=True)
    scale = lax.rsqrt(spread + EPSILON)
    return center * scale, scale


def norm_back(grad, unit, scale, gain):
    scaled = grad * gain
    first = jnp.mean(scaled, axis=-1, keepdims=True)
    second = jnp.mean(scaled * unit, axis=-1, keepdims=True)
    return scale * (scaled - first - unit * second)


def whole(shape):
    zeros = (0,) * len(shape)
    return pl.BlockSpec(shape, lambda i, meta: zeros, pipeline_mode=pl.Buffered(1))


def rows_spec(width):
    return pl.BlockSpec((BLOCK, width), lambda i, meta: (jnp.minimum(i, meta[NBLK] - 1), 0))


PART_BLOCKS = META_BLOCKS // CHUNKS


def part_specs(width):
    def index(at, i, meta):
        return jnp.clip(jnp.minimum(i, meta[NBLK] - 1) - at * PART_BLOCKS, 0, PART_BLOCKS - 1), 0

    return [pl.BlockSpec((BLOCK, width), functools.partial(index, at)) for at in range(CHUNKS)]


def part_outs(width):
    def index(at, i, meta):
        return jnp.clip(i - at * PART_BLOCKS, 0, PART_BLOCKS - 1), 0

    return tuple(pl.BlockSpec((BLOCK, width), functools.partial(index, at)) for at in range(CHUNKS))


def part_shapes(rows, width):
    return (jax.ShapeDtypeStruct((rows // CHUNKS, width), LOW),) * CHUNKS


def add_parts(step, mine, far, rows):
    for at, (a, b) in enumerate(zip(mine, far)):

        @pl.when(step // PART_BLOCKS == at)
        def _():
            rows[...] = a[...].astype(F32) + b[...].astype(F32)


def put_part(step, value, parts):
    for at, part in enumerate(parts):

        @pl.when(step // PART_BLOCKS == at)
        def _():
            part[...] = value


def rows_out(width):
    return pl.BlockSpec((BLOCK, width), lambda i, meta: (i, 0))


ANYWHERE = pl.BlockSpec(memory_space=pl.ANY)


def call(kernel, meta, operands, in_specs, out_shape, out_specs, grid, scratch=(), cost=5, name=None):
    return pl.pallas_call(
        kernel,
        grid_spec=pltpu.PrefetchScalarGridSpec(
            num_scalar_prefetch=1,
            grid=grid,
            in_specs=in_specs,
            out_specs=out_specs,
            scratch_shapes=list(scratch),
        ),
        out_shape=out_shape,
        compiler_params=pltpu.CompilerParams(
            dimension_semantics=("arbitrary",) * len(grid), vmem_limit_bytes=VMEM_BYTES
        ),
        cost_estimate=pl.CostEstimate(flops=0, bytes_accessed=cost * BYTES_PER_US, transcendentals=0),
        name=name,
    )(meta, *operands)


def load_tiles(sources, tiles, sems, count):
    copies = [
        pltpu.make_async_copy(source, tiles.at[pl.ds(at * count, count)], sems.at[at])
        for at, source in enumerate(sources)
    ]
    for copy in copies:
        copy.start()
    for copy in copies:
        copy.wait()


def begin_kernel(count, meta, a0, a1, a2, a3, table, gain, shift, weight, bias, start, normed, projected, tiles, sems):
    step = pl.program_id(0)

    @pl.when(step == 0)
    def _():
        load_tiles((a0, a1, a2, a3), tiles, sems, count)

    @pl.when(step < meta[NBLK])
    def _():
        for j in range(BLOCK // TILE):
            at = step * (BLOCK // TILE) + j
            tile = tiles[meta[TILE_SRC + at]].astype(F32)
            start[j * TILE : (j + 1) * TILE, :] = tile + table[pl.ds(meta[TILE_SET + at], 1), :]
        unit, _ = row_norm(start[...])
        low = (unit * gain[...] + shift[...]).astype(LOW)
        normed[...] = low
        projected[...] = (dot(low, weight[...]) + bias[...]).astype(LOW)

    @pl.when(step >= meta[NBLK])
    def _():
        projected[...] = jnp.zeros_like(projected)


def project_kernel(meta, normed, eighths, bias, projected, weight, sems):
    step = pl.program_id(0)

    @pl.when(step == 0)
    def _():
        load_eighths(eighths, [weight], sems)

    @pl.when(step < meta[NBLK])
    def _():
        projected[...] = (dot(normed[...], weight[...]) + bias[...]).astype(LOW)

    @pl.when(step >= meta[NBLK])
    def _():
        projected[...] = jnp.zeros_like(projected)


def head_masks(cell, heads, shard):
    lane = lax.broadcasted_iota(jnp.int32, (cell, shard), 1)
    return [(lane >= h * HEAD_DIM) & (lane < (h + 1) * HEAD_DIM) for h in range(heads)]


def spread_heads(rows, masks, heads, low, high):
    part = rows[:, low:high]
    zero = jnp.zeros_like(part)
    return jnp.concatenate([jnp.where(masks[h][:, low:high], part, zero) for h in heads], axis=0)


def head_groups(heads, shard):
    groups = []
    at = 0
    while at < heads:
        end = min(at + 4, heads)
        low = at * HEAD_DIM // 128 * 128
        high = min(-(-end * HEAD_DIM // 128) * 128, shard)
        groups.append((tuple(range(at, end)), low, high))
        at = end
    return groups


def attention_kernel(heads, shard, cell, meta, projected, context, attend):
    context[...] = jnp.zeros_like(context)
    masks = head_masks(cell, heads, shard)
    scale = 1.0 / math.sqrt(HEAD_DIM)
    row = lax.broadcasted_iota(jnp.int32, (cell, 2 * cell), 0)
    lane = lax.broadcasted_iota(jnp.int32, (cell, 2 * cell), 1)
    left = lane < cell
    causal = row >= jnp.where(left, lane, lane - cell)

    def one(index):
        at = pl.multiple_of(meta[CELL_OFF + index] * TILE, TILE)
        queries = projected[pl.ds(at, cell), 0:shard]
        keys = projected[pl.ds(at, cell), shard : 2 * shard]
        values = projected[pl.ds(at, cell), 2 * shard : 3 * shard]
        total = None
        for group, low, high in head_groups(heads, shard):
            spread = spread_heads(keys, masks, group, low, high)
            scores = dot_nt(queries[:, low:high], spread) * scale
            parts = []
            for pair in range(0, len(group), 2):
                if pair + 1 < len(group):
                    both = jnp.where(causal, scores[:, pair * cell : (pair + 2) * cell], -1e30)
                    top_left = jnp.max(jnp.where(left, both, -1e30), axis=1, keepdims=True)
                    top_right = jnp.max(jnp.where(left, -1e30, both), axis=1, keepdims=True)
                    weights = jnp.exp(both - jnp.where(left, top_left, top_right))
                    sum_left = jnp.sum(jnp.where(left, weights, 0.0), axis=1, keepdims=True)
                    sum_right = jnp.sum(jnp.where(left, 0.0, weights), axis=1, keepdims=True)
                    parts.append((weights * jnp.where(left, 1.0 / sum_left, 1.0 / sum_right)).astype(LOW))
                else:
                    single = jnp.where(causal[:, :cell], scores[:, pair * cell :], -1e30)
                    weights = jnp.exp(single - jnp.max(single, axis=1, keepdims=True))
                    parts.append((weights * (1.0 / jnp.sum(weights, axis=1, keepdims=True))).astype(LOW))
            probs = jnp.concatenate(parts, axis=1) if len(parts) > 1 else parts[0]
            first = group[0] * cell
            attend[index, :, first : first + len(group) * cell] = probs
            part = dot(probs, spread_heads(values, masks, group, low, high))
            if total is None:
                total = jnp.pad(part, ((0, 0), (low, shard - high))) if high - low < shard else part
            else:
                total = total + jnp.pad(part, ((0, 0), (low, shard - high)))
        context[pl.ds(at, cell), :] = total.astype(LOW)

    def body(step, carry):
        one(2 * step)
        one(2 * step + 1)
        return carry

    lax.fori_loop(0, (meta[NCELL] + 1) // 2, body, 0)


def attention_back_kernel(heads, shard, cell, meta, projected, attend, context_grad, result, sums):
    result[...] = jnp.zeros_like(result)
    sums[...] = jnp.zeros_like(sums)
    masks = head_masks(cell, heads, shard)
    scale = 1.0 / math.sqrt(HEAD_DIM)
    row = lax.broadcasted_iota(jnp.int32, (cell, shard), 0)
    left = lax.broadcasted_iota(jnp.int32, (cell, 2 * cell), 1) < cell

    def fold(stacked, group, low, high):
        total = None
        for place, h in enumerate(group):
            part = jnp.where(masks[h][:, low:high], stacked[place * cell : (place + 1) * cell, :], 0.0)
            total = part if total is None else total + part
        return total

    def widen(part, low, high):
        return jnp.pad(part, ((0, 0), (low, shard - high))) if high - low < shard else part

    def one(index):
        at = pl.multiple_of(meta[CELL_OFF + index] * TILE, TILE)
        queries = projected[pl.ds(at, cell), 0:shard]
        keys = projected[pl.ds(at, cell), shard : 2 * shard]
        values = projected[pl.ds(at, cell), 2 * shard : 3 * shard]
        grads = context_grad[pl.ds(at, cell), :]
        grads = jnp.where(row < meta[CELL_ROWS + index], grads, jnp.zeros_like(grads))
        query_total = key_total = value_total = None
        for group, low, high in head_groups(heads, shard):
            first = group[0] * cell
            probs = attend[index, :, first : first + len(group) * cell]
            attend_grad = dot_nt(grads[:, low:high], spread_heads(values, masks, group, low, high))
            parts = []
            for pair in range(0, len(group), 2):
                if pair + 1 < len(group):
                    span = slice(pair * cell, (pair + 2) * cell)
                    weights = probs[:, span].astype(F32)
                    both = attend_grad[:, span]
                    product = weights * both
                    sum_left = jnp.sum(jnp.where(left, product, 0.0), axis=1, keepdims=True)
                    sum_right = jnp.sum(jnp.where(left, 0.0, product), axis=1, keepdims=True)
                    parts.append((product - weights * jnp.where(left, sum_left, sum_right)).astype(LOW))
                else:
                    span = slice(pair * cell, (pair + 1) * cell)
                    weights = probs[:, span].astype(F32)
                    product = weights * attend_grad[:, span]
                    total = jnp.sum(product, axis=1, keepdims=True)
                    parts.append((product - weights * total).astype(LOW))
            score_grad = jnp.concatenate(parts, axis=1) if len(parts) > 1 else parts[0]
            query_part = dot(score_grad, spread_heads(keys, masks, group, low, high)) * scale
            key_part = fold(dot_tn(score_grad, queries[:, low:high]), group, low, high) * scale
            value_part = fold(dot_tn(probs, grads[:, low:high]), group, low, high)
            query_part, key_part, value_part = (widen(p, low, high) for p in (query_part, key_part, value_part))
            if query_total is None:
                query_total, key_total, value_total = query_part, key_part, value_part
            else:
                query_total, key_total, value_total = (
                    query_total + query_part,
                    key_total + key_part,
                    value_total + value_part,
                )
        for place, part in enumerate((query_total, key_total, value_total)):
            low_part = part.astype(LOW)
            result[pl.ds(at, cell), place * shard : (place + 1) * shard] = low_part
            sums[place : place + 1, :] += jnp.sum(low_part.astype(F32), axis=0, keepdims=True)

    def body(step, carry):
        one(2 * step)
        one(2 * step + 1)
        return carry

    lax.fori_loop(0, (meta[NCELL] + 1) // 2, body, 0)


def out_project_kernel(meta, a, b, weight_a, weight_b, *parts):
    step = pl.program_id(0)

    @pl.when(step < meta[NBLK])
    def _():
        put_part(step, (dot(a[...], weight_a[...]) + dot(b[...], weight_b[...])).astype(LOW), parts)


def first_part_kernel(meta, a, b, weight_a, eighths, *refs):
    step = pl.program_id(0)
    *parts, weight_b, sems = refs

    @pl.when(step == 0)
    def _():
        load_eighths(eighths, [weight_b], sems)

    @pl.when(step < meta[NBLK])
    def _():
        put_part(step, (dot_nt(a[...], weight_a[...]) + dot_nt(b[...], weight_b[...])).astype(LOW), parts)


def gelu_pair(hidden):
    chance = 0.5 * (1.0 + lax.erf(hidden * (1.0 / math.sqrt(2.0))))
    slope = chance + hidden * (jnp.exp(-0.5 * hidden * hidden) * (1.0 / math.sqrt(2.0 * math.pi)))
    return hidden * chance, slope


def mlp_block(second, grad, up, bias, down, active, hidden_grad, bias_grad):
    hidden = dot(second, up[...]) + bias[...]
    value, slope = gelu_pair(hidden)
    low = value.astype(LOW)
    active[...] = low
    back = (slope * dot_nt(grad, down[...])).astype(LOW)
    hidden_grad[...] = back
    bias_grad[0:1, :] += jnp.sum(back.astype(F32), axis=0, keepdims=True)
    return dot(low, down[...]), dot_nt(back, up[...])


def mlp_first_kernel(
    count, meta, start, p0, p1, p2, p3, f0, f1, f2, f3, bias_row, gain, shift, a0, a1, a2, a3, up, up_bias, down,
    middle, second, grad, active, hidden_grad, branch, second_grad, bias_grad, tiles, sems, sums,
):
    step = pl.program_id(0)

    @pl.when(step == 0)
    def _():
        load_tiles((a0, a1, a2, a3), tiles, sems, count)
        bias_grad[...] = jnp.zeros_like(bias_grad)

    @pl.when(step < meta[NBLK])
    def _():
        add_parts(step, (p0, p1, p2, p3), (f0, f1, f2, f3), sums)
        inner = lax.broadcasted_iota(jnp.int32, (TILE, 1), 0)
        for j in range(BLOCK // TILE):
            at = step * (BLOCK // TILE) + j
            tile = tiles[meta[TILE_SRC + at]]
            grad[j * TILE : (j + 1) * TILE, :] = jnp.where(
                inner < meta[TILE_LEN + at], tile, jnp.zeros_like(tile)
            )
        rows = start[...] + sums[...] + bias_row[...]
        middle[...] = rows
        unit, _ = row_norm(rows)
        low = (unit * gain[...] + shift[...]).astype(LOW)
        second[...] = low
        out, back = mlp_block(low, grad[...], up, up_bias, down, active, hidden_grad, bias_grad)
        branch[...] = out.astype(LOW)
        second_grad[...] = back.astype(LOW)


def mlp_second_kernel(
    meta, second, grad, branch_in, second_grad_in, eighths, up_bias,
    active, hidden_grad, b0, b1, b2, b3, g0, g1, g2, g3, bias_grad, up, down, sems,
):
    step = pl.program_id(0)

    @pl.when(step == 0)
    def _():
        load_eighths(eighths, [up, down], sems)
        bias_grad[...] = jnp.zeros_like(bias_grad)

    @pl.when(step < meta[NBLK])
    def _():
        out, back = mlp_block(second[...], grad[...], up, up_bias, down, active, hidden_grad, bias_grad)
        put_part(step, (out + branch_in[...].astype(F32)).astype(LOW), (b0, b1, b2, b3))
        put_part(step, (back + second_grad_in[...].astype(F32)).astype(LOW), (g0, g1, g2, g3))


def weight_grad_kernel(pairs, meta, *refs):
    step = pl.program_id(0)
    result, total = refs[2 * pairs :]

    @pl.when(step == 0)
    def _():
        total[...] = jnp.zeros_like(total)

    @pl.when(step < meta[NBLK])
    def _():
        base = 0
        for a, b in zip(refs[: 2 * pairs : 2], refs[1 : 2 * pairs : 2]):
            count = a.shape[1]
            total[base : base + count, :] += dot_tn(a[...], b[...])
            base += count

    @pl.when(step == pl.num_programs(0) - 1)
    def _():
        result[...] = total[...].astype(LOW)


def middle_back_kernel(
    meta, p0, p1, p2, p3, f0, f1, f2, f3, middle, grad, gain, out_a, out_b,
    middle_grad, attn_grad, context_a, context_b, sums, added,
):
    step = pl.program_id(0)

    @pl.when(step == 0)
    def _():
        sums[...] = jnp.zeros_like(sums)

    @pl.when(step < meta[NBLK])
    def _():
        add_parts(step, (p0, p1, p2, p3), (f0, f1, f2, f3), added)
        unit, scale = row_norm(middle[...])
        second_grad = added[...]
        grad_rows = grad[...].astype(F32)
        total = grad_rows + norm_back(second_grad, unit, scale, gain[...])
        middle_grad[...] = total
        low = total.astype(LOW)
        attn_grad[...] = low
        context_a[...] = dot_nt(low, out_a[...]).astype(LOW)
        context_b[...] = dot_nt(low, out_b[...]).astype(LOW)
        for at, rows in enumerate((second_grad * unit, second_grad, total, grad_rows)):
            sums[at : at + 1, :] += jnp.sum(rows, axis=0, keepdims=True)


def scatter_tiles(meta, step, rows, out):
    for j in range(BLOCK // TILE):
        place = meta[TILE_DST + step * (BLOCK // TILE) + j]

        @pl.when(place >= 0)
        def _():
            out[place] = rows[j * TILE : (j + 1) * TILE, :].astype(LOW)


def start_back_kernel(
    meta, p0, p1, p2, p3, f0, f1, f2, f3, start, middle_grad, gain, out, sums, table, rows, added,
):
    step = pl.program_id(0)

    @pl.when(step == 0)
    def _():
        out[...] = jnp.zeros_like(out)
        sums[...] = jnp.zeros_like(sums)
        table[...] = jnp.zeros_like(table)

    @pl.when(step < meta[NBLK])
    def _():
        add_parts(step, (p0, p1, p2, p3), (f0, f1, f2, f3), added)
        unit, scale = row_norm(start[...])
        first_grad = added[...]
        rows[...] = middle_grad[...] + norm_back(first_grad, unit, scale, gain[...])
        for at, value in enumerate((first_grad * unit, first_grad)):
            sums[at : at + 1, :] += jnp.sum(value, axis=0, keepdims=True)
        for j in range(BLOCK // TILE):
            at = meta[TILE_SET + step * (BLOCK // TILE) + j]
            table[pl.ds(at, 1), :] += jnp.sum(rows[j * TILE : (j + 1) * TILE, :], axis=0, keepdims=True)
        scatter_tiles(meta, step, rows, out)


def finish_kernel(meta, middle, p0, p1, p2, p3, f0, f1, f2, f3, bias_row, out, rows):
    step = pl.program_id(0)

    @pl.when(step == 0)
    def _():
        out[...] = jnp.zeros_like(out)

    @pl.when(step < meta[NBLK])
    def _():
        add_parts(step, (p0, p1, p2, p3), (f0, f1, f2, f3), rows)
        rows[...] += middle[...] + bias_row[...]
        inner = lax.broadcasted_iota(jnp.int32, (TILE, 1), 0)
        for j in range(BLOCK // TILE):
            at = step * (BLOCK // TILE) + j
            place = meta[TILE_DST + at]

            @pl.when(place >= 0)
            def _():
                out[place] = jnp.where(
                    inner < meta[TILE_LEN + at], rows[j * TILE : (j + 1) * TILE, :], 0.0
                ).astype(LOW)


def window_size(half):
    return -(-half // (4 * TILE)) * TILE


def window_at(quarter, half):
    size = window_size(half)
    return pl.multiple_of(jnp.minimum(quarter * size, half - size), TILE)


def assemble_kernel(half, meta, p0, p1, p2, p3, out, sems):
    size = window_size(half)
    extra = 4 * size - half

    def each(act):
        for other, piece in enumerate((p0, p1, p2, p3)):
            quarter = meta[QUARTER] ^ other

            @pl.when(quarter < 3)
            def _():
                at = window_at(jnp.minimum(quarter, 2), half)
                act(pltpu.make_async_copy(piece, out.at[pl.ds(at, size)], sems.at[other]))

            @pl.when(quarter == 3)
            def _():
                rest = size - extra
                act(pltpu.make_async_copy(piece.at[pl.ds(extra, rest)], out.at[pl.ds(half - rest, rest)], sems.at[other]))

    each(lambda copy: copy.start())
    each(lambda copy: copy.wait())


def assemble(meta, pieces, half):
    width = pieces[0].shape[1]
    (result,) = call(
        functools.partial(assemble_kernel, half), meta, pieces, [ANYWHERE] * 4,
        (jax.ShapeDtypeStruct((half, width), LOW),), (whole((half, width)),),
        (1,), [pltpu.SemaphoreType.DMA((4,))], 3, "assemble",
    )
    return result


def gather_eighths(piece):
    groups = lax.axis_size("dp")
    spans = [list(range(at, at + 8)) for at in range(0, groups, 8)] if groups > 8 else None
    tiled = piece.reshape(piece.shape[0] // TILE, TILE, piece.shape[1])
    whole_block = lax.all_gather(tiled, "dp", axis=0, tiled=True, axis_index_groups=spans)
    return whole_block.reshape(8 * piece.shape[0], piece.shape[1])


def load_eighths(gathered, scratches, sems):
    copies = []
    for at, scratch in enumerate(scratches):
        half = scratch.shape[0] // 2
        size = window_size(half)
        extra = 4 * size - half
        for group in range(8):
            quarter = (group >> 1) & 3
            skip = extra if quarter == 3 else 0
            begin = (group & 1) * half + min(quarter * size, half - size) + skip
            copies.append(
                pltpu.make_async_copy(
                    gathered.at[pl.ds((group * len(scratches) + at) * size + skip, size - skip)],
                    scratch.at[pl.ds(begin, size - skip)],
                    sems.at[8 * at + group],
                )
            )
    for copy in copies:
        copy.start()
    for copy in copies:
        copy.wait()


def first_sum_kernel(meta, own, far, sent):
    sent[...] = (own[...].astype(F32) + far[...].astype(F32)).astype(LOW)


def first_sum(meta, own, far):
    rows, width = own.shape
    half = rows // 2
    steps = 5 if half % (5 * TILE) == 0 else 4
    block = half // steps
    source = pl.BlockSpec((block, width), lambda i, meta: ((1 - meta[HALF]) * steps + i, 0))
    (sent,) = call(
        first_sum_kernel, meta, (own, far), [source, source], (jax.ShapeDtypeStruct((half, width), LOW),),
        (pl.BlockSpec((block, width), lambda i, meta: (i, 0)),), (steps,), cost=5, name="first_sum",
    )
    return sent


def second_sum_kernel(half, meta, mine, far, arrived, own, s1, s2, s3):
    size = window_size(half)
    for other, out in enumerate((own, s1, s2, s3)):
        at = window_at(meta[QUARTER] ^ other, half)
        rows = pl.ds(at, size)
        total = mine[rows, :].astype(F32) + far[rows, :].astype(F32) + arrived[rows, :].astype(F32)
        out[...] = total.astype(out.dtype)


def second_sum(meta, own, far, arrived):
    half, width = arrived.shape
    size = window_size(half)
    outs = tuple(jax.ShapeDtypeStruct((size, width), kind) for kind in (F32, LOW, LOW, LOW))
    kept = pl.BlockSpec((half, width), lambda i, meta: (meta[HALF], 0), pipeline_mode=pl.Buffered(1))
    return call(
        functools.partial(second_sum_kernel, half), meta, (own, far, arrived), [kept, kept, whole((half, width))],
        outs, (whole((size, width)),) * 4, (1,), cost=4, name="second_sum",
    )


def third_sum_kernel(meta, own, r1, r2, r3, out):
    out[...] = (own[...] + r1[...].astype(F32) + r2[...].astype(F32) + r3[...].astype(F32)).astype(LOW)


def third_sum(meta, own, arrived):
    shape = own.shape
    (result,) = call(
        third_sum_kernel, meta, (own, *arrived), [whole(shape)] * 4,
        (jax.ShapeDtypeStruct(shape, LOW),), (whole(shape),), (1,), (), 3, "third_sum",
    )
    return result


def widen_kernel(parts, meta, mine, far, out):
    share = mine.shape[1] // parts
    for at in range(parts):
        lanes = slice(at * share, (at + 1) * share)
        out[at, meta[HALF]] = mine[:, lanes].astype(F32)
        out[at, 1 - meta[HALF]] = far[:, lanes].astype(F32)


def widen_halves(meta, mine, far, parts):
    half, width = mine.shape
    steps = 5
    block = half // steps
    share = width // parts
    spec = pl.BlockSpec((block, width), lambda i, meta: (i, 0))
    (result,) = call(
        functools.partial(widen_kernel, parts), meta, (mine, far), [spec, spec],
        (jax.ShapeDtypeStruct((parts, 2, half, share), F32),),
        (pl.BlockSpec((parts, 2, block, share), lambda i, meta: (0, 0, i, 0)),),
        (steps,), cost=6, name="widen",
    )
    return result.reshape(parts, 2 * half, share)


def widen_eighths_kernel(meta, gathered, *outs):
    size = gathered.shape[0] // 8
    half = -(-sum(out.shape[0] for out in outs) // (2 * TILE)) * TILE
    for group in range(8):
        quarter = group >> 1
        skip = 4 * size - half if quarter == 3 else 0
        begin = (group & 1) * half + min(quarter * size, half - size) + skip
        base = 0
        for out in outs:
            low, high = max(begin, base), min(begin + size - skip, base + out.shape[0])
            if low < high:
                at = group * size + skip + low - begin
                out[low - base : high - base, :] = gathered[at : at + high - low, :].astype(F32)
            base += out.shape[0]


def widen_eighths(meta, gathered, rows):
    width = gathered.shape[1]
    return call(
        widen_eighths_kernel, meta, (gathered,), [whole(gathered.shape)],
        tuple(jax.ShapeDtypeStruct((count, width), F32) for count in rows),
        tuple(whole((count, width)) for count in rows), (1,), cost=5, name="widen_eighths",
    )


class Reduction:
    def __init__(self, meta, other):
        self.meta = meta
        self.far = swap(other, "tp", 2)

    def arrive(self, order):
        (self.far,) = order.step(self.far)

    def first(self, order, own):
        self.own, self.far = order.then(own, self.far)
        sent = first_sum(self.meta, self.own, self.far)
        order.done(sent)
        self.arrived = swap(sent, "dp", 1)

    def second(self, order):
        (arrived,) = order.then(self.arrived)
        self.half = arrived.shape[0]
        self.own, *sent = second_sum(self.meta, self.own, self.far, arrived)
        order.done(self.own)
        self.parts = [swap(part, "dp", 2 * (at + 1)) for at, part in enumerate(sent)]

    def third(self, order, spread):
        own, *parts = order.then(self.own, *self.parts)
        piece = third_sum(self.meta, own, parts)
        level = 3
        while (1 << level) < lax.axis_size("dp"):
            piece = (piece.astype(F32) + swap(piece, "dp", 1 << level).astype(F32)).astype(LOW)
            level += 1
        order.done(piece)
        if spread:
            self.spread = Spread(self.meta, piece, self.half)
        else:
            self.gathered = gather_eighths(piece)

    def fourth(self, order):
        self.spread.join(order)

    def last_halves(self, order, parts):
        mine, far = order.then(*self.spread.halves())
        result = widen_halves(self.meta, mine, far, parts)
        order.done(result)
        return result

    def last_eighths(self, order, rows):
        (gathered,) = order.then(self.gathered)
        results = widen_eighths(self.meta, gathered, rows)
        order.done(results[0])
        return results


class Spread:
    def __init__(self, meta, piece, half):
        self.meta, self.half = meta, half
        self.pieces = [piece] + [swap(piece, "dp", 2 * other) for other in (1, 2, 3)]

    def join(self, order):
        pieces = order.then(*self.pieces)
        self.mine = assemble(self.meta, pieces, self.half)
        order.done(self.mine)
        self.far = swap(self.mine, "dp", 1)

    def halves(self):
        return self.mine, self.far


def eighth(block):
    half = block.shape[0] // 2
    index = lax.axis_index("dp")
    size = window_size(half)
    at = (index & 1) * half + jnp.minimum(((index >> 1) & 3) * size, half - size)
    return lax.dynamic_slice_in_dim(block, at, size, 0)


def on_device(
    cell_inputs,
    out_grad,
    lengths,
    datasets,
    norm_gain,
    norm_bias,
    qkv_weight,
    qv_bias,
    out_weight,
    out_bias,
    up_weight,
    up_bias,
    down_weight,
    dataset_table,
):
    slots, quarter, width = cell_inputs.shape
    tensor = lax.axis_index("tp")
    chip = tensor // 2
    core = tensor % 2
    blocks_per_cell = lax.axis_size("tp")
    cell = quarter * blocks_per_cell
    shard = qkv_weight.shape[2]
    ff = up_weight.shape[1]
    heads = shard // HEAD_DIM
    kept = (slots - slots // 16) // 2
    tile_cap = 128
    cap = tile_cap * TILE
    grid = (cap // BLOCK,)

    def mine_of(rows):
        pairs = rows.reshape(slots // 2, 2, *rows.shape[1:])[:kept]
        mine = lax.dynamic_index_in_dim(pairs, chip, 1, keepdims=False)
        theirs = lax.dynamic_index_in_dim(pairs, 1 - chip, 1, keepdims=False)
        return mine, theirs

    def send_cells(pair):
        pair = pair.reshape(2, kept, quarter, width)
        mine = lax.dynamic_index_in_dim(pair, chip, 0, keepdims=False)
        theirs = lax.dynamic_index_in_dim(pair, 1 - chip, 0, keepdims=False)
        return mine, swap(theirs, "tp", 2)

    def place_cells(mine, other):
        even = jnp.where(chip == 0, mine, other)
        odd = jnp.where(chip == 0, other, mine)
        both = jnp.stack([even, odd], axis=1).reshape(2 * kept, quarter, width)
        return jnp.pad(both, ((0, slots - 2 * kept), (0, 0), (0, 0)))

    cell_lengths, _ = mine_of(lengths)
    cell_sets, _ = mine_of(datasets)
    cell_tiles = (cell_lengths + TILE - 1) // TILE
    index = jnp.arange(kept, dtype=jnp.int32)
    ends = jnp.sum(jnp.where(index[None, :] <= index[:, None], cell_tiles[None, :], 0), axis=1)
    begins = ends - cell_tiles
    tile_count = ends[-1]
    tile = jnp.arange(tile_cap, dtype=jnp.int32)
    owner = jnp.sum((ends[None, :] <= tile[:, None]).astype(jnp.int32), axis=1)
    live = tile < tile_count
    owned = (owner[:, None] == index[None, :]) & live[:, None]

    def of_owner(values):
        return jnp.sum(jnp.where(owned, values[None, :], 0), axis=1)

    block = tile - of_owner(begins)
    tile_src = jnp.where(live, (block ^ tensor) * kept + owner, 0)
    tile_set = of_owner(cell_sets)
    tile_len = jnp.clip(of_owner(cell_lengths) - block * TILE, 0, TILE) * live
    tile_dst = jnp.where(live & (block % 2 == core), block // 2 * kept + owner, -1)
    cell_count = jnp.sum((cell_lengths > 0).astype(jnp.int32))
    block_count = (tile_count + BLOCK // TILE - 1) // (BLOCK // TILE)
    group = lax.axis_index("dp")
    head = jnp.stack([block_count, cell_count, group & 1, (group >> 1) & 3])

    def widen(values):
        return jnp.pad(values, (0, 32 - kept))

    meta = jnp.concatenate(
        [head, jnp.zeros((4,), jnp.int32), tile_src, tile_set, tile_len, tile_dst, widen(begins), widen(cell_tiles * TILE)]
    ).astype(jnp.int32)

    order = Sequence()
    qkv_own = qkv_weight.reshape(width, 3 * shard)
    vectors = jnp.concatenate([qv_bias.reshape(-1), up_bias])
    in_mine, in_theirs = mine_of(cell_inputs)
    in_other = swap(in_theirs, "tp", 2)
    in_far = swap(in_mine, "tp", 1)
    qkv_piece, mlp_piece, _ = lax.optimization_barrier(
        (eighth(qkv_own), jnp.concatenate([eighth(up_weight), eighth(down_weight)], axis=0), in_theirs)
    )
    qkv_piece = swap(qkv_piece, "tp", 2)
    mlp_piece = swap(mlp_piece, "tp", 2)
    order.step(qkv_own, meta)
    in_far, in_other = order.step(in_far, in_other)
    in_tiles = (in_mine, in_far, in_other, swap(in_other, "tp", 1))
    (qkv_piece,) = order.step(qkv_piece)
    qkv_other = gather_eighths(qkv_piece)

    def biases(vector):
        zeros = jnp.zeros((shard,), LOW)
        qkv_row = jnp.concatenate([vector[:shard], zeros, vector[shard : 2 * shard]])
        return qkv_row.astype(F32)[None], vector[2 * shard :].astype(F32)[None]

    qkv_bias_own, up_bias_own = biases(vectors)
    gains = norm_gain.astype(F32)
    shifts = norm_bias.astype(F32)
    out_rows = out_bias.astype(F32)
    table = dataset_table.astype(F32)

    def shape(rows, cols, kind=LOW):
        return jax.ShapeDtypeStruct((rows, cols), kind)

    row_f32, row_low = shape(cap, width, F32), shape(cap, width)
    row_scratch = pltpu.VMEM((BLOCK, width), F32)
    tile_scratch = [pltpu.VMEM((4 * kept, TILE, width), LOW), pltpu.SemaphoreType.DMA((4,))]

    in_tiles = order.then(*in_tiles)
    start, normed, proj_own = call(
        functools.partial(begin_kernel, kept), meta,
        (*in_tiles, table, gains[0:1], shifts[0:1], qkv_own, qkv_bias_own),
        [ANYWHERE] * 4 + [whole(table.shape), whole((1, width)), whole((1, width)), whole((width, 3 * shard)), whole((1, 3 * shard))],
        (row_f32, row_low, shape(cap, 3 * shard)),
        (rows_out(width), rows_out(width), rows_out(3 * shard)),
        grid, tile_scratch, 15, "begin",
    )
    order.done(proj_own)

    def attend_shard(projected):
        (projected,) = order.then(projected)
        context, attend = call(
            functools.partial(attention_kernel, heads, shard, cell), meta, (projected,),
            [whole((cap, 3 * shard))],
            (shape(cap, shard), jax.ShapeDtypeStruct((kept, cell, heads * cell), LOW)),
            (whole((cap, shard)), whole((kept, cell, heads * cell))),
            (1,), (), 24, "attend",
        )
        order.done(context)
        return context, attend

    (mlp_piece,) = order.step(mlp_piece)
    mlp_other = gather_eighths(mlp_piece)
    head_rows = jnp.pad(vectors, (0, 2 * width - vectors.shape[0])).reshape(2, width)
    out_and_vectors = jnp.concatenate([out_weight, head_rows, jnp.zeros((6, width), LOW)], axis=0)
    out_and_vectors = swap(order.then(out_and_vectors)[0], "tp", 2)
    context_own, attend_own = attend_shard(proj_own)
    (out_and_vectors,) = order.step(out_and_vectors)
    out_other = out_and_vectors[:shard]
    vectors_other = out_and_vectors[shard : shard + 2].reshape(-1)[: vectors.shape[0]]
    grad_mine, grad_theirs = mine_of(order.then(out_grad)[0])
    grad_other = swap(grad_theirs, "tp", 2)
    grad_far = swap(grad_mine, "tp", 1)
    normed_now, qkv_now = order.then(normed, qkv_other)
    qkv_bias_other, up_bias_other = biases(vectors_other)
    (proj_other,) = call(
        project_kernel, meta, (normed_now, qkv_now, qkv_bias_other),
        [rows_spec(width), ANYWHERE, whole((1, 3 * shard))],
        (shape(cap, 3 * shard),), (rows_out(3 * shard),),
        grid, [pltpu.VMEM((width, 3 * shard), LOW), pltpu.SemaphoreType.DMA((8,))],
        11, "project",
    )
    order.done(proj_other)
    context_other, attend_other = attend_shard(proj_other)
    (grad_other,) = order.step(grad_other)
    grad_tiles = (grad_mine, grad_far, grad_other, swap(grad_other, "tp", 1))
    (context_now,) = order.then(context_other)
    attn_part = call(
        out_project_kernel, meta, (context_own, context_now, out_weight, out_other),
        [rows_spec(shard), rows_spec(shard), whole((shard, width)), whole((shard, width))],
        part_shapes(cap, width), part_outs(width),
        grid, (), 10, "out_project",
    )
    order.done(*attn_part)
    attn_far = swap_cores(attn_part)

    mlp_outs = (shape(cap, ff), shape(cap, ff), row_low, row_low, shape(8, ff, F32))
    mlp_out_specs = (rows_out(ff), rows_out(ff), rows_out(width), rows_out(width), whole((8, ff)))
    start_now, *attn_far = order.then(start, *attn_far)
    middle, second, grad_low, active_own, hidden_own, branch_own, second_grad_own, up_vec_own = call(
        functools.partial(mlp_first_kernel, kept), meta,
        (start_now, *attn_part, *attn_far, out_rows[0:1], gains[1:2], shifts[1:2], *grad_tiles, up_weight, up_bias_own, down_weight),
        [rows_spec(width)] + part_specs(width) * 2 + [whole((1, width))] * 3 + [ANYWHERE] * 4 + [whole((width, ff)), whole((1, ff)), whole((ff, width))],
        (row_f32, row_low, row_low, *mlp_outs),
        (rows_out(width), rows_out(width), rows_out(width), *mlp_out_specs),
        grid, tile_scratch + [row_scratch], 36, "mlp_first",
    )
    order.done(branch_own)
    second_now, mlp_now = order.then(second, mlp_other)
    active_other, hidden_other, *parts, up_vec_other = call(
        mlp_second_kernel, meta,
        (second_now, grad_low, branch_own, second_grad_own, mlp_now, up_bias_other),
        [rows_spec(width)] * 4 + [ANYWHERE, whole((1, ff))],
        (*mlp_outs[:2], *part_shapes(cap, width), *part_shapes(cap, width), mlp_outs[-1]),
        (*mlp_out_specs[:2], *part_outs(width), *part_outs(width), mlp_out_specs[-1]),
        grid, [pltpu.VMEM((width, ff), LOW), pltpu.VMEM((ff, width), LOW), pltpu.SemaphoreType.DMA((16,))],
        30, "mlp_second",
    )
    branch, second_grad = parts[:CHUNKS], parts[CHUNKS:]
    order.done(*second_grad)
    second_grad_far = swap_cores(second_grad)

    def weight_grad(*operands, rows=None):
        operands = order.then(*operands)
        pairs = len(operands) // 2
        cols = operands[1].shape[1]
        rows = rows or operands[0].shape[1]
        (result,) = call(
            functools.partial(weight_grad_kernel, pairs), meta, operands,
            [rows_spec(operand.shape[1]) for operand in operands],
            (shape(rows, cols),), (whole((rows, cols)),),
            grid, [pltpu.VMEM((rows, cols), F32)], cost=11, name="weight_grad",
        )
        order.done(result)
        return result

    down_sum = Reduction(meta, weight_grad(active_other, grad_low))

    pair_shape = jax.ShapeDtypeStruct((2 * kept, TILE, width), LOW)
    pair_spec = whole((2 * kept, TILE, width))

    second_grad_far = order.then(*second_grad_far)
    middle_grad, attn_grad, context_grad_own, context_grad_other, second_sums = call(
        middle_back_kernel, meta,
        (*second_grad, *second_grad_far, middle, grad_low, gains[1:2], out_weight, out_other),
        part_specs(width) * 2 + [rows_spec(width)] * 2 + [whole((1, width)), whole((shard, width)), whole((shard, width))],
        (row_f32, row_low, shape(cap, shard), shape(cap, shard), shape(8, width, F32)),
        (rows_out(width), rows_out(width), rows_out(shard), rows_out(shard), whole((8, width))),
        grid, [row_scratch], 18, "middle_back",
    )
    order.done(context_grad_other)

    def attend_back(projected, attend, context_grad):
        projected, attend, context_grad = order.then(projected, attend, context_grad)
        grads, sums = call(
            functools.partial(attention_back_kernel, heads, shard, cell), meta,
            (projected, attend, context_grad),
            [whole((cap, 3 * shard)), whole((kept, cell, heads * cell)), whole((cap, shard))],
            (shape(cap, 3 * shard), shape(8, shard, F32)), (whole((cap, 3 * shard)), whole((8, shard))),
            (1,), (), 30, "attend_back",
        )
        order.done(grads)
        return grads, sums

    rows_both = -(-(width + shard) // (2 * TILE)) * 2 * TILE

    def up_and_out(hidden, context):
        return weight_grad(second, hidden, context, attn_grad, rows=rows_both)

    both_sum = Reduction(meta, up_and_out(hidden_other, context_other))
    down_sum.first(order, weight_grad(active_own, grad_low))
    proj_grad_other, qkv_vec_other = attend_back(proj_other, attend_other, context_grad_other)
    down_sum.second(order)
    qkv_sum = Reduction(meta, weight_grad(normed, proj_grad_other))
    both_own = up_and_out(hidden_own, context_own)
    down_sum.third(order, False)
    both_sum.first(order, both_own)
    proj_grad_own, qkv_vec_own = attend_back(proj_own, attend_own, context_grad_own)
    (first_grads,) = order.then(proj_grad_own)
    first_part = call(
        first_part_kernel, meta,
        (first_grads, proj_grad_other, qkv_own, qkv_other),
        [rows_spec(3 * shard)] * 2 + [whole((width, 3 * shard)), ANYWHERE],
        part_shapes(cap, width), part_outs(width),
        grid, [pltpu.VMEM((width, 3 * shard), LOW), pltpu.SemaphoreType.DMA((8,))],
        15, "first_part",
    )
    order.done(*first_part)
    first_far = swap_cores(first_part)
    both_sum.second(order)
    qkv_own_grad = weight_grad(normed, proj_grad_own)
    qkv_sum.first(order, qkv_own_grad)
    first_far = order.then(*first_far)
    input_pair, first_sums, table_grad = call(
        start_back_kernel, meta, (*first_part, *first_far, start, middle_grad, gains[0:1]),
        part_specs(width) * 2 + [rows_spec(width)] * 2 + [whole((1, width))],
        (pair_shape, shape(8, width, F32), shape(table.shape[0], width, F32)),
        (pair_spec, whole((8, width)), whole(table.shape)),
        grid, [row_scratch, row_scratch], 14, "start_back",
    )
    order.done(input_pair)
    input_keep, input_far = send_cells(input_pair)
    branch_far = swap_cores(order.then(*branch))
    shared = jnp.concatenate(
        [first_sums[0:1], second_sums[0:1], first_sums[1:2], second_sums[1:4], table_grad]
    )

    def vector_rows(qkv_vec, up_vec):
        row = jnp.concatenate([qkv_vec[0], qkv_vec[2], jnp.zeros((width - 2 * shard,), F32)])
        return jnp.stack([row, up_vec[0]])

    small = jnp.concatenate([shared, vector_rows(qkv_vec_own, up_vec_own)])
    small_other = jnp.concatenate([shared, vector_rows(qkv_vec_other, up_vec_other)])
    small_far = swap(small_other, "tp", 2)
    middle_now, *branch_far = order.then(middle, *branch_far)
    (output_pair,) = call(
        finish_kernel, meta, (middle_now, *branch, *branch_far, out_rows[1:2]),
        [rows_spec(width)] + part_specs(width) * 2 + [whole((1, width))],
        (pair_shape,), (pair_spec,),
        grid, [row_scratch], 9, "finish",
    )
    order.done(output_pair)
    (small_far,) = order.step(small_far)
    small = small + small_far
    small_far = swap(small, "dp", 1)
    qkv_sum.second(order)
    both_sum.third(order, False)
    output_keep, output_far = send_cells(output_pair)
    (down_total,) = down_sum.last_eighths(order, (width,))
    (small_far,) = order.step(small_far)
    small = small + small_far
    small_far = swap(small, "dp", 2)
    qkv_sum.third(order, True)
    (small_far,) = order.step(small_far)
    small = small + small_far
    small_far = swap(small, "dp", 4)
    input_far, output_far = order.step(input_far, output_far)
    input_grad = place_cells(input_keep, input_far)
    cell_outputs = place_cells(output_keep, output_far)
    qkv_sum.fourth(order)
    small = small + small_far
    level = 3
    while (1 << level) < lax.axis_size("dp"):
        small = small + swap(small, "dp", 1 << level)
        level += 1
    up_total, out_total = both_sum.last_eighths(order, (width, shard))
    qkv_total = qkv_sum.last_halves(order, 3)

    return (
        cell_outputs,
        input_grad,
        small[0:2],
        small[2:4],
        qkv_total.transpose(1, 0, 2),
        small[-2, : 2 * shard].reshape(2, shard),
        out_total,
        small[4:6],
        up_total,
        small[-1],
        down_total,
        small[6:-2],
    )


def solution(mesh):
    in_specs = (
        P("dp", "tp", None),
        P("dp", "tp", None),
        P("dp"),
        P("dp"),
        P(),
        P(),
        P(None, None, "tp"),
        P(None, "tp"),
        P("tp", None),
        P(),
        P(None, "tp"),
        P("tp"),
        P("tp", None),
        P(),
    )
    out_specs = (
        P("dp", "tp", None),
        P("dp", "tp", None),
        P(),
        P(),
        P(None, None, "tp"),
        P(None, "tp"),
        P("tp", None),
        P(),
        P(None, "tp"),
        P("tp"),
        P("tp", None),
        P(),
    )
    return jax.shard_map(
        on_device, mesh=mesh, in_specs=in_specs, out_specs=out_specs, check_vma=False
    )
```

time: 1730 us -> 675 us (0.39)
  waiting for transfers between devices: 987 us -> 126 us
  Pallas kernels: 0 us -> 401 us
  blocking collectives: 301 us -> 0 us
  matrix products: 203 us -> 0 us
  other arithmetic: 99.3 us -> 11.2 us
  local copies, waits for them, and re-layouts: 98.6 us -> 63.4 us
  starting transfers between devices: 14.3 us -> 45.8 us
    pallas_call x0 -> x32, Pallas kernels: none -> 401 us  [call(): pl.pallas_call(kernel, grid_spec=pltpu.PrefetchScalarGridSpec(num_scalar_...]
    psum x2 -> x0, waiting for transfers between devices: 386 us -> none  [the longest x1 261 us: on_device(): lax.psum((qkv_grad, qv_bias_grad, out_weight_grad, up_grad, up_bias_grad,...]
    reduce_scatter x5 -> x0, waiting for transfers between devices: 312 us -> none  [the longest x2 155 us: forward_pass(): lax.psum_scatter(attn_part, 'tp', scatter_dimension=1, tiled=True)]
    dot_general x23 -> x0, matrix products: 188 us -> none  [the longest x1 28.2 us: forward_pass(): jnp.einsum('ocf,fd->ocd', active, down_weight, preferred_element_type=jnp...]
    all_gather x6 -> x4, waiting for transfers between devices: 186 us -> 0.03 us  [gather_eighths(): lax.all_gather(tiled, 'dp', axis=0, tiled=True, axis_index_groups=spans)]
    psum x2 -> x0, blocking collectives: 171 us -> none  [the longest x1 128 us: on_device(): lax.psum((qkv_grad, qv_bias_grad, out_weight_grad, up_grad, up_bias_grad,...]
    ppermute x0 -> x50, waiting for transfers between devices: none -> 126 us  [swap(): return lax.ppermute(value, axis, [(i, i ^ bit) for i in range(count)])]
    all_to_all x1 -> x0, blocking collectives: 117 us -> none  [on_device(): lax.all_to_all(send_start, 'dp', split_axis=0, concat_axis=0, tiled=True)]
  transfers between devices with their start and end apart: 16 -> 54, of which waited for: 13 -> 15; matrix products, arithmetic and copies ran while one was open for 5% -> 7% of each run, Pallas kernels for 0% -> 54%
where the time goes in v1:
time: 675 us; the launch traced here: 663 us
  Pallas kernels  401 us (59%)
  waiting for transfers between devices  126 us (19%)
  local copies, waits for them, and re-layouts  63.4 us (9%)
  starting transfers between devices  45.8 us (7%)
  between operations  15.3 us (2%)
  other arithmetic  11.2 us (2%)
    pallas_call x32, Pallas kernels, call(): pl.pallas_call(kernel, grid_spec=pltpu.PrefetchScalarGridSpec(num_scalar_...  401 us
    ppermute x50, waiting for transfers between devices, swap(): return lax.ppermute(value, axis, [(i, i ^ bit) for i in range(count)])  126 us
    ppermute x50, starting transfers between devices, swap(): return lax.ppermute(value, axis, [(i, i ^ bit) for i in range(count)])  45.6 us
    unnamed x100, local copies, waits for them, and re-layouts  17.4 us
  transfers between devices with their start and end apart: 54, of which 15 were waited for; matrix products, arithmetic and copies ran while one was open for 7% of the time, Pallas kernels for 54%

profile of v1, /device:TPU:0, one launch (start us, length us, event | category | flops | bytes accessed | tf_op | source)
XLA Modules:
  0.0 662.7 jit_solution(13486026779966068459)
XLA Ops:
  7.3 1.6 slice-done
  10.0 2.9 collective-permute-start.1
  16.2 1.9 copy.66
  23.8 14.7 %collective-permute-done.1.a2 = bf16[30,16,1120]{2,1,0:T(8,128)(2,1)} collective-permute-done((bf16[30,16,1120]{2,1,0:T(8,128)(2,1)}, bf16[30,16,1120]{2,1,0:T(8,128)(2,1)}, u32[]{:S(2)}, u32[]{:S(2)}) %collective-permute-start.1) | collective-permute-done | bytes 1075232 | tf_op jit(solution)/shard_map/ppermute | solution.py:30
  38.5 4.6 collective-permute-done.3
  43.9 1.8 collective-permute-start.4
  46.3 2.4 copy.67.weight.weight_a
  51.7 14.9 %begin.1 = (f32[2048,1120]{1,0:T(8,128)}, bf16[2048,1120]{1,0:T(8,128)(2,1)}, bf16[2048,840]{1,0:T(8,128)(2,1)}) custom-call(s32[584]{0:T(1024)} %concatenate.53.meta, bf16[30,16,1120]{2,1,0:T(8,128)(2,1)} %copy-done.6, bf16[30,16,1120]{2,1,0:T(8,128)(2,1)} %collective-permute-done.a1, bf16[30,16,1120]{2,1,0:T(8,128)(2,1)} %collective-permute-done.1.a2, ...), custom_call_target="tpu_custom_call" | custom-call | bytes 55350000 | tf_op jit(solution)/shard_map/begin/pallas_call | solution.py:138
  67.7 23.7 %attend.2 = (bf16[2048,280]{1,0:T(8,128)(2,1)}, bf16[30,64,320]{2,1,0:T(8,128)(2,1)}) custom-call(s32[584]{0:T(1024)} %concatenate.53.meta, bf16[2048,840]{1,0:T(8,128)(2,1)} %get-tuple-element.264.projected), custom_call_target="tpu_custom_call" | custom-call | bytes 88560000 | tf_op jit(solution)/shard_map/attend/pallas_call | solution.py:138
  91.4 1.6 slice-done.1
  95.4 11.0 %project.1.projected = bf16[2048,840]{1,0:T(8,128)(2,1)} custom-call(s32[584]{0:T(1024)} %concatenate.53.meta, bf16[2048,1120]{1,0:T(8,128)(2,1)} %get-tuple-element.275.normed.refs_0_, bf16[1152,840]{1,0:T(8,128)(2,1)} %bitcast.153, f32[1,840]{1,0:T(1,128)} %fusion.11.bias), custom_call_target="tpu_custom_call" | custom-call | bytes 40590000 | tf_op jit(solution)/shard_map/project/pallas_call | solution.py:138
  106.4 23.9 %attend.3 = (bf16[2048,280]{1,0:T(8,128)(2,1)}, bf16[30,64,320]{2,1,0:T(8,128)(2,1)}) custom-call(s32[584]{0:T(1024)} %concatenate.53.meta, bf16[2048,840]{1,0:T(8,128)(2,1)} %project.1.projected), custom_call_target="tpu_custom_call" | custom-call | bytes 88560000 | tf_op jit(solution)/shard_map/attend/pallas_call | solution.py:138
  130.3 10.3 %out_project.1 = (bf16[512,1120]{1,0:T(8,128)(2,1)}, bf16[512,1120]{1,0:T(8,128)(2,1)}, bf16[512,1120]{1,0:T(8,128)(2,1)}, bf16[512,1120]{1,0:T(8,128)(2,1)}) custom-call(s32[584]{0:T(1024)} %concatenate.53.meta, bf16[2048,280]{1,0:T(8,128)(2,1)} %get-tuple-element.253.a.refs_2_, bf16[2048,280]{1,0:T(8,128)(2,1)} %get-tuple-element.237.b.refs_2_, ...), custom_call_target="tpu_custom_call" | custom-call | bytes 36900000 | tf_op jit(solution)/shard_map/out_project/pallas_call | solution.py:138
  141.7 1.9 collective-permute-done.10
  147.0 3.2 collective-permute-done.8
  150.2 1.7 collective-permute-done.7
  153.6 38.1 %mlp_first.1 = (f32[2048,1120]{1,0:T(8,128)}, bf16[2048,1120]{1,0:T(8,128)(2,1)}, bf16[2048,1120]{1,0:T(8,128)(2,1)}, bf16[2048,1120]{1,0:T(8,128)(2,1)}, bf16[2...) custom-call(s32[584]{0:T(1024)} %concatenate.53.meta, ...), custom_call_target="tpu_custom_call" | custom-call | bytes 132840000 | tf_op jit(solution)/shard_map/mlp_first/pallas_call | solution.py:138
  191.7 34.6 %mlp_second.1 = (bf16[2048,1120]{1,0:T(8,128)(2,1)}, bf16[2048,1120]{1,0:T(8,128)(2,1)}, bf16[512,1120]{1,0:T(8,128)(2,1)}, bf16[512,1120]{1,0:T(8,128)(2,1)}, b...) custom-call(s32[584]{0:T(1024)} %concatenate.53.meta, ...), custom_call_target="tpu_custom_call" | custom-call | bytes 110700000 | tf_op jit(solution)/shard_map/mlp_second/pallas_call | solution.py:138
  227.4 10.6 %weight_grad.6 = bf16[1120,1120]{1,0:T(8,128)(2,1)} custom-call(s32[584]{0:T(1024)} %concatenate.53.meta, bf16[2048,1120]{1,0:T(8,128)(2,1)} %get-tuple-element.222.refs_0_, bf16[2048,1120]{1,0:T(8,128)(2,1)} %get-tuple-element.240.grad.refs_1_), custom_call_target="tpu_custom_call" | custom-call | bytes 40590000 | tf_op jit(solution)/shard_map/weight_grad/pallas_call | solution.py:138
  240.7 19.3 %middle_back.1 = (f32[2048,1120]{1,0:T(8,128)}, bf16[2048,1120]{1,0:T(8,128)(2,1)}, bf16[2048,280]{1,0:T(8,128)(2,1)}, bf16[2048,280]{1,0:T(8,128)(2,1)}, f32[8,1120]{1,0:T(8,128)}) custom-call(s32[584]{0:T(1024)} %concatenate.53.meta, bf16[512,1120]{1,0:T(8,128)(2,1)} %get-tuple-element.217.p0, bf16[512,1120]{1,0:T(8,128)(2,1)} %get-tuple-element.218.p1, ...), custom_call_target="tpu_custom_call" | custom-call | bytes 66420000 | tf_op jit(solution)/shard_map/middle_back/pallas_call | solution.py:138
  260.0 12.6 %weight_grad.7 = bf16[1408,1120]{1,0:T(8,128)(2,1)} custom-call(s32[584]{0:T(1024)} %concatenate.53.meta, bf16[2048,1120]{1,0:T(8,128)(2,1)} %get-tuple-element.251.second.refs_0_, bf16[2048,1120]{1,0:T(8,128)(2,1)} %get-tuple-element.236.refs_1_, bf16[2048,280]{1,0:T(8,128)(2,1)} %get-tuple-element.237.b.refs_2_, bf16[2048,1120]{1,0:T(8,128)(2,1)} %get-tuple-element.254.refs_3_), custom_call_target="tpu_custom_call" | custom-call | bytes 40590000 | tf_op jit(solution)/shard_map/weight_grad/pallas_call | solution.py:138
  272.6 1.6 collective-permute-start.19
  274.2 10.6 %weight_grad.8.own.mine = bf16[1120,1120]{1,0:T(8,128)(2,1)} custom-call(s32[584]{0:T(1024)} %concatenate.53.meta, bf16[2048,1120]{1,0:T(8,128)(2,1)} %get-tuple-element.239.refs_0_, bf16[2048,1120]{1,0:T(8,128)(2,1)} %get-tuple-element.240.grad.refs_1_), custom_call_target="tpu_custom_call" | custom-call | bytes 40590000 | tf_op jit(solution)/shard_map/weight_grad/pallas_call | solution.py:138
  284.8 12.2 %collective-permute-done.17 = bf16[70,16,1120]{2,1,0:T(8,128)(2,1)S(1)} collective-permute-done((bf16[70,16,1120]{2,1,0:T(8,128)(2,1)}, bf16[70,16,1120]{2,1,0:T(8,128)(2,1)S(1)}, u32[]{:S(2)}, u32[]{:S(2)}) %collective-permute-start.17) | collective-permute-done | bytes 2508832 | tf_op jit(solution)/shard_map/ppermute | solution.py:30
  298.5 5.2 first_sum.3
  303.7 29.9 %attend_back.2 = (bf16[2048,840]{1,0:T(8,128)(2,1)}, f32[8,280]{1,0:T(8,128)}) custom-call(s32[584]{0:T(1024)} %concatenate.53.meta, bf16[2048,840]{1,0:T(8,128)(2,1)} %project.1.projected, bf16[30,64,320]{2,1,0:T(8,128)(2,1)} %get-tuple-element.244.attend, bf16[2048,280]{1,0:T(8,128)(2,1)} %get-tuple-element.245.context_grad), custom_call_target="tpu_custom_call" | custom-call | bytes 110700000 | tf_op jit(solution)/shard_map/attend_back/pallas_call | solution.py:138
  334.7 4.1 second_sum.3
  338.8 4.5 collective-permute-start.20
  343.3 9.5 %weight_grad.9 = bf16[1120,840]{1,0:T(8,128)(2,1)} custom-call(s32[584]{0:T(1024)} %concatenate.53.meta, bf16[2048,1120]{1,0:T(8,128)(2,1)} %get-tuple-element.275.normed.refs_0_, bf16[2048,840]{1,0:T(8,128)(2,1)} %get-tuple-element.250.refs_1_.b), custom_call_target="tpu_custom_call" | custom-call | bytes 40590000 | tf_op jit(solution)/shard_map/weight_grad/pallas_call | solution.py:138
  352.8 12.5 %weight_grad.10.own.mine = bf16[1408,1120]{1,0:T(8,128)(2,1)} custom-call(s32[584]{0:T(1024)} %concatenate.53.meta, bf16[2048,1120]{1,0:T(8,128)(2,1)} %get-tuple-element.251.second.refs_0_, bf16[2048,1120]{1,0:T(8,128)(2,1)} %get-tuple-element.252.refs_1_, bf16[2048,280]{1,0:T(8,128)(2,1)} %get-tuple-element.253.a.refs_2_, ...), custom_call_target="tpu_custom_call" | custom-call | bytes 40590000 | tf_op jit(solution)/shard_map/weight_grad/pallas_call | solution.py:138
  366.3 3.0 third_sum.3
  369.3 1.7 copy-done
  371.1 5.3 first_sum.4
  377.6 30.1 %attend_back.3 = (bf16[2048,840]{1,0:T(8,128)(2,1)}, f32[8,280]{1,0:T(8,128)}) custom-call(s32[584]{0:T(1024)} %concatenate.53.meta, bf16[2048,840]{1,0:T(8,128)(2,1)} %get-tuple-element.264.projected, bf16[30,64,320]{2,1,0:T(8,128)(2,1)} %get-tuple-element.265.attend, bf16[2048,280]{1,0:T(8,128)(2,1)} %get-tuple-element.266.context_grad), custom_call_target="tpu_custom_call" | custom-call | bytes 110700000 | tf_op jit(solution)/shard_map/attend_back/pallas_call | solution.py:138
  407.8 16.4 %first_part.1 = (bf16[512,1120]{1,0:T(8,128)(2,1)}, bf16[512,1120]{1,0:T(8,128)(2,1)}, bf16[512,1120]{1,0:T(8,128)(2,1)}, bf16[512,1120]{1,0:T(8,128)(2,1)}) custom-call(s32[584]{0:T(1024)} %concatenate.53.meta, bf16[2048,840]{1,0:T(8,128)(2,1)} %get-tuple-element.276.a.refs_1_, bf16[2048,840]{1,0:T(8,128)(2,1)} %get-tuple-element.250.refs_1_.b, ...), custom_call_target="tpu_custom_call" | custom-call | bytes 55350000 | tf_op jit(solution)/shard_map/first_part/pallas_call | solution.py:138
  424.8 4.4 collective-permute-done.27
  430.4 4.6 second_sum.4
  435.0 9.5 %weight_grad.11.own.mine = bf16[1120,840]{1,0:T(8,128)(2,1)} custom-call(s32[584]{0:T(1024)} %concatenate.53.meta, bf16[2048,1120]{1,0:T(8,128)(2,1)} %get-tuple-element.275.normed.refs_0_, bf16[2048,840]{1,0:T(8,128)(2,1)} %get-tuple-element.276.a.refs_1_), custom_call_target="tpu_custom_call" | custom-call | bytes 40590000 | tf_op jit(solution)/shard_map/weight_grad/pallas_call | solution.py:138
  445.8 4.9 first_sum.5
  451.7 15.8 %start_back.1 = (bf16[60,16,1120]{2,1,0:T(8,128)(2,1)}, f32[8,1120]{1,0:T(8,128)}, f32[32,1120]{1,0:T(8,128)}) custom-call(s32[584]{0:T(1024)} %concatenate.53.meta, bf16[512,1120]{1,0:T(8,128)(2,1)} %get-tuple-element.269.p0, bf16[512,1120]{1,0:T(8,128)(2,1)} %get-tuple-element.270.p1, bf16[512,1120]{1,0:T(8,128)(2,1)} %get-tuple-element.271.p2, ...), custom_call_target="tpu_custom_call" | custom-call | bytes 51660000 | tf_op jit(solution)/shard_map/start_back/pallas_call | solution.py:138
  474.7 1.9 collective-permute-start.38
  476.5 5.3 collective-permute-start.37
  482.7 2.5 concatenate.65
  485.7 10.8 %finish.1 = bf16[60,16,1120]{2,1,0:T(8,128)(2,1)} custom-call(s32[584]{0:T(1024)} %concatenate.53.meta, f32[2048,1120]{1,0:T(8,128)} %get-tuple-element.289.middle, bf16[512,1120]{1,0:T(8,128)(2,1)} %get-tuple-element.285.p0, bf16[512,1120]{1,0:T(8,128)(2,1)} %get-tuple-element.286.p1, bf16[512,1120]{1,0:T(8,128)(2,1)} %get-tuple-element.287.p2, ...), custom_call_target="tpu_custom_call" | custom-call | bytes 33210000 | tf_op jit(solution)/shard_map/finish/pallas_call | solution.py:138
  496.5 3.7 second_sum.5
  500.2 8.2 %collective-permute-done.39 = bf16[11,16,1120]{2,1,0:T(8,128)(2,1)S(1)} collective-permute-done((bf16[11,16,1120]{2,1,0:T(8,128)(2,1)}, bf16[11,16,1120]{2,1,0:T(8,128)(2,1)S(1)}, u32[]{:S(2)}, u32[]{:S(2)}) %collective-permute-start.39) | collective-permute-done | bytes 394272 | tf_op jit(solution)/shard_map/ppermute | solution.py:30
  509.1 3.1 third_sum.4
  515.3 1.6 collective-permute-start.34
  519.2 2.0 concatenate.63
  523.1 7.9 %collective-permute-start.43 = (bf16[9,16,840]{2,1,0:T(8,128)(2,1)}, bf16[9,16,840]{2,1,0:T(8,128)(2,1)}, u32[]{:S(2)}, u32[]{:S(2)}) collective-permute-start(bf16[9,16,840]{2,1,0:T(8,128)(2,1)} %bitcast.224), channel_id=1, source_target_pairs={{0,16},{4,20},{8,24},{12,28},{16,0},{20,4},{24,8},{28,12},{1,17},{... | collective-permute-start | bytes 725768 | tf_op jit(solution)/shard_map/ppermute | solution.py:30
  533.2 5.2 widen_eighths.2
  538.4 13.9 %collective-permute-done.43 = bf16[9,16,840]{2,1,0:T(8,128)(2,1)} collective-permute-done((bf16[9,16,840]{2,1,0:T(8,128)(2,1)}, bf16[9,16,840]{2,1,0:T(8,128)(2,1)}, u32[]{:S(2)}, u32[]{:S(2)}) %collective-permute-start.43) | collective-permute-done | bytes 241952 | tf_op jit(solution)/shard_map/ppermute | solution.py:30
  552.4 6.9 %collective-permute-done.44 = bf16[9,16,840]{2,1,0:T(8,128)(2,1)} collective-permute-done((bf16[9,16,840]{2,1,0:T(8,128)(2,1)}, bf16[9,16,840]{2,1,0:T(8,128)(2,1)}, u32[]{:S(2)}, u32[]{:S(2)}) %collective-permute-start.44) | collective-permute-done | bytes 241952 | tf_op jit(solution)/shard_map/ppermute | solution.py:30
  559.3 2.8 third_sum.5.p0
  562.7 5.4 collective-permute-start.47
  569.1 1.8 fusion
  574.4 4.0 collective-permute-done.48
  578.4 37.5 %collective-permute-done.47 = bf16[9,16,840]{2,1,0:T(8,128)(2,1)} collective-permute-done((bf16[9,16,840]{2,1,0:T(8,128)(2,1)}, bf16[9,16,840]{2,1,0:T(8,128)(2,1)}, u32[]{:S(2)}, u32[]{:S(2)}) %collective-permute-start.47) | collective-permute-done | bytes 241952 | tf_op jit(solution)/shard_map/ppermute | solution.py:30
  615.9 3.0 assemble.1.mine
  620.7 1.6 pad.22
  626.5 5.7 widen_eighths.3
  632.2 10.7 %collective-permute-done.49 = bf16[35,16,840]{2,1,0:T(8,128)(2,1)S(1)} collective-permute-done((bf16[35,16,840]{2,1,0:T(8,128)(2,1)}, bf16[35,16,840]{2,1,0:T(8,128)(2,1)S(1)}, u32[]{:S(2)}, u32[]{:S(2)}) %collective-permute-start.49) | collective-permute-done | bytes 940832 | tf_op jit(solution)/shard_map/ppermute | solution.py:30
  643.8 6.2 widen.1
  650.1 5.9 copy.73
  (263 shorter events, 66.4 us)
Async XLA Ops:
  7.2 88.2 %all-gather.5.cloned.1.call-start = ((), (), s32[]{:S(2)}) async-start(), calls=%async_computation | async-start | bytes 2322432 | tf_op jit(solution)/shard_map/all_gather | solution.py:587
  10.0 28.5 %collective-permute-start.1 = (bf16[30,16,1120]{2,1,0:T(8,128)(2,1)}, bf16[30,16,1120]{2,1,0:T(8,128)(2,1)}, u32[]{:S(2)}, u32[]{:S(2)}) collective-permute-start(bf16[30,16,1120]{2,1,0:T(8,128)(2,1)} %get-tuple-element.347), channel_id=1, source_target_pairs={{0,2},{1,3},{2,0},{3,1},{4,6},{5,7},{6,4},{7,5},{8,10},{9,11},{10,... | collective-permute-start | bytes 3225608 | tf_op jit(solution)/shard_map/ppermute | solution.py:30
  13.0 25.5 %collective-permute-start = (bf16[30,16,1120]{2,1,0:T(8,128)(2,1)S(1)}, bf16[30,16,1120]{2,1,0:T(8,128)(2,1)}, u32[]{:S(2)}, u32[]{:S(2)}) collective-permute-start(bf16[30,16,1120]{2,1,0:T(8,128)(2,1)S(1)} %get-tuple-element.176.a0), channel_id=1, source_target_pairs={{0,1},{1,0},{2,3},{3,2},{4,5},{5,4},{6,7},{7,6},{8,9},{9,8},{10,11... | collective-permute-start | bytes 3225608 | tf_op jit(solution)/shard_map/ppermute | solution.py:30
  15.3 30.4 %copy-start.42 = (bf16[2,1120]{1,0:T(2,128)(2,1)S(1)}, bf16[2,1120]{1,0:T(2,128)(2,1)}, u32[]{:S(2)}) copy-start(bf16[2,1120]{1,0:T(2,128)(2,1)} %param.18) | copy-start | bytes 13444
  15.3 31.0 %copy-start.47 = (bf16[2,280]{1,0:T(2,128)(2,1)S(1)}, bf16[2,280]{1,0:T(2,128)(2,1)}, u32[]{:S(2)}) copy-start(bf16[2,280]{1,0:T(2,128)(2,1)} %param.21) | copy-start | bytes 3364
  18.1 25.0 %collective-permute-start.3 = (bf16[9,16,840]{2,1,0:T(8,128)(2,1)}, bf16[9,16,840]{2,1,0:T(8,128)(2,1)S(1)}, u32[]{:S(2)}, u32[]{:S(2)}) collective-permute-start(bf16[9,16,840]{2,1,0:T(8,128)(2,1)} %bitcast.213), channel_id=1, source_target_pairs={{0,2},{1,3},{2,0},{3,1},{4,6},{5,7},{6,4},{7,5},{8,10},{9,11},{10,... | collective-permute-start | bytes 725768 | tf_op jit(solution)/shard_map/ppermute | solution.py:30
  43.8 147.9 %all-gather.7.cloned.1.call-start = ((), (), s32[]{:S(2)}) async-start(), calls=%async_computation.1 | async-start | bytes 5971968 | tf_op jit(solution)/shard_map/all_gather | solution.py:587
  43.9 22.8 %collective-permute-start.4 = (bf16[18,16,1120]{2,1,0:T(8,128)(2,1)}, bf16[18,16,1120]{2,1,0:T(8,128)(2,1)}, u32[]{:S(2)}, u32[]{:S(2)}) collective-permute-start(bf16[18,16,1120]{2,1,0:T(8,128)(2,1)} %bitcast.203), channel_id=1, source_target_pairs={{0,2},{1,3},{2,0},{3,1},{4,6},{5,7},{6,4},{7,5},{8,10},{9,11},{10,... | collective-permute-start | bytes 1935368 | tf_op jit(solution)/shard_map/ppermute | solution.py:30
  45.7 5.0 collective-permute-start.2
  51.7 15.2 %copy-start.45 = (bf16[1120]{0:T(1024)(128)(2,1)S(1)}, bf16[1120]{0:T(1024)(128)(2,1)}, u32[]{:S(2)}) copy-start(bf16[1120]{0:T(1024)(128)(2,1)} %param.25) | copy-start | bytes 6724
  51.7 15.3 %copy-start.4 = (bf16[280,1120]{1,0:T(8,128)(2,1)S(1)}, bf16[280,1120]{1,0:T(8,128)(2,1)}, u32[]{:S(2)}) copy-start(bf16[280,1120]{1,0:T(8,128)(2,1)} %out_a.1) | copy-start | bytes 1881604
  66.7 466.5 %all-gather.9.cloned.1.call-start = ((), (), s32[]{:S(2)}) async-start(), calls=%async_computation.2 | async-start | bytes 2985984 | tf_op jit(solution)/shard_map/all_gather | solution.py:587
  67.2 24.2 %collective-permute-start.5 = (bf16[18,16,1120]{2,1,0:T(8,128)(2,1)S(1)}, bf16[18,16,1120]{2,1,0:T(8,128)(2,1)S(1)}, u32[]{:S(2)}, u32[]{:S(2)}) collective-permute-start(bf16[18,16,1120]{2,1,0:T(8,128)(2,1)S(1)} %bitcast.204), channel_id=1, source_target_pairs={{0,2},{1,3},{2,0},{3,1},{4,6},{5,7},{6,4},{7,5},{8,10},{9,11},{10,... | collective-permute-start | bytes 1935368 | tf_op jit(solution)/shard_map/ppermute | solution.py:30
  93.2 48.4 %copy-start.5 = (bf16[30,16,1120]{2,1,0:T(8,128)(2,1)}, bf16[30,16,1120]{2,1,0:T(8,128)(2,1)S(1)}, u32[]{:S(2)}) copy-start(bf16[30,16,1120]{2,1,0:T(8,128)(2,1)S(1)} %get-tuple-element.345.a0) | copy-start | bytes 3225604
  93.2 37.0 %collective-permute-start.6 = (bf16[30,16,1120]{2,1,0:T(8,128)(2,1)S(1)}, bf16[30,16,1120]{2,1,0:T(8,128)(2,1)S(1)}, u32[]{:S(2)}, u32[]{:S(2)}) collective-permute-start(bf16[30,16,1120]{2,1,0:T(8,128)(2,1)S(1)} %get-tuple-element.346), channel_id=1, source_target_pairs={{0,2},{1,3},{2,0},{3,1},{4,6},{5,7},{6,4},{7,5},{8,10},{9,11},{10,... | collective-permute-start | bytes 3225608 | tf_op jit(solution)/shard_map/ppermute | solution.py:30
  130.3 14.3 %copy-start.44 = (bf16[2,1120]{1,0:T(2,128)(2,1)S(1)}, bf16[2,1120]{1,0:T(2,128)(2,1)}, u32[]{:S(2)}) copy-start(bf16[2,1120]{1,0:T(2,128)(2,1)} %param.23) | copy-start | bytes 13444
  140.6 3.1 collective-permute-start.10
  140.7 6.3 collective-permute-start.9
  141.1 9.1 %collective-permute-start.8 = (bf16[32,16,1120]{2,1,0:T(8,128)(2,1)}, bf16[32,16,1120]{2,1,0:T(8,128)(2,1)S(1)}, u32[]{:S(2)}, u32[]{:S(2)}) collective-permute-start(bf16[32,16,1120]{2,1,0:T(8,128)(2,1)} %bitcast.179), channel_id=1, source_target_pairs={{0,1},{1,0},{2,3},{3,2},{4,5},{5,4},{6,7},{7,6},{8,9},{9,8},{10,11... | collective-permute-start | bytes 3440648 | tf_op jit(solution)/shard_map/ppermute | solution.py:30
  141.2 10.6 %collective-permute-start.7 = (bf16[32,16,1120]{2,1,0:T(8,128)(2,1)}, bf16[32,16,1120]{2,1,0:T(8,128)(2,1)S(1)}, u32[]{:S(2)}, u32[]{:S(2)}) collective-permute-start(bf16[32,16,1120]{2,1,0:T(8,128)(2,1)} %bitcast.178), channel_id=1, source_target_pairs={{0,1},{1,0},{2,3},{3,2},{4,5},{5,4},{6,7},{7,6},{8,9},{9,8},{10,11... | collective-permute-start | bytes 3440648 | tf_op jit(solution)/shard_map/ppermute | solution.py:30
  141.6 10.3 %collective-permute-start.11 = (bf16[30,16,1120]{2,1,0:T(8,128)(2,1)S(1)}, bf16[30,16,1120]{2,1,0:T(8,128)(2,1)S(1)}, u32[]{:S(2)}, u32[]{:S(2)}) collective-permute-start(bf16[30,16,1120]{2,1,0:T(8,128)(2,1)S(1)} %get-tuple-element.345.a0), channel_id=1, source_target_pairs={{0,1},{1,0},{2,3},{3,2},{4,5},{5,4},{6,7},{7,6},{8,9},{9,8},{10,11... | collective-permute-start | bytes 3225608 | tf_op jit(solution)/shard_map/ppermute | solution.py:30
  143.6 8.2 %collective-permute-start.12 = (bf16[30,16,1120]{2,1,0:T(8,128)(2,1)S(1)}, bf16[30,16,1120]{2,1,0:T(8,128)(2,1)S(1)}, u32[]{:S(2)}, u32[]{:S(2)}) collective-permute-start(bf16[30,16,1120]{2,1,0:T(8,128)(2,1)S(1)} %collective-permute-done.6.a2), channel_id=1, source_target_pairs={{0,1},{1,0},{2,3},{3,2},{4,5},{5,4},{6,7},{7,6},{8,9},{9,8},{10,11... | collective-permute-start | bytes 3225608 | tf_op jit(solution)/shard_map/ppermute | solution.py:30
  226.3 12.1 %collective-permute-start.16 = (bf16[32,16,1120]{2,1,0:T(8,128)(2,1)}, bf16[32,16,1120]{2,1,0:T(8,128)(2,1)S(1)}, u32[]{:S(2)}, u32[]{:S(2)}) collective-permute-start(bf16[32,16,1120]{2,1,0:T(8,128)(2,1)} %bitcast.194), channel_id=1, source_target_pairs={{0,1},{1,0},{2,3},{3,2},{4,5},{5,4},{6,7},{7,6},{8,9},{9,8},{10,11... | collective-permute-start | bytes 3440648 | tf_op jit(solution)/shard_map/ppermute | solution.py:30
  226.5 11.9 %collective-permute-start.15 = (bf16[32,16,1120]{2,1,0:T(8,128)(2,1)}, bf16[32,16,1120]{2,1,0:T(8,128)(2,1)S(1)}, u32[]{:S(2)}, u32[]{:S(2)}) collective-permute-start(bf16[32,16,1120]{2,1,0:T(8,128)(2,1)} %bitcast.193), channel_id=1, source_target_pairs={{0,1},{1,0},{2,3},{3,2},{4,5},{5,4},{6,7},{7,6},{8,9},{9,8},{10,11... | collective-permute-start | bytes 3440648 | tf_op jit(solution)/shard_map/ppermute | solution.py:30
  226.9 11.6 %collective-permute-start.14 = (bf16[32,16,1120]{2,1,0:T(8,128)(2,1)}, bf16[32,16,1120]{2,1,0:T(8,128)(2,1)S(1)}, u32[]{:S(2)}, u32[]{:S(2)}) collective-permute-start(bf16[32,16,1120]{2,1,0:T(8,128)(2,1)} %bitcast.192), channel_id=1, source_target_pairs={{0,1},{1,0},{2,3},{3,2},{4,5},{5,4},{6,7},{7,6},{8,9},{9,8},{10,11... | collective-permute-start | bytes 3440648 | tf_op jit(solution)/shard_map/ppermute | solution.py:30
  227.1 11.4 %collective-permute-start.13 = (bf16[32,16,1120]{2,1,0:T(8,128)(2,1)}, bf16[32,16,1120]{2,1,0:T(8,128)(2,1)S(1)}, u32[]{:S(2)}, u32[]{:S(2)}) collective-permute-start(bf16[32,16,1120]{2,1,0:T(8,128)(2,1)} %bitcast.191), channel_id=1, source_target_pairs={{0,1},{1,0},{2,3},{3,2},{4,5},{5,4},{6,7},{7,6},{8,9},{9,8},{10,11... | collective-permute-start | bytes 3440648 | tf_op jit(solution)/shard_map/ppermute | solution.py:30
  238.0 59.0 %collective-permute-start.17 = (bf16[70,16,1120]{2,1,0:T(8,128)(2,1)}, bf16[70,16,1120]{2,1,0:T(8,128)(2,1)S(1)}, u32[]{:S(2)}, u32[]{:S(2)}) collective-permute-start(bf16[70,16,1120]{2,1,0:T(8,128)(2,1)} %bitcast.165), channel_id=1, source_target_pairs={{0,2},{1,3},{2,0},{3,1},{4,6},{5,7},{6,4},{7,5},{8,10},{9,11},{10,... | collective-permute-start | bytes 7526408 | tf_op jit(solution)/shard_map/ppermute | solution.py:30
  272.6 96.7 %collective-permute-start.19 = (bf16[88,16,1120]{2,1,0:T(8,128)(2,1)}, bf16[88,16,1120]{2,1,0:T(8,128)(2,1)S(1)}, u32[]{:S(2)}, u32[]{:S(2)}) collective-permute-start(bf16[88,16,1120]{2,1,0:T(8,128)(2,1)} %bitcast.161), channel_id=1, source_target_pairs={{0,2},{1,3},{2,0},{3,1},{4,6},{5,7},{6,4},{7,5},{8,10},{9,11},{10,... | collective-permute-start | bytes 9461768 | tf_op jit(solution)/shard_map/ppermute | solution.py:30
  303.7 29.9 %collective-permute-start.18 = (bf16[35,16,1120]{2,1,0:T(8,128)(2,1)}, bf16[35,16,1120]{2,1,0:T(8,128)(2,1)S(1)}, u32[]{:S(2)}, u32[]{:S(2)}) collective-permute-start(bf16[35,16,1120]{2,1,0:T(8,128)(2,1)} %bitcast.174), channel_id=1, source_target_pairs={{0,4},{4,0},{8,12},{12,8},{16,20},{20,16},{24,28},{28,24},{1,5},{5... | collective-permute-start | bytes 3763208 | tf_op jit(solution)/shard_map/ppermute | solution.py:30
  338.8 26.6 %collective-permute-start.21 = (bf16[9,16,1120]{2,1,0:T(8,128)(2,1)}, bf16[9,16,1120]{2,1,0:T(8,128)(2,1)S(1)}, u32[]{:S(2)}, u32[]{:S(2)}) collective-permute-start(bf16[9,16,1120]{2,1,0:T(8,128)(2,1)} %bitcast.221), channel_id=1, source_target_pairs={{0,16},{4,20},{8,24},{12,28},{16,0},{20,4},{24,8},{28,12},{1,17},{... | collective-permute-start | bytes 967688 | tf_op jit(solution)/shard_map/ppermute | solution.py:30
  338.8 26.6 %collective-permute-start.20 = (bf16[9,16,1120]{2,1,0:T(8,128)(2,1)}, bf16[9,16,1120]{2,1,0:T(8,128)(2,1)S(1)}, u32[]{:S(2)}, u32[]{:S(2)}) collective-permute-start(bf16[9,16,1120]{2,1,0:T(8,128)(2,1)} %bitcast.220), channel_id=1, source_target_pairs={{0,8},{4,12},{8,0},{12,4},{16,24},{20,28},{24,16},{28,20},{1,9},{5... | collective-permute-start | bytes 967688 | tf_op jit(solution)/shard_map/ppermute | solution.py:30
  343.3 22.1 %collective-permute-start.22 = (bf16[9,16,1120]{2,1,0:T(8,128)(2,1)}, bf16[9,16,1120]{2,1,0:T(8,128)(2,1)S(1)}, u32[]{:S(2)}, u32[]{:S(2)}) collective-permute-start(bf16[9,16,1120]{2,1,0:T(8,128)(2,1)} %bitcast.219), channel_id=1, source_target_pairs={{0,24},{4,28},{8,16},{12,20},{16,8},{20,12},{24,0},{28,4},{1,25},{... | collective-permute-start | bytes 967688 | tf_op jit(solution)/shard_map/ppermute | solution.py:30
  369.3 257.2 %all-gather.11.cloned.1.call-start = ((), (), s32[]{:S(2)}) async-start(), calls=%async_computation.3 | async-start | bytes 3649536 | tf_op jit(solution)/shard_map/all_gather | solution.py:587
  376.3 52.9 %collective-permute-start.27 = (bf16[44,16,1120]{2,1,0:T(8,128)(2,1)}, bf16[44,16,1120]{2,1,0:T(8,128)(2,1)S(1)}, u32[]{:S(2)}, u32[]{:S(2)}) collective-permute-start(bf16[44,16,1120]{2,1,0:T(8,128)(2,1)} %bitcast.170), channel_id=1, source_target_pairs={{0,4},{4,0},{8,12},{12,8},{16,20},{20,16},{24,28},{28,24},{1,5},{5... | collective-permute-start | bytes 4730888 | tf_op jit(solution)/shard_map/ppermute | solution.py:30
  377.3 67.3 %collective-permute-start.28 = (bf16[70,16,840]{2,1,0:T(8,128)(2,1)S(1)}, bf16[70,16,840]{2,1,0:T(8,128)(2,1)S(1)}, u32[]{:S(2)}, u32[]{:S(2)}) collective-permute-start(bf16[70,16,840]{2,1,0:T(8,128)(2,1)S(1)} %bitcast.168), channel_id=1, source_target_pairs={{0,2},{1,3},{2,0},{3,1},{4,6},{5,7},{6,4},{7,5},{8,10},{9,11},{10,... | collective-permute-start | bytes 5644808 | tf_op jit(solution)/shard_map/ppermute | solution.py:30
  424.2 26.5 %collective-permute-start.26 = (bf16[32,16,1120]{2,1,0:T(8,128)(2,1)}, bf16[32,16,1120]{2,1,0:T(8,128)(2,1)S(1)}, u32[]{:S(2)}, u32[]{:S(2)}) collective-permute-start(bf16[32,16,1120]{2,1,0:T(8,128)(2,1)} %bitcast.187), channel_id=1, source_target_pairs={{0,1},{1,0},{2,3},{3,2},{4,5},{5,4},{6,7},{7,6},{8,9},{9,8},{10,11... | collective-permute-start | bytes 3440648 | tf_op jit(solution)/shard_map/ppermute | solution.py:30
  424.2 26.5 %collective-permute-start.25 = (bf16[32,16,1120]{2,1,0:T(8,128)(2,1)}, bf16[32,16,1120]{2,1,0:T(8,128)(2,1)}, u32[]{:S(2)}, u32[]{:S(2)}) collective-permute-start(bf16[32,16,1120]{2,1,0:T(8,128)(2,1)} %bitcast.186), channel_id=1, source_target_pairs={{0,1},{1,0},{2,3},{3,2},{4,5},{5,4},{6,7},{7,6},{8,9},{9,8},{10,11... | collective-permute-start | bytes 3440648 | tf_op jit(solution)/shard_map/ppermute | solution.py:30
  424.7 26.0 %collective-permute-start.24 = (bf16[32,16,1120]{2,1,0:T(8,128)(2,1)}, bf16[32,16,1120]{2,1,0:T(8,128)(2,1)}, u32[]{:S(2)}, u32[]{:S(2)}) collective-permute-start(bf16[32,16,1120]{2,1,0:T(8,128)(2,1)} %bitcast.185), channel_id=1, source_target_pairs={{0,1},{1,0},{2,3},{3,2},{4,5},{5,4},{6,7},{7,6},{8,9},{9,8},{10,11... | collective-permute-start | bytes 3440648 | tf_op jit(solution)/shard_map/ppermute | solution.py:30
  429.2 21.5 %collective-permute-start.23 = (bf16[32,16,1120]{2,1,0:T(8,128)(2,1)}, bf16[32,16,1120]{2,1,0:T(8,128)(2,1)}, u32[]{:S(2)}, u32[]{:S(2)}) collective-permute-start(bf16[32,16,1120]{2,1,0:T(8,128)(2,1)} %bitcast.184), channel_id=1, source_target_pairs={{0,1},{1,0},{2,3},{3,2},{4,5},{5,4},{6,7},{7,6},{8,9},{9,8},{10,11... | collective-permute-start | bytes 3440648 | tf_op jit(solution)/shard_map/ppermute | solution.py:30
  451.7 15.9 %copy-start.12 = (bf16[512,1120]{1,0:T(8,128)(2,1)S(1)}, bf16[512,1120]{1,0:T(8,128)(2,1)}, u32[]{:S(2)}) copy-start(bf16[512,1120]{1,0:T(8,128)(2,1)} %get-tuple-element.286.p1) | copy-start | bytes 3440644
  451.7 15.9 %copy-start.11 = (bf16[512,1120]{1,0:T(8,128)(2,1)S(1)}, bf16[512,1120]{1,0:T(8,128)(2,1)}, u32[]{:S(2)}) copy-start(bf16[512,1120]{1,0:T(8,128)(2,1)} %get-tuple-element.285.p0) | copy-start | bytes 3440644
  451.7 16.4 %copy-start.13 = (bf16[512,1120]{1,0:T(8,128)(2,1)S(1)}, bf16[512,1120]{1,0:T(8,128)(2,1)}, u32[]{:S(2)}) copy-start(bf16[512,1120]{1,0:T(8,128)(2,1)} %get-tuple-element.287.p2) | copy-start | bytes 3440644
  451.7 18.3 %copy-start.46 = (f32[8,1120]{1,0:T(8,128)S(1)}, f32[8,1120]{1,0:T(8,128)}, u32[]{:S(2)}) copy-start(f32[8,1120]{1,0:T(8,128)} %get-tuple-element.295) | copy-start | bytes 107524
  467.6 7.1 %collective-permute-start.30 = (bf16[32,16,1120]{2,1,0:T(8,128)(2,1)S(1)}, bf16[32,16,1120]{2,1,0:T(8,128)(2,1)}, u32[]{:S(2)}, u32[]{:S(2)}) collective-permute-start(bf16[32,16,1120]{2,1,0:T(8,128)(2,1)S(1)} %bitcast.176), channel_id=1, source_target_pairs={{0,1},{1,0},{2,3},{3,2},{4,5},{5,4},{6,7},{7,6},{8,9},{9,8},{10,11... | collective-permute-start | bytes 3440648 | tf_op jit(solution)/shard_map/ppermute | solution.py:30
  467.7 8.9 %collective-permute-start.29 = (bf16[32,16,1120]{2,1,0:T(8,128)(2,1)S(1)}, bf16[32,16,1120]{2,1,0:T(8,128)(2,1)}, u32[]{:S(2)}, u32[]{:S(2)}) collective-permute-start(bf16[32,16,1120]{2,1,0:T(8,128)(2,1)S(1)} %bitcast.175), channel_id=1, source_target_pairs={{0,1},{1,0},{2,3},{3,2},{4,5},{5,4},{6,7},{7,6},{8,9},{9,8},{10,11... | collective-permute-start | bytes 3440648 | tf_op jit(solution)/shard_map/ppermute | solution.py:30
  468.2 13.7 %collective-permute-start.31 = (bf16[32,16,1120]{2,1,0:T(8,128)(2,1)S(1)}, bf16[32,16,1120]{2,1,0:T(8,128)(2,1)}, u32[]{:S(2)}, u32[]{:S(2)}) collective-permute-start(bf16[32,16,1120]{2,1,0:T(8,128)(2,1)S(1)} %bitcast.177), channel_id=1, source_target_pairs={{0,1},{1,0},{2,3},{3,2},{4,5},{5,4},{6,7},{7,6},{8,9},{9,8},{10,11... | collective-permute-start | bytes 3440648 | tf_op jit(solution)/shard_map/ppermute | solution.py:30
  468.2 17.0 %collective-permute-start.32 = (bf16[32,16,1120]{2,1,0:T(8,128)(2,1)}, bf16[32,16,1120]{2,1,0:T(8,128)(2,1)}, u32[]{:S(2)}, u32[]{:S(2)}) collective-permute-start(bf16[32,16,1120]{2,1,0:T(8,128)(2,1)} %bitcast.68), channel_id=1, source_target_pairs={{0,1},{1,0},{2,3},{3,2},{4,5},{5,4},{6,7},{7,6},{8,9},{9,8},{10,11... | collective-permute-start | bytes 3440648 | tf_op jit(solution)/shard_map/ppermute | solution.py:30
  468.7 27.8 %collective-permute-start.40 = (bf16[35,16,840]{2,1,0:T(8,128)(2,1)}, bf16[35,16,840]{2,1,0:T(8,128)(2,1)}, u32[]{:S(2)}, u32[]{:S(2)}) collective-permute-start(bf16[35,16,840]{2,1,0:T(8,128)(2,1)} %bitcast.83), channel_id=1, source_target_pairs={{0,4},{4,0},{8,12},{12,8},{16,20},{20,16},{24,28},{28,24},{1,5},{5... | collective-permute-start | bytes 2822408 | tf_op jit(solution)/shard_map/ppermute | solution.py:30
  474.7 25.5 %collective-permute-start.38 = (bf16[11,16,1120]{2,1,0:T(8,128)(2,1)}, bf16[11,16,1120]{2,1,0:T(8,128)(2,1)S(1)}, u32[]{:S(2)}, u32[]{:S(2)}) collective-permute-start(bf16[11,16,1120]{2,1,0:T(8,128)(2,1)} %bitcast.218), channel_id=1, source_target_pairs={{0,16},{4,20},{8,24},{12,28},{16,0},{20,4},{24,8},{28,12},{1,17},{... | collective-permute-start | bytes 1182728 | tf_op jit(solution)/shard_map/ppermute | solution.py:30
  476.5 23.6 %collective-permute-start.37 = (bf16[11,16,1120]{2,1,0:T(8,128)(2,1)}, bf16[11,16,1120]{2,1,0:T(8,128)(2,1)S(1)}, u32[]{:S(2)}, u32[]{:S(2)}) collective-permute-start(bf16[11,16,1120]{2,1,0:T(8,128)(2,1)} %bitcast.217), channel_id=1, source_target_pairs={{0,8},{4,12},{8,0},{12,4},{16,24},{20,28},{24,16},{28,20},{1,9},{5... | collective-permute-start | bytes 1182728 | tf_op jit(solution)/shard_map/ppermute | solution.py:30
  481.9 26.5 %collective-permute-start.39 = (bf16[11,16,1120]{2,1,0:T(8,128)(2,1)}, bf16[11,16,1120]{2,1,0:T(8,128)(2,1)S(1)}, u32[]{:S(2)}, u32[]{:S(2)}) collective-permute-start(bf16[11,16,1120]{2,1,0:T(8,128)(2,1)} %bitcast.216), channel_id=1, source_target_pairs={{0,24},{4,28},{8,16},{12,20},{16,8},{20,12},{24,0},{28,4},{1,25},{... | collective-permute-start | bytes 1182728 | tf_op jit(solution)/shard_map/ppermute | solution.py:30
  485.2 11.2 %collective-permute-start.35 = (f32[40,1120]{1,0:T(8,128)S(1)}, f32[40,1120]{1,0:T(8,128)S(1)}, u32[]{:S(2)}, u32[]{:S(2)}) collective-permute-start(f32[40,1120]{1,0:T(8,128)S(1)} %concatenate.65), channel_id=1, source_target_pairs={{0,2},{1,3},{2,0},{3,1},{4,6},{5,7},{6,4},{7,5},{8,10},{9,11},{10,... | collective-permute-start | bytes 537608 | tf_op jit(solution)/shard_map/ppermute | solution.py:30
  513.8 55.3 %collective-permute-start.33 = (bf16[30,16,1120]{2,1,0:T(8,128)(2,1)S(1)}, bf16[30,16,1120]{2,1,0:T(8,128)(2,1)}, u32[]{:S(2)}, u32[]{:S(2)}) collective-permute-start(bf16[30,16,1120]{2,1,0:T(8,128)(2,1)S(1)} %dynamic-slice_bitcast_fusion.1), channel_id=1, source_target_pairs={{0,2},{1,3},{2,0},{3,1},{4,6},{5,7},{6,4},{7,5},{8,10},{9,11},{10,... | collective-permute-start | bytes 3225608 | tf_op jit(solution)/shard_map/ppermute | solution.py:30
  515.3 53.7 %collective-permute-start.34 = (bf16[30,16,1120]{2,1,0:T(8,128)(2,1)}, bf16[30,16,1120]{2,1,0:T(8,128)(2,1)}, u32[]{:S(2)}, u32[]{:S(2)}) collective-permute-start(bf16[30,16,1120]{2,1,0:T(8,128)(2,1)} %dynamic-slice_bitcast_fusion), channel_id=1, source_target_pairs={{0,2},{1,3},{2,0},{3,1},{4,6},{5,7},{6,4},{7,5},{8,10},{9,11},{10,... | collective-permute-start | bytes 3225608 | tf_op jit(solution)/shard_map/ppermute | solution.py:30
  522.8 9.0 %collective-permute-start.36 = (f32[40,1120]{1,0:T(8,128)S(1)}, f32[40,1120]{1,0:T(8,128)S(1)}, u32[]{:S(2)}, u32[]{:S(2)}) collective-permute-start(f32[40,1120]{1,0:T(8,128)S(1)} %add.104), channel_id=1, source_target_pairs={{0,4},{4,0},{8,12},{12,8},{16,20},{20,16},{24,28},{28,24},{1,5},{5... | collective-permute-start | bytes 537608 | tf_op jit(solution)/shard_map/ppermute | solution.py:30
  523.1 29.3 %collective-permute-start.43 = (bf16[9,16,840]{2,1,0:T(8,128)(2,1)}, bf16[9,16,840]{2,1,0:T(8,128)(2,1)}, u32[]{:S(2)}, u32[]{:S(2)}) collective-permute-start(bf16[9,16,840]{2,1,0:T(8,128)(2,1)} %bitcast.224), channel_id=1, source_target_pairs={{0,16},{4,20},{8,24},{12,28},{16,0},{20,4},{24,8},{28,12},{1,17},{... | collective-permute-start | bytes 725768 | tf_op jit(solution)/shard_map/ppermute | solution.py:30
  531.0 21.3 %collective-permute-start.42 = (bf16[9,16,840]{2,1,0:T(8,128)(2,1)}, bf16[9,16,840]{2,1,0:T(8,128)(2,1)}, u32[]{:S(2)}, u32[]{:S(2)}) collective-permute-start(bf16[9,16,840]{2,1,0:T(8,128)(2,1)} %bitcast.223), channel_id=1, source_target_pairs={{0,8},{4,12},{8,0},{12,4},{16,24},{20,28},{24,16},{28,20},{1,9},{5... | collective-permute-start | bytes 725768 | tf_op jit(solution)/shard_map/ppermute | solution.py:30
  532.5 26.8 %collective-permute-start.44 = (bf16[9,16,840]{2,1,0:T(8,128)(2,1)}, bf16[9,16,840]{2,1,0:T(8,128)(2,1)}, u32[]{:S(2)}, u32[]{:S(2)}) collective-permute-start(bf16[9,16,840]{2,1,0:T(8,128)(2,1)} %bitcast.222), channel_id=1, source_target_pairs={{0,24},{4,28},{8,16},{12,20},{16,8},{20,12},{24,0},{28,4},{1,25},{... | collective-permute-start | bytes 725768 | tf_op jit(solution)/shard_map/ppermute | solution.py:30
  552.4 15.7 %collective-permute-start.41 = (f32[40,1120]{1,0:T(8,128)S(1)}, f32[40,1120]{1,0:T(8,128)}, u32[]{:S(2)}, u32[]{:S(2)}) collective-permute-start(f32[40,1120]{1,0:T(8,128)S(1)} %add.105), channel_id=1, source_target_pairs={{0,8},{4,12},{8,0},{12,4},{16,24},{20,28},{24,16},{28,20},{1,9},{5... | collective-permute-start | bytes 537608 | tf_op jit(solution)/shard_map/ppermute | solution.py:30
  562.1 16.3 %collective-permute-start.48 = (bf16[9,16,840]{2,1,0:T(8,128)(2,1)}, bf16[9,16,840]{2,1,0:T(8,128)(2,1)}, u32[]{:S(2)}, u32[]{:S(2)}) collective-permute-start(bf16[9,16,840]{2,1,0:T(8,128)(2,1)} %bitcast.199), channel_id=1, source_target_pairs={{0,24},{4,28},{8,16},{12,20},{16,8},{20,12},{24,0},{28,4},{1,25},{... | collective-permute-start | bytes 725768 | tf_op jit(solution)/shard_map/ppermute | solution.py:30
  562.7 53.3 %collective-permute-start.47 = (bf16[9,16,840]{2,1,0:T(8,128)(2,1)}, bf16[9,16,840]{2,1,0:T(8,128)(2,1)}, u32[]{:S(2)}, u32[]{:S(2)}) collective-permute-start(bf16[9,16,840]{2,1,0:T(8,128)(2,1)} %bitcast.200), channel_id=1, source_target_pairs={{0,16},{4,20},{8,24},{12,28},{16,0},{20,4},{24,8},{28,12},{1,17},{... | collective-permute-start | bytes 725768 | tf_op jit(solution)/shard_map/ppermute | solution.py:30
  568.1 47.8 %collective-permute-start.46 = (bf16[9,16,840]{2,1,0:T(8,128)(2,1)}, bf16[9,16,840]{2,1,0:T(8,128)(2,1)}, u32[]{:S(2)}, u32[]{:S(2)}) collective-permute-start(bf16[9,16,840]{2,1,0:T(8,128)(2,1)} %bitcast.201), channel_id=1, source_target_pairs={{0,8},{4,12},{8,0},{12,4},{16,24},{20,28},{24,16},{28,20},{1,9},{5... | collective-permute-start | bytes 725768 | tf_op jit(solution)/shard_map/ppermute | solution.py:30
  572.8 51.1 %collective-permute-start.45 = (f32[40,1120]{1,0:T(8,128)S(1)}, f32[40,1120]{1,0:T(8,128)S(1)}, u32[]{:S(2)}, u32[]{:S(2)}) collective-permute-start(f32[40,1120]{1,0:T(8,128)S(1)} %add.106), channel_id=1, source_target_pairs={{0,16},{4,20},{8,24},{12,28},{16,0},{20,4},{24,8},{28,12},{1,17},{... | collective-permute-start | bytes 537608 | tf_op jit(solution)/shard_map/ppermute | solution.py:30
  619.0 23.9 %collective-permute-start.49 = (bf16[35,16,840]{2,1,0:T(8,128)(2,1)}, bf16[35,16,840]{2,1,0:T(8,128)(2,1)S(1)}, u32[]{:S(2)}, u32[]{:S(2)}) collective-permute-start(bf16[35,16,840]{2,1,0:T(8,128)(2,1)} %bitcast.158), channel_id=1, source_target_pairs={{0,4},{4,0},{8,12},{12,8},{16,20},{20,16},{24,28},{28,24},{1,5},{5... | collective-permute-start | bytes 2822408 | tf_op jit(solution)/shard_map/ppermute | solution.py:30
  (42 other events, 126.3 us)
Sparse Core Ops, SparseCore 0:
  43.9 49.9 all-gather.4
  96.1 86.1 all-gather.6
  369.4 73.7 all-gather.8
  512.4 107.0 all-gather.10

commit v2 on v1

v2 whole, which is shorter than its diff:
```python
import functools
import math

import jax
import jax.numpy as jnp
from jax import lax
from jax.experimental import pallas as pl
from jax.experimental.pallas import tpu as pltpu
from jax.sharding import PartitionSpec as P

HEAD_DIM = 56
EPSILON = 1e-05
BLOCK = 256
META_BLOCKS = 8
TILE = 16
F32 = jnp.float32
LOW = jnp.bfloat16
VMEM_BYTES = 56 * 1024 * 1024
FLOPS_PER_US = 450000000

NBLK, NCELL, BITS, TILE_SRC, TILE_SET, TILE_LEN, TILE_DST, CELL_OFF, CELL_ROWS = 0, 1, 2, 8, 136, 264, 392, 520, 552


def swap(value, axis, bit):
    count = lax.axis_size(axis)
    if value.ndim == 2 and value.shape[0] % TILE == 0:
        chunk = TILE if value.shape[0] // TILE % 128 else 2 * TILE
        tiled = value.reshape(value.shape[0] // chunk, chunk, value.shape[1])
        return swap(tiled, axis, bit).reshape(value.shape)
    return lax.ppermute(value, axis, [(i, i ^ bit) for i in range(count)])


CHUNKS = 2


def swap_cores(parts):
    return tuple(swap(part, "tp", 1) for part in parts)


class Sequence:
    def __init__(self):
        self.last = ()

    def then(self, *values):
        if not self.last:
            return values
        return lax.optimization_barrier((*values, *self.last))[: len(values)]

    def done(self, *values):
        self.last = (values[-1],)

    def step(self, *values):
        values = self.then(*values)
        self.last = (values[-1],)
        return values


def dot(a, b):
    return jnp.dot(a, b, preferred_element_type=F32)


def dot_nt(a, b):
    return lax.dot_general(a, b, (((1,), (1,)), ((), ())), preferred_element_type=F32)


def dot_tn(a, b):
    return lax.dot_general(a, b, (((0,), (0,)), ((), ())), preferred_element_type=F32)


def row_norm(rows):
    center = rows - jnp.mean(rows, axis=-1, keepdims=True)
    spread = jnp.mean(center * center, axis=-1, keepdims=True)
    scale = lax.rsqrt(spread + EPSILON)
    return center * scale, scale


def norm_back(grad, unit, scale, gain):
    scaled = grad * gain
    first = jnp.mean(scaled, axis=-1, keepdims=True)
    second = jnp.mean(scaled * unit, axis=-1, keepdims=True)
    return scale * (scaled - first - unit * second)


def whole(shape):
    zeros = (0,) * len(shape)
    return pl.BlockSpec(shape, lambda i, meta: zeros, pipeline_mode=pl.Buffered(1))


def rows_spec(width):
    return pl.BlockSpec((BLOCK, width), lambda i, meta: (jnp.minimum(i, meta[NBLK] - 1), 0))


PART_BLOCKS = META_BLOCKS // CHUNKS
PART_ROWS = PART_BLOCKS * BLOCK


def part_shapes(rows, width):
    return (jax.ShapeDtypeStruct((rows // CHUNKS, width), LOW),) * CHUNKS


def parts_scratch(width):
    return [pltpu.VMEM((META_BLOCKS * BLOCK, width), LOW), pltpu.SemaphoreType.DMA((CHUNKS,))]


def out_scratch(width):
    return [pltpu.VMEM((2, BLOCK, width), LOW), pltpu.SemaphoreType.DMA((2,))]


def each_part(parts, rows, sems):
    return [
        pltpu.make_async_copy(part, rows.at[pl.ds(at * PART_ROWS, PART_ROWS)], sems.at[at])
        for at, part in enumerate(parts)
    ]


def fetch_parts(step, blocks, *groups):
    for parts, rows, sems in groups:
        for at, copy in enumerate(each_part(parts, rows, sems)):

            @pl.when((step == 0) & (at * PART_BLOCKS < blocks))
            def _():
                copy.start()

    for parts, rows, sems in groups:
        for at, copy in enumerate(each_part(parts, rows, sems)):

            @pl.when(step == at * PART_BLOCKS)
            def _():
                copy.wait()


def block_of(step, rows):
    return rows[pl.ds(pl.multiple_of(step * BLOCK, BLOCK), BLOCK), :].astype(F32)


def put_part(step, last, value, parts, slots, sems):
    slot = lax.rem(step, 2)

    def copy_to(part, slot):
        begin = pl.multiple_of(lax.rem(step, PART_BLOCKS) * BLOCK, BLOCK)
        return pltpu.make_async_copy(slots.at[slot], part.at[pl.ds(begin, BLOCK)], sems.at[slot])

    @pl.when(step >= 2)
    def _():
        copy_to(parts[0], slot).wait()

    slots[slot] = value
    for at, part in enumerate(parts):

        @pl.when(step // PART_BLOCKS == at)
        def _():
            copy_to(part, slot).start()

    @pl.when(last)
    def _():
        copy_to(parts[0], slot).wait()

        @pl.when(step >= 1)
        def _():
            copy_to(parts[0], 1 - slot).wait()


def rows_out(width):
    return rows_spec(width)


def rows_more(width):
    return pl.BlockSpec((BLOCK, width), lambda i, meta: (jnp.minimum(i, meta[NBLK]), 0))


def live_step(meta):
    return pl.when(pl.program_id(0) < meta[NBLK])


ANYWHERE = pl.BlockSpec(memory_space=pl.ANY)


def call(kernel, meta, operands, in_specs, out_shape, out_specs, grid, scratch=(), cost=5, name=None):
    return pl.pallas_call(
        kernel,
        grid_spec=pltpu.PrefetchScalarGridSpec(
            num_scalar_prefetch=1,
            grid=grid,
            in_specs=in_specs,
            out_specs=out_specs,
            scratch_shapes=list(scratch),
        ),
        out_shape=out_shape,
        compiler_params=pltpu.CompilerParams(
            dimension_semantics=("arbitrary",) * len(grid), vmem_limit_bytes=VMEM_BYTES
        ),
        cost_estimate=pl.CostEstimate(flops=cost * FLOPS_PER_US, bytes_accessed=0, transcendentals=0),
        name=name,
    )(meta, *operands)


def load_tiles(sources, tiles, sems, count):
    copies = [
        pltpu.make_async_copy(source, tiles.at[pl.ds(at * count, count)], sems.at[at])
        for at, source in enumerate(sources)
    ]
    for copy in copies:
        copy.start()
    for copy in copies:
        copy.wait()


def begin_kernel(count, meta, a0, a1, a2, a3, table, gain, shift, weight, bias, start, normed, projected, tiles, sems):
    step = pl.program_id(0)

    @pl.when(step == 0)
    def _():
        load_tiles((a0, a1, a2, a3), tiles, sems, count)

    @pl.when(step < meta[NBLK])
    def _():
        for j in range(BLOCK // TILE):
            at = step * (BLOCK // TILE) + j
            tile = tiles[meta[TILE_SRC + at]].astype(F32)
            start[j * TILE : (j + 1) * TILE, :] = tile + table[pl.ds(meta[TILE_SET + at], 1), :]
        unit, _ = row_norm(start[...])
        low = (unit * gain[...] + shift[...]).astype(LOW)
        normed[...] = low
        projected[...] = (dot_nt(low, weight[...]) + bias[...]).astype(LOW)

    @pl.when(step == meta[NBLK])
    def _():
        projected[...] = jnp.zeros_like(projected)


def project_kernel(meta, normed, eighths, bias, projected, weight, sems):
    step = pl.program_id(0)

    @pl.when(step == 0)
    def _():
        load_eighths(eighths, [weight], sems)

    @pl.when(step < meta[NBLK])
    def _():
        projected[...] = (dot_nt(normed[...], weight[: bias.shape[1], :]) + bias[...]).astype(LOW)

    @pl.when(step == meta[NBLK])
    def _():
        projected[...] = jnp.zeros_like(projected)


def head_masks(cell, heads, shard):
    lane = lax.broadcasted_iota(jnp.int32, (cell, shard), 1)
    return [(lane >= h * HEAD_DIM) & (lane < (h + 1) * HEAD_DIM) for h in range(heads)]


def spread_heads(rows, masks, heads, low, high):
    part = rows[:, low:high]
    zero = jnp.zeros_like(part)
    return jnp.concatenate([jnp.where(masks[h][:, low:high], part, zero) for h in heads], axis=0)


def head_groups(heads, shard):
    groups = []
    at = 0
    while at < heads:
        end = min(at + 4, heads)
        low = at * HEAD_DIM // 128 * 128
        high = min(-(-end * HEAD_DIM // 128) * 128, shard)
        groups.append((tuple(range(at, end)), low, high))
        at = end
    return groups


def attention_kernel(heads, shard, cell, meta, projected, context, attend):
    context[...] = jnp.zeros_like(context)
    masks = head_masks(cell, heads, shard)
    scale = 1.0 / math.sqrt(HEAD_DIM)
    row = lax.broadcasted_iota(jnp.int32, (cell, 2 * cell), 0)
    lane = lax.broadcasted_iota(jnp.int32, (cell, 2 * cell), 1)
    left = lane < cell
    causal = row >= jnp.where(left, lane, lane - cell)

    def one(index):
        at = pl.multiple_of(meta[CELL_OFF + index] * TILE, TILE)
        queries = projected[pl.ds(at, cell), 0:shard]
        keys = projected[pl.ds(at, cell), shard : 2 * shard]
        values = projected[pl.ds(at, cell), 2 * shard : 3 * shard]
        total = None
        for group, low, high in head_groups(heads, shard):
            spread = spread_heads(keys, masks, group, low, high)
            scores = dot_nt(queries[:, low:high], spread) * scale
            parts = []
            for pair in range(0, len(group), 2):
                if pair + 1 < len(group):
                    both = jnp.where(causal, scores[:, pair * cell : (pair + 2) * cell], -1e30)
                    top_left = jnp.max(jnp.where(left, both, -1e30), axis=1, keepdims=True)
                    top_right = jnp.max(jnp.where(left, -1e30, both), axis=1, keepdims=True)
                    weights = jnp.exp(both - jnp.where(left, top_left, top_right))
                    sum_left = jnp.sum(jnp.where(left, weights, 0.0), axis=1, keepdims=True)
                    sum_right = jnp.sum(jnp.where(left, 0.0, weights), axis=1, keepdims=True)
                    parts.append((weights * jnp.where(left, 1.0 / sum_left, 1.0 / sum_right)).astype(LOW))
                else:
                    single = jnp.where(causal[:, :cell], scores[:, pair * cell :], -1e30)
                    weights = jnp.exp(single - jnp.max(single, axis=1, keepdims=True))
                    parts.append((weights * (1.0 / jnp.sum(weights, axis=1, keepdims=True))).astype(LOW))
            probs = jnp.concatenate(parts, axis=1) if len(parts) > 1 else parts[0]
            first = group[0] * cell
            attend[index, :, first : first + len(group) * cell] = probs
            part = dot(probs, spread_heads(values, masks, group, low, high))
            if total is None:
                total = jnp.pad(part, ((0, 0), (low, shard - high))) if high - low < shard else part
            else:
                total = total + jnp.pad(part, ((0, 0), (low, shard - high)))
        context[pl.ds(at, cell), :] = total.astype(LOW)

    def body(step, carry):
        one(2 * step)
        one(2 * step + 1)
        return carry

    lax.fori_loop(0, (meta[NCELL] + 1) // 2, body, 0)


def attention_back_kernel(heads, shard, cell, meta, projected, attend, context_grad, result, sums):
    result[...] = jnp.zeros_like(result)
    sums[...] = jnp.zeros_like(sums)
    masks = head_masks(cell, heads, shard)
    scale = 1.0 / math.sqrt(HEAD_DIM)
    row = lax.broadcasted_iota(jnp.int32, (cell, shard), 0)
    left = lax.broadcasted_iota(jnp.int32, (cell, 2 * cell), 1) < cell

    def fold(stacked, group, low, high):
        total = None
        for place, h in enumerate(group):
            part = jnp.where(masks[h][:, low:high], stacked[place * cell : (place + 1) * cell, :], 0.0)
            total = part if total is None else total + part
        return total

    def widen(part, low, high):
        return jnp.pad(part, ((0, 0), (low, shard - high))) if high - low < shard else part

    def one(index):
        at = pl.multiple_of(meta[CELL_OFF + index] * TILE, TILE)
        queries = projected[pl.ds(at, cell), 0:shard]
        keys = projected[pl.ds(at, cell), shard : 2 * shard]
        values = projected[pl.ds(at, cell), 2 * shard : 3 * shard]
        grads = context_grad[pl.ds(at, cell), :]
        grads = jnp.where(row < meta[CELL_ROWS + index], grads, jnp.zeros_like(grads))
        query_total = key_total = value_total = None
        for group, low, high in head_groups(heads, shard):
            first = group[0] * cell
            probs = attend[index, :, first : first + len(group) * cell]
            attend_grad = dot_nt(grads[:, low:high], spread_heads(values, masks, group, low, high))
            parts = []
            for pair in range(0, len(group), 2):
                if pair + 1 < len(group):
                    span = slice(pair * cell, (pair + 2) * cell)
                    weights = probs[:, span].astype(F32)
                    both = attend_grad[:, span]
                    product = weights * both
                    sum_left = jnp.sum(jnp.where(left, product, 0.0), axis=1, keepdims=True)
                    sum_right = jnp.sum(jnp.where(left, 0.0, product), axis=1, keepdims=True)
                    parts.append((product - weights * jnp.where(left, sum_left, sum_right)).astype(LOW))
                else:
                    span = slice(pair * cell, (pair + 1) * cell)
                    weights = probs[:, span].astype(F32)
                    product = weights * attend_grad[:, span]
                    total = jnp.sum(product, axis=1, keepdims=True)
                    parts.append((product - weights * total).astype(LOW))
            score_grad = jnp.concatenate(parts, axis=1) if len(parts) > 1 else parts[0]
            query_part = dot(score_grad, spread_heads(keys, masks, group, low, high)) * scale
            key_part = fold(dot_tn(score_grad, queries[:, low:high]), group, low, high) * scale
            value_part = fold(dot_tn(probs, grads[:, low:high]), group, low, high)
            query_part, key_part, value_part = (widen(p, low, high) for p in (query_part, key_part, value_part))
            if query_total is None:
                query_total, key_total, value_total = query_part, key_part, value_part
            else:
                query_total, key_total, value_total = (
                    query_total + query_part,
                    key_total + key_part,
                    value_total + value_part,
                )
        for place, part in enumerate((query_total, key_total, value_total)):
            low_part = part.astype(LOW)
            result[pl.ds(at, cell), place * shard : (place + 1) * shard] = low_part
            sums[place : place + 1, :] += jnp.sum(low_part.astype(F32), axis=0, keepdims=True)

    def body(step, carry):
        one(2 * step)
        one(2 * step + 1)
        return carry

    lax.fori_loop(0, (meta[NCELL] + 1) // 2, body, 0)


def out_project_kernel(meta, a, b, weight_a, weight_b, *refs):
    *parts, slots, sems = refs
    step = pl.program_id(0)

    @live_step(meta)
    def _():
        value = (dot(a[...], weight_a[...]) + dot(b[...], weight_b[...])).astype(LOW)
        put_part(step, step == meta[NBLK] - 1, value, parts, slots, sems)


def first_part_kernel(meta, a, b, weight_a, eighths, *refs):
    step = pl.program_id(0)
    *parts, weight_b, weight_sems, slots, sems = refs

    @pl.when(step == 0)
    def _():
        load_eighths(eighths, [weight_b], weight_sems)

    @live_step(meta)
    def _():
        value = (dot(a[...], weight_a[...]) + dot(b[...], weight_b[: b.shape[1], :])).astype(LOW)
        put_part(step, step == meta[NBLK] - 1, value, parts, slots, sems)


def gelu_pair(hidden):
    chance = 0.5 * (1.0 + lax.erf(hidden * (1.0 / math.sqrt(2.0))))
    slope = chance + hidden * (jnp.exp(-0.5 * hidden * hidden) * (1.0 / math.sqrt(2.0 * math.pi)))
    return hidden * chance, slope


def mlp_block(second, grad, up, bias, down, active, hidden_grad, bias_grad):
    hidden = dot(second, up[...]) + bias[...]
    value, slope = gelu_pair(hidden)
    low = value.astype(LOW)
    active[...] = low
    back = (slope * dot_nt(grad, down[...])).astype(LOW)
    hidden_grad[...] = back
    bias_grad[...] += jnp.sum(back.astype(F32), axis=0, keepdims=True)
    return dot(low, down[...]), dot_nt(back, up[...])


def mlp_kernel(count, meta, start, *refs):
    near_parts, far_parts, refs = refs[:CHUNKS], refs[CHUNKS : 2 * CHUNKS], refs[2 * CHUNKS :]
    bias_row, gain, shift, a0, a1, a2, a3, up, up_bias, down, other_up, other_bias, eighths, *refs = refs
    middle, second, grad, active, hidden_grad, other_active, other_hidden, *refs = refs
    branch, second_grad, refs = refs[:CHUNKS], refs[CHUNKS : 2 * CHUNKS], refs[2 * CHUNKS :]
    bias_grad, tiles, sems, near_rows, near_sems, far_rows, far_sems, *refs = refs
    other_down, other_sems, branch_slots, branch_sems, grad_slots, grad_sems = refs
    step = pl.program_id(0)
    copies = eighths_copies(eighths, [other_down], other_sems)

    @pl.when(step == 0)
    def _():
        load_tiles((a0, a1, a2, a3), tiles, sems, count)
        for copy in copies:
            copy.start()
        bias_grad[...] = jnp.zeros_like(bias_grad)

    @live_step(meta)
    def _():
        last = step == meta[NBLK] - 1
        fetch_parts(step, meta[NBLK], (near_parts, near_rows, near_sems), (far_parts, far_rows, far_sems))
        inner = lax.broadcasted_iota(jnp.int32, (TILE, 1), 0)
        for j in range(BLOCK // TILE):
            at = step * (BLOCK // TILE) + j
            tile = tiles[meta[TILE_SRC + at]]
            grad[j * TILE : (j + 1) * TILE, :] = jnp.where(inner < meta[TILE_LEN + at], tile, jnp.zeros_like(tile))
        rows = start[...] + (block_of(step, near_rows) + block_of(step, far_rows)) + bias_row[...]
        middle[...] = rows
        unit, _ = row_norm(rows)
        low = (unit * gain[...] + shift[...]).astype(LOW)
        second[...] = low
        own = mlp_block(low, grad[...], up, up_bias, down, active, hidden_grad, bias_grad.at[0:1])

        @pl.when(step == 0)
        def _():
            for copy in copies:
                copy.wait()

        other = mlp_block(
            low, grad[...], other_up, other_bias, other_down, other_active, other_hidden, bias_grad.at[1:2]
        )
        put_part(step, last, (own[1] + other[1]).astype(LOW), second_grad, grad_slots, grad_sems)
        put_part(step, last, (own[0] + other[0]).astype(LOW), branch, branch_slots, branch_sems)


def weight_grad_kernel(pairs, meta, *refs):
    step = pl.program_id(0)
    result, total = refs[2 * pairs :]

    @live_step(meta)
    def _():
        base = 0
        for a, b in zip(refs[: 2 * pairs : 2], refs[1 : 2 * pairs : 2]):
            rows = slice(base, base + a.shape[1])
            part = dot_tn(a[...], b[...])
            base += a.shape[1]

            @pl.when(step == 0)
            def _():
                total[rows, :] = part

            @pl.when(step > 0)
            def _():
                total[rows, :] += part

        @pl.when(step == meta[NBLK] - 1)
        def _():
            result[...] = total[...].astype(LOW)


def middle_back_kernel(meta, *refs):
    near_parts, far_parts, refs = refs[:CHUNKS], refs[CHUNKS : 2 * CHUNKS], refs[2 * CHUNKS :]
    middle, grad, gain, out_a, out_b, middle_grad, attn_grad, context_a, context_b, sums, *refs = refs
    near_rows, near_sems, far_rows, far_sems = refs
    step = pl.program_id(0)

    @pl.when(step == 0)
    def _():
        sums[...] = jnp.zeros_like(sums)

    @live_step(meta)
    def _():
        fetch_parts(step, meta[NBLK], (near_parts, near_rows, near_sems), (far_parts, far_rows, far_sems))
        unit, scale = row_norm(middle[...])
        second_grad = block_of(step, near_rows) + block_of(step, far_rows)
        grad_rows = grad[...].astype(F32)
        total = grad_rows + norm_back(second_grad, unit, scale, gain[...])
        middle_grad[...] = total
        low = total.astype(LOW)
        attn_grad[...] = low
        context_a[...] = dot_nt(low, out_a[...]).astype(LOW)
        context_b[...] = dot_nt(low, out_b[...]).astype(LOW)
        for at, rows in enumerate((second_grad * unit, second_grad, total, grad_rows)):
            sums[at : at + 1, :] += jnp.sum(rows, axis=0, keepdims=True)


def scatter_tiles(meta, step, rows, out):
    for j in range(BLOCK // TILE):
        place = meta[TILE_DST + step * (BLOCK // TILE) + j]

        @pl.when(place >= 0)
        def _():
            out[place] = rows[j * TILE : (j + 1) * TILE, :].astype(LOW)


def start_back_kernel(meta, *refs):
    near_parts, far_parts, refs = refs[:CHUNKS], refs[CHUNKS : 2 * CHUNKS], refs[2 * CHUNKS :]
    start, middle_grad, gain, out, sums, table, rows, near_rows, near_sems, far_rows, far_sems = refs
    step = pl.program_id(0)

    @pl.when(step == 0)
    def _():
        out[...] = jnp.zeros_like(out)
        sums[...] = jnp.zeros_like(sums)
        table[...] = jnp.zeros_like(table)

    @live_step(meta)
    def _():
        fetch_parts(step, meta[NBLK], (near_parts, near_rows, near_sems), (far_parts, far_rows, far_sems))
        unit, scale = row_norm(start[...])
        first_grad = block_of(step, near_rows) + block_of(step, far_rows)
        rows[...] = middle_grad[...] + norm_back(first_grad, unit, scale, gain[...])
        for at, value in enumerate((first_grad * unit, first_grad)):
            sums[at : at + 1, :] += jnp.sum(value, axis=0, keepdims=True)
        for j in range(BLOCK // TILE):
            at = meta[TILE_SET + step * (BLOCK // TILE) + j]
            table[pl.ds(at, 1), :] += jnp.sum(rows[j * TILE : (j + 1) * TILE, :], axis=0, keepdims=True)
        scatter_tiles(meta, step, rows, out)


def finish_kernel(meta, middle, *refs):
    near_parts, far_parts, refs = refs[:CHUNKS], refs[CHUNKS : 2 * CHUNKS], refs[2 * CHUNKS :]
    bias_row, out, rows, near_rows, near_sems, far_rows, far_sems = refs
    step = pl.program_id(0)

    @pl.when(step == 0)
    def _():
        out[...] = jnp.zeros_like(out)

    @live_step(meta)
    def _():
        fetch_parts(step, meta[NBLK], (near_parts, near_rows, near_sems), (far_parts, far_rows, far_sems))
        rows[...] = middle[...] + (block_of(step, near_rows) + block_of(step, far_rows)) + bias_row[...]
        inner = lax.broadcasted_iota(jnp.int32, (TILE, 1), 0)
        for j in range(BLOCK // TILE):
            at = step * (BLOCK // TILE) + j
            place = meta[TILE_DST + at]

            @pl.when(place >= 0)
            def _():
                out[place] = jnp.where(inner < meta[TILE_LEN + at], rows[j * TILE : (j + 1) * TILE, :], 0.0).astype(LOW)


def vectors_kernel(shard, meta, first, second, table, own, other, up, small, small_other):
    for out, qkv, at in ((small, own, 0), (small_other, other, 1)):
        out[0:1, :] = first[0:1, :]
        out[1:2, :] = second[0:1, :]
        out[2:3, :] = first[1:2, :]
        out[3:6, :] = second[1:4, :]
        out[6:38, :] = table[...]
        out[38:40, :] = jnp.zeros((2, out.shape[1]), F32)
        out[38:39, :shard] = qkv[0:1, :]
        out[38:39, shard : 2 * shard] = qkv[2:3, :]
        out[39:40, :] = up[at : at + 1, :]


def window_size(half):
    return -(-half // (4 * TILE)) * TILE


def window_at(low, high, half):
    size = window_size(half)
    return low * (half - 2 * size) + high * size


def run_copies(copies):
    for copy in copies:
        copy.start()
    for copy in copies:
        copy.wait()


def join_kernel(extra, level, meta, mine, far, out, sems):
    rows = mine.shape[0]

    def put(first, second):
        run_copies(
            [
                pltpu.make_async_copy(first, out.at[pl.ds(0, rows)], sems.at[0]),
                pltpu.make_async_copy(second.at[pl.ds(extra, rows - extra)], out.at[pl.ds(rows, rows - extra)], sems.at[1]),
            ]
        )

    @pl.when(meta[BITS + level] == 0)
    def _():
        put(mine, far)

    @pl.when(meta[BITS + level] == 1)
    def _():
        put(far, mine)


def join(meta, mine, far, level, total):
    rows, width = mine.shape
    (result,) = call(
        functools.partial(join_kernel, 2 * rows - total, level), meta, (mine, far), [ANYWHERE] * 2,
        (jax.ShapeDtypeStruct((total, width), LOW),), (whole((total, width)),),
        (1,), [pltpu.SemaphoreType.DMA((2,))], cost=3, name="join",
    )
    return result


def gather_eighths(piece):
    groups = lax.axis_size("dp")
    spans = [list(range(at, at + 8)) for at in range(0, groups, 8)] if groups > 8 else None
    tiled = piece.reshape(piece.shape[0] // TILE, TILE, piece.shape[1])
    whole_block = lax.all_gather(tiled, "dp", axis=0, tiled=True, axis_index_groups=spans)
    return whole_block.reshape(8 * piece.shape[0], piece.shape[1])


def eighths_copies(gathered, scratches, sems):
    copies = []
    for at, scratch in enumerate(scratches):
        half = scratch.shape[0] // 2
        size = window_size(half)
        for group in range(8):
            low, high = (group >> 1) & 1, group >> 2
            skip = 4 * size - half if (low, high) == (1, 0) else 0
            begin = (group & 1) * half + window_at(low, high, half) + skip
            copies.append(
                pltpu.make_async_copy(
                    gathered.at[pl.ds((group * len(scratches) + at) * size + skip, size - skip)],
                    scratch.at[pl.ds(begin, size - skip)],
                    sems.at[8 * at + group],
                )
            )
    return copies


def load_eighths(gathered, scratches, sems):
    copies = eighths_copies(gathered, scratches, sems)
    for copy in copies:
        copy.start()
    for copy in copies:
        copy.wait()


def first_sum_kernel(meta, own, far, sent):
    sent[...] = (own[...].astype(F32) + far[...].astype(F32)).astype(LOW)


def first_sum(meta, own, far):
    rows, width = own.shape
    half = rows // 2
    steps = next(count for count in (5, 4, 3, 1) if half % (count * TILE) == 0)
    block = half // steps
    source = pl.BlockSpec((block, width), lambda i, meta: ((1 - meta[BITS]) * steps + i, 0))
    (sent,) = call(
        first_sum_kernel, meta, (own, far), [source, source], (jax.ShapeDtypeStruct((half, width), LOW),),
        (pl.BlockSpec((block, width), lambda i, meta: (i, 0)),), (steps,), cost=5, name="first_sum",
    )
    return sent


def second_sum_kernel(half, meta, mine, far, arrived, kept, sent):
    size = 2 * window_size(half)
    bit = meta[BITS + 1]
    for out, place in ((kept, bit), (sent, 1 - bit)):
        rows = pl.ds(pl.multiple_of(place * (half - size), TILE), size)
        total = mine[rows, :].astype(F32) + far[rows, :].astype(F32) + arrived[rows, :].astype(F32)
        out[...] = total.astype(out.dtype)


def second_sum(meta, own, far, arrived, cost):
    half, width = arrived.shape
    size = 2 * window_size(half)
    kept = pl.BlockSpec((half, width), lambda i, meta: (meta[BITS], 0), pipeline_mode=pl.Buffered(1))
    return call(
        functools.partial(second_sum_kernel, half), meta, (own, far, arrived), [kept, kept, whole((half, width))],
        (jax.ShapeDtypeStruct((size, width), F32), jax.ShapeDtypeStruct((size, width), LOW)),
        (whole((size, width)),) * 2, (1,), cost=cost, name="second_sum",
    )


def third_sum_kernel(count, meta, *refs):
    kept, arrived, own, sent = refs[:count], refs[count], refs[count + 1 : 2 * count + 1], refs[-1]
    size = own[0].shape[0]
    bit = meta[BITS + 2]
    for at in range(count):
        for place in (bit, 1 - bit):
            begin = pl.multiple_of(place * size, TILE)
            far = arrived[pl.ds(pl.multiple_of(2 * at * size + begin, TILE), size), :].astype(F32)
            total = kept[at][pl.ds(begin, size), :] + far
            if place is bit:
                own[at][...] = total
            else:
                sent[at * size : (at + 1) * size, :] = total.astype(LOW)


def third_sum(meta, kept, arrived, cost=3):
    count = len(kept)
    size, width = kept[0].shape[0] // 2, kept[0].shape[1]
    *own, sent = call(
        functools.partial(third_sum_kernel, count), meta, (*kept, arrived),
        [whole(each.shape) for each in (*kept, arrived)],
        (jax.ShapeDtypeStruct((size, width), F32),) * count + (jax.ShapeDtypeStruct((count * size, width), LOW),),
        (whole((size, width)),) * count + (whole((count * size, width)),), (1,), cost=cost, name="third_sum",
    )
    return own, sent


def fourth_sum_kernel(count, meta, *refs):
    own, arrived, outs = refs[:count], refs[count], refs[count + 1 :]
    size = own[0].shape[0]
    for at, out in enumerate(outs):
        out[...] = (own[at][...] + arrived[at * size : (at + 1) * size, :].astype(F32)).astype(out.dtype)


def fourth_sum(meta, own, arrived, kinds):
    shape = own[0].shape
    return call(
        functools.partial(fourth_sum_kernel, len(own)), meta, (*own, arrived),
        [whole(each.shape) for each in (*own, arrived)],
        tuple(jax.ShapeDtypeStruct(shape, kind) for kind in kinds), (whole(shape),) * len(own),
        (1,), cost=3, name="fourth_sum",
    )


def widen_rows_kernel(meta, mine, far, *outs):
    half = mine.shape[0]

    def put(lower, upper):
        base = 0
        for out in outs:
            count = out.shape[0]
            split = min(max(half - base, 0), count)
            if split:
                out[:split, :] = lower[base : base + split, :].astype(F32)
            if split < count:
                begin = base + split - half
                out[split:, :] = upper[begin : begin + count - split, :].astype(F32)
            base += count

    @pl.when(meta[BITS] == 0)
    def _():
        put(mine, far)

    @pl.when(meta[BITS] == 1)
    def _():
        put(far, mine)


def widen_rows(meta, mine, far, rows):
    half, width = mine.shape
    return call(
        widen_rows_kernel, meta, (mine, far), [whole((half, width))] * 2,
        tuple(jax.ShapeDtypeStruct((count, width), F32) for count in rows),
        tuple(whole((count, width)) for count in rows), (1,), name="widen_rows",
    )


def later_groups(value):
    level = 3
    while (1 << level) < lax.axis_size("dp"):
        value = (value.astype(F32) + swap(value, "dp", 1 << level).astype(F32)).astype(value.dtype)
        level += 1
    return value


class Reduction:
    def __init__(self, meta, other):
        self.meta = meta
        self.far = swap(other, "tp", 2)

    def arrive(self, order):
        (self.far,) = order.step(self.far)

    def first(self, order, own):
        self.own, self.far = order.then(own, self.far)
        sent = first_sum(self.meta, self.own, self.far)
        order.done(sent)
        self.arrived = swap(sent, "dp", 1)

    def wait_second(self, order):
        (self.arrived,) = order.step(self.arrived)

    def second(self, order, cost=4):
        (arrived,) = order.then(self.arrived)
        self.half = arrived.shape[0]
        self.kept, sent = second_sum(self.meta, self.own, self.far, arrived, cost)
        order.done(sent)
        self.arrived = swap(sent, "dp", 2)

    def third(self, order, cost=3):
        (arrived,) = order.then(self.arrived)
        self.kept, sent = third_sum(self.meta, [self.kept], arrived, cost)
        order.done(sent)
        self.arrived = swap(sent, "dp", 4)

    def fourth(self, order):
        (arrived,) = order.then(self.arrived)
        (piece,) = fourth_sum(self.meta, self.kept, arrived, (LOW,))
        order.done(piece)
        piece = later_groups(piece)
        self.mine, self.far = piece, swap(piece, "dp", 4)

    def spread(self, order, level):
        mine, far = order.then(self.mine, self.far)
        rows = 2 * mine.shape[0] if level == 2 else self.half
        self.mine = join(self.meta, mine, far, level, rows)
        order.done(self.mine)
        self.far = swap(self.mine, "dp", 1 << (level - 1))

    def last_halves(self, order, rows):
        mine, far = order.then(self.mine, self.far)
        results = widen_rows(self.meta, mine, far, rows)
        order.done(results[0])
        return results


def eighth(block):
    half = block.shape[0] // 2
    index = lax.axis_index("dp")
    at = (index & 1) * half + window_at((index >> 1) & 1, (index >> 2) & 1, half)
    return lax.dynamic_slice_in_dim(block, at, window_size(half), 0)


def on_device(
    cell_inputs,
    out_grad,
    lengths,
    datasets,
    norm_gain,
    norm_bias,
    qkv_weight,
    qv_bias,
    out_weight,
    out_bias,
    up_weight,
    up_bias,
    down_weight,
    dataset_table,
):
    slots, quarter, width = cell_inputs.shape
    tensor = lax.axis_index("tp")
    chip = tensor // 2
    core = tensor % 2
    blocks_per_cell = lax.axis_size("tp")
    cell = quarter * blocks_per_cell
    shard = qkv_weight.shape[2]
    ff = up_weight.shape[1]
    heads = shard // HEAD_DIM
    kept = slots // 2
    tile_cap = META_BLOCKS * BLOCK // TILE
    cap = META_BLOCKS * BLOCK
    grid = (META_BLOCKS,)
    group = lax.axis_index("dp")
    index = jnp.arange(kept, dtype=jnp.int32)

    def mine_of(rows):
        pairs = rows.reshape(kept, 2, *rows.shape[1:])
        mine = lax.dynamic_index_in_dim(pairs, chip, 1, keepdims=False)
        theirs = lax.dynamic_index_in_dim(pairs, 1 - chip, 1, keepdims=False)
        return mine, theirs

    def place_cells(mine, other):
        even = jnp.where(chip == 0, mine, other)
        odd = jnp.where(chip == 0, other, mine)
        return jnp.stack([even, odd], axis=1).reshape(slots, quarter, width)

    cell_lengths, _ = mine_of(lengths)
    cell_sets, _ = mine_of(datasets)
    cell_tiles = (cell_lengths + TILE - 1) // TILE
    ends = jnp.sum(jnp.where(index[None, :] <= index[:, None], cell_tiles[None, :], 0), axis=1)
    begins = ends - cell_tiles
    tile_count = ends[-1]
    tile = jnp.arange(tile_cap, dtype=jnp.int32)
    owner = jnp.sum((ends[None, :] <= tile[:, None]).astype(jnp.int32), axis=1)
    live = tile < tile_count
    owned = (owner[:, None] == index[None, :]) & live[:, None]

    def of_owner(values):
        return jnp.sum(jnp.where(owned, values[None, :], 0), axis=1)

    block = tile - of_owner(begins)
    shelf = jnp.where(block // 2 == chip, 0, kept) + owner
    tile_src = jnp.where(live, jnp.where(block % 2 == core, 0, slots) + shelf, 0)
    tile_set = of_owner(cell_sets)
    tile_len = jnp.clip(of_owner(cell_lengths) - block * TILE, 0, TILE) * live
    tile_dst = jnp.where(live & (block % 2 == core), shelf, -1)
    cell_count = jnp.sum((cell_lengths > 0).astype(jnp.int32))
    block_count = (tile_count + BLOCK // TILE - 1) // (BLOCK // TILE)
    grid = (META_BLOCKS,)
    head = jnp.stack([block_count, cell_count, group & 1, (group >> 1) & 1, (group >> 2) & 1])

    meta = jnp.concatenate(
        [head, jnp.zeros((3,), jnp.int32), tile_src, tile_set, tile_len, tile_dst, begins, cell_tiles * TILE]
    ).astype(jnp.int32)

    order = Sequence()
    qkv_own = qkv_weight.transpose(1, 2, 0).reshape(3 * shard, width)
    qkv_rows = -(-3 * shard // (2 * TILE)) * 2 * TILE
    vectors = jnp.concatenate([qv_bias.reshape(-1), up_bias])
    piece_source, cells_now = lax.optimization_barrier(
        (eighth(jnp.pad(qkv_own, ((0, qkv_rows - 3 * shard), (0, 0)))), cell_inputs)
    )
    qkv_piece = swap(piece_source, "tp", 2)
    in_mine, in_theirs = mine_of(cells_now)
    in_other = swap(in_theirs, "tp", 2)
    in_far = swap(in_mine, "tp", 1)
    head_rows = jnp.pad(vectors, (0, 2 * width - vectors.shape[0])).reshape(2, width)
    out_and_vectors = jnp.concatenate([out_weight, head_rows, jnp.zeros((6, width), LOW)], axis=0)
    meta, qkv_own, out_and_vectors, down_piece = order.step(meta, qkv_own, out_and_vectors, eighth(down_weight))
    (qkv_piece,) = order.step(qkv_piece)
    qkv_other = gather_eighths(qkv_piece)
    in_far, in_other = order.step(in_far, in_other)
    in_other_far = swap(in_other, "tp", 1)
    down_piece, out_and_vectors = order.then(down_piece, out_and_vectors)
    down_piece = swap(down_piece, "tp", 2)
    out_and_vectors = swap(out_and_vectors, "tp", 2)
    (in_other_far,) = order.step(in_other_far)

    def biases(vector):
        zeros = jnp.zeros((shard,), LOW)
        qkv_row = jnp.concatenate([vector[:shard], zeros, vector[shard : 2 * shard]])
        return qkv_row.astype(F32)[None], vector[2 * shard :].astype(F32)[None]

    qkv_bias_own, up_bias_own = biases(vectors)
    gains = norm_gain.astype(F32)
    shifts = norm_bias.astype(F32)
    out_rows = out_bias.astype(F32)
    table = dataset_table.astype(F32)

    def shape(rows, cols, kind=LOW):
        return jax.ShapeDtypeStruct((rows, cols), kind)

    row_f32, row_low = shape(cap, width, F32), shape(cap, width)
    row_scratch = pltpu.VMEM((BLOCK, width), F32)
    tile_scratch = [pltpu.VMEM((2 * slots, TILE, width), LOW), pltpu.SemaphoreType.DMA((4,))]

    start, normed, proj_own = call(
        functools.partial(begin_kernel, kept), meta,
        (in_mine, in_other, in_far, in_other_far, table, gains[0:1], shifts[0:1], qkv_own, qkv_bias_own),
        [ANYWHERE] * 4 + [whole(table.shape), whole((1, width)), whole((1, width)), whole((3 * shard, width)), whole((1, 3 * shard))],
        (row_f32, row_low, shape(cap, 3 * shard)),
        (rows_out(width), rows_out(width), rows_more(3 * shard)),
        grid, tile_scratch, 15, "begin",
    )
    order.done(proj_own)

    def attend_shard(projected):
        (projected,) = order.then(projected)
        context, attend = call(
            functools.partial(attention_kernel, heads, shard, cell), meta, (projected,),
            [whole((cap, 3 * shard))],
            (shape(cap, shard), jax.ShapeDtypeStruct((kept, cell, heads * cell), LOW)),
            (whole((cap, shard)), whole((kept, cell, heads * cell))),
            (1,), (), 4, "attend",
        )
        order.done(context)
        return context, attend

    down_piece, out_and_vectors = order.step(down_piece, out_and_vectors)
    down_other = gather_eighths(down_piece)
    grad_mine, grad_theirs = mine_of(order.then(out_grad)[0])
    grad_other = swap(grad_theirs, "tp", 2)
    grad_far = swap(grad_mine, "tp", 1)
    context_own, attend_own = attend_shard(proj_own)
    (grad_far,) = order.step(grad_far)
    up_other = swap(order.then(up_weight)[0], "tp", 2)
    out_other = out_and_vectors[:shard]
    vectors_other = out_and_vectors[shard : shard + 2].reshape(-1)[: vectors.shape[0]]
    normed_now, qkv_now = order.then(normed, qkv_other)
    qkv_bias_other, up_bias_other = biases(vectors_other)
    (proj_other,) = call(
        project_kernel, meta, (normed_now, qkv_now, qkv_bias_other),
        [rows_spec(width), ANYWHERE, whole((1, 3 * shard))],
        (shape(cap, 3 * shard),), (rows_more(3 * shard),),
        grid, [pltpu.VMEM((qkv_rows, width), LOW), pltpu.SemaphoreType.DMA((8,))],
        6, "project",
    )
    order.done(proj_other)
    context_other, attend_other = attend_shard(proj_other)
    (grad_other,) = order.step(grad_other)
    grad_other_far = swap(grad_other, "tp", 1)
    (context_now,) = order.then(context_other)
    attn_part = call(
        out_project_kernel, meta, (context_own, context_now, out_weight, out_other),
        [rows_spec(shard), rows_spec(shard), whole((shard, width)), whole((shard, width))],
        part_shapes(cap, width), (ANYWHERE,) * CHUNKS,
        grid, out_scratch(width), 10, "out_project",
    )
    order.done(*attn_part)
    attn_far = swap_cores(attn_part)
    (grad_other_far,) = order.step(grad_other_far)

    start_now, grad_far, grad_other_far, up_other, down_other, *attn_far = order.then(
        start, grad_far, grad_other_far, up_other, down_other, *attn_far
    )
    middle, second, grad_low, active_own, hidden_own, active_other, hidden_other, *parts, up_vecs = call(
        functools.partial(mlp_kernel, kept), meta,
        (start_now, *attn_part, *attn_far, out_rows[0:1], gains[1:2], shifts[1:2], grad_mine, grad_other, grad_far, grad_other_far,
         up_weight, up_bias_own, down_weight, up_other, up_bias_other, down_other),
        [rows_spec(width)] + [ANYWHERE] * (2 * CHUNKS) + [whole((1, width))] * 3 + [ANYWHERE] * 4
        + [whole((width, ff)), whole((1, ff)), whole((ff, width)), whole((width, ff)), whole((1, ff)), ANYWHERE],
        (row_f32, row_low, row_low, *(shape(cap, ff),) * 4, *part_shapes(cap, width), *part_shapes(cap, width), shape(8, ff, F32)),
        (rows_out(width),) * 3 + (rows_out(ff),) * 4 + (ANYWHERE,) * (2 * CHUNKS) + (whole((8, ff)),),
        grid,
        tile_scratch + parts_scratch(width) * 2
        + [pltpu.VMEM((ff, width), LOW), pltpu.SemaphoreType.DMA((8,))]
        + out_scratch(width) * 2,
        65, "mlp",
    )
    branch, second_grad = parts[:CHUNKS], parts[CHUNKS:]
    order.done(*second_grad)
    second_grad_far = swap_cores(second_grad)
    branch_far = swap_cores(branch)

    def weight_grad(*operands, rows=None):
        operands = order.then(*operands)
        pairs = len(operands) // 2
        cols = operands[1].shape[1]
        rows = rows or operands[0].shape[1]
        (result,) = call(
            functools.partial(weight_grad_kernel, pairs), meta, operands,
            [rows_spec(operand.shape[1]) for operand in operands],
            (shape(rows, cols),), (whole((rows, cols)),),
            grid, [pltpu.VMEM((rows, cols), F32)], cost=13, name="weight_grad",
        )
        order.done(result)
        return result

    up_sum = Reduction(meta, weight_grad(second, hidden_other))
    down_sum = Reduction(meta, weight_grad(active_other, grad_low))

    pair_shape = jax.ShapeDtypeStruct((slots, TILE, width), LOW)
    pair_spec = whole((slots, TILE, width))

    second_grad_far = order.then(*second_grad_far)
    middle_grad, attn_grad, context_grad_own, context_grad_other, second_sums = call(
        middle_back_kernel, meta,
        (*second_grad, *second_grad_far, middle, grad_low, gains[1:2], out_weight, out_other),
        [ANYWHERE] * (2 * CHUNKS) + [rows_spec(width)] * 2 + [whole((1, width)), whole((shard, width)), whole((shard, width))],
        (row_f32, row_low, shape(cap, shard), shape(cap, shard), shape(8, width, F32)),
        (rows_out(width), rows_out(width), rows_out(shard), rows_out(shard), whole((8, width))),
        grid, parts_scratch(width) * 2, 18, "middle_back",
    )
    order.done(context_grad_other)


    branch_far = order.step(*branch_far)

    def attend_back(projected, attend, context_grad):
        projected, attend, context_grad = order.then(projected, attend, context_grad)
        grads, sums = call(
            functools.partial(attention_back_kernel, heads, shard, cell), meta,
            (projected, attend, context_grad),
            [whole((cap, 3 * shard)), whole((kept, cell, heads * cell)), whole((cap, shard))],
            (shape(cap, 3 * shard), shape(8, shard, F32)), (whole((cap, 3 * shard)), whole((8, shard))),
            (1,), (), 30, "attend_back",
        )
        order.done(grads)
        return grads, sums

    up_own = weight_grad(second, hidden_own)
    proj_grad_other, qkv_vec_other = attend_back(proj_other, attend_other, context_grad_other)
    up_sum.first(order, up_own)
    down_own = weight_grad(active_own, grad_low)

    def attn_grads(proj_grad, context):
        return weight_grad(proj_grad, normed, context, attn_grad, rows=width)

    attn_sum = Reduction(meta, attn_grads(proj_grad_other, context_other))
    down_sum.first(order, down_own)
    up_sum.second(order)
    proj_grad_own, qkv_vec_own = attend_back(proj_own, attend_own, context_grad_own)
    up_sum.third(order)
    down_sum.second(order)
    attn_own = attn_grads(proj_grad_own, context_own)
    attn_sum.first(order, attn_own)
    up_sum.fourth(order)
    down_sum.third(order)
    (first_grads,) = order.then(proj_grad_own)
    first_part = call(
        first_part_kernel, meta,
        (first_grads, proj_grad_other, qkv_own, qkv_other),
        [rows_spec(3 * shard)] * 2 + [whole((3 * shard, width)), ANYWHERE],
        part_shapes(cap, width), (ANYWHERE,) * CHUNKS,
        grid, [pltpu.VMEM((qkv_rows, width), LOW), pltpu.SemaphoreType.DMA((8,)), *out_scratch(width)],
        15, "first_part",
    )
    order.done(*first_part)
    first_far = swap_cores(first_part)
    up_sum.spread(order, 2)
    down_sum.fourth(order)
    attn_sum.second(order, 60)
    first_far = order.then(*first_far)
    input_pair, first_sums, table_grad = call(
        start_back_kernel, meta, (*first_part, *first_far, start, middle_grad, gains[0:1]),
        [ANYWHERE] * (2 * CHUNKS) + [rows_spec(width)] * 2 + [whole((1, width))],
        (pair_shape, shape(8, width, F32), shape(table.shape[0], width, F32)),
        (pair_spec, whole((8, width)), whole(table.shape)),
        grid, [row_scratch] + parts_scratch(width) * 2, 15, "start_back",
    )
    order.done(input_pair)
    up_sum.spread(order, 1)
    attn_sum.third(order)
    down_sum.spread(order, 2)
    rows_small = 8 + table.shape[0]
    vector_inputs = (first_sums, second_sums, table_grad, qkv_vec_own, qkv_vec_other, up_vecs)
    small, small_other = call(
        functools.partial(vectors_kernel, shard), meta, vector_inputs,
        [whole(value.shape) for value in vector_inputs],
        (shape(rows_small, width, F32),) * 2, (whole((rows_small, width)),) * 2, (1,), (), 2, "vectors",
    )
    small_far = swap(small_other, "tp", 2)
    input_far = swap(input_pair[kept:], "tp", 2)
    attn_sum.fourth(order)
    (small_far,) = order.step(small_far)
    small = small + small_far
    small_far = swap(small, "dp", 1)
    down_sum.spread(order, 1)
    middle_now, *branch_far = order.then(middle, *branch_far)
    (output_pair,) = call(
        finish_kernel, meta, (middle_now, *branch, *branch_far, out_rows[1:2]),
        [rows_spec(width)] + [ANYWHERE] * (2 * CHUNKS) + [whole((1, width))],
        (pair_shape,), (pair_spec,),
        grid, [row_scratch] + parts_scratch(width) * 2, 10, "finish",
    )
    order.done(output_pair)
    output_far = swap(output_pair[kept:], "tp", 2)
    attn_sum.spread(order, 2)
    (input_far,) = order.step(input_far)
    (up_total,) = up_sum.last_halves(order, (width,))
    (down_total,) = down_sum.last_halves(order, (width,))
    attn_sum.spread(order, 1)
    (small_far,) = order.step(small_far)
    small = small + small_far
    small_far = swap(small, "dp", 2)
    input_grad = place_cells(input_pair[:kept], order.then(input_far)[0])
    order.done(input_grad)
    (small_far,) = order.step(small_far)
    small = small + small_far
    small_far = swap(small, "dp", 4)
    cell_outputs = place_cells(output_pair[:kept], order.then(output_far)[0])
    order.done(cell_outputs)
    (small_far,) = order.step(small_far)
    small = later_groups(small + small_far)
    qkv_total, out_total = attn_sum.last_halves(order, (3 * shard, shard))

    return (
        cell_outputs,
        input_grad,
        small[0:2],
        small[2:4],
        qkv_total.reshape(3, shard, width).transpose(2, 0, 1),
        small[-2, : 2 * shard].reshape(2, shard),
        out_total,
        small[4:6],
        up_total,
        small[-1],
        down_total,
        small[6:-2],
    )


def solution(mesh):
    in_specs = (
        P("dp", "tp", None),
        P("dp", "tp", None),
        P("dp"),
        P("dp"),
        P(),
        P(),
        P(None, None, "tp"),
        P(None, "tp"),
        P("tp", None),
        P(),
        P(None, "tp"),
        P("tp"),
        P("tp", None),
        P(),
    )
    out_specs = (
        P("dp", "tp", None),
        P("dp", "tp", None),
        P(),
        P(),
        P(None, None, "tp"),
        P(None, "tp"),
        P("tp", None),
        P(),
        P(None, "tp"),
        P("tp"),
        P("tp", None),
        P(),
    )
    return jax.shard_map(
        on_device, mesh=mesh, in_specs=in_specs, out_specs=out_specs, check_vma=False
    )
```

time: 675 us -> 628 us (0.930)
  Pallas kernels: 401 us -> 298 us
  starting transfers between devices: 45.8 us -> 108 us
  local copies, waits for them, and re-layouts: 63.4 us -> 46 us
  waiting for transfers between devices: 126 us -> 139 us
    pallas_call x32 -> x40, Pallas kernels: 401 us -> 298 us  [call(): pl.pallas_call(kernel, grid_spec=pltpu.PrefetchScalarGridSpec(num_scalar_...]
    ppermute x50 -> x45, starting transfers between devices: 45.6 us -> 108 us  [swap(): return lax.ppermute(value, axis, [(i, i ^ bit) for i in range(count)])]
    ppermute x50 -> x45, waiting for transfers between devices: 126 us -> 139 us  [swap(): return lax.ppermute(value, axis, [(i, i ^ bit) for i in range(count)])]
    slice x13 -> x2, local copies, waits for them, and re-layouts: 9.78 us -> 1.19 us  [the longest x1 1.1 us: on_device(): input_far = swap(input_pair[kept:], 'tp', 2)]
    reshape x2, local copies, waits for them, and re-layouts: 8.3 us -> 0.89 us  [mine_of(): pairs = rows.reshape(kept, 2, *rows.shape[1:])]
    unnamed x100 -> x78, local copies, waits for them, and re-layouts: 17.4 us -> 20.5 us
  transfers between devices with their start and end apart: 54 -> 47, of which waited for: 15 -> 16; matrix products, arithmetic and copies ran while one was open for 7% -> 6% of each run, Pallas kernels for 54% -> 40%
where the time goes in v2:
time: 628 us; the launch traced here: 619 us
  Pallas kernels  298 us (47%)
  waiting for transfers between devices  139 us (22%)
  starting transfers between devices  108 us (17%)
  local copies, waits for them, and re-layouts  46 us (7%)
  between operations  15.4 us (2%)
  other arithmetic  12.8 us (2%)
    pallas_call x40, Pallas kernels, call(): pl.pallas_call(kernel, grid_spec=pltpu.PrefetchScalarGridSpec(num_scalar_...  298 us
    ppermute x45, waiting for transfers between devices, swap(): return lax.ppermute(value, axis, [(i, i ^ bit) for i in range(count)])  139 us
    ppermute x45, starting transfers between devices, swap(): return lax.ppermute(value, axis, [(i, i ^ bit) for i in range(count)])  108 us
    unnamed x78, local copies, waits for them, and re-layouts  20.5 us
  transfers between devices with their start and end apart: 47, of which 16 were waited for; matrix products, arithmetic and copies ran while one was open for 6% of the time, Pallas kernels for 40%

profile of v2, /device:TPU:0, one launch (start us, length us, event | category | flops | bytes accessed | tf_op | source)
XLA Modules:
  0.0 618.9 jit_solution(3422201378166693668)
XLA Ops:
  8.2 3.0 collective-permute-start.2
  26.8 16.0 %collective-permute-done.1.a1 = bf16[32,16,1120]{2,1,0:T(8,128)(2,1)} collective-permute-done((bf16[32,16,1120]{2,1,0:T(8,128)(2,1)S(1)}, bf16[32,16,1120]{2,1,0:T(8,128)(2,1)}, u32[]{:S(2)}, u32[]{:S(2)}) %collective-permute-start.1) | collective-permute-done | bytes 1146912 | tf_op jit(solution)/shard_map/ppermute | solution.py:30
  53.5 10.7 %begin.1 = (f32[2048,1120]{1,0:T(8,128)}, bf16[2048,1120]{1,0:T(8,128)(2,1)}, bf16[2048,840]{1,0:T(8,128)(2,1)}) custom-call(s32[584]{0:T(1024)} %concatenate.35.meta, bf16[32,16,1120]{2,1,0:T(8,128)(2,1)} %copy-done.8, bf16[32,16,1120]{2,1,0:T(8,128)(2,1)} %collective-permute-done.1.a1, bf16[32,16,1120]{2,1,0:T(8,128)(2,1)} %collective-permute-done.a2, ...), custom_call_target="tpu_custom_call" | custom-call | flops 6750000128 | tf_op jit(solution)/shard_map/begin/pallas_call | solution.py:179
  64.2 6.8 %collective-permute-done.4 = bf16[9,16,1120]{2,1,0:T(8,128)(2,1)} collective-permute-done((bf16[9,16,1120]{2,1,0:T(8,128)(2,1)}, bf16[9,16,1120]{2,1,0:T(8,128)(2,1)}, u32[]{:S(2)}, u32[]{:S(2)}) %collective-permute-start.4) | collective-permute-done | bytes 322592 | tf_op jit(solution)/shard_map/ppermute | solution.py:30
  74.7 2.0 slice.88.weight_b.refs_8_
  77.5 12.3 %attend.2 = (bf16[2048,280]{1,0:T(8,128)(2,1)}, bf16[32,64,320]{2,1,0:T(8,128)(2,1)}) custom-call(s32[584]{0:T(1024)} %concatenate.35.meta, bf16[2048,840]{1,0:T(8,128)(2,1)} %get-tuple-element.239.projected), custom_call_target="tpu_custom_call" | custom-call | flops 1800000000 | tf_op jit(solution)/shard_map/attend/pallas_call | solution.py:179
  91.1 8.0 %project.1.projected = bf16[2048,840]{1,0:T(8,128)(2,1)} custom-call(s32[584]{0:T(1024)} %concatenate.35.meta, bf16[2048,1120]{1,0:T(8,128)(2,1)} %get-tuple-element.250.normed.refs_1_, bf16[896,1120]{1,0:T(8,128)(2,1)} %bitcast.122, f32[1,840]{1,0:T(1,128)} %fusion.7.bias), custom_call_target="tpu_custom_call" | custom-call | flops 2700000000 | tf_op jit(solution)/shard_map/project/pallas_call | solution.py:179
  99.1 12.8 %attend.3 = (bf16[2048,280]{1,0:T(8,128)(2,1)}, bf16[32,64,320]{2,1,0:T(8,128)(2,1)}) custom-call(s32[584]{0:T(1024)} %concatenate.35.meta, bf16[2048,840]{1,0:T(8,128)(2,1)} %project.1.projected), custom_call_target="tpu_custom_call" | custom-call | flops 1800000000 | tf_op jit(solution)/shard_map/attend/pallas_call | solution.py:179
  111.9 6.2 out_project.1
  120.6 5.7 collective-permute-done.8.refs_10_
  126.2 29.9 %collective-permute-done.9 = bf16[70,16,1120]{2,1,0:T(8,128)(2,1)S(1)} collective-permute-done((bf16[70,16,1120]{2,1,0:T(8,128)(2,1)}, bf16[70,16,1120]{2,1,0:T(8,128)(2,1)S(1)}, u32[]{:S(2)}, u32[]{:S(2)}) %collective-permute-start.9) | collective-permute-done | bytes 2508832 | tf_op jit(solution)/shard_map/ppermute | solution.py:30
  157.7 39.7 %mlp.1 = (f32[2048,1120]{1,0:T(8,128)}, bf16[2048,1120]{1,0:T(8,128)(2,1)}, bf16[2048,1120]{1,0:T(8,128)(2,1)}, bf16[2048,1120]{1,0:T(8,128)(2,1)}, bf16[2048,11...) custom-call(s32[584]{0:T(1024)} %concatenate.35.meta, ...), custom_call_target="tpu_custom_call" | custom-call | flops 29250000896 | tf_op jit(solution)/shard_map/mlp/pallas_call | solution.py:179
  198.5 8.1 %weight_grad.6 = bf16[1120,1120]{1,0:T(8,128)(2,1)} custom-call(s32[584]{0:T(1024)} %concatenate.35.meta, bf16[2048,1120]{1,0:T(8,128)(2,1)} %get-tuple-element.216.refs_0_, bf16[2048,1120]{1,0:T(8,128)(2,1)} %get-tuple-element.206.refs_1_), custom_call_target="tpu_custom_call" | custom-call | flops 5849999872 | tf_op jit(solution)/shard_map/weight_grad/pallas_call | solution.py:179
  206.6 8.3 %weight_grad.7 = bf16[1120,1120]{1,0:T(8,128)(2,1)} custom-call(s32[584]{0:T(1024)} %concatenate.35.meta, bf16[2048,1120]{1,0:T(8,128)(2,1)} %get-tuple-element.207.refs_0_, bf16[2048,1120]{1,0:T(8,128)(2,1)} %get-tuple-element.226.refs_1_.refs_5_), custom_call_target="tpu_custom_call" | custom-call | flops 5849999872 | tf_op jit(solution)/shard_map/weight_grad/pallas_call | solution.py:179
  216.3 12.7 %middle_back.1 = (f32[2048,1120]{1,0:T(8,128)}, bf16[2048,1120]{1,0:T(8,128)(2,1)}, bf16[2048,280]{1,0:T(8,128)(2,1)}, bf16[2048,280]{1,0:T(8,128)(2,1)}, f32[8,1120]{1,0:T(8,128)}) custom-call(s32[584]{0:T(1024)} %concatenate.35.meta, bf16[1024,1120]{1,0:T(8,128)(2,1)} %get-tuple-element.199.refs_0_, bf16[1024,1120]{1,0:T(8,128)(2,1)} %get-tuple-element.200.refs_1_, ...), custom_call_target="tpu_custom_call" | custom-call | flops 8099999744 | tf_op jit(solution)/shard_map/middle_back/pallas_call | solution.py:179
  229.0 9.0 %weight_grad.8.own.mine = bf16[1120,1120]{1,0:T(8,128)(2,1)} custom-call(s32[584]{0:T(1024)} %concatenate.35.meta, bf16[2048,1120]{1,0:T(8,128)(2,1)} %get-tuple-element.216.refs_0_, bf16[2048,1120]{1,0:T(8,128)(2,1)} %get-tuple-element.217.refs_1_), custom_call_target="tpu_custom_call" | custom-call | flops 5849999872 | tf_op jit(solution)/shard_map/weight_grad/pallas_call | solution.py:179
  238.0 15.6 %attend_back.2 = (bf16[2048,840]{1,0:T(8,128)(2,1)}, f32[8,280]{1,0:T(8,128)}) custom-call(s32[584]{0:T(1024)} %concatenate.35.meta, bf16[2048,840]{1,0:T(8,128)(2,1)} %project.1.projected, bf16[32,64,320]{2,1,0:T(8,128)(2,1)} %get-tuple-element.220.attend, bf16[2048,280]{1,0:T(8,128)(2,1)} %get-tuple-element.221.context_grad), custom_call_target="tpu_custom_call" | custom-call | flops 13500000256 | tf_op jit(solution)/shard_map/attend_back/pallas_call | solution.py:179
  253.6 12.1 %collective-permute-done.16 = bf16[70,16,1120]{2,1,0:T(8,128)(2,1)} collective-permute-done((bf16[70,16,1120]{2,1,0:T(8,128)(2,1)}, bf16[70,16,1120]{2,1,0:T(8,128)(2,1)}, u32[]{:S(2)}, u32[]{:S(2)}) %collective-permute-start.16) | collective-permute-done | bytes 2508832 | tf_op jit(solution)/shard_map/ppermute | solution.py:30
  265.7 5.4 first_sum.3
  271.2 27.0 %collective-permute-start.19 = (bf16[35,16,1120]{2,1,0:T(8,128)(2,1)}, bf16[35,16,1120]{2,1,0:T(8,128)(2,1)S(1)}, u32[]{:S(2)}, u32[]{:S(2)}) collective-permute-start(bf16[35,16,1120]{2,1,0:T(8,128)(2,1)} %bitcast.146), channel_id=1, source_target_pairs={{0,4},{4,0},{8,12},{12,8},{16,20},{20,16},{24,28},{28,24},{1,5},{5... | collective-permute-start | bytes 3763208 | tf_op jit(solution)/shard_map/ppermute | solution.py:30
  298.1 8.1 %weight_grad.9.own.mine = bf16[1120,1120]{1,0:T(8,128)(2,1)} custom-call(s32[584]{0:T(1024)} %concatenate.35.meta, bf16[2048,1120]{1,0:T(8,128)(2,1)} %get-tuple-element.225.refs_0_, bf16[2048,1120]{1,0:T(8,128)(2,1)} %get-tuple-element.226.refs_1_.refs_5_), custom_call_target="tpu_custom_call" | custom-call | flops 5849999872 | tf_op jit(solution)/shard_map/weight_grad/pallas_call | solution.py:179
  306.2 9.7 %weight_grad.10 = bf16[1120,1120]{1,0:T(8,128)(2,1)} custom-call(s32[584]{0:T(1024)} %concatenate.35.meta, bf16[2048,840]{1,0:T(8,128)(2,1)} %get-tuple-element.228.refs_0_.b, bf16[2048,1120]{1,0:T(8,128)(2,1)} %get-tuple-element.250.normed.refs_1_, bf16[2048,280]{1,0:T(8,128)(2,1)} %get-tuple-element.230.b.refs_2_, ...), custom_call_target="tpu_custom_call" | custom-call | flops 5849999872 | tf_op jit(solution)/shard_map/weight_grad/pallas_call | solution.py:179
  315.9 5.2 collective-permute-done.17
  321.0 5.2 first_sum.4
  326.2 21.4 %collective-permute-start.18 = (bf16[35,16,1120]{2,1,0:T(8,128)(2,1)}, bf16[35,16,1120]{2,1,0:T(8,128)(2,1)S(1)}, u32[]{:S(2)}, u32[]{:S(2)}) collective-permute-start(bf16[35,16,1120]{2,1,0:T(8,128)(2,1)} %bitcast.144), channel_id=1, source_target_pairs={{0,4},{4,0},{8,12},{12,8},{16,20},{20,16},{24,28},{28,24},{1,5},{5... | collective-permute-start | bytes 3763208 | tf_op jit(solution)/shard_map/ppermute | solution.py:30
  348.7 4.3 second_sum.3
  352.9 14.4 %collective-permute-start.20 = (bf16[18,16,1120]{2,1,0:T(8,128)(2,1)}, bf16[18,16,1120]{2,1,0:T(8,128)(2,1)S(1)}, u32[]{:S(2)}, u32[]{:S(2)}) collective-permute-start(bf16[18,16,1120]{2,1,0:T(8,128)(2,1)} %bitcast.156), channel_id=1, source_target_pairs={{0,8},{4,12},{8,0},{12,4},{16,24},{20,28},{24,16},{28,20},{1,9},{5... | collective-permute-start | bytes 1935368 | tf_op jit(solution)/shard_map/ppermute | solution.py:30
  367.3 15.5 %attend_back.3 = (bf16[2048,840]{1,0:T(8,128)(2,1)}, f32[8,280]{1,0:T(8,128)}) custom-call(s32[584]{0:T(1024)} %concatenate.35.meta, bf16[2048,840]{1,0:T(8,128)(2,1)} %get-tuple-element.239.projected, bf16[32,64,320]{2,1,0:T(8,128)(2,1)} %get-tuple-element.240.attend, bf16[2048,280]{1,0:T(8,128)(2,1)} %get-tuple-element.241.context_grad), custom_call_target="tpu_custom_call" | custom-call | flops 13500000256 | tf_op jit(solution)/shard_map/attend_back/pallas_call | solution.py:179
  383.7 3.2 third_sum.3
  387.9 4.5 second_sum.4
  392.4 14.5 %collective-permute-start.21 = (bf16[18,16,1120]{2,1,0:T(8,128)(2,1)}, bf16[18,16,1120]{2,1,0:T(8,128)(2,1)S(1)}, u32[]{:S(2)}, u32[]{:S(2)}) collective-permute-start(bf16[18,16,1120]{2,1,0:T(8,128)(2,1)} %bitcast.152), channel_id=1, source_target_pairs={{0,8},{4,12},{8,0},{12,4},{16,24},{20,28},{24,16},{28,20},{1,9},{5... | collective-permute-start | bytes 1935368 | tf_op jit(solution)/shard_map/ppermute | solution.py:30
  406.9 10.1 %weight_grad.11.own.mine = bf16[1120,1120]{1,0:T(8,128)(2,1)} custom-call(s32[584]{0:T(1024)} %concatenate.35.meta, bf16[2048,840]{1,0:T(8,128)(2,1)} %get-tuple-element.259.refs_0_.a, bf16[2048,1120]{1,0:T(8,128)(2,1)} %get-tuple-element.250.normed.refs_1_, bf16[2048,280]{1,0:T(8,128)(2,1)} %get-tuple-element.251.a.refs_2_, ...), custom_call_target="tpu_custom_call" | custom-call | flops 5849999872 | tf_op jit(solution)/shard_map/weight_grad/pallas_call | solution.py:179
  418.5 5.2 first_sum.5
  425.4 2.7 fourth_sum.3.mine
  429.1 3.3 third_sum.4
  432.3 2.7 collective-permute-start.24
  435.1 9.8 %first_part.1 = (bf16[1024,1120]{1,0:T(8,128)(2,1)}, bf16[1024,1120]{1,0:T(8,128)(2,1)}) custom-call(s32[584]{0:T(1024)} %concatenate.35.meta, bf16[2048,840]{1,0:T(8,128)(2,1)} %get-tuple-element.259.refs_0_.a, bf16[2048,840]{1,0:T(8,128)(2,1)} %get-tuple-element.228.refs_0_.b, bf16[840,1120]{1,0:T(8,128)(2,1)} %bitcast.126, bf16[896,1120]{1,0:T(8,128)(2,1)} %bitcast.123), custom_call_target="tpu_custom_call" | custom-call | flops 6750000128 | tf_op jit(solution)/shard_map/first_part/pallas_call | solution.py:179
  445.4 8.2 %collective-permute-done.25 = bf16[9,16,1120]{2,1,0:T(8,128)(2,1)S(1)} collective-permute-done((bf16[9,16,1120]{2,1,0:T(8,128)(2,1)}, bf16[9,16,1120]{2,1,0:T(8,128)(2,1)S(1)}, u32[]{:S(2)}, u32[]{:S(2)}) %collective-permute-start.25) | collective-permute-done | bytes 322592 | tf_op jit(solution)/shard_map/ppermute | solution.py:30
  454.4 2.7 join.6.mine
  459.2 2.6 fourth_sum.4.mine
  462.9 4.3 second_sum.5
  470.6 11.1 %start_back.1 = (bf16[64,16,1120]{2,1,0:T(8,128)(2,1)}, f32[8,1120]{1,0:T(8,128)}, f32[32,1120]{1,0:T(8,128)}) custom-call(s32[584]{0:T(1024)} %concatenate.35.meta, bf16[1024,1120]{1,0:T(8,128)(2,1)} %get-tuple-element.267.refs_0_, bf16[1024,1120]{1,0:T(8,128)(2,1)} %get-tuple-element.260.refs_1_, bf16[1024,1120]{1,0:T(8,128)(2,1)} %bitcast.112, ...), custom_call_target="tpu_custom_call" | custom-call | flops 6750000128 | tf_op jit(solution)/shard_map/start_back/pallas_call | solution.py:179
  483.1 3.0 join.7.mine
  486.2 9.0 %collective-permute-done.28 = bf16[18,16,1120]{2,1,0:T(8,128)(2,1)S(1)} collective-permute-done((bf16[18,16,1120]{2,1,0:T(8,128)(2,1)}, bf16[18,16,1120]{2,1,0:T(8,128)(2,1)S(1)}, u32[]{:S(2)}, u32[]{:S(2)}) %collective-permute-start.28) | collective-permute-done | bytes 645152 | tf_op jit(solution)/shard_map/ppermute | solution.py:30
  496.0 3.2 third_sum.5
  500.0 2.8 join.8.mine
  504.6 2.5 vectors.1
  508.2 2.0 collective-permute-start.41
  510.6 14.9 %collective-permute-done.34 = bf16[9,16,1120]{2,1,0:T(8,128)(2,1)S(1)} collective-permute-done((bf16[9,16,1120]{2,1,0:T(8,128)(2,1)S(1)}, bf16[9,16,1120]{2,1,0:T(8,128)(2,1)S(1)}, u32[]{:S(2)}, u32[]{:S(2)}) %collective-permute-start.34) | collective-permute-done | bytes 322592 | tf_op jit(solution)/shard_map/ppermute | solution.py:30
  526.2 2.7 fourth_sum.5.mine
  529.7 3.2 join.9.mine
  533.4 3.4 collective-permute-start.37
  536.7 8.2 %finish.1 = bf16[64,16,1120]{2,1,0:T(8,128)(2,1)} custom-call(s32[584]{0:T(1024)} %concatenate.35.meta, f32[2048,1120]{1,0:T(8,128)} %get-tuple-element.290.refs_4_.middle, bf16[1024,1120]{1,0:T(8,128)(2,1)} %get-tuple-element.197.refs_0_, bf16[1024,1120]{1,0:T(8,128)(2,1)} %get-tuple-element.198.refs_1_, bf16[1024,1120]{1,0:T(8,128)(2,1)} %bitcast.120, ...), custom_call_target="tpu_custom_call" | custom-call | flops 4499999744 | tf_op jit(solution)/shard_map/finish/pallas_call | solution.py:179
  545.0 4.3 collective-permute-done.37
  550.0 2.8 join.10.mine
  556.8 5.1 widen_rows.3
  561.8 6.9 %collective-permute-done.39 = bf16[35,16,1120]{2,1,0:T(8,128)(2,1)} collective-permute-done((bf16[35,16,1120]{2,1,0:T(8,128)(2,1)}, bf16[35,16,1120]{2,1,0:T(8,128)(2,1)}, u32[]{:S(2)}, u32[]{:S(2)}) %collective-permute-start.39) | collective-permute-done | bytes 1254432 | tf_op jit(solution)/shard_map/ppermute | solution.py:30
  568.8 5.2 widen_rows.4
  574.0 3.2 join.11.mine
  581.3 2.7 collective-permute-done.42
  584.0 2.8 collective-permute-start.43
  588.9 3.6 collective-permute-done.43
  595.1 11.7 %collective-permute-done.44 = bf16[35,16,1120]{2,1,0:T(8,128)(2,1)} collective-permute-done((bf16[35,16,1120]{2,1,0:T(8,128)(2,1)}, bf16[35,16,1120]{2,1,0:T(8,128)(2,1)}, u32[]{:S(2)}, u32[]{:S(2)}) %collective-permute-start.44) | collective-permute-done | bytes 1254432 | tf_op jit(solution)/shard_map/ppermute | solution.py:30
  606.8 5.1 widen_rows.5
  (209 shorter events, 75.7 us)
Async XLA Ops:
  7.2 83.9 %all-gather.3.cloned.1.call-start = ((), (), s32[]{:S(2)}) async-start(), calls=%async_computation | async-start | bytes 2322432 | tf_op jit(solution)/shard_map/all_gather | solution.py:649
  8.2 10.1 %collective-permute-start.2 = (bf16[7,16,1120]{2,1,0:T(8,128)(2,1)S(1)}, bf16[7,16,1120]{2,1,0:T(8,128)(2,1)S(1)}, u32[]{:S(2)}, u32[]{:S(2)}) collective-permute-start(bf16[7,16,1120]{2,1,0:T(8,128)(2,1)S(1)} %bitcast.127), channel_id=1, source_target_pairs={{0,2},{1,3},{2,0},{3,1},{4,6},{5,7},{6,4},{7,5},{8,10},{9,11},{10,... | collective-permute-start | bytes 752648 | tf_op jit(solution)/shard_map/ppermute | solution.py:30
  11.2 34.0 %copy-start.10 = (bf16[280,1120]{1,0:T(8,128)(2,1)S(1)}, bf16[280,1120]{1,0:T(8,128)(2,1)}, u32[]{:S(2)}) copy-start(bf16[280,1120]{1,0:T(8,128)(2,1)} %refs_7_.1) | copy-start | bytes 1881604
  13.1 40.4 %copy-start.8 = (bf16[32,16,1120]{2,1,0:T(8,128)(2,1)}, bf16[32,16,1120]{2,1,0:T(8,128)(2,1)S(1)}, u32[]{:S(2)}) copy-start(bf16[32,16,1120]{2,1,0:T(8,128)(2,1)S(1)} %get-tuple-element.326.a0) | copy-start | bytes 3440644
  13.1 13.7 %collective-permute-start = (bf16[32,16,1120]{2,1,0:T(8,128)(2,1)S(1)}, bf16[32,16,1120]{2,1,0:T(8,128)(2,1)}, u32[]{:S(2)}, u32[]{:S(2)}) collective-permute-start(bf16[32,16,1120]{2,1,0:T(8,128)(2,1)S(1)} %get-tuple-element.326.a0), channel_id=1, source_target_pairs={{0,1},{1,0},{2,3},{3,2},{4,5},{5,4},{6,7},{7,6},{8,9},{9,8},{10,11... | collective-permute-start | bytes 3440648 | tf_op jit(solution)/shard_map/ppermute | solution.py:30
  13.2 29.6 %collective-permute-start.1 = (bf16[32,16,1120]{2,1,0:T(8,128)(2,1)S(1)}, bf16[32,16,1120]{2,1,0:T(8,128)(2,1)}, u32[]{:S(2)}, u32[]{:S(2)}) collective-permute-start(bf16[32,16,1120]{2,1,0:T(8,128)(2,1)S(1)} %get-tuple-element.325), channel_id=1, source_target_pairs={{0,2},{1,3},{2,0},{3,1},{4,6},{5,7},{6,4},{7,5},{8,10},{9,11},{10,... | collective-permute-start | bytes 3440648 | tf_op jit(solution)/shard_map/ppermute | solution.py:30
  19.0 137.2 %all-gather.5.cloned.1.call-start = ((), (), s32[]{:S(2)}) async-start(), calls=%async_computation.1 | async-start | bytes 2985984 | tf_op jit(solution)/shard_map/all_gather | solution.py:649
  42.8 9.7 %collective-permute-start.3 = (bf16[32,16,1120]{2,1,0:T(8,128)(2,1)}, bf16[32,16,1120]{2,1,0:T(8,128)(2,1)S(1)}, u32[]{:S(2)}, u32[]{:S(2)}) collective-permute-start(bf16[32,16,1120]{2,1,0:T(8,128)(2,1)} %collective-permute-done.1.a1), channel_id=1, source_target_pairs={{0,1},{1,0},{2,3},{3,2},{4,5},{5,4},{6,7},{7,6},{8,9},{9,8},{10,11... | collective-permute-start | bytes 3440648 | tf_op jit(solution)/shard_map/ppermute | solution.py:30
  46.2 24.7 %collective-permute-start.5 = (bf16[18,16,1120]{2,1,0:T(8,128)(2,1)}, bf16[18,16,1120]{2,1,0:T(8,128)(2,1)}, u32[]{:S(2)}, u32[]{:S(2)}) collective-permute-start(bf16[18,16,1120]{2,1,0:T(8,128)(2,1)} %bitcast.15), channel_id=1, source_target_pairs={{0,2},{1,3},{2,0},{3,1},{4,6},{5,7},{6,4},{7,5},{8,10},{9,11},{10,... | collective-permute-start | bytes 1935368 | tf_op jit(solution)/shard_map/ppermute | solution.py:30
  52.2 18.8 %collective-permute-start.4 = (bf16[9,16,1120]{2,1,0:T(8,128)(2,1)}, bf16[9,16,1120]{2,1,0:T(8,128)(2,1)}, u32[]{:S(2)}, u32[]{:S(2)}) collective-permute-start(bf16[9,16,1120]{2,1,0:T(8,128)(2,1)} %bitcast.13), channel_id=1, source_target_pairs={{0,2},{1,3},{2,0},{3,1},{4,6},{5,7},{6,4},{7,5},{8,10},{9,11},{10,... | collective-permute-start | bytes 967688 | tf_op jit(solution)/shard_map/ppermute | solution.py:30
  53.5 17.5 %copy-start.3 = (bf16[64,16,1120]{2,1,0:T(8,128)(2,1)S(1)}, bf16[64,16,1120]{2,1,0:T(8,128)(2,1)}, u32[]{:S(2)}) copy-start(bf16[64,16,1120]{2,1,0:T(8,128)(2,1)} %param.15) | copy-start | bytes 6881284
  72.2 17.6 %copy-start.9 = (bf16[32,16,1120]{2,1,0:T(8,128)(2,1)}, bf16[32,16,1120]{2,1,0:T(8,128)(2,1)S(1)}, u32[]{:S(2)}) copy-start(bf16[32,16,1120]{2,1,0:T(8,128)(2,1)S(1)} %get-tuple-element.324.refs_7_) | copy-start | bytes 3440644
  72.2 17.6 %collective-permute-start.6 = (bf16[32,16,1120]{2,1,0:T(8,128)(2,1)S(1)}, bf16[32,16,1120]{2,1,0:T(8,128)(2,1)S(1)}, u32[]{:S(2)}, u32[]{:S(2)}) collective-permute-start(bf16[32,16,1120]{2,1,0:T(8,128)(2,1)S(1)} %get-tuple-element.324.refs_7_), channel_id=1, source_target_pairs={{0,1},{1,0},{2,3},{3,2},{4,5},{5,4},{6,7},{7,6},{8,9},{9,8},{10,11... | collective-permute-start | bytes 3440648 | tf_op jit(solution)/shard_map/ppermute | solution.py:30
  72.2 39.6 %collective-permute-start.7 = (bf16[32,16,1120]{2,1,0:T(8,128)(2,1)}, bf16[32,16,1120]{2,1,0:T(8,128)(2,1)}, u32[]{:S(2)}, u32[]{:S(2)}) collective-permute-start(bf16[32,16,1120]{2,1,0:T(8,128)(2,1)} %get-tuple-element.323), channel_id=1, source_target_pairs={{0,2},{1,3},{2,0},{3,1},{4,6},{5,7},{6,4},{7,5},{8,10},{9,11},{10,... | collective-permute-start | bytes 3440648 | tf_op jit(solution)/shard_map/ppermute | solution.py:30
  90.9 65.2 %collective-permute-start.9 = (bf16[70,16,1120]{2,1,0:T(8,128)(2,1)}, bf16[70,16,1120]{2,1,0:T(8,128)(2,1)S(1)}, u32[]{:S(2)}, u32[]{:S(2)}) collective-permute-start(bf16[70,16,1120]{2,1,0:T(8,128)(2,1)} %bitcast.22), channel_id=1, source_target_pairs={{0,2},{1,3},{2,0},{3,1},{4,6},{5,7},{6,4},{7,5},{8,10},{9,11},{10,... | collective-permute-start | bytes 7526408 | tf_op jit(solution)/shard_map/ppermute | solution.py:30
  111.9 6.8 %copy-start.14 = (bf16[1120]{0:T(1024)(128)(2,1)S(1)}, bf16[1120]{0:T(1024)(128)(2,1)}, u32[]{:S(2)}) copy-start(bf16[1120]{0:T(1024)(128)(2,1)} %param.25) | copy-start | bytes 6724
  111.9 7.4 %copy-start.13 = (bf16[2,1120]{1,0:T(2,128)(2,1)S(1)}, bf16[2,1120]{1,0:T(2,128)(2,1)}, u32[]{:S(2)}) copy-start(bf16[2,1120]{1,0:T(2,128)(2,1)} %param.23) | copy-start | bytes 13444
  118.1 38.1 %collective-permute-start.10 = (bf16[64,16,1120]{2,1,0:T(8,128)(2,1)}, bf16[64,16,1120]{2,1,0:T(8,128)(2,1)}, u32[]{:S(2)}, u32[]{:S(2)}) collective-permute-start(bf16[64,16,1120]{2,1,0:T(8,128)(2,1)} %bitcast.137), channel_id=1, source_target_pairs={{0,1},{1,0},{2,3},{3,2},{4,5},{5,4},{6,7},{7,6},{8,9},{9,8},{10,11... | collective-permute-start | bytes 6881288 | tf_op jit(solution)/shard_map/ppermute | solution.py:30
  118.1 38.0 %collective-permute-start.11 = (bf16[64,16,1120]{2,1,0:T(8,128)(2,1)}, bf16[64,16,1120]{2,1,0:T(8,128)(2,1)}, u32[]{:S(2)}, u32[]{:S(2)}) collective-permute-start(bf16[64,16,1120]{2,1,0:T(8,128)(2,1)} %bitcast.138), channel_id=1, source_target_pairs={{0,1},{1,0},{2,3},{3,2},{4,5},{5,4},{6,7},{7,6},{8,9},{9,8},{10,11... | collective-permute-start | bytes 6881288 | tf_op jit(solution)/shard_map/ppermute | solution.py:30
  118.6 7.6 %collective-permute-start.8 = (bf16[32,16,1120]{2,1,0:T(8,128)(2,1)}, bf16[32,16,1120]{2,1,0:T(8,128)(2,1)S(1)}, u32[]{:S(2)}, u32[]{:S(2)}) collective-permute-start(bf16[32,16,1120]{2,1,0:T(8,128)(2,1)} %collective-permute-done.7.refs_8_), channel_id=1, source_target_pairs={{0,1},{1,0},{2,3},{3,2},{4,5},{5,4},{6,7},{7,6},{8,9},{9,8},{10,11... | collective-permute-start | bytes 3440648 | tf_op jit(solution)/shard_map/ppermute | solution.py:30
  126.2 29.9 %copy-start.24 = (bf16[32,16,1120]{2,1,0:T(8,128)(2,1)}, bf16[32,16,1120]{2,1,0:T(8,128)(2,1)S(1)}, u32[]{:S(2)}) copy-start(bf16[32,16,1120]{2,1,0:T(8,128)(2,1)S(1)} %collective-permute-done.8.refs_10_) | copy-start | bytes 3440644
  197.4 17.5 %collective-permute-start.14 = (bf16[64,16,1120]{2,1,0:T(8,128)(2,1)}, bf16[64,16,1120]{2,1,0:T(8,128)(2,1)S(1)}, u32[]{:S(2)}, u32[]{:S(2)}) collective-permute-start(bf16[64,16,1120]{2,1,0:T(8,128)(2,1)} %bitcast.135), channel_id=1, source_target_pairs={{0,1},{1,0},{2,3},{3,2},{4,5},{5,4},{6,7},{7,6},{8,9},{9,8},{10,11... | collective-permute-start | bytes 6881288 | tf_op jit(solution)/shard_map/ppermute | solution.py:30
  197.5 18.0 %collective-permute-start.15 = (bf16[64,16,1120]{2,1,0:T(8,128)(2,1)}, bf16[64,16,1120]{2,1,0:T(8,128)(2,1)}, u32[]{:S(2)}, u32[]{:S(2)}) collective-permute-start(bf16[64,16,1120]{2,1,0:T(8,128)(2,1)} %bitcast.136), channel_id=1, source_target_pairs={{0,1},{1,0},{2,3},{3,2},{4,5},{5,4},{6,7},{7,6},{8,9},{9,8},{10,11... | collective-permute-start | bytes 6881288 | tf_op jit(solution)/shard_map/ppermute | solution.py:30
  198.0 31.0 %collective-permute-start.12 = (bf16[64,16,1120]{2,1,0:T(8,128)(2,1)}, bf16[64,16,1120]{2,1,0:T(8,128)(2,1)S(1)}, u32[]{:S(2)}, u32[]{:S(2)}) collective-permute-start(bf16[64,16,1120]{2,1,0:T(8,128)(2,1)} %bitcast.118), channel_id=1, source_target_pairs={{0,1},{1,0},{2,3},{3,2},{4,5},{5,4},{6,7},{7,6},{8,9},{9,8},{10,11... | collective-permute-start | bytes 6881288 | tf_op jit(solution)/shard_map/ppermute | solution.py:30
  198.1 30.9 %collective-permute-start.13 = (bf16[64,16,1120]{2,1,0:T(8,128)(2,1)}, bf16[64,16,1120]{2,1,0:T(8,128)(2,1)S(1)}, u32[]{:S(2)}, u32[]{:S(2)}) collective-permute-start(bf16[64,16,1120]{2,1,0:T(8,128)(2,1)} %bitcast.119), channel_id=1, source_target_pairs={{0,1},{1,0},{2,3},{3,2},{4,5},{5,4},{6,7},{7,6},{8,9},{9,8},{10,11... | collective-permute-start | bytes 6881288 | tf_op jit(solution)/shard_map/ppermute | solution.py:30
  206.6 59.2 %collective-permute-start.16 = (bf16[70,16,1120]{2,1,0:T(8,128)(2,1)}, bf16[70,16,1120]{2,1,0:T(8,128)(2,1)}, u32[]{:S(2)}, u32[]{:S(2)}) collective-permute-start(bf16[70,16,1120]{2,1,0:T(8,128)(2,1)} %bitcast.134), channel_id=1, source_target_pairs={{0,2},{1,3},{2,0},{3,1},{4,6},{5,7},{6,4},{7,5},{8,10},{9,11},{10,... | collective-permute-start | bytes 7526408 | tf_op jit(solution)/shard_map/ppermute | solution.py:30
  214.9 106.1 %collective-permute-start.17 = (bf16[70,16,1120]{2,1,0:T(8,128)(2,1)}, bf16[70,16,1120]{2,1,0:T(8,128)(2,1)}, u32[]{:S(2)}, u32[]{:S(2)}) collective-permute-start(bf16[70,16,1120]{2,1,0:T(8,128)(2,1)} %bitcast.133), channel_id=1, source_target_pairs={{0,2},{1,3},{2,0},{3,1},{4,6},{5,7},{6,4},{7,5},{8,10},{9,11},{10,... | collective-permute-start | bytes 7526408 | tf_op jit(solution)/shard_map/ppermute | solution.py:30
  229.0 9.1 %copy-start.6 = (bf16[64,16,1120]{2,1,0:T(8,128)(2,1)}, bf16[64,16,1120]{2,1,0:T(8,128)(2,1)S(1)}, u32[]{:S(2)}) copy-start(bf16[64,16,1120]{2,1,0:T(8,128)(2,1)S(1)} %collective-permute-done.12) | copy-start | bytes 6881284
  229.0 9.0 %copy-start.7 = (bf16[64,16,1120]{2,1,0:T(8,128)(2,1)}, bf16[64,16,1120]{2,1,0:T(8,128)(2,1)S(1)}, u32[]{:S(2)}) copy-start(bf16[64,16,1120]{2,1,0:T(8,128)(2,1)S(1)} %collective-permute-done.13) | copy-start | bytes 6881284
  271.2 76.4 %collective-permute-start.19 = (bf16[35,16,1120]{2,1,0:T(8,128)(2,1)}, bf16[35,16,1120]{2,1,0:T(8,128)(2,1)S(1)}, u32[]{:S(2)}, u32[]{:S(2)}) collective-permute-start(bf16[35,16,1120]{2,1,0:T(8,128)(2,1)} %bitcast.146), channel_id=1, source_target_pairs={{0,4},{4,0},{8,12},{12,8},{16,20},{20,16},{24,28},{28,24},{1,5},{5... | collective-permute-start | bytes 3763208 | tf_op jit(solution)/shard_map/ppermute | solution.py:30
  315.9 101.2 %collective-permute-start.23 = (bf16[70,16,1120]{2,1,0:T(8,128)(2,1)}, bf16[70,16,1120]{2,1,0:T(8,128)(2,1)S(1)}, u32[]{:S(2)}, u32[]{:S(2)}) collective-permute-start(bf16[70,16,1120]{2,1,0:T(8,128)(2,1)} %bitcast.132), channel_id=1, source_target_pairs={{0,2},{1,3},{2,0},{3,1},{4,6},{5,7},{6,4},{7,5},{8,10},{9,11},{10,... | collective-permute-start | bytes 7526408 | tf_op jit(solution)/shard_map/ppermute | solution.py:30
  326.2 60.7 %collective-permute-start.18 = (bf16[35,16,1120]{2,1,0:T(8,128)(2,1)}, bf16[35,16,1120]{2,1,0:T(8,128)(2,1)S(1)}, u32[]{:S(2)}, u32[]{:S(2)}) collective-permute-start(bf16[35,16,1120]{2,1,0:T(8,128)(2,1)} %bitcast.144), channel_id=1, source_target_pairs={{0,4},{4,0},{8,12},{12,8},{16,20},{20,16},{24,28},{28,24},{1,5},{5... | collective-permute-start | bytes 3763208 | tf_op jit(solution)/shard_map/ppermute | solution.py:30
  352.9 29.9 %collective-permute-start.20 = (bf16[18,16,1120]{2,1,0:T(8,128)(2,1)}, bf16[18,16,1120]{2,1,0:T(8,128)(2,1)S(1)}, u32[]{:S(2)}, u32[]{:S(2)}) collective-permute-start(bf16[18,16,1120]{2,1,0:T(8,128)(2,1)} %bitcast.156), channel_id=1, source_target_pairs={{0,8},{4,12},{8,0},{12,4},{16,24},{20,28},{24,16},{28,20},{1,9},{5... | collective-permute-start | bytes 1935368 | tf_op jit(solution)/shard_map/ppermute | solution.py:30
  387.9 4.5 copy-start.32
  392.4 32.2 %collective-permute-start.22 = (bf16[9,16,1120]{2,1,0:T(8,128)(2,1)S(1)}, bf16[9,16,1120]{2,1,0:T(8,128)(2,1)S(1)}, u32[]{:S(2)}, u32[]{:S(2)}) collective-permute-start(bf16[9,16,1120]{2,1,0:T(8,128)(2,1)S(1)} %bitcast.162), channel_id=1, source_target_pairs={{0,16},{4,20},{8,24},{12,28},{16,0},{20,4},{24,8},{28,12},{1,17},{... | collective-permute-start | bytes 967688 | tf_op jit(solution)/shard_map/ppermute | solution.py:30
  392.4 35.8 %collective-permute-start.21 = (bf16[18,16,1120]{2,1,0:T(8,128)(2,1)}, bf16[18,16,1120]{2,1,0:T(8,128)(2,1)S(1)}, u32[]{:S(2)}, u32[]{:S(2)}) collective-permute-start(bf16[18,16,1120]{2,1,0:T(8,128)(2,1)} %bitcast.152), channel_id=1, source_target_pairs={{0,8},{4,12},{8,0},{12,4},{16,24},{20,28},{24,16},{28,20},{1,9},{5... | collective-permute-start | bytes 1935368 | tf_op jit(solution)/shard_map/ppermute | solution.py:30
  423.7 38.1 %collective-permute-start.27 = (bf16[35,16,1120]{2,1,0:T(8,128)(2,1)}, bf16[35,16,1120]{2,1,0:T(8,128)(2,1)S(1)}, u32[]{:S(2)}, u32[]{:S(2)}) collective-permute-start(bf16[35,16,1120]{2,1,0:T(8,128)(2,1)} %bitcast.141), channel_id=1, source_target_pairs={{0,4},{4,0},{8,12},{12,8},{16,20},{20,16},{24,28},{28,24},{1,5},{5... | collective-permute-start | bytes 3763208 | tf_op jit(solution)/shard_map/ppermute | solution.py:30
  428.0 25.6 %collective-permute-start.25 = (bf16[9,16,1120]{2,1,0:T(8,128)(2,1)}, bf16[9,16,1120]{2,1,0:T(8,128)(2,1)S(1)}, u32[]{:S(2)}, u32[]{:S(2)}) collective-permute-start(bf16[9,16,1120]{2,1,0:T(8,128)(2,1)} %bitcast.161), channel_id=1, source_target_pairs={{0,16},{4,20},{8,24},{12,28},{16,0},{20,4},{24,8},{28,12},{1,17},{... | collective-permute-start | bytes 967688 | tf_op jit(solution)/shard_map/ppermute | solution.py:30
  432.3 26.1 %collective-permute-start.24 = (bf16[9,16,1120]{2,1,0:T(8,128)(2,1)}, bf16[9,16,1120]{2,1,0:T(8,128)(2,1)S(1)}, u32[]{:S(2)}, u32[]{:S(2)}) collective-permute-start(bf16[9,16,1120]{2,1,0:T(8,128)(2,1)} %bitcast.165), channel_id=1, source_target_pairs={{0,16},{4,20},{8,24},{12,28},{16,0},{20,4},{24,8},{28,12},{1,17},{... | collective-permute-start | bytes 967688 | tf_op jit(solution)/shard_map/ppermute | solution.py:30
  444.9 23.6 %collective-permute-start.30 = (bf16[64,16,1120]{2,1,0:T(8,128)(2,1)}, bf16[64,16,1120]{2,1,0:T(8,128)(2,1)S(1)}, u32[]{:S(2)}, u32[]{:S(2)}) collective-permute-start(bf16[64,16,1120]{2,1,0:T(8,128)(2,1)} %bitcast.110), channel_id=1, source_target_pairs={{0,1},{1,0},{2,3},{3,2},{4,5},{5,4},{6,7},{7,6},{8,9},{9,8},{10,11... | collective-permute-start | bytes 6881288 | tf_op jit(solution)/shard_map/ppermute | solution.py:30
  444.9 23.5 %collective-permute-start.31 = (bf16[64,16,1120]{2,1,0:T(8,128)(2,1)}, bf16[64,16,1120]{2,1,0:T(8,128)(2,1)S(1)}, u32[]{:S(2)}, u32[]{:S(2)}) collective-permute-start(bf16[64,16,1120]{2,1,0:T(8,128)(2,1)} %bitcast.111), channel_id=1, source_target_pairs={{0,1},{1,0},{2,3},{3,2},{4,5},{5,4},{6,7},{7,6},{8,9},{9,8},{10,11... | collective-permute-start | bytes 6881288 | tf_op jit(solution)/shard_map/ppermute | solution.py:30
  457.1 25.2 %collective-permute-start.29 = (bf16[18,16,1120]{2,1,0:T(8,128)(2,1)}, bf16[18,16,1120]{2,1,0:T(8,128)(2,1)S(1)}, u32[]{:S(2)}, u32[]{:S(2)}) collective-permute-start(bf16[18,16,1120]{2,1,0:T(8,128)(2,1)} %bitcast.147), channel_id=1, source_target_pairs={{0,8},{4,12},{8,0},{12,4},{16,24},{20,28},{24,16},{28,20},{1,9},{5... | collective-permute-start | bytes 1935368 | tf_op jit(solution)/shard_map/ppermute | solution.py:30
  461.8 37.4 %collective-permute-start.26 = (bf16[9,16,1120]{2,1,0:T(8,128)(2,1)}, bf16[9,16,1120]{2,1,0:T(8,128)(2,1)S(1)}, u32[]{:S(2)}, u32[]{:S(2)}) collective-permute-start(bf16[9,16,1120]{2,1,0:T(8,128)(2,1)} %bitcast.158), channel_id=1, source_target_pairs={{0,16},{4,20},{8,24},{12,28},{16,0},{20,4},{24,8},{28,12},{1,17},{... | collective-permute-start | bytes 967688 | tf_op jit(solution)/shard_map/ppermute | solution.py:30
  467.2 28.0 %collective-permute-start.28 = (bf16[18,16,1120]{2,1,0:T(8,128)(2,1)}, bf16[18,16,1120]{2,1,0:T(8,128)(2,1)S(1)}, u32[]{:S(2)}, u32[]{:S(2)}) collective-permute-start(bf16[18,16,1120]{2,1,0:T(8,128)(2,1)} %bitcast.154), channel_id=1, source_target_pairs={{0,8},{4,12},{8,0},{12,4},{16,24},{20,28},{24,16},{28,20},{1,9},{5... | collective-permute-start | bytes 1935368 | tf_op jit(solution)/shard_map/ppermute | solution.py:30
  468.4 2.2 copy-start.2
  500.0 4.6 copy-start.31
  502.7 4.3 copy-start.4
  502.7 26.1 %collective-permute-start.32 = (bf16[18,16,1120]{2,1,0:T(8,128)(2,1)}, bf16[18,16,1120]{2,1,0:T(8,128)(2,1)S(1)}, u32[]{:S(2)}, u32[]{:S(2)}) collective-permute-start(bf16[18,16,1120]{2,1,0:T(8,128)(2,1)} %bitcast.148), channel_id=1, source_target_pairs={{0,8},{4,12},{8,0},{12,4},{16,24},{20,28},{24,16},{28,20},{1,9},{5... | collective-permute-start | bytes 1935368 | tf_op jit(solution)/shard_map/ppermute | solution.py:30
  504.5 20.9 %collective-permute-start.34 = (bf16[9,16,1120]{2,1,0:T(8,128)(2,1)S(1)}, bf16[9,16,1120]{2,1,0:T(8,128)(2,1)S(1)}, u32[]{:S(2)}, u32[]{:S(2)}) collective-permute-start(bf16[9,16,1120]{2,1,0:T(8,128)(2,1)S(1)} %bitcast.160), channel_id=1, source_target_pairs={{0,16},{4,20},{8,24},{12,28},{16,0},{20,4},{24,8},{28,12},{1,17},{... | collective-permute-start | bytes 967688 | tf_op jit(solution)/shard_map/ppermute | solution.py:30
  507.0 21.8 %collective-permute-start.33 = (f32[40,1120]{1,0:T(8,128)}, f32[40,1120]{1,0:T(8,128)S(1)}, u32[]{:S(2)}, u32[]{:S(2)}) collective-permute-start(f32[40,1120]{1,0:T(8,128)} %get-tuple-element.284), channel_id=1, source_target_pairs={{0,2},{1,3},{2,0},{3,1},{4,6},{5,7},{6,4},{7,5},{8,10},{9,11},{10,... | collective-permute-start | bytes 537608 | tf_op jit(solution)/shard_map/ppermute | solution.py:30
  508.2 46.9 %collective-permute-start.41 = (bf16[32,16,1120]{2,1,0:T(8,128)(2,1)}, bf16[32,16,1120]{2,1,0:T(8,128)(2,1)S(1)}, u32[]{:S(2)}, u32[]{:S(2)}) collective-permute-start(bf16[32,16,1120]{2,1,0:T(8,128)(2,1)} %slice.96), channel_id=1, source_target_pairs={{0,2},{1,3},{2,0},{3,1},{4,6},{5,7},{6,4},{7,5},{8,10},{9,11},{10,... | collective-permute-start | bytes 3440648 | tf_op jit(solution)/shard_map/ppermute | solution.py:30
  510.2 46.6 %collective-permute-start.40 = (bf16[35,16,1120]{2,1,0:T(8,128)(2,1)}, bf16[35,16,1120]{2,1,0:T(8,128)(2,1)}, u32[]{:S(2)}, u32[]{:S(2)}) collective-permute-start(bf16[35,16,1120]{2,1,0:T(8,128)(2,1)} %bitcast.81), channel_id=1, source_target_pairs={{0,4},{4,0},{8,12},{12,8},{16,20},{20,16},{24,28},{28,24},{1,5},{5... | collective-permute-start | bytes 3763208 | tf_op jit(solution)/shard_map/ppermute | solution.py:30
  528.8 16.1 %copy-start.12 = (f32[40,1120]{1,0:T(8,128)}, f32[40,1120]{1,0:T(8,128)S(1)}, u32[]{:S(2)}) copy-start(f32[40,1120]{1,0:T(8,128)S(1)} %collective-permute-done.33) | copy-start | bytes 537604
  529.7 3.6 copy-start.36
  532.9 35.8 %collective-permute-start.39 = (bf16[35,16,1120]{2,1,0:T(8,128)(2,1)}, bf16[35,16,1120]{2,1,0:T(8,128)(2,1)}, u32[]{:S(2)}, u32[]{:S(2)}) collective-permute-start(bf16[35,16,1120]{2,1,0:T(8,128)(2,1)} %bitcast.142), channel_id=1, source_target_pairs={{0,4},{4,0},{8,12},{12,8},{16,20},{20,16},{24,28},{28,24},{1,5},{5... | collective-permute-start | bytes 3763208 | tf_op jit(solution)/shard_map/ppermute | solution.py:30
  533.4 15.9 %collective-permute-start.37 = (bf16[9,16,1120]{2,1,0:T(8,128)(2,1)S(1)}, bf16[9,16,1120]{2,1,0:T(8,128)(2,1)S(1)}, u32[]{:S(2)}, u32[]{:S(2)}) collective-permute-start(bf16[9,16,1120]{2,1,0:T(8,128)(2,1)S(1)} %bitcast.167), channel_id=1, source_target_pairs={{0,16},{4,20},{8,24},{12,28},{16,0},{20,4},{24,8},{28,12},{1,17},{... | collective-permute-start | bytes 967688 | tf_op jit(solution)/shard_map/ppermute | solution.py:30
  550.0 4.9 copy-start
  552.8 21.2 %collective-permute-start.38 = (bf16[18,16,1120]{2,1,0:T(8,128)(2,1)}, bf16[18,16,1120]{2,1,0:T(8,128)(2,1)}, u32[]{:S(2)}, u32[]{:S(2)}) collective-permute-start(bf16[18,16,1120]{2,1,0:T(8,128)(2,1)} %bitcast.151), channel_id=1, source_target_pairs={{0,8},{4,12},{8,0},{12,4},{16,24},{20,28},{24,16},{28,20},{1,9},{5... | collective-permute-start | bytes 1935368 | tf_op jit(solution)/shard_map/ppermute | solution.py:30
  554.6 22.6 %collective-permute-start.36 = (f32[40,1120]{1,0:T(8,128)}, f32[40,1120]{1,0:T(8,128)}, u32[]{:S(2)}, u32[]{:S(2)}) collective-permute-start(f32[40,1120]{1,0:T(8,128)} %add.107), channel_id=1, source_target_pairs={{0,4},{4,0},{8,12},{12,8},{16,20},{20,16},{24,28},{28,24},{1,5},{5... | collective-permute-start | bytes 537608 | tf_op jit(solution)/shard_map/ppermute | solution.py:30
  555.1 31.7 %collective-permute-start.35 = (bf16[32,16,1120]{2,1,0:T(8,128)(2,1)S(1)}, bf16[32,16,1120]{2,1,0:T(8,128)(2,1)S(1)}, u32[]{:S(2)}, u32[]{:S(2)}) collective-permute-start(bf16[32,16,1120]{2,1,0:T(8,128)(2,1)S(1)} %slice.114), channel_id=1, source_target_pairs={{0,2},{1,3},{2,0},{3,1},{4,6},{5,7},{6,4},{7,5},{8,10},{9,11},{10,... | collective-permute-start | bytes 3440648 | tf_op jit(solution)/shard_map/ppermute | solution.py:30
  574.0 4.8 copy-start.5
  578.2 5.8 collective-permute-start.42
  580.9 25.9 %collective-permute-start.44 = (bf16[35,16,1120]{2,1,0:T(8,128)(2,1)}, bf16[35,16,1120]{2,1,0:T(8,128)(2,1)}, u32[]{:S(2)}, u32[]{:S(2)}) collective-permute-start(bf16[35,16,1120]{2,1,0:T(8,128)(2,1)} %bitcast.89), channel_id=1, source_target_pairs={{0,4},{4,0},{8,12},{12,8},{16,20},{20,16},{24,28},{28,24},{1,5},{5... | collective-permute-start | bytes 3763208 | tf_op jit(solution)/shard_map/ppermute | solution.py:30
  584.0 8.5 %collective-permute-start.43 = (f32[40,1120]{1,0:T(8,128)S(1)}, f32[40,1120]{1,0:T(8,128)S(1)}, u32[]{:S(2)}, u32[]{:S(2)}) collective-permute-start(f32[40,1120]{1,0:T(8,128)S(1)} %add.109), channel_id=1, source_target_pairs={{0,16},{4,20},{8,24},{12,28},{16,0},{20,4},{24,8},{28,12},{1,17},{... | collective-permute-start | bytes 537608 | tf_op jit(solution)/shard_map/ppermute | solution.py:30
  (22 other events, 22.5 us)
Sparse Core Ops, SparseCore 0:
  19.1 50.9 all-gather.2
  72.3 55.6 all-gather.4

commit v3 on v2

--- a/solution.py
+++ b/solution.py
@@ -13,6 +13,7 @@
 BLOCK = 256
 META_BLOCKS = 8
 TILE = 16
+UNROLL = 4
 F32 = jnp.float32
 LOW = jnp.bfloat16
 VMEM_BYTES = 56 * 1024 * 1024
@@ -267,14 +268,13 @@
     return groups
 
 
-def attention_kernel(heads, shard, cell, meta, projected, context, attend):
+def attention_kernel(heads, shard, cell, meta, projected, context, attend, same_head):
     context[...] = jnp.zeros_like(context)
     masks = head_masks(cell, heads, shard)
     scale = 1.0 / math.sqrt(HEAD_DIM)
-    row = lax.broadcasted_iota(jnp.int32, (cell, 2 * cell), 0)
-    lane = lax.broadcasted_iota(jnp.int32, (cell, 2 * cell), 1)
-    left = lane < cell
-    causal = row >= jnp.where(left, lane, lane - cell)
+    span = same_head.shape[0]
+    head_of = [lax.broadcasted_iota(jnp.int32, (span, span), axis) // cell for axis in (0, 1)]
+    same_head[...] = jnp.where(head_of[0] == head_of[1], 1.0, 0.0).astype(LOW)
 
     def one(index):
         at = pl.multiple_of(meta[CELL_OFF + index] * TILE, TILE)
@@ -283,38 +283,41 @@
         values = projected[pl.ds(at, cell), 2 * shard : 3 * shard]
         total = None
         for group, low, high in head_groups(heads, shard):
-            spread = spread_heads(keys, masks, group, low, high)
-            scores = dot_nt(queries[:, low:high], spread) * scale
-            parts = []
+            count = len(group) * cell
+            scores = dot_nt(queries[:, low:high], spread_heads(keys, masks, group, low, high)) * scale
+            row = lax.broadcasted_iota(jnp.int32, (cell, count), 0)
+            lane = lax.broadcasted_iota(jnp.int32, (cell, count), 1)
+            scores = jnp.where(row >= lax.rem(lane, cell), scores, -1e30)
+            shifted = []
             for pair in range(0, len(group), 2):
+                both = scores[:, pair * cell : min(pair + 2, len(group)) * cell]
                 if pair + 1 < len(group):
-                    both = jnp.where(causal, scores[:, pair * cell : (pair + 2) * cell], -1e30)
+                    left = lax.broadcasted_iota(jnp.int32, both.shape, 1) < cell
                     top_left = jnp.max(jnp.where(left, both, -1e30), axis=1, keepdims=True)
                     top_right = jnp.max(jnp.where(left, -1e30, both), axis=1, keepdims=True)
-                    weights = jnp.exp(both - jnp.where(left, top_left, top_right))
-                    sum_left = jnp.sum(jnp.where(left, weights, 0.0), axis=1, keepdims=True)
-                    sum_right = jnp.sum(jnp.where(left, 0.0, weights), axis=1, keepdims=True)
-                    parts.append((weights * jnp.where(left, 1.0 / sum_left, 1.0 / sum_right)).astype(LOW))
+                    shifted.append(both - jnp.where(left, top_left, top_right))
                 else:
-                    single = jnp.where(causal[:, :cell], scores[:, pair * cell :], -1e30)
-                    weights = jnp.exp(single - jnp.max(single, axis=1, keepdims=True))
-                    parts.append((weights * (1.0 / jnp.sum(weights, axis=1, keepdims=True))).astype(LOW))
-            probs = jnp.concatenate(parts, axis=1) if len(parts) > 1 else parts[0]
+                    shifted.append(both - jnp.max(both, axis=1, keepdims=True))
+            weights = jnp.exp(jnp.concatenate(shifted, axis=1) if len(shifted) > 1 else shifted[0])
+            if len(group) > 1:
+                sums = dot(weights.astype(LOW), same_head[:count, :count])
+            else:
+                sums = jnp.sum(weights, axis=1, keepdims=True)
+            probs = (weights * (1.0 / sums)).astype(LOW)
             first = group[0] * cell
-            attend[index, :, first : first + len(group) * cell] = probs
+            attend[index, :, first : first + count] = probs
             part = dot(probs, spread_heads(values, masks, group, low, high))
-            if total is None:
-                total = jnp.pad(part, ((0, 0), (low, shard - high))) if high - low < shard else part
-            else:
-                total = total + jnp.pad(part, ((0, 0), (low, shard - high)))
+            if high - low < shard:
+                part = jnp.pad(part, ((0, 0), (low, shard - high)))
+            total = part if total is None else total + part
         context[pl.ds(at, cell), :] = total.astype(LOW)
 
     def body(step, carry):
-        one(2 * step)
-        one(2 * step + 1)
+        for place in range(UNROLL):
+            one(UNROLL * step + place)
         return carry
 
-    lax.fori_loop(0, (meta[NCELL] + 1) // 2, body, 0)
+    lax.fori_loop(0, (meta[NCELL] + UNROLL - 1) // UNROLL, body, 0)
 
 
 def attention_back_kernel(heads, shard, cell, meta, projected, attend, context_grad, result, sums):
@@ -419,12 +422,12 @@
     return hidden * chance, slope
 
 
-def mlp_block(second, grad, up, bias, down, active, hidden_grad, bias_grad):
+def mlp_block(second, product, up, bias, down, active, hidden_grad, bias_grad):
     hidden = dot(second, up[...]) + bias[...]
     value, slope = gelu_pair(hidden)
     low = value.astype(LOW)
     active[...] = low
-    back = (slope * dot_nt(grad, down[...])).astype(LOW)
+    back = (slope * product).astype(LOW)
     hidden_grad[...] = back
     bias_grad[...] += jnp.sum(back.astype(F32), axis=0, keepdims=True)
     return dot(low, down[...]), dot_nt(back, up[...])
@@ -456,20 +459,22 @@
             at = step * (BLOCK // TILE) + j
             tile = tiles[meta[TILE_SRC + at]]
             grad[j * TILE : (j + 1) * TILE, :] = jnp.where(inner < meta[TILE_LEN + at], tile, jnp.zeros_like(tile))
+
+        @pl.when(step == 0)
+        def _():
+            for copy in copies:
+                copy.wait()
+
+        own_product = dot_nt(grad[...], down[...])
+        other_product = dot_nt(grad[...], other_down[...])
         rows = start[...] + (block_of(step, near_rows) + block_of(step, far_rows)) + bias_row[...]
         middle[...] = rows
         unit, _ = row_norm(rows)
         low = (unit * gain[...] + shift[...]).astype(LOW)
         second[...] = low
-        own = mlp_block(low, grad[...], up, up_bias, down, active, hidden_grad, bias_grad.at[0:1])
-
-        @pl.when(step == 0)
-        def _():
-            for copy in copies:
-                copy.wait()
-
+        own = mlp_block(low, own_product, up, up_bias, down, active, hidden_grad, bias_grad.at[0:1])
         other = mlp_block(
-            low, grad[...], other_up, other_bias, other_down, other_active, other_hidden, bias_grad.at[1:2]
+            low, other_product, other_up, other_bias, other_down, other_active, other_hidden, bias_grad.at[1:2]
         )
         put_part(step, last, (own[1] + other[1]).astype(LOW), second_grad, grad_slots, grad_sems)
         put_part(step, last, (own[0] + other[0]).astype(LOW), branch, branch_slots, branch_sems)
@@ -942,14 +947,18 @@
     in_far = swap(in_mine, "tp", 1)
     head_rows = jnp.pad(vectors, (0, 2 * width - vectors.shape[0])).reshape(2, width)
     out_and_vectors = jnp.concatenate([out_weight, head_rows, jnp.zeros((6, width), LOW)], axis=0)
-    meta, qkv_own, out_and_vectors, down_piece = order.step(meta, qkv_own, out_and_vectors, eighth(down_weight))
+    down_piece, out_and_vectors, grad_now, _ = lax.optimization_barrier(
+        (eighth(down_weight), out_and_vectors, out_grad, in_theirs)
+    )
+    down_piece = swap(down_piece, "tp", 2)
+    out_and_vectors = swap(out_and_vectors, "tp", 2)
+    grad_mine, grad_theirs = mine_of(grad_now)
+    meta, qkv_own, grad_mine, grad_theirs = order.step(meta, qkv_own, grad_mine, grad_theirs)
     (qkv_piece,) = order.step(qkv_piece)
     qkv_other = gather_eighths(qkv_piece)
     in_far, in_other = order.step(in_far, in_other)
     in_other_far = swap(in_other, "tp", 1)
-    down_piece, out_and_vectors = order.then(down_piece, out_and_vectors)
-    down_piece = swap(down_piece, "tp", 2)
-    out_and_vectors = swap(out_and_vectors, "tp", 2)
+    grad_other = swap(order.then(grad_theirs)[0], "tp", 2)
     (in_other_far,) = order.step(in_other_far)
 
     def biases(vector):
@@ -987,19 +996,18 @@
             [whole((cap, 3 * shard))],
             (shape(cap, shard), jax.ShapeDtypeStruct((kept, cell, heads * cell), LOW)),
             (whole((cap, shard)), whole((kept, cell, heads * cell))),
-            (1,), (), 4, "attend",
+            (1,), [pltpu.VMEM((4 * cell, 4 * cell), LOW)], 4, "attend",
         )
         order.done(context)
         return context, attend
 
     down_piece, out_and_vectors = order.step(down_piece, out_and_vectors)
     down_other = gather_eighths(down_piece)
-    grad_mine, grad_theirs = mine_of(order.then(out_grad)[0])
-    grad_other = swap(grad_theirs, "tp", 2)
-    grad_far = swap(grad_mine, "tp", 1)
+    grad_now, up_now = order.then(grad_mine, up_weight)
+    up_other = swap(up_now, "tp", 2)
+    grad_far = swap(grad_now, "tp", 1)
     context_own, attend_own = attend_shard(proj_own)
-    (grad_far,) = order.step(grad_far)
-    up_other = swap(order.then(up_weight)[0], "tp", 2)
+    grad_far, grad_other = order.step(grad_far, grad_other)
     out_other = out_and_vectors[:shard]
     vectors_other = out_and_vectors[shard : shard + 2].reshape(-1)[: vectors.shape[0]]
     normed_now, qkv_now = order.then(normed, qkv_other)
@@ -1013,7 +1021,6 @@
     )
     order.done(proj_other)
     context_other, attend_other = attend_shard(proj_other)
-    (grad_other,) = order.step(grad_other)
     grad_other_far = swap(grad_other, "tp", 1)
     (context_now,) = order.then(context_other)
     attn_part = call(

time: 628 us -> 621 us (0.989)
  Pallas kernels: 298 us -> 411 us
  starting transfers between devices: 108 us -> 39.7 us
  waiting for transfers between devices: 139 us -> 85.4 us
    pallas_call x40, Pallas kernels: 298 us -> 411 us  [call(): pl.pallas_call(kernel, grid_spec=pltpu.PrefetchScalarGridSpec(num_scalar_...]
    ppermute x45, starting transfers between devices: 108 us -> 39.6 us  [swap(): return lax.ppermute(value, axis, [(i, i ^ bit) for i in range(count)])]
    ppermute x45, waiting for transfers between devices: 139 us -> 85.4 us  [swap(): return lax.ppermute(value, axis, [(i, i ^ bit) for i in range(count)])]
  transfers between devices with their start and end apart: 47 -> 47, of which waited for: 16 -> 14; matrix products, arithmetic and copies ran while one was open for 6% -> 6% of each run, Pallas kernels for 40% -> 56%
where the time goes in v3:
time: 621 us; the launch traced here: 611 us
  Pallas kernels  411 us (66%)
  waiting for transfers between devices  85.4 us (14%)
  local copies, waits for them, and re-layouts  47.4 us (8%)
  starting transfers between devices  39.7 us (6%)
  between operations  15.5 us (2%)
  other arithmetic  12.8 us (2%)
    pallas_call x40, Pallas kernels, call(): pl.pallas_call(kernel, grid_spec=pltpu.PrefetchScalarGridSpec(num_scalar_...  411 us
    ppermute x45, waiting for transfers between devices, swap(): return lax.ppermute(value, axis, [(i, i ^ bit) for i in range(count)])  85.4 us
    ppermute x45, starting transfers between devices, swap(): return lax.ppermute(value, axis, [(i, i ^ bit) for i in range(count)])  39.6 us
    unnamed x78, local copies, waits for them, and re-layouts  19.2 us
  transfers between devices with their start and end apart: 47, of which 14 were waited for; matrix products, arithmetic and copies ran while one was open for 6% of the time, Pallas kernels for 56%

profile of v3, /device:TPU:0, one launch (start us, length us, event | category | flops | bytes accessed | tf_op | source)
XLA Modules:
  0.0 611.3 jit_solution(14517482461930428179)
XLA Ops:
  7.2 1.8 pad_dynamic-slice_fusion
  9.1 2.9 collective-permute-start.2
  18.7 1.8 collective-permute-start.1
  32.2 15.7 %collective-permute-done.1.a1 = bf16[32,16,1120]{2,1,0:T(8,128)(2,1)} collective-permute-done((bf16[32,16,1120]{2,1,0:T(8,128)(2,1)}, bf16[32,16,1120]{2,1,0:T(8,128)(2,1)}, u32[]{:S(2)}, u32[]{:S(2)}) %collective-permute-start.1) | collective-permute-done | bytes 1146912 | tf_op jit(solution)/shard_map/ppermute | solution.py:31
  54.1 1.9 concatenate.35.meta
  56.1 14.4 %begin.1 = (f32[2048,1120]{1,0:T(8,128)}, bf16[2048,1120]{1,0:T(8,128)(2,1)}, bf16[2048,840]{1,0:T(8,128)(2,1)}) custom-call(s32[584]{0:T(1024)} %concatenate.35.meta, bf16[32,16,1120]{2,1,0:T(8,128)(2,1)} %copy-done.10, bf16[32,16,1120]{2,1,0:T(8,128)(2,1)} %collective-permute-done.1.a1, bf16[32,16,1120]{2,1,0:T(8,128)(2,1)} %collective-permute-done.a2, ...), custom_call_target="tpu_custom_call" | custom-call | flops 6750000128 | tf_op jit(solution)/shard_map/begin/pallas_call | solution.py:180
  70.5 1.8 collective-permute-start.7
  73.4 2.0 slice.88.weight_b.refs_8_
  76.6 14.8 %attend.2 = (bf16[2048,280]{1,0:T(8,128)(2,1)}, bf16[32,64,320]{2,1,0:T(8,128)(2,1)}) custom-call(s32[584]{0:T(1024)} %concatenate.35.meta, bf16[2048,840]{1,0:T(8,128)(2,1)} %get-tuple-element.243.projected), custom_call_target="tpu_custom_call" | custom-call | flops 1800000000 | tf_op jit(solution)/shard_map/attend/pallas_call | solution.py:180
  91.4 8.1 %collective-permute-done.7.refs_8_ = bf16[32,16,1120]{2,1,0:T(8,128)(2,1)} collective-permute-done((bf16[32,16,1120]{2,1,0:T(8,128)(2,1)S(1)}, bf16[32,16,1120]{2,1,0:T(8,128)(2,1)}, u32[]{:S(2)}, u32[]{:S(2)}) %collective-permute-start.7) | collective-permute-done | bytes 1146912 | tf_op jit(solution)/shard_map/ppermute | solution.py:31
  99.5 11.1 %project.1.projected = bf16[2048,840]{1,0:T(8,128)(2,1)} custom-call(s32[584]{0:T(1024)} %concatenate.35.meta, bf16[2048,1120]{1,0:T(8,128)(2,1)} %get-tuple-element.254.normed.refs_1_, bf16[896,1120]{1,0:T(8,128)(2,1)} %bitcast.122, f32[1,840]{1,0:T(1,128)} %fusion.7.bias), custom_call_target="tpu_custom_call" | custom-call | flops 2700000000 | tf_op jit(solution)/shard_map/project/pallas_call | solution.py:180
  110.6 14.9 %attend.3 = (bf16[2048,280]{1,0:T(8,128)(2,1)}, bf16[32,64,320]{2,1,0:T(8,128)(2,1)}) custom-call(s32[584]{0:T(1024)} %concatenate.35.meta, bf16[2048,840]{1,0:T(8,128)(2,1)} %project.1.projected), custom_call_target="tpu_custom_call" | custom-call | flops 1800000000 | tf_op jit(solution)/shard_map/attend/pallas_call | solution.py:180
  125.5 9.3 %out_project.1 = (bf16[1024,1120]{1,0:T(8,128)(2,1)}, bf16[1024,1120]{1,0:T(8,128)(2,1)}) custom-call(s32[584]{0:T(1024)} %concatenate.35.meta, bf16[2048,280]{1,0:T(8,128)(2,1)} %get-tuple-element.255.a.refs_2_, bf16[2048,280]{1,0:T(8,128)(2,1)} %get-tuple-element.234.b.refs_2_, bf16[280,1120]{1,0:T(8,128)(2,1)} %refs_7_.1, ...), custom_call_target="tpu_custom_call" | custom-call | flops 4499999744 | tf_op jit(solution)/shard_map/out_project/pallas_call | solution.py:180
  137.3 7.3 %collective-permute-done.8.refs_10_ = bf16[32,16,1120]{2,1,0:T(8,128)(2,1)S(1)} collective-permute-done((bf16[32,16,1120]{2,1,0:T(8,128)(2,1)}, bf16[32,16,1120]{2,1,0:T(8,128)(2,1)S(1)}, u32[]{:S(2)}, u32[]{:S(2)}) %collective-permute-start.8) | collective-permute-done | bytes 1146912 | tf_op jit(solution)/shard_map/ppermute | solution.py:31
  144.7 9.8 %collective-permute-done.9 = bf16[70,16,1120]{2,1,0:T(8,128)(2,1)} collective-permute-done((bf16[70,16,1120]{2,1,0:T(8,128)(2,1)}, bf16[70,16,1120]{2,1,0:T(8,128)(2,1)}, u32[]{:S(2)}, u32[]{:S(2)}) %collective-permute-start.9) | collective-permute-done | bytes 2508832 | tf_op jit(solution)/shard_map/ppermute | solution.py:31
  155.8 63.2 %mlp.1 = (f32[2048,1120]{1,0:T(8,128)}, bf16[2048,1120]{1,0:T(8,128)(2,1)}, bf16[2048,1120]{1,0:T(8,128)(2,1)}, bf16[2048,1120]{1,0:T(8,128)(2,1)}, bf16[2048,11...) custom-call(s32[584]{0:T(1024)} %concatenate.35.meta, ...), custom_call_target="tpu_custom_call" | custom-call | flops 29250000896 | tf_op jit(solution)/shard_map/mlp/pallas_call | solution.py:180
  220.1 12.5 %weight_grad.6 = bf16[1120,1120]{1,0:T(8,128)(2,1)} custom-call(s32[584]{0:T(1024)} %concatenate.35.meta, bf16[2048,1120]{1,0:T(8,128)(2,1)} %get-tuple-element.220.refs_0_, bf16[2048,1120]{1,0:T(8,128)(2,1)} %get-tuple-element.210.refs_1_), custom_call_target="tpu_custom_call" | custom-call | flops 5849999872 | tf_op jit(solution)/shard_map/weight_grad/pallas_call | solution.py:180
  232.6 1.8 collective-permute-start.16
  234.3 12.7 %weight_grad.7 = bf16[1120,1120]{1,0:T(8,128)(2,1)} custom-call(s32[584]{0:T(1024)} %concatenate.35.meta, bf16[2048,1120]{1,0:T(8,128)(2,1)} %get-tuple-element.211.refs_0_, bf16[2048,1120]{1,0:T(8,128)(2,1)} %get-tuple-element.230.refs_1_.refs_5_), custom_call_target="tpu_custom_call" | custom-call | flops 5849999872 | tf_op jit(solution)/shard_map/weight_grad/pallas_call | solution.py:180
  247.3 18.3 %middle_back.1 = (f32[2048,1120]{1,0:T(8,128)}, bf16[2048,1120]{1,0:T(8,128)(2,1)}, bf16[2048,280]{1,0:T(8,128)(2,1)}, bf16[2048,280]{1,0:T(8,128)(2,1)}, f32[8,1120]{1,0:T(8,128)}) custom-call(s32[584]{0:T(1024)} %concatenate.35.meta, bf16[1024,1120]{1,0:T(8,128)(2,1)} %get-tuple-element.203.refs_0_, bf16[1024,1120]{1,0:T(8,128)(2,1)} %get-tuple-element.204.refs_1_, ...), custom_call_target="tpu_custom_call" | custom-call | flops 8099999744 | tf_op jit(solution)/shard_map/middle_back/pallas_call | solution.py:180
  265.6 13.3 %weight_grad.8.own.mine = bf16[1120,1120]{1,0:T(8,128)(2,1)} custom-call(s32[584]{0:T(1024)} %concatenate.35.meta, bf16[2048,1120]{1,0:T(8,128)(2,1)} %get-tuple-element.220.refs_0_, bf16[2048,1120]{1,0:T(8,128)(2,1)} %get-tuple-element.221.refs_1_), custom_call_target="tpu_custom_call" | custom-call | flops 5849999872 | tf_op jit(solution)/shard_map/weight_grad/pallas_call | solution.py:180
  278.9 30.1 %attend_back.2 = (bf16[2048,840]{1,0:T(8,128)(2,1)}, f32[8,280]{1,0:T(8,128)}) custom-call(s32[584]{0:T(1024)} %concatenate.35.meta, bf16[2048,840]{1,0:T(8,128)(2,1)} %project.1.projected, bf16[32,64,320]{2,1,0:T(8,128)(2,1)} %get-tuple-element.224.attend, bf16[2048,280]{1,0:T(8,128)(2,1)} %get-tuple-element.225.context_grad), custom_call_target="tpu_custom_call" | custom-call | flops 13500000256 | tf_op jit(solution)/shard_map/attend_back/pallas_call | solution.py:180
  310.5 5.4 first_sum.3
  315.9 12.5 %weight_grad.9.own.mine = bf16[1120,1120]{1,0:T(8,128)(2,1)} custom-call(s32[584]{0:T(1024)} %concatenate.35.meta, bf16[2048,1120]{1,0:T(8,128)(2,1)} %get-tuple-element.229.refs_0_, bf16[2048,1120]{1,0:T(8,128)(2,1)} %get-tuple-element.230.refs_1_.refs_5_), custom_call_target="tpu_custom_call" | custom-call | flops 5849999872 | tf_op jit(solution)/shard_map/weight_grad/pallas_call | solution.py:180
  328.4 15.2 %weight_grad.10 = bf16[1120,1120]{1,0:T(8,128)(2,1)} custom-call(s32[584]{0:T(1024)} %concatenate.35.meta, bf16[2048,840]{1,0:T(8,128)(2,1)} %get-tuple-element.232.refs_0_.b, bf16[2048,1120]{1,0:T(8,128)(2,1)} %get-tuple-element.254.normed.refs_1_, bf16[2048,280]{1,0:T(8,128)(2,1)} %get-tuple-element.234.b.refs_2_, ...), custom_call_target="tpu_custom_call" | custom-call | flops 5849999872 | tf_op jit(solution)/shard_map/weight_grad/pallas_call | solution.py:180
  346.2 5.2 first_sum.4
  352.4 4.3 second_sum.3
  356.7 30.0 %attend_back.3 = (bf16[2048,840]{1,0:T(8,128)(2,1)}, f32[8,280]{1,0:T(8,128)}) custom-call(s32[584]{0:T(1024)} %concatenate.35.meta, bf16[2048,840]{1,0:T(8,128)(2,1)} %get-tuple-element.243.projected, bf16[32,64,320]{2,1,0:T(8,128)(2,1)} %get-tuple-element.244.attend, bf16[2048,280]{1,0:T(8,128)(2,1)} %get-tuple-element.245.context_grad), custom_call_target="tpu_custom_call" | custom-call | flops 13500000256 | tf_op jit(solution)/shard_map/attend_back/pallas_call | solution.py:180
  387.6 3.2 third_sum.3
  391.9 4.4 second_sum.4
  397.7 15.7 %weight_grad.11.own.mine = bf16[1120,1120]{1,0:T(8,128)(2,1)} custom-call(s32[584]{0:T(1024)} %concatenate.35.meta, bf16[2048,840]{1,0:T(8,128)(2,1)} %get-tuple-element.263.refs_0_.a, bf16[2048,1120]{1,0:T(8,128)(2,1)} %get-tuple-element.254.normed.refs_1_, bf16[2048,280]{1,0:T(8,128)(2,1)} %get-tuple-element.255.a.refs_2_, ...), custom_call_target="tpu_custom_call" | custom-call | flops 5849999872 | tf_op jit(solution)/shard_map/weight_grad/pallas_call | solution.py:180
  414.9 5.2 first_sum.5
  420.9 2.7 fourth_sum.3.mine
  424.4 3.3 third_sum.4
  427.7 2.9 collective-permute-start.24
  430.6 14.6 %first_part.1 = (bf16[1024,1120]{1,0:T(8,128)(2,1)}, bf16[1024,1120]{1,0:T(8,128)(2,1)}) custom-call(s32[584]{0:T(1024)} %concatenate.35.meta, bf16[2048,840]{1,0:T(8,128)(2,1)} %get-tuple-element.263.refs_0_.a, bf16[2048,840]{1,0:T(8,128)(2,1)} %get-tuple-element.232.refs_0_.b, bf16[840,1120]{1,0:T(8,128)(2,1)} %bitcast.126, bf16[896,1120]{1,0:T(8,128)(2,1)} %bitcast.123), custom_call_target="tpu_custom_call" | custom-call | flops 6750000128 | tf_op jit(solution)/shard_map/first_part/pallas_call | solution.py:180
  446.5 2.7 join.6.mine
  449.3 2.6 collective-permute-done.24
  452.6 2.6 fourth_sum.4.mine
  456.3 4.3 second_sum.5
  463.8 15.4 %start_back.1 = (bf16[64,16,1120]{2,1,0:T(8,128)(2,1)}, f32[8,1120]{1,0:T(8,128)}, f32[32,1120]{1,0:T(8,128)}) custom-call(s32[584]{0:T(1024)} %concatenate.35.meta, bf16[1024,1120]{1,0:T(8,128)(2,1)} %get-tuple-element.271.refs_0_, bf16[1024,1120]{1,0:T(8,128)(2,1)} %get-tuple-element.264.refs_1_, bf16[1024,1120]{1,0:T(8,128)(2,1)} %bitcast.112, ...), custom_call_target="tpu_custom_call" | custom-call | flops 6750000128 | tf_op jit(solution)/shard_map/start_back/pallas_call | solution.py:180
  480.1 3.0 join.7.mine
  483.1 4.6 collective-permute-done.28
  488.5 3.2 third_sum.5
  492.5 2.8 join.8.mine
  495.9 2.6 vectors.1
  498.6 2.8 collective-permute-start.33
  503.3 13.5 %collective-permute-done.34 = bf16[9,16,1120]{2,1,0:T(8,128)(2,1)S(1)} collective-permute-done((bf16[9,16,1120]{2,1,0:T(8,128)(2,1)S(1)}, bf16[9,16,1120]{2,1,0:T(8,128)(2,1)S(1)}, u32[]{:S(2)}, u32[]{:S(2)}) %collective-permute-start.34) | collective-permute-done | bytes 322592 | tf_op jit(solution)/shard_map/ppermute | solution.py:31
  517.6 2.7 fourth_sum.5.mine
  521.1 3.2 join.9.mine
  524.3 1.9 collective-permute-start.39
  526.2 3.4 collective-permute-start.37
  529.6 10.5 %finish.1 = bf16[64,16,1120]{2,1,0:T(8,128)(2,1)} custom-call(s32[584]{0:T(1024)} %concatenate.35.meta, f32[2048,1120]{1,0:T(8,128)} %get-tuple-element.294.refs_4_.middle, bf16[1024,1120]{1,0:T(8,128)(2,1)} %get-tuple-element.201.refs_0_, bf16[1024,1120]{1,0:T(8,128)(2,1)} %get-tuple-element.202.refs_1_, bf16[1024,1120]{1,0:T(8,128)(2,1)} %bitcast.120, ...), custom_call_target="tpu_custom_call" | custom-call | flops 4499999744 | tf_op jit(solution)/shard_map/finish/pallas_call | solution.py:180
  541.4 2.8 join.10.mine
  546.9 4.2 collective-permute-start.35
  551.1 5.1 widen_rows.3
  556.2 5.1 collective-permute-done.39
  561.3 5.2 widen_rows.4
  566.5 3.2 join.11.mine
  574.4 2.9 collective-permute-done.42
  577.3 1.9 collective-permute-start.43
  582.6 3.2 collective-permute-done.43
  588.4 10.8 %collective-permute-done.44 = bf16[35,16,1120]{2,1,0:T(8,128)(2,1)} collective-permute-done((bf16[35,16,1120]{2,1,0:T(8,128)(2,1)}, bf16[35,16,1120]{2,1,0:T(8,128)(2,1)}, u32[]{:S(2)}, u32[]{:S(2)}) %collective-permute-start.44) | collective-permute-done | bytes 1254432 | tf_op jit(solution)/shard_map/ppermute | solution.py:31
  599.2 5.1 widen_rows.5
  (209 shorter events, 70.6 us)
Async XLA Ops:
  7.2 8.3 %copy-start.3 = (bf16[64,16,1120]{2,1,0:T(8,128)(2,1)S(1)}, bf16[64,16,1120]{2,1,0:T(8,128)(2,1)}, u32[]{:S(2)}) copy-start(bf16[64,16,1120]{2,1,0:T(8,128)(2,1)} %param.14) | copy-start | bytes 6881284
  7.2 92.3 %all-gather.3.cloned.1.call-start = ((), (), s32[]{:S(2)}) async-start(), calls=%async_computation | async-start | bytes 2322432 | tf_op jit(solution)/shard_map/all_gather | solution.py:654
  9.1 9.5 %collective-permute-start.2 = (bf16[7,16,1120]{2,1,0:T(8,128)(2,1)}, bf16[7,16,1120]{2,1,0:T(8,128)(2,1)}, u32[]{:S(2)}, u32[]{:S(2)}) collective-permute-start(bf16[7,16,1120]{2,1,0:T(8,128)(2,1)} %bitcast.11), channel_id=1, source_target_pairs={{0,2},{1,3},{2,0},{3,1},{4,6},{5,7},{6,4},{7,5},{8,10},{9,11},{10,... | collective-permute-start | bytes 752648 | tf_op jit(solution)/shard_map/ppermute | solution.py:31
  15.4 2.6 copy-start.4
  18.2 54.1 %copy-start.9 = (bf16[32,16,1120]{2,1,0:T(8,128)(2,1)}, bf16[32,16,1120]{2,1,0:T(8,128)(2,1)S(1)}, u32[]{:S(2)}) copy-start(bf16[32,16,1120]{2,1,0:T(8,128)(2,1)S(1)} %get-tuple-element.176.refs_7_) | copy-start | bytes 3440644
  18.6 135.9 %all-gather.5.cloned.1.call-start = ((), (), s32[]{:S(2)}) async-start(), calls=%async_computation.1 | async-start | bytes 2985984 | tf_op jit(solution)/shard_map/all_gather | solution.py:654
  18.6 13.5 %collective-permute-start = (bf16[32,16,1120]{2,1,0:T(8,128)(2,1)S(1)}, bf16[32,16,1120]{2,1,0:T(8,128)(2,1)}, u32[]{:S(2)}, u32[]{:S(2)}) collective-permute-start(bf16[32,16,1120]{2,1,0:T(8,128)(2,1)S(1)} %get-tuple-element.330.a0), channel_id=1, source_target_pairs={{0,1},{1,0},{2,3},{3,2},{4,5},{5,4},{6,7},{7,6},{8,9},{9,8},{10,11... | collective-permute-start | bytes 3440648 | tf_op jit(solution)/shard_map/ppermute | solution.py:31
  18.7 29.1 %collective-permute-start.1 = (bf16[32,16,1120]{2,1,0:T(8,128)(2,1)}, bf16[32,16,1120]{2,1,0:T(8,128)(2,1)}, u32[]{:S(2)}, u32[]{:S(2)}) collective-permute-start(bf16[32,16,1120]{2,1,0:T(8,128)(2,1)} %get-tuple-element.329), channel_id=1, source_target_pairs={{0,2},{1,3},{2,0},{3,1},{4,6},{5,7},{6,4},{7,5},{8,10},{9,11},{10,... | collective-permute-start | bytes 3440648 | tf_op jit(solution)/shard_map/ppermute | solution.py:31
  20.5 50.0 %collective-permute-start.5 = (bf16[18,16,1120]{2,1,0:T(8,128)(2,1)}, bf16[18,16,1120]{2,1,0:T(8,128)(2,1)}, u32[]{:S(2)}, u32[]{:S(2)}) collective-permute-start(bf16[18,16,1120]{2,1,0:T(8,128)(2,1)} %bitcast.127), channel_id=1, source_target_pairs={{0,2},{1,3},{2,0},{3,1},{4,6},{5,7},{6,4},{7,5},{8,10},{9,11},{10,... | collective-permute-start | bytes 1935368 | tf_op jit(solution)/shard_map/ppermute | solution.py:31
  20.8 49.7 %collective-permute-start.4 = (bf16[9,16,1120]{2,1,0:T(8,128)(2,1)}, bf16[9,16,1120]{2,1,0:T(8,128)(2,1)}, u32[]{:S(2)}, u32[]{:S(2)}) collective-permute-start(bf16[9,16,1120]{2,1,0:T(8,128)(2,1)} %bitcast.128), channel_id=1, source_target_pairs={{0,2},{1,3},{2,0},{3,1},{4,6},{5,7},{6,4},{7,5},{8,10},{9,11},{10,... | collective-permute-start | bytes 967688 | tf_op jit(solution)/shard_map/ppermute | solution.py:31
  27.4 3.4 copy-start.16
  47.9 8.2 %collective-permute-start.3 = (bf16[32,16,1120]{2,1,0:T(8,128)(2,1)}, bf16[32,16,1120]{2,1,0:T(8,128)(2,1)}, u32[]{:S(2)}, u32[]{:S(2)}) collective-permute-start(bf16[32,16,1120]{2,1,0:T(8,128)(2,1)} %collective-permute-done.1.a1), channel_id=1, source_target_pairs={{0,1},{1,0},{2,3},{3,2},{4,5},{5,4},{6,7},{7,6},{8,9},{9,8},{10,11... | collective-permute-start | bytes 3440648 | tf_op jit(solution)/shard_map/ppermute | solution.py:31
  70.5 28.9 %collective-permute-start.7 = (bf16[32,16,1120]{2,1,0:T(8,128)(2,1)S(1)}, bf16[32,16,1120]{2,1,0:T(8,128)(2,1)}, u32[]{:S(2)}, u32[]{:S(2)}) collective-permute-start(bf16[32,16,1120]{2,1,0:T(8,128)(2,1)S(1)} %get-tuple-element.177), channel_id=1, source_target_pairs={{0,2},{1,3},{2,0},{3,1},{4,6},{5,7},{6,4},{7,5},{8,10},{9,11},{10,... | collective-permute-start | bytes 3440648 | tf_op jit(solution)/shard_map/ppermute | solution.py:31
  72.3 27.1 %collective-permute-start.6 = (bf16[32,16,1120]{2,1,0:T(8,128)(2,1)S(1)}, bf16[32,16,1120]{2,1,0:T(8,128)(2,1)}, u32[]{:S(2)}, u32[]{:S(2)}) collective-permute-start(bf16[32,16,1120]{2,1,0:T(8,128)(2,1)S(1)} %get-tuple-element.176.refs_7_), channel_id=1, source_target_pairs={{0,1},{1,0},{2,3},{3,2},{4,5},{5,4},{6,7},{7,6},{8,9},{9,8},{10,11... | collective-permute-start | bytes 3440648 | tf_op jit(solution)/shard_map/ppermute | solution.py:31
  75.5 78.9 %collective-permute-start.9 = (bf16[70,16,1120]{2,1,0:T(8,128)(2,1)}, bf16[70,16,1120]{2,1,0:T(8,128)(2,1)}, u32[]{:S(2)}, u32[]{:S(2)}) collective-permute-start(bf16[70,16,1120]{2,1,0:T(8,128)(2,1)} %bitcast.130), channel_id=1, source_target_pairs={{0,2},{1,3},{2,0},{3,1},{4,6},{5,7},{6,4},{7,5},{8,10},{9,11},{10,... | collective-permute-start | bytes 7526408 | tf_op jit(solution)/shard_map/ppermute | solution.py:31
  125.5 10.0 %copy-start.14 = (bf16[1120]{0:T(1024)(128)(2,1)S(1)}, bf16[1120]{0:T(1024)(128)(2,1)}, u32[]{:S(2)}) copy-start(bf16[1120]{0:T(1024)(128)(2,1)} %param.25) | copy-start | bytes 6724
  125.5 10.5 %copy-start.13 = (bf16[2,1120]{1,0:T(2,128)(2,1)S(1)}, bf16[2,1120]{1,0:T(2,128)(2,1)}, u32[]{:S(2)}) copy-start(bf16[2,1120]{1,0:T(2,128)(2,1)} %param.23) | copy-start | bytes 13444
  134.8 19.7 %collective-permute-start.10 = (bf16[64,16,1120]{2,1,0:T(8,128)(2,1)}, bf16[64,16,1120]{2,1,0:T(8,128)(2,1)S(1)}, u32[]{:S(2)}, u32[]{:S(2)}) collective-permute-start(bf16[64,16,1120]{2,1,0:T(8,128)(2,1)} %bitcast.140), channel_id=1, source_target_pairs={{0,1},{1,0},{2,3},{3,2},{4,5},{5,4},{6,7},{7,6},{8,9},{9,8},{10,11... | collective-permute-start | bytes 6881288 | tf_op jit(solution)/shard_map/ppermute | solution.py:31
  134.9 19.6 %collective-permute-start.11 = (bf16[64,16,1120]{2,1,0:T(8,128)(2,1)}, bf16[64,16,1120]{2,1,0:T(8,128)(2,1)}, u32[]{:S(2)}, u32[]{:S(2)}) collective-permute-start(bf16[64,16,1120]{2,1,0:T(8,128)(2,1)} %bitcast.141), channel_id=1, source_target_pairs={{0,1},{1,0},{2,3},{3,2},{4,5},{5,4},{6,7},{7,6},{8,9},{9,8},{10,11... | collective-permute-start | bytes 6881288 | tf_op jit(solution)/shard_map/ppermute | solution.py:31
  135.4 9.3 %collective-permute-start.8 = (bf16[32,16,1120]{2,1,0:T(8,128)(2,1)}, bf16[32,16,1120]{2,1,0:T(8,128)(2,1)S(1)}, u32[]{:S(2)}, u32[]{:S(2)}) collective-permute-start(bf16[32,16,1120]{2,1,0:T(8,128)(2,1)} %collective-permute-done.7.refs_8_), channel_id=1, source_target_pairs={{0,1},{1,0},{2,3},{3,2},{4,5},{5,4},{6,7},{7,6},{8,9},{9,8},{10,11... | collective-permute-start | bytes 3440648 | tf_op jit(solution)/shard_map/ppermute | solution.py:31
  144.7 9.8 %copy-start.23 = (bf16[32,16,1120]{2,1,0:T(8,128)(2,1)}, bf16[32,16,1120]{2,1,0:T(8,128)(2,1)S(1)}, u32[]{:S(2)}) copy-start(bf16[32,16,1120]{2,1,0:T(8,128)(2,1)S(1)} %collective-permute-done.8.refs_10_) | copy-start | bytes 3440644
  219.0 28.0 %collective-permute-start.14 = (bf16[64,16,1120]{2,1,0:T(8,128)(2,1)}, bf16[64,16,1120]{2,1,0:T(8,128)(2,1)}, u32[]{:S(2)}, u32[]{:S(2)}) collective-permute-start(bf16[64,16,1120]{2,1,0:T(8,128)(2,1)} %bitcast.138), channel_id=1, source_target_pairs={{0,1},{1,0},{2,3},{3,2},{4,5},{5,4},{6,7},{7,6},{8,9},{9,8},{10,11... | collective-permute-start | bytes 6881288 | tf_op jit(solution)/shard_map/ppermute | solution.py:31
  219.1 28.2 %collective-permute-start.15 = (bf16[64,16,1120]{2,1,0:T(8,128)(2,1)}, bf16[64,16,1120]{2,1,0:T(8,128)(2,1)}, u32[]{:S(2)}, u32[]{:S(2)}) collective-permute-start(bf16[64,16,1120]{2,1,0:T(8,128)(2,1)} %bitcast.139), channel_id=1, source_target_pairs={{0,1},{1,0},{2,3},{3,2},{4,5},{5,4},{6,7},{7,6},{8,9},{9,8},{10,11... | collective-permute-start | bytes 6881288 | tf_op jit(solution)/shard_map/ppermute | solution.py:31
  219.6 46.0 %collective-permute-start.12 = (bf16[64,16,1120]{2,1,0:T(8,128)(2,1)}, bf16[64,16,1120]{2,1,0:T(8,128)(2,1)S(1)}, u32[]{:S(2)}, u32[]{:S(2)}) collective-permute-start(bf16[64,16,1120]{2,1,0:T(8,128)(2,1)} %bitcast.118), channel_id=1, source_target_pairs={{0,1},{1,0},{2,3},{3,2},{4,5},{5,4},{6,7},{7,6},{8,9},{9,8},{10,11... | collective-permute-start | bytes 6881288 | tf_op jit(solution)/shard_map/ppermute | solution.py:31
  219.7 45.9 %collective-permute-start.13 = (bf16[64,16,1120]{2,1,0:T(8,128)(2,1)}, bf16[64,16,1120]{2,1,0:T(8,128)(2,1)S(1)}, u32[]{:S(2)}, u32[]{:S(2)}) collective-permute-start(bf16[64,16,1120]{2,1,0:T(8,128)(2,1)} %bitcast.119), channel_id=1, source_target_pairs={{0,1},{1,0},{2,3},{3,2},{4,5},{5,4},{6,7},{7,6},{8,9},{9,8},{10,11... | collective-permute-start | bytes 6881288 | tf_op jit(solution)/shard_map/ppermute | solution.py:31
  232.6 76.5 %collective-permute-start.16 = (bf16[70,16,1120]{2,1,0:T(8,128)(2,1)}, bf16[70,16,1120]{2,1,0:T(8,128)(2,1)S(1)}, u32[]{:S(2)}, u32[]{:S(2)}) collective-permute-start(bf16[70,16,1120]{2,1,0:T(8,128)(2,1)} %bitcast.137), channel_id=1, source_target_pairs={{0,2},{1,3},{2,0},{3,1},{4,6},{5,7},{6,4},{7,5},{8,10},{9,11},{10,... | collective-permute-start | bytes 7526408 | tf_op jit(solution)/shard_map/ppermute | solution.py:31
  247.0 99.2 %collective-permute-start.17 = (bf16[70,16,1120]{2,1,0:T(8,128)(2,1)}, bf16[70,16,1120]{2,1,0:T(8,128)(2,1)}, u32[]{:S(2)}, u32[]{:S(2)}) collective-permute-start(bf16[70,16,1120]{2,1,0:T(8,128)(2,1)} %bitcast.136), channel_id=1, source_target_pairs={{0,2},{1,3},{2,0},{3,1},{4,6},{5,7},{6,4},{7,5},{8,10},{9,11},{10,... | collective-permute-start | bytes 7526408 | tf_op jit(solution)/shard_map/ppermute | solution.py:31
  265.6 13.4 %copy-start.7 = (bf16[64,16,1120]{2,1,0:T(8,128)(2,1)}, bf16[64,16,1120]{2,1,0:T(8,128)(2,1)S(1)}, u32[]{:S(2)}) copy-start(bf16[64,16,1120]{2,1,0:T(8,128)(2,1)S(1)} %collective-permute-done.12) | copy-start | bytes 6881284
  265.6 13.3 %copy-start.8 = (bf16[64,16,1120]{2,1,0:T(8,128)(2,1)}, bf16[64,16,1120]{2,1,0:T(8,128)(2,1)S(1)}, u32[]{:S(2)}) copy-start(bf16[64,16,1120]{2,1,0:T(8,128)(2,1)S(1)} %collective-permute-done.13) | copy-start | bytes 6881284
  315.9 35.4 %collective-permute-start.19 = (bf16[35,16,1120]{2,1,0:T(8,128)(2,1)}, bf16[35,16,1120]{2,1,0:T(8,128)(2,1)S(1)}, u32[]{:S(2)}, u32[]{:S(2)}) collective-permute-start(bf16[35,16,1120]{2,1,0:T(8,128)(2,1)} %bitcast.149), channel_id=1, source_target_pairs={{0,4},{4,0},{8,12},{12,8},{16,20},{20,16},{24,28},{28,24},{1,5},{5... | collective-permute-start | bytes 3763208 | tf_op jit(solution)/shard_map/ppermute | solution.py:31
  343.6 69.8 %collective-permute-start.23 = (bf16[70,16,1120]{2,1,0:T(8,128)(2,1)}, bf16[70,16,1120]{2,1,0:T(8,128)(2,1)S(1)}, u32[]{:S(2)}, u32[]{:S(2)}) collective-permute-start(bf16[70,16,1120]{2,1,0:T(8,128)(2,1)} %bitcast.135), channel_id=1, source_target_pairs={{0,2},{1,3},{2,0},{3,1},{4,6},{5,7},{6,4},{7,5},{8,10},{9,11},{10,... | collective-permute-start | bytes 7526408 | tf_op jit(solution)/shard_map/ppermute | solution.py:31
  351.4 39.4 %collective-permute-start.18 = (bf16[35,16,1120]{2,1,0:T(8,128)(2,1)}, bf16[35,16,1120]{2,1,0:T(8,128)(2,1)S(1)}, u32[]{:S(2)}, u32[]{:S(2)}) collective-permute-start(bf16[35,16,1120]{2,1,0:T(8,128)(2,1)} %bitcast.147), channel_id=1, source_target_pairs={{0,4},{4,0},{8,12},{12,8},{16,20},{20,16},{24,28},{28,24},{1,5},{5... | collective-permute-start | bytes 3763208 | tf_op jit(solution)/shard_map/ppermute | solution.py:31
  356.7 30.0 %collective-permute-start.20 = (bf16[18,16,1120]{2,1,0:T(8,128)(2,1)}, bf16[18,16,1120]{2,1,0:T(8,128)(2,1)S(1)}, u32[]{:S(2)}, u32[]{:S(2)}) collective-permute-start(bf16[18,16,1120]{2,1,0:T(8,128)(2,1)} %bitcast.159), channel_id=1, source_target_pairs={{0,8},{4,12},{8,0},{12,4},{16,24},{20,28},{24,16},{28,20},{1,9},{5... | collective-permute-start | bytes 1935368 | tf_op jit(solution)/shard_map/ppermute | solution.py:31
  391.9 4.4 copy-start.31
  396.2 23.9 %collective-permute-start.22 = (bf16[9,16,1120]{2,1,0:T(8,128)(2,1)S(1)}, bf16[9,16,1120]{2,1,0:T(8,128)(2,1)S(1)}, u32[]{:S(2)}, u32[]{:S(2)}) collective-permute-start(bf16[9,16,1120]{2,1,0:T(8,128)(2,1)S(1)} %bitcast.165), channel_id=1, source_target_pairs={{0,16},{4,20},{8,24},{12,28},{16,0},{20,4},{24,8},{28,12},{1,17},{... | collective-permute-start | bytes 967688 | tf_op jit(solution)/shard_map/ppermute | solution.py:31
  397.7 25.8 %collective-permute-start.21 = (bf16[18,16,1120]{2,1,0:T(8,128)(2,1)}, bf16[18,16,1120]{2,1,0:T(8,128)(2,1)S(1)}, u32[]{:S(2)}, u32[]{:S(2)}) collective-permute-start(bf16[18,16,1120]{2,1,0:T(8,128)(2,1)} %bitcast.155), channel_id=1, source_target_pairs={{0,8},{4,12},{8,0},{12,4},{16,24},{20,28},{24,16},{28,20},{1,9},{5... | collective-permute-start | bytes 1935368 | tf_op jit(solution)/shard_map/ppermute | solution.py:31
  420.1 35.2 %collective-permute-start.27 = (bf16[35,16,1120]{2,1,0:T(8,128)(2,1)}, bf16[35,16,1120]{2,1,0:T(8,128)(2,1)S(1)}, u32[]{:S(2)}, u32[]{:S(2)}) collective-permute-start(bf16[35,16,1120]{2,1,0:T(8,128)(2,1)} %bitcast.144), channel_id=1, source_target_pairs={{0,4},{4,0},{8,12},{12,8},{16,20},{20,16},{24,28},{28,24},{1,5},{5... | collective-permute-start | bytes 3763208 | tf_op jit(solution)/shard_map/ppermute | solution.py:31
  423.5 22.3 %collective-permute-start.25 = (bf16[9,16,1120]{2,1,0:T(8,128)(2,1)}, bf16[9,16,1120]{2,1,0:T(8,128)(2,1)S(1)}, u32[]{:S(2)}, u32[]{:S(2)}) collective-permute-start(bf16[9,16,1120]{2,1,0:T(8,128)(2,1)} %bitcast.164), channel_id=1, source_target_pairs={{0,16},{4,20},{8,24},{12,28},{16,0},{20,4},{24,8},{28,12},{1,17},{... | collective-permute-start | bytes 967688 | tf_op jit(solution)/shard_map/ppermute | solution.py:31
  427.7 24.2 %collective-permute-start.24 = (bf16[9,16,1120]{2,1,0:T(8,128)(2,1)}, bf16[9,16,1120]{2,1,0:T(8,128)(2,1)S(1)}, u32[]{:S(2)}, u32[]{:S(2)}) collective-permute-start(bf16[9,16,1120]{2,1,0:T(8,128)(2,1)} %bitcast.168), channel_id=1, source_target_pairs={{0,16},{4,20},{8,24},{12,28},{16,0},{20,4},{24,8},{28,12},{1,17},{... | collective-permute-start | bytes 967688 | tf_op jit(solution)/shard_map/ppermute | solution.py:31
  445.2 16.4 %collective-permute-start.30 = (bf16[64,16,1120]{2,1,0:T(8,128)(2,1)}, bf16[64,16,1120]{2,1,0:T(8,128)(2,1)S(1)}, u32[]{:S(2)}, u32[]{:S(2)}) collective-permute-start(bf16[64,16,1120]{2,1,0:T(8,128)(2,1)} %bitcast.110), channel_id=1, source_target_pairs={{0,1},{1,0},{2,3},{3,2},{4,5},{5,4},{6,7},{7,6},{8,9},{9,8},{10,11... | collective-permute-start | bytes 6881288 | tf_op jit(solution)/shard_map/ppermute | solution.py:31
  445.3 16.3 %collective-permute-start.31 = (bf16[64,16,1120]{2,1,0:T(8,128)(2,1)}, bf16[64,16,1120]{2,1,0:T(8,128)(2,1)S(1)}, u32[]{:S(2)}, u32[]{:S(2)}) collective-permute-start(bf16[64,16,1120]{2,1,0:T(8,128)(2,1)} %bitcast.111), channel_id=1, source_target_pairs={{0,1},{1,0},{2,3},{3,2},{4,5},{5,4},{6,7},{7,6},{8,9},{9,8},{10,11... | collective-permute-start | bytes 6881288 | tf_op jit(solution)/shard_map/ppermute | solution.py:31
  449.2 30.0 %collective-permute-start.29 = (bf16[18,16,1120]{2,1,0:T(8,128)(2,1)}, bf16[18,16,1120]{2,1,0:T(8,128)(2,1)S(1)}, u32[]{:S(2)}, u32[]{:S(2)}) collective-permute-start(bf16[18,16,1120]{2,1,0:T(8,128)(2,1)} %bitcast.150), channel_id=1, source_target_pairs={{0,8},{4,12},{8,0},{12,4},{16,24},{20,28},{24,16},{28,20},{1,9},{5... | collective-permute-start | bytes 1935368 | tf_op jit(solution)/shard_map/ppermute | solution.py:31
  455.3 36.5 %collective-permute-start.26 = (bf16[9,16,1120]{2,1,0:T(8,128)(2,1)}, bf16[9,16,1120]{2,1,0:T(8,128)(2,1)S(1)}, u32[]{:S(2)}, u32[]{:S(2)}) collective-permute-start(bf16[9,16,1120]{2,1,0:T(8,128)(2,1)} %bitcast.161), channel_id=1, source_target_pairs={{0,16},{4,20},{8,24},{12,28},{16,0},{20,4},{24,8},{28,12},{1,17},{... | collective-permute-start | bytes 967688 | tf_op jit(solution)/shard_map/ppermute | solution.py:31
  460.6 27.1 %collective-permute-start.28 = (bf16[18,16,1120]{2,1,0:T(8,128)(2,1)}, bf16[18,16,1120]{2,1,0:T(8,128)(2,1)S(1)}, u32[]{:S(2)}, u32[]{:S(2)}) collective-permute-start(bf16[18,16,1120]{2,1,0:T(8,128)(2,1)} %bitcast.157), channel_id=1, source_target_pairs={{0,8},{4,12},{8,0},{12,4},{16,24},{20,28},{24,16},{28,20},{1,9},{5... | collective-permute-start | bytes 1935368 | tf_op jit(solution)/shard_map/ppermute | solution.py:31
  461.6 2.2 copy-start.2
  492.5 3.1 copy-start.30
  495.3 6.1 copy-start.5
  495.3 25.0 %collective-permute-start.32 = (bf16[18,16,1120]{2,1,0:T(8,128)(2,1)}, bf16[18,16,1120]{2,1,0:T(8,128)(2,1)S(1)}, u32[]{:S(2)}, u32[]{:S(2)}) collective-permute-start(bf16[18,16,1120]{2,1,0:T(8,128)(2,1)} %bitcast.151), channel_id=1, source_target_pairs={{0,8},{4,12},{8,0},{12,4},{16,24},{20,28},{24,16},{28,20},{1,9},{5... | collective-permute-start | bytes 1935368 | tf_op jit(solution)/shard_map/ppermute | solution.py:31
  495.6 21.2 %collective-permute-start.34 = (bf16[9,16,1120]{2,1,0:T(8,128)(2,1)S(1)}, bf16[9,16,1120]{2,1,0:T(8,128)(2,1)S(1)}, u32[]{:S(2)}, u32[]{:S(2)}) collective-permute-start(bf16[9,16,1120]{2,1,0:T(8,128)(2,1)S(1)} %bitcast.163), channel_id=1, source_target_pairs={{0,16},{4,20},{8,24},{12,28},{16,0},{20,4},{24,8},{28,12},{1,17},{... | collective-permute-start | bytes 967688 | tf_op jit(solution)/shard_map/ppermute | solution.py:31
  498.6 21.7 %collective-permute-start.33 = (f32[40,1120]{1,0:T(8,128)}, f32[40,1120]{1,0:T(8,128)S(1)}, u32[]{:S(2)}, u32[]{:S(2)}) collective-permute-start(f32[40,1120]{1,0:T(8,128)} %get-tuple-element.288), channel_id=1, source_target_pairs={{0,2},{1,3},{2,0},{3,1},{4,6},{5,7},{6,4},{7,5},{8,10},{9,11},{10,... | collective-permute-start | bytes 537608 | tf_op jit(solution)/shard_map/ppermute | solution.py:31
  502.4 44.4 %collective-permute-start.41 = (bf16[32,16,1120]{2,1,0:T(8,128)(2,1)}, bf16[32,16,1120]{2,1,0:T(8,128)(2,1)S(1)}, u32[]{:S(2)}, u32[]{:S(2)}) collective-permute-start(bf16[32,16,1120]{2,1,0:T(8,128)(2,1)} %slice.96), channel_id=1, source_target_pairs={{0,2},{1,3},{2,0},{3,1},{4,6},{5,7},{6,4},{7,5},{8,10},{9,11},{10,... | collective-permute-start | bytes 3440648 | tf_op jit(solution)/shard_map/ppermute | solution.py:31
  502.4 48.6 %collective-permute-start.40 = (bf16[35,16,1120]{2,1,0:T(8,128)(2,1)}, bf16[35,16,1120]{2,1,0:T(8,128)(2,1)}, u32[]{:S(2)}, u32[]{:S(2)}) collective-permute-start(bf16[35,16,1120]{2,1,0:T(8,128)(2,1)} %bitcast.81), channel_id=1, source_target_pairs={{0,4},{4,0},{8,12},{12,8},{16,20},{20,16},{24,28},{28,24},{1,5},{5... | collective-permute-start | bytes 3763208 | tf_op jit(solution)/shard_map/ppermute | solution.py:31
  520.2 4.1 copy-start.12
  521.1 5.1 copy-start.35
  524.3 36.9 %collective-permute-start.39 = (bf16[35,16,1120]{2,1,0:T(8,128)(2,1)}, bf16[35,16,1120]{2,1,0:T(8,128)(2,1)}, u32[]{:S(2)}, u32[]{:S(2)}) collective-permute-start(bf16[35,16,1120]{2,1,0:T(8,128)(2,1)} %bitcast.145), channel_id=1, source_target_pairs={{0,4},{4,0},{8,12},{12,8},{16,20},{20,16},{24,28},{28,24},{1,5},{5... | collective-permute-start | bytes 3763208 | tf_op jit(solution)/shard_map/ppermute | solution.py:31
  526.2 14.5 %collective-permute-start.37 = (bf16[9,16,1120]{2,1,0:T(8,128)(2,1)S(1)}, bf16[9,16,1120]{2,1,0:T(8,128)(2,1)S(1)}, u32[]{:S(2)}, u32[]{:S(2)}) collective-permute-start(bf16[9,16,1120]{2,1,0:T(8,128)(2,1)S(1)} %bitcast.170), channel_id=1, source_target_pairs={{0,16},{4,20},{8,24},{12,28},{16,0},{20,4},{24,8},{28,12},{1,17},{... | collective-permute-start | bytes 967688 | tf_op jit(solution)/shard_map/ppermute | solution.py:31
  541.4 4.3 copy-start
  544.2 22.3 %collective-permute-start.38 = (bf16[18,16,1120]{2,1,0:T(8,128)(2,1)}, bf16[18,16,1120]{2,1,0:T(8,128)(2,1)}, u32[]{:S(2)}, u32[]{:S(2)}) collective-permute-start(bf16[18,16,1120]{2,1,0:T(8,128)(2,1)} %bitcast.154), channel_id=1, source_target_pairs={{0,8},{4,12},{8,0},{12,4},{16,24},{20,28},{24,16},{28,20},{1,9},{5... | collective-permute-start | bytes 1935368 | tf_op jit(solution)/shard_map/ppermute | solution.py:31
  545.3 24.3 %collective-permute-start.36 = (f32[40,1120]{1,0:T(8,128)S(1)}, f32[40,1120]{1,0:T(8,128)S(1)}, u32[]{:S(2)}, u32[]{:S(2)}) collective-permute-start(f32[40,1120]{1,0:T(8,128)S(1)} %add.107), channel_id=1, source_target_pairs={{0,4},{4,0},{8,12},{12,8},{16,20},{20,16},{24,28},{28,24},{1,5},{5... | collective-permute-start | bytes 537608 | tf_op jit(solution)/shard_map/ppermute | solution.py:31
  546.9 32.4 %collective-permute-start.35 = (bf16[32,16,1120]{2,1,0:T(8,128)(2,1)}, bf16[32,16,1120]{2,1,0:T(8,128)(2,1)}, u32[]{:S(2)}, u32[]{:S(2)}) collective-permute-start(bf16[32,16,1120]{2,1,0:T(8,128)(2,1)} %slice.114), channel_id=1, source_target_pairs={{0,2},{1,3},{2,0},{3,1},{4,6},{5,7},{6,4},{7,5},{8,10},{9,11},{10,... | collective-permute-start | bytes 3440648 | tf_op jit(solution)/shard_map/ppermute | solution.py:31
  566.5 4.8 copy-start.6
  569.7 7.6 %collective-permute-start.42 = (f32[40,1120]{1,0:T(8,128)S(1)}, f32[40,1120]{1,0:T(8,128)S(1)}, u32[]{:S(2)}, u32[]{:S(2)}) collective-permute-start(f32[40,1120]{1,0:T(8,128)S(1)} %add.108), channel_id=1, source_target_pairs={{0,8},{4,12},{8,0},{12,4},{16,24},{20,28},{24,16},{28,20},{1,9},{5... | collective-permute-start | bytes 537608 | tf_op jit(solution)/shard_map/ppermute | solution.py:31
  573.4 25.8 %collective-permute-start.44 = (bf16[35,16,1120]{2,1,0:T(8,128)(2,1)}, bf16[35,16,1120]{2,1,0:T(8,128)(2,1)}, u32[]{:S(2)}, u32[]{:S(2)}) collective-permute-start(bf16[35,16,1120]{2,1,0:T(8,128)(2,1)} %bitcast.89), channel_id=1, source_target_pairs={{0,4},{4,0},{8,12},{12,8},{16,20},{20,16},{24,28},{28,24},{1,5},{5... | collective-permute-start | bytes 3763208 | tf_op jit(solution)/shard_map/ppermute | solution.py:31
  577.3 8.5 %collective-permute-start.43 = (f32[40,1120]{1,0:T(8,128)S(1)}, f32[40,1120]{1,0:T(8,128)S(1)}, u32[]{:S(2)}, u32[]{:S(2)}) collective-permute-start(f32[40,1120]{1,0:T(8,128)S(1)} %add.109), channel_id=1, source_target_pairs={{0,16},{4,20},{8,24},{12,28},{16,0},{20,4},{24,8},{28,12},{1,17},{... | collective-permute-start | bytes 537608 | tf_op jit(solution)/shard_map/ppermute | solution.py:31
  (22 other events, 21.9 us)
Sparse Core Ops, SparseCore 0:
  18.7 50.6 all-gather.2
  71.5 53.9 all-gather.4

commit v4 on v3

--- a/solution.py
+++ b/solution.py
@@ -163,6 +163,10 @@
 
 def rows_out(width):
     return rows_spec(width)
+
+
+def deep_spec(width):
+    return pl.BlockSpec((2 * BLOCK, width), lambda i, meta: (jnp.minimum(i, (meta[NBLK] + 1) // 2 - 1), 0))
 
 
 def rows_more(width):
@@ -483,13 +487,13 @@
 def weight_grad_kernel(pairs, meta, *refs):
     step = pl.program_id(0)
     result, total = refs[2 * pairs :]
-
-    @live_step(meta)
-    def _():
+    blocks = meta[NBLK] - 2 * step
+
+    def add(count):
         base = 0
         for a, b in zip(refs[: 2 * pairs : 2], refs[1 : 2 * pairs : 2]):
             rows = slice(base, base + a.shape[1])
-            part = dot_tn(a[...], b[...])
+            part = dot_tn(a[:count, :], b[:count, :])
             base += a.shape[1]
 
             @pl.when(step == 0)
@@ -500,9 +504,17 @@
             def _():
                 total[rows, :] += part
 
-        @pl.when(step == meta[NBLK] - 1)
-        def _():
-            result[...] = total[...].astype(LOW)
+    @pl.when(blocks >= 2)
+    def _():
+        add(2 * BLOCK)
+
+    @pl.when(blocks == 1)
+    def _():
+        add(BLOCK)
+
+    @pl.when((blocks > 0) & (blocks <= 2))
+    def _():
+        result[...] = total[...].astype(LOW)
 
 
 def middle_back_kernel(meta, *refs):
@@ -1062,9 +1074,9 @@
         rows = rows or operands[0].shape[1]
         (result,) = call(
             functools.partial(weight_grad_kernel, pairs), meta, operands,
-            [rows_spec(operand.shape[1]) for operand in operands],
+            [deep_spec(operand.shape[1]) for operand in operands],
             (shape(rows, cols),), (whole((rows, cols)),),
-            grid, [pltpu.VMEM((rows, cols), F32)], cost=13, name="weight_grad",
+            (META_BLOCKS // 2,), [pltpu.VMEM((rows, cols), F32)], cost=13, name="weight_grad",
         )
         order.done(result)
         return result

time: 621 us -> 626 us (level); the launches traced: 611 us -> 624 us
  Pallas kernels: 411 us -> 216 us
  waiting for transfers between devices: 85.4 us -> 208 us
  starting transfers between devices: 39.7 us -> 125 us
    pallas_call x40, Pallas kernels: 411 us -> 216 us  [call(): pl.pallas_call(kernel, grid_spec=pltpu.PrefetchScalarGridSpec(num_scalar_...]
    ppermute x45, waiting for transfers between devices: 85.4 us -> 207 us  [swap(): return lax.ppermute(value, axis, [(i, i ^ bit) for i in range(count)])]
    ppermute x45, starting transfers between devices: 39.6 us -> 125 us  [swap(): return lax.ppermute(value, axis, [(i, i ^ bit) for i in range(count)])]
  transfers between devices with their start and end apart: 47 -> 47, of which waited for: 14 -> 19; matrix products, arithmetic and copies ran while one was open for 6% -> 6% of each run, Pallas kernels for 56% -> 30%
where the time goes in v4:
time: 626 us; the launch traced here: 624 us
  Pallas kernels  216 us (35%)
  waiting for transfers between devices  208 us (33%)
  starting transfers between devices  125 us (20%)
  local copies, waits for them, and re-layouts  47.4 us (8%)
  between operations  15.5 us (2%)
  other arithmetic  12.8 us (2%)
    pallas_call x40, Pallas kernels, call(): pl.pallas_call(kernel, grid_spec=pltpu.PrefetchScalarGridSpec(num_scalar_...  216 us
    ppermute x45, waiting for transfers between devices, swap(): return lax.ppermute(value, axis, [(i, i ^ bit) for i in range(count)])  207 us
    ppermute x45, starting transfers between devices, swap(): return lax.ppermute(value, axis, [(i, i ^ bit) for i in range(count)])  125 us
    unnamed x78, local copies, waits for them, and re-layouts  19.2 us
  transfers between devices with their start and end apart: 47, of which 19 were waited for; matrix products, arithmetic and copies ran while one was open for 6% of the time, Pallas kernels for 30%

profile of v4, /device:TPU:0, one launch (start us, length us, event | category | flops | bytes accessed | tf_op | source)
XLA Modules:
  0.0 624.3 jit_solution(3104738343832093482)
XLA Ops:
  9.1 2.9 collective-permute-start.2
  32.2 15.7 %collective-permute-done.1.a1 = bf16[32,16,1120]{2,1,0:T(8,128)(2,1)} collective-permute-done((bf16[32,16,1120]{2,1,0:T(8,128)(2,1)}, bf16[32,16,1120]{2,1,0:T(8,128)(2,1)}, u32[]{:S(2)}, u32[]{:S(2)}) %collective-permute-start.1) | collective-permute-done | bytes 1146912 | tf_op jit(solution)/shard_map/ppermute | solution.py:31
  56.1 8.0 %begin.1 = (f32[2048,1120]{1,0:T(8,128)}, bf16[2048,1120]{1,0:T(8,128)(2,1)}, bf16[2048,840]{1,0:T(8,128)(2,1)}) custom-call(s32[584]{0:T(1024)} %concatenate.35.meta, bf16[32,16,1120]{2,1,0:T(8,128)(2,1)} %copy-done.10, bf16[32,16,1120]{2,1,0:T(8,128)(2,1)} %collective-permute-done.1.a1, bf16[32,16,1120]{2,1,0:T(8,128)(2,1)} %collective-permute-done.a2, ...), custom_call_target="tpu_custom_call" | custom-call | flops 6750000128 | tf_op jit(solution)/shard_map/begin/pallas_call | solution.py:184
  64.1 4.6 collective-permute-done.4
  74.5 5.9 attend.2
  80.3 17.5 %collective-permute-done.7.refs_8_ = bf16[32,16,1120]{2,1,0:T(8,128)(2,1)} collective-permute-done((bf16[32,16,1120]{2,1,0:T(8,128)(2,1)S(1)}, bf16[32,16,1120]{2,1,0:T(8,128)(2,1)}, u32[]{:S(2)}, u32[]{:S(2)}) %collective-permute-start.7) | collective-permute-done | bytes 1146912 | tf_op jit(solution)/shard_map/ppermute | solution.py:31
  97.8 6.2 project.1.projected
  104.1 6.1 attend.3
  110.1 4.0 out_project.1
  116.7 7.3 %collective-permute-done.8.refs_10_ = bf16[32,16,1120]{2,1,0:T(8,128)(2,1)S(1)} collective-permute-done((bf16[32,16,1120]{2,1,0:T(8,128)(2,1)}, bf16[32,16,1120]{2,1,0:T(8,128)(2,1)S(1)}, u32[]{:S(2)}, u32[]{:S(2)}) %collective-permute-start.8) | collective-permute-done | bytes 1146912 | tf_op jit(solution)/shard_map/ppermute | solution.py:31
  124.0 27.7 %collective-permute-done.9 = bf16[70,16,1120]{2,1,0:T(8,128)(2,1)} collective-permute-done((bf16[70,16,1120]{2,1,0:T(8,128)(2,1)}, bf16[70,16,1120]{2,1,0:T(8,128)(2,1)}, u32[]{:S(2)}, u32[]{:S(2)}) %collective-permute-start.9) | collective-permute-done | bytes 2508832 | tf_op jit(solution)/shard_map/ppermute | solution.py:31
  153.2 22.3 %mlp.1 = (f32[2048,1120]{1,0:T(8,128)}, bf16[2048,1120]{1,0:T(8,128)(2,1)}, bf16[2048,1120]{1,0:T(8,128)(2,1)}, bf16[2048,1120]{1,0:T(8,128)(2,1)}, bf16[2048,11...) custom-call(s32[584]{0:T(1024)} %concatenate.35.meta, ...), custom_call_target="tpu_custom_call" | custom-call | flops 29250000896 | tf_op jit(solution)/shard_map/mlp/pallas_call | solution.py:184
  176.6 5.9 weight_grad.6
  184.2 5.5 weight_grad.7
  190.0 8.8 %middle_back.1 = (f32[2048,1120]{1,0:T(8,128)}, bf16[2048,1120]{1,0:T(8,128)(2,1)}, bf16[2048,280]{1,0:T(8,128)(2,1)}, bf16[2048,280]{1,0:T(8,128)(2,1)}, f32[8,1120]{1,0:T(8,128)}) custom-call(s32[584]{0:T(1024)} %concatenate.35.meta, bf16[1024,1120]{1,0:T(8,128)(2,1)} %get-tuple-element.203.refs_0_, bf16[1024,1120]{1,0:T(8,128)(2,1)} %get-tuple-element.204.refs_1_, ...), custom_call_target="tpu_custom_call" | custom-call | flops 8099999744 | tf_op jit(solution)/shard_map/middle_back/pallas_call | solution.py:184
  198.9 6.4 %weight_grad.8.own.mine = bf16[1120,1120]{1,0:T(8,128)(2,1)} custom-call(s32[584]{0:T(1024)} %concatenate.35.meta, bf16[2048,1120]{1,0:T(8,128)(2,1)} %get-tuple-element.220.refs_0_, bf16[2048,1120]{1,0:T(8,128)(2,1)} %get-tuple-element.221.refs_1_), custom_call_target="tpu_custom_call" | custom-call | flops 5849999872 | tf_op jit(solution)/shard_map/weight_grad/pallas_call | solution.py:184
  205.3 7.5 %attend_back.2 = (bf16[2048,840]{1,0:T(8,128)(2,1)}, f32[8,280]{1,0:T(8,128)}) custom-call(s32[584]{0:T(1024)} %concatenate.35.meta, bf16[2048,840]{1,0:T(8,128)(2,1)} %project.1.projected, bf16[32,64,320]{2,1,0:T(8,128)(2,1)} %get-tuple-element.224.attend, bf16[2048,280]{1,0:T(8,128)(2,1)} %get-tuple-element.225.context_grad), custom_call_target="tpu_custom_call" | custom-call | flops 13500000256 | tf_op jit(solution)/shard_map/attend_back/pallas_call | solution.py:184
  212.8 28.8 %collective-permute-done.16 = bf16[70,16,1120]{2,1,0:T(8,128)(2,1)S(1)} collective-permute-done((bf16[70,16,1120]{2,1,0:T(8,128)(2,1)}, bf16[70,16,1120]{2,1,0:T(8,128)(2,1)S(1)}, u32[]{:S(2)}, u32[]{:S(2)}) %collective-permute-start.16) | collective-permute-done | bytes 2508832 | tf_op jit(solution)/shard_map/ppermute | solution.py:31
  243.0 5.4 first_sum.3
  250.1 5.5 weight_grad.9.own.mine
  255.6 6.3 %weight_grad.10 = bf16[1120,1120]{1,0:T(8,128)(2,1)} custom-call(s32[584]{0:T(1024)} %concatenate.35.meta, bf16[2048,840]{1,0:T(8,128)(2,1)} %get-tuple-element.232.refs_0_.b, bf16[2048,1120]{1,0:T(8,128)(2,1)} %get-tuple-element.254.normed.refs_1_, bf16[2048,280]{1,0:T(8,128)(2,1)} %get-tuple-element.234.b.refs_2_, ...), custom_call_target="tpu_custom_call" | custom-call | flops 5849999872 | tf_op jit(solution)/shard_map/weight_grad/pallas_call | solution.py:184
  263.5 33.5 %collective-permute-done.17 = bf16[70,16,1120]{2,1,0:T(8,128)(2,1)} collective-permute-done((bf16[70,16,1120]{2,1,0:T(8,128)(2,1)}, bf16[70,16,1120]{2,1,0:T(8,128)(2,1)}, u32[]{:S(2)}, u32[]{:S(2)}) %collective-permute-start.17) | collective-permute-done | bytes 2508832 | tf_op jit(solution)/shard_map/ppermute | solution.py:31
  296.9 5.2 first_sum.4
  305.0 4.3 second_sum.3
  309.2 48.7 %collective-permute-start.20 = (bf16[18,16,1120]{2,1,0:T(8,128)(2,1)}, bf16[18,16,1120]{2,1,0:T(8,128)(2,1)S(1)}, u32[]{:S(2)}, u32[]{:S(2)}) collective-permute-start(bf16[18,16,1120]{2,1,0:T(8,128)(2,1)} %bitcast.159), channel_id=1, source_target_pairs={{0,8},{4,12},{8,0},{12,4},{16,24},{20,28},{24,16},{28,20},{1,9},{5... | collective-permute-start | bytes 1935368 | tf_op jit(solution)/shard_map/ppermute | solution.py:31
  358.0 7.4 %attend_back.3 = (bf16[2048,840]{1,0:T(8,128)(2,1)}, f32[8,280]{1,0:T(8,128)}) custom-call(s32[584]{0:T(1024)} %concatenate.35.meta, bf16[2048,840]{1,0:T(8,128)(2,1)} %get-tuple-element.243.projected, bf16[32,64,320]{2,1,0:T(8,128)(2,1)} %get-tuple-element.244.attend, bf16[2048,280]{1,0:T(8,128)(2,1)} %get-tuple-element.245.context_grad), custom_call_target="tpu_custom_call" | custom-call | flops 13500000256 | tf_op jit(solution)/shard_map/attend_back/pallas_call | solution.py:184
  365.4 6.2 %collective-permute-done.20 = bf16[18,16,1120]{2,1,0:T(8,128)(2,1)S(1)} collective-permute-done((bf16[18,16,1120]{2,1,0:T(8,128)(2,1)}, bf16[18,16,1120]{2,1,0:T(8,128)(2,1)S(1)}, u32[]{:S(2)}, u32[]{:S(2)}) %collective-permute-start.20) | collective-permute-done | bytes 645152 | tf_op jit(solution)/shard_map/ppermute | solution.py:31
  372.4 3.2 third_sum.3
  376.7 4.4 second_sum.4
  381.1 14.1 %collective-permute-start.22 = (bf16[9,16,1120]{2,1,0:T(8,128)(2,1)S(1)}, bf16[9,16,1120]{2,1,0:T(8,128)(2,1)S(1)}, u32[]{:S(2)}, u32[]{:S(2)}) collective-permute-start(bf16[9,16,1120]{2,1,0:T(8,128)(2,1)S(1)} %bitcast.165), channel_id=1, source_target_pairs={{0,16},{4,20},{8,24},{12,28},{16,0},{20,4},{24,8},{28,12},{1,17},{... | collective-permute-start | bytes 967688 | tf_op jit(solution)/shard_map/ppermute | solution.py:31
  395.3 11.8 %collective-permute-start.21 = (bf16[18,16,1120]{2,1,0:T(8,128)(2,1)}, bf16[18,16,1120]{2,1,0:T(8,128)(2,1)S(1)}, u32[]{:S(2)}, u32[]{:S(2)}) collective-permute-start(bf16[18,16,1120]{2,1,0:T(8,128)(2,1)} %bitcast.155), channel_id=1, source_target_pairs={{0,8},{4,12},{8,0},{12,4},{16,24},{20,28},{24,16},{28,20},{1,9},{5... | collective-permute-start | bytes 1935368 | tf_op jit(solution)/shard_map/ppermute | solution.py:31
  407.0 6.6 %weight_grad.11.own.mine = bf16[1120,1120]{1,0:T(8,128)(2,1)} custom-call(s32[584]{0:T(1024)} %concatenate.35.meta, bf16[2048,840]{1,0:T(8,128)(2,1)} %get-tuple-element.263.refs_0_.a, bf16[2048,1120]{1,0:T(8,128)(2,1)} %get-tuple-element.254.normed.refs_1_, bf16[2048,280]{1,0:T(8,128)(2,1)} %get-tuple-element.255.a.refs_2_, ...), custom_call_target="tpu_custom_call" | custom-call | flops 5849999872 | tf_op jit(solution)/shard_map/weight_grad/pallas_call | solution.py:184
  415.1 5.2 first_sum.5
  420.3 4.9 collective-permute-start.27
  425.9 2.7 fourth_sum.3.mine
  428.5 6.7 %collective-permute-start.25 = (bf16[9,16,1120]{2,1,0:T(8,128)(2,1)}, bf16[9,16,1120]{2,1,0:T(8,128)(2,1)S(1)}, u32[]{:S(2)}, u32[]{:S(2)}) collective-permute-start(bf16[9,16,1120]{2,1,0:T(8,128)(2,1)} %bitcast.164), channel_id=1, source_target_pairs={{0,16},{4,20},{8,24},{12,28},{16,0},{20,4},{24,8},{28,12},{1,17},{... | collective-permute-start | bytes 967688 | tf_op jit(solution)/shard_map/ppermute | solution.py:31
  436.1 3.3 third_sum.4
  439.3 6.6 %first_part.1 = (bf16[1024,1120]{1,0:T(8,128)(2,1)}, bf16[1024,1120]{1,0:T(8,128)(2,1)}) custom-call(s32[584]{0:T(1024)} %concatenate.35.meta, bf16[2048,840]{1,0:T(8,128)(2,1)} %get-tuple-element.263.refs_0_.a, bf16[2048,840]{1,0:T(8,128)(2,1)} %get-tuple-element.232.refs_0_.b, bf16[840,1120]{1,0:T(8,128)(2,1)} %bitcast.126, bf16[896,1120]{1,0:T(8,128)(2,1)} %bitcast.123), custom_call_target="tpu_custom_call" | custom-call | flops 6750000128 | tf_op jit(solution)/shard_map/first_part/pallas_call | solution.py:184
  446.5 11.8 %collective-permute-done.25 = bf16[9,16,1120]{2,1,0:T(8,128)(2,1)S(1)} collective-permute-done((bf16[9,16,1120]{2,1,0:T(8,128)(2,1)}, bf16[9,16,1120]{2,1,0:T(8,128)(2,1)S(1)}, u32[]{:S(2)}, u32[]{:S(2)}) %collective-permute-start.25) | collective-permute-done | bytes 322592 | tf_op jit(solution)/shard_map/ppermute | solution.py:31
  459.1 2.7 join.6.mine
  463.2 2.6 fourth_sum.4.mine
  467.6 4.3 second_sum.5
  471.9 3.5 collective-permute-start.28
  477.6 8.1 %start_back.1 = (bf16[64,16,1120]{2,1,0:T(8,128)(2,1)}, f32[8,1120]{1,0:T(8,128)}, f32[32,1120]{1,0:T(8,128)}) custom-call(s32[584]{0:T(1024)} %concatenate.35.meta, bf16[1024,1120]{1,0:T(8,128)(2,1)} %get-tuple-element.271.refs_0_, bf16[1024,1120]{1,0:T(8,128)(2,1)} %get-tuple-element.264.refs_1_, bf16[1024,1120]{1,0:T(8,128)(2,1)} %bitcast.112, ...), custom_call_target="tpu_custom_call" | custom-call | flops 6750000128 | tf_op jit(solution)/shard_map/start_back/pallas_call | solution.py:184
  487.8 3.0 join.7.mine
  490.9 7.7 %collective-permute-done.28 = bf16[18,16,1120]{2,1,0:T(8,128)(2,1)S(1)} collective-permute-done((bf16[18,16,1120]{2,1,0:T(8,128)(2,1)}, bf16[18,16,1120]{2,1,0:T(8,128)(2,1)S(1)}, u32[]{:S(2)}, u32[]{:S(2)}) %collective-permute-start.28) | collective-permute-done | bytes 645152 | tf_op jit(solution)/shard_map/ppermute | solution.py:31
  499.4 3.2 third_sum.5
  503.4 2.8 join.8.mine
  509.8 2.5 vectors.1
  515.5 2.7 collective-permute-start.40
  518.1 10.7 %collective-permute-done.34 = bf16[9,16,1120]{2,1,0:T(8,128)(2,1)S(1)} collective-permute-done((bf16[9,16,1120]{2,1,0:T(8,128)(2,1)S(1)}, bf16[9,16,1120]{2,1,0:T(8,128)(2,1)S(1)}, u32[]{:S(2)}, u32[]{:S(2)}) %collective-permute-start.34) | collective-permute-done | bytes 322592 | tf_op jit(solution)/shard_map/ppermute | solution.py:31
  529.6 2.7 fourth_sum.5.mine
  533.1 3.2 join.9.mine
  536.4 3.4 collective-permute-start.37
  539.8 6.6 %finish.1 = bf16[64,16,1120]{2,1,0:T(8,128)(2,1)} custom-call(s32[584]{0:T(1024)} %concatenate.35.meta, f32[2048,1120]{1,0:T(8,128)} %get-tuple-element.294.refs_4_.middle, bf16[1024,1120]{1,0:T(8,128)(2,1)} %get-tuple-element.201.refs_0_, bf16[1024,1120]{1,0:T(8,128)(2,1)} %get-tuple-element.202.refs_1_, bf16[1024,1120]{1,0:T(8,128)(2,1)} %bitcast.120, ...), custom_call_target="tpu_custom_call" | custom-call | flops 4499999744 | tf_op jit(solution)/shard_map/finish/pallas_call | solution.py:184
  546.4 6.8 %collective-permute-done.37 = bf16[9,16,1120]{2,1,0:T(8,128)(2,1)S(1)} collective-permute-done((bf16[9,16,1120]{2,1,0:T(8,128)(2,1)S(1)}, bf16[9,16,1120]{2,1,0:T(8,128)(2,1)S(1)}, u32[]{:S(2)}, u32[]{:S(2)}) %collective-permute-start.37) | collective-permute-done | bytes 322592 | tf_op jit(solution)/shard_map/ppermute | solution.py:31
  554.0 2.8 join.10.mine
  561.1 5.1 widen_rows.3
  566.2 8.5 %collective-permute-done.39 = bf16[35,16,1120]{2,1,0:T(8,128)(2,1)} collective-permute-done((bf16[35,16,1120]{2,1,0:T(8,128)(2,1)}, bf16[35,16,1120]{2,1,0:T(8,128)(2,1)}, u32[]{:S(2)}, u32[]{:S(2)}) %collective-permute-start.39) | collective-permute-done | bytes 1254432 | tf_op jit(solution)/shard_map/ppermute | solution.py:31
  574.7 5.3 widen_rows.4
  580.0 3.2 join.11.mine
  593.7 4.7 collective-permute-done.43
  601.1 11.1 %collective-permute-done.44 = bf16[35,16,1120]{2,1,0:T(8,128)(2,1)} collective-permute-done((bf16[35,16,1120]{2,1,0:T(8,128)(2,1)}, bf16[35,16,1120]{2,1,0:T(8,128)(2,1)}, u32[]{:S(2)}, u32[]{:S(2)}) %collective-permute-start.44) | collective-permute-done | bytes 1254432 | tf_op jit(solution)/shard_map/ppermute | solution.py:31
  612.1 5.1 widen_rows.5
  (209 shorter events, 91.8 us)
Async XLA Ops:
  7.2 8.3 %copy-start.3 = (bf16[64,16,1120]{2,1,0:T(8,128)(2,1)S(1)}, bf16[64,16,1120]{2,1,0:T(8,128)(2,1)}, u32[]{:S(2)}) copy-start(bf16[64,16,1120]{2,1,0:T(8,128)(2,1)} %param.14) | copy-start | bytes 6881284
  7.2 90.6 %all-gather.3.cloned.1.call-start = ((), (), s32[]{:S(2)}) async-start(), calls=%async_computation | async-start | bytes 2322432 | tf_op jit(solution)/shard_map/all_gather | solution.py:666
  9.1 9.5 %collective-permute-start.2 = (bf16[7,16,1120]{2,1,0:T(8,128)(2,1)}, bf16[7,16,1120]{2,1,0:T(8,128)(2,1)}, u32[]{:S(2)}, u32[]{:S(2)}) collective-permute-start(bf16[7,16,1120]{2,1,0:T(8,128)(2,1)} %bitcast.11), channel_id=1, source_target_pairs={{0,2},{1,3},{2,0},{3,1},{4,6},{5,7},{6,4},{7,5},{8,10},{9,11},{10,... | collective-permute-start | bytes 752648 | tf_op jit(solution)/shard_map/ppermute | solution.py:31
  15.4 2.6 copy-start.4
  18.2 52.4 %copy-start.9 = (bf16[32,16,1120]{2,1,0:T(8,128)(2,1)}, bf16[32,16,1120]{2,1,0:T(8,128)(2,1)S(1)}, u32[]{:S(2)}) copy-start(bf16[32,16,1120]{2,1,0:T(8,128)(2,1)S(1)} %get-tuple-element.176.refs_7_) | copy-start | bytes 3440644
  18.6 133.2 %all-gather.5.cloned.1.call-start = ((), (), s32[]{:S(2)}) async-start(), calls=%async_computation.1 | async-start | bytes 2985984 | tf_op jit(solution)/shard_map/all_gather | solution.py:666
  18.6 13.5 %collective-permute-start = (bf16[32,16,1120]{2,1,0:T(8,128)(2,1)S(1)}, bf16[32,16,1120]{2,1,0:T(8,128)(2,1)}, u32[]{:S(2)}, u32[]{:S(2)}) collective-permute-start(bf16[32,16,1120]{2,1,0:T(8,128)(2,1)S(1)} %get-tuple-element.330.a0), channel_id=1, source_target_pairs={{0,1},{1,0},{2,3},{3,2},{4,5},{5,4},{6,7},{7,6},{8,9},{9,8},{10,11... | collective-permute-start | bytes 3440648 | tf_op jit(solution)/shard_map/ppermute | solution.py:31
  18.7 29.1 %collective-permute-start.1 = (bf16[32,16,1120]{2,1,0:T(8,128)(2,1)}, bf16[32,16,1120]{2,1,0:T(8,128)(2,1)}, u32[]{:S(2)}, u32[]{:S(2)}) collective-permute-start(bf16[32,16,1120]{2,1,0:T(8,128)(2,1)} %get-tuple-element.329), channel_id=1, source_target_pairs={{0,2},{1,3},{2,0},{3,1},{4,6},{5,7},{6,4},{7,5},{8,10},{9,11},{10,... | collective-permute-start | bytes 3440648 | tf_op jit(solution)/shard_map/ppermute | solution.py:31
  20.5 48.2 %collective-permute-start.5 = (bf16[18,16,1120]{2,1,0:T(8,128)(2,1)}, bf16[18,16,1120]{2,1,0:T(8,128)(2,1)}, u32[]{:S(2)}, u32[]{:S(2)}) collective-permute-start(bf16[18,16,1120]{2,1,0:T(8,128)(2,1)} %bitcast.127), channel_id=1, source_target_pairs={{0,2},{1,3},{2,0},{3,1},{4,6},{5,7},{6,4},{7,5},{8,10},{9,11},{10,... | collective-permute-start | bytes 1935368 | tf_op jit(solution)/shard_map/ppermute | solution.py:31
  20.8 47.9 %collective-permute-start.4 = (bf16[9,16,1120]{2,1,0:T(8,128)(2,1)}, bf16[9,16,1120]{2,1,0:T(8,128)(2,1)}, u32[]{:S(2)}, u32[]{:S(2)}) collective-permute-start(bf16[9,16,1120]{2,1,0:T(8,128)(2,1)} %bitcast.128), channel_id=1, source_target_pairs={{0,2},{1,3},{2,0},{3,1},{4,6},{5,7},{6,4},{7,5},{8,10},{9,11},{10,... | collective-permute-start | bytes 967688 | tf_op jit(solution)/shard_map/ppermute | solution.py:31
  27.4 3.4 copy-start.16
  47.9 8.2 %collective-permute-start.3 = (bf16[32,16,1120]{2,1,0:T(8,128)(2,1)}, bf16[32,16,1120]{2,1,0:T(8,128)(2,1)}, u32[]{:S(2)}, u32[]{:S(2)}) collective-permute-start(bf16[32,16,1120]{2,1,0:T(8,128)(2,1)} %collective-permute-done.1.a1), channel_id=1, source_target_pairs={{0,1},{1,0},{2,3},{3,2},{4,5},{5,4},{6,7},{7,6},{8,9},{9,8},{10,11... | collective-permute-start | bytes 3440648 | tf_op jit(solution)/shard_map/ppermute | solution.py:31
  68.8 29.1 %collective-permute-start.7 = (bf16[32,16,1120]{2,1,0:T(8,128)(2,1)S(1)}, bf16[32,16,1120]{2,1,0:T(8,128)(2,1)}, u32[]{:S(2)}, u32[]{:S(2)}) collective-permute-start(bf16[32,16,1120]{2,1,0:T(8,128)(2,1)S(1)} %get-tuple-element.177), channel_id=1, source_target_pairs={{0,2},{1,3},{2,0},{3,1},{4,6},{5,7},{6,4},{7,5},{8,10},{9,11},{10,... | collective-permute-start | bytes 3440648 | tf_op jit(solution)/shard_map/ppermute | solution.py:31
  70.6 27.2 %collective-permute-start.6 = (bf16[32,16,1120]{2,1,0:T(8,128)(2,1)S(1)}, bf16[32,16,1120]{2,1,0:T(8,128)(2,1)}, u32[]{:S(2)}, u32[]{:S(2)}) collective-permute-start(bf16[32,16,1120]{2,1,0:T(8,128)(2,1)S(1)} %get-tuple-element.176.refs_7_), channel_id=1, source_target_pairs={{0,1},{1,0},{2,3},{3,2},{4,5},{5,4},{6,7},{7,6},{8,9},{9,8},{10,11... | collective-permute-start | bytes 3440648 | tf_op jit(solution)/shard_map/ppermute | solution.py:31
  73.5 78.3 %collective-permute-start.9 = (bf16[70,16,1120]{2,1,0:T(8,128)(2,1)}, bf16[70,16,1120]{2,1,0:T(8,128)(2,1)}, u32[]{:S(2)}, u32[]{:S(2)}) collective-permute-start(bf16[70,16,1120]{2,1,0:T(8,128)(2,1)} %bitcast.130), channel_id=1, source_target_pairs={{0,2},{1,3},{2,0},{3,1},{4,6},{5,7},{6,4},{7,5},{8,10},{9,11},{10,... | collective-permute-start | bytes 7526408 | tf_op jit(solution)/shard_map/ppermute | solution.py:31
  110.1 4.7 copy-start.14
  110.1 5.3 copy-start.13
  114.2 37.6 %collective-permute-start.10 = (bf16[64,16,1120]{2,1,0:T(8,128)(2,1)}, bf16[64,16,1120]{2,1,0:T(8,128)(2,1)S(1)}, u32[]{:S(2)}, u32[]{:S(2)}) collective-permute-start(bf16[64,16,1120]{2,1,0:T(8,128)(2,1)} %bitcast.140), channel_id=1, source_target_pairs={{0,1},{1,0},{2,3},{3,2},{4,5},{5,4},{6,7},{7,6},{8,9},{9,8},{10,11... | collective-permute-start | bytes 6881288 | tf_op jit(solution)/shard_map/ppermute | solution.py:31
  114.2 37.5 %collective-permute-start.11 = (bf16[64,16,1120]{2,1,0:T(8,128)(2,1)}, bf16[64,16,1120]{2,1,0:T(8,128)(2,1)}, u32[]{:S(2)}, u32[]{:S(2)}) collective-permute-start(bf16[64,16,1120]{2,1,0:T(8,128)(2,1)} %bitcast.141), channel_id=1, source_target_pairs={{0,1},{1,0},{2,3},{3,2},{4,5},{5,4},{6,7},{7,6},{8,9},{9,8},{10,11... | collective-permute-start | bytes 6881288 | tf_op jit(solution)/shard_map/ppermute | solution.py:31
  114.7 9.3 %collective-permute-start.8 = (bf16[32,16,1120]{2,1,0:T(8,128)(2,1)}, bf16[32,16,1120]{2,1,0:T(8,128)(2,1)S(1)}, u32[]{:S(2)}, u32[]{:S(2)}) collective-permute-start(bf16[32,16,1120]{2,1,0:T(8,128)(2,1)} %collective-permute-done.7.refs_8_), channel_id=1, source_target_pairs={{0,1},{1,0},{2,3},{3,2},{4,5},{5,4},{6,7},{7,6},{8,9},{9,8},{10,11... | collective-permute-start | bytes 3440648 | tf_op jit(solution)/shard_map/ppermute | solution.py:31
  124.0 27.8 %copy-start.23 = (bf16[32,16,1120]{2,1,0:T(8,128)(2,1)}, bf16[32,16,1120]{2,1,0:T(8,128)(2,1)S(1)}, u32[]{:S(2)}) copy-start(bf16[32,16,1120]{2,1,0:T(8,128)(2,1)S(1)} %collective-permute-done.8.refs_10_) | copy-start | bytes 3440644
  175.5 14.2 %collective-permute-start.14 = (bf16[64,16,1120]{2,1,0:T(8,128)(2,1)}, bf16[64,16,1120]{2,1,0:T(8,128)(2,1)}, u32[]{:S(2)}, u32[]{:S(2)}) collective-permute-start(bf16[64,16,1120]{2,1,0:T(8,128)(2,1)} %bitcast.138), channel_id=1, source_target_pairs={{0,1},{1,0},{2,3},{3,2},{4,5},{5,4},{6,7},{7,6},{8,9},{9,8},{10,11... | collective-permute-start | bytes 6881288 | tf_op jit(solution)/shard_map/ppermute | solution.py:31
  175.6 14.4 %collective-permute-start.15 = (bf16[64,16,1120]{2,1,0:T(8,128)(2,1)}, bf16[64,16,1120]{2,1,0:T(8,128)(2,1)}, u32[]{:S(2)}, u32[]{:S(2)}) collective-permute-start(bf16[64,16,1120]{2,1,0:T(8,128)(2,1)} %bitcast.139), channel_id=1, source_target_pairs={{0,1},{1,0},{2,3},{3,2},{4,5},{5,4},{6,7},{7,6},{8,9},{9,8},{10,11... | collective-permute-start | bytes 6881288 | tf_op jit(solution)/shard_map/ppermute | solution.py:31
  176.1 22.8 %collective-permute-start.12 = (bf16[64,16,1120]{2,1,0:T(8,128)(2,1)}, bf16[64,16,1120]{2,1,0:T(8,128)(2,1)S(1)}, u32[]{:S(2)}, u32[]{:S(2)}) collective-permute-start(bf16[64,16,1120]{2,1,0:T(8,128)(2,1)} %bitcast.118), channel_id=1, source_target_pairs={{0,1},{1,0},{2,3},{3,2},{4,5},{5,4},{6,7},{7,6},{8,9},{9,8},{10,11... | collective-permute-start | bytes 6881288 | tf_op jit(solution)/shard_map/ppermute | solution.py:31
  176.2 22.7 %collective-permute-start.13 = (bf16[64,16,1120]{2,1,0:T(8,128)(2,1)}, bf16[64,16,1120]{2,1,0:T(8,128)(2,1)S(1)}, u32[]{:S(2)}, u32[]{:S(2)}) collective-permute-start(bf16[64,16,1120]{2,1,0:T(8,128)(2,1)} %bitcast.119), channel_id=1, source_target_pairs={{0,1},{1,0},{2,3},{3,2},{4,5},{5,4},{6,7},{7,6},{8,9},{9,8},{10,11... | collective-permute-start | bytes 6881288 | tf_op jit(solution)/shard_map/ppermute | solution.py:31
  182.5 59.1 %collective-permute-start.16 = (bf16[70,16,1120]{2,1,0:T(8,128)(2,1)}, bf16[70,16,1120]{2,1,0:T(8,128)(2,1)S(1)}, u32[]{:S(2)}, u32[]{:S(2)}) collective-permute-start(bf16[70,16,1120]{2,1,0:T(8,128)(2,1)} %bitcast.137), channel_id=1, source_target_pairs={{0,2},{1,3},{2,0},{3,1},{4,6},{5,7},{6,4},{7,5},{8,10},{9,11},{10,... | collective-permute-start | bytes 7526408 | tf_op jit(solution)/shard_map/ppermute | solution.py:31
  189.7 107.2 %collective-permute-start.17 = (bf16[70,16,1120]{2,1,0:T(8,128)(2,1)}, bf16[70,16,1120]{2,1,0:T(8,128)(2,1)}, u32[]{:S(2)}, u32[]{:S(2)}) collective-permute-start(bf16[70,16,1120]{2,1,0:T(8,128)(2,1)} %bitcast.136), channel_id=1, source_target_pairs={{0,2},{1,3},{2,0},{3,1},{4,6},{5,7},{6,4},{7,5},{8,10},{9,11},{10,... | collective-permute-start | bytes 7526408 | tf_op jit(solution)/shard_map/ppermute | solution.py:31
  198.9 6.4 %copy-start.7 = (bf16[64,16,1120]{2,1,0:T(8,128)(2,1)}, bf16[64,16,1120]{2,1,0:T(8,128)(2,1)S(1)}, u32[]{:S(2)}) copy-start(bf16[64,16,1120]{2,1,0:T(8,128)(2,1)S(1)} %collective-permute-done.12) | copy-start | bytes 6881284
  198.9 6.4 %copy-start.8 = (bf16[64,16,1120]{2,1,0:T(8,128)(2,1)}, bf16[64,16,1120]{2,1,0:T(8,128)(2,1)S(1)}, u32[]{:S(2)}) copy-start(bf16[64,16,1120]{2,1,0:T(8,128)(2,1)S(1)} %collective-permute-done.13) | copy-start | bytes 6881284
  248.4 55.5 %collective-permute-start.19 = (bf16[35,16,1120]{2,1,0:T(8,128)(2,1)}, bf16[35,16,1120]{2,1,0:T(8,128)(2,1)S(1)}, u32[]{:S(2)}, u32[]{:S(2)}) collective-permute-start(bf16[35,16,1120]{2,1,0:T(8,128)(2,1)} %bitcast.149), channel_id=1, source_target_pairs={{0,4},{4,0},{8,12},{12,8},{16,20},{20,16},{24,28},{28,24},{1,5},{5... | collective-permute-start | bytes 3763208 | tf_op jit(solution)/shard_map/ppermute | solution.py:31
  262.0 151.6 %collective-permute-start.23 = (bf16[70,16,1120]{2,1,0:T(8,128)(2,1)}, bf16[70,16,1120]{2,1,0:T(8,128)(2,1)S(1)}, u32[]{:S(2)}, u32[]{:S(2)}) collective-permute-start(bf16[70,16,1120]{2,1,0:T(8,128)(2,1)} %bitcast.135), channel_id=1, source_target_pairs={{0,2},{1,3},{2,0},{3,1},{4,6},{5,7},{6,4},{7,5},{8,10},{9,11},{10,... | collective-permute-start | bytes 7526408 | tf_op jit(solution)/shard_map/ppermute | solution.py:31
  302.1 73.6 %collective-permute-start.18 = (bf16[35,16,1120]{2,1,0:T(8,128)(2,1)}, bf16[35,16,1120]{2,1,0:T(8,128)(2,1)S(1)}, u32[]{:S(2)}, u32[]{:S(2)}) collective-permute-start(bf16[35,16,1120]{2,1,0:T(8,128)(2,1)} %bitcast.147), channel_id=1, source_target_pairs={{0,4},{4,0},{8,12},{12,8},{16,20},{20,16},{24,28},{28,24},{1,5},{5... | collective-permute-start | bytes 3763208 | tf_op jit(solution)/shard_map/ppermute | solution.py:31
  309.2 62.4 %collective-permute-start.20 = (bf16[18,16,1120]{2,1,0:T(8,128)(2,1)}, bf16[18,16,1120]{2,1,0:T(8,128)(2,1)S(1)}, u32[]{:S(2)}, u32[]{:S(2)}) collective-permute-start(bf16[18,16,1120]{2,1,0:T(8,128)(2,1)} %bitcast.159), channel_id=1, source_target_pairs={{0,8},{4,12},{8,0},{12,4},{16,24},{20,28},{24,16},{28,20},{1,9},{5... | collective-permute-start | bytes 1935368 | tf_op jit(solution)/shard_map/ppermute | solution.py:31
  376.7 4.4 copy-start.31
  381.1 44.0 %collective-permute-start.22 = (bf16[9,16,1120]{2,1,0:T(8,128)(2,1)S(1)}, bf16[9,16,1120]{2,1,0:T(8,128)(2,1)S(1)}, u32[]{:S(2)}, u32[]{:S(2)}) collective-permute-start(bf16[9,16,1120]{2,1,0:T(8,128)(2,1)S(1)} %bitcast.165), channel_id=1, source_target_pairs={{0,16},{4,20},{8,24},{12,28},{16,0},{20,4},{24,8},{28,12},{1,17},{... | collective-permute-start | bytes 967688 | tf_op jit(solution)/shard_map/ppermute | solution.py:31
  395.3 40.0 %collective-permute-start.21 = (bf16[18,16,1120]{2,1,0:T(8,128)(2,1)}, bf16[18,16,1120]{2,1,0:T(8,128)(2,1)S(1)}, u32[]{:S(2)}, u32[]{:S(2)}) collective-permute-start(bf16[18,16,1120]{2,1,0:T(8,128)(2,1)} %bitcast.155), channel_id=1, source_target_pairs={{0,8},{4,12},{8,0},{12,4},{16,24},{20,28},{24,16},{28,20},{1,9},{5... | collective-permute-start | bytes 1935368 | tf_op jit(solution)/shard_map/ppermute | solution.py:31
  420.3 46.3 %collective-permute-start.27 = (bf16[35,16,1120]{2,1,0:T(8,128)(2,1)}, bf16[35,16,1120]{2,1,0:T(8,128)(2,1)S(1)}, u32[]{:S(2)}, u32[]{:S(2)}) collective-permute-start(bf16[35,16,1120]{2,1,0:T(8,128)(2,1)} %bitcast.144), channel_id=1, source_target_pairs={{0,4},{4,0},{8,12},{12,8},{16,20},{20,16},{24,28},{28,24},{1,5},{5... | collective-permute-start | bytes 3763208 | tf_op jit(solution)/shard_map/ppermute | solution.py:31
  428.5 29.8 %collective-permute-start.25 = (bf16[9,16,1120]{2,1,0:T(8,128)(2,1)}, bf16[9,16,1120]{2,1,0:T(8,128)(2,1)S(1)}, u32[]{:S(2)}, u32[]{:S(2)}) collective-permute-start(bf16[9,16,1120]{2,1,0:T(8,128)(2,1)} %bitcast.164), channel_id=1, source_target_pairs={{0,16},{4,20},{8,24},{12,28},{16,0},{20,4},{24,8},{28,12},{1,17},{... | collective-permute-start | bytes 967688 | tf_op jit(solution)/shard_map/ppermute | solution.py:31
  439.3 23.2 %collective-permute-start.24 = (bf16[9,16,1120]{2,1,0:T(8,128)(2,1)}, bf16[9,16,1120]{2,1,0:T(8,128)(2,1)S(1)}, u32[]{:S(2)}, u32[]{:S(2)}) collective-permute-start(bf16[9,16,1120]{2,1,0:T(8,128)(2,1)} %bitcast.168), channel_id=1, source_target_pairs={{0,16},{4,20},{8,24},{12,28},{16,0},{20,4},{24,8},{28,12},{1,17},{... | collective-permute-start | bytes 967688 | tf_op jit(solution)/shard_map/ppermute | solution.py:31
  446.0 29.4 %collective-permute-start.30 = (bf16[64,16,1120]{2,1,0:T(8,128)(2,1)}, bf16[64,16,1120]{2,1,0:T(8,128)(2,1)S(1)}, u32[]{:S(2)}, u32[]{:S(2)}) collective-permute-start(bf16[64,16,1120]{2,1,0:T(8,128)(2,1)} %bitcast.110), channel_id=1, source_target_pairs={{0,1},{1,0},{2,3},{3,2},{4,5},{5,4},{6,7},{7,6},{8,9},{9,8},{10,11... | collective-permute-start | bytes 6881288 | tf_op jit(solution)/shard_map/ppermute | solution.py:31
  446.1 29.4 %collective-permute-start.31 = (bf16[64,16,1120]{2,1,0:T(8,128)(2,1)}, bf16[64,16,1120]{2,1,0:T(8,128)(2,1)S(1)}, u32[]{:S(2)}, u32[]{:S(2)}) collective-permute-start(bf16[64,16,1120]{2,1,0:T(8,128)(2,1)} %bitcast.111), channel_id=1, source_target_pairs={{0,1},{1,0},{2,3},{3,2},{4,5},{5,4},{6,7},{7,6},{8,9},{9,8},{10,11... | collective-permute-start | bytes 6881288 | tf_op jit(solution)/shard_map/ppermute | solution.py:31
  461.7 25.2 %collective-permute-start.29 = (bf16[18,16,1120]{2,1,0:T(8,128)(2,1)}, bf16[18,16,1120]{2,1,0:T(8,128)(2,1)S(1)}, u32[]{:S(2)}, u32[]{:S(2)}) collective-permute-start(bf16[18,16,1120]{2,1,0:T(8,128)(2,1)} %bitcast.150), channel_id=1, source_target_pairs={{0,8},{4,12},{8,0},{12,4},{16,24},{20,28},{24,16},{28,20},{1,9},{5... | collective-permute-start | bytes 1935368 | tf_op jit(solution)/shard_map/ppermute | solution.py:31
  465.9 36.7 %collective-permute-start.26 = (bf16[9,16,1120]{2,1,0:T(8,128)(2,1)}, bf16[9,16,1120]{2,1,0:T(8,128)(2,1)S(1)}, u32[]{:S(2)}, u32[]{:S(2)}) collective-permute-start(bf16[9,16,1120]{2,1,0:T(8,128)(2,1)} %bitcast.161), channel_id=1, source_target_pairs={{0,16},{4,20},{8,24},{12,28},{16,0},{20,4},{24,8},{28,12},{1,17},{... | collective-permute-start | bytes 967688 | tf_op jit(solution)/shard_map/ppermute | solution.py:31
  471.9 26.7 %collective-permute-start.28 = (bf16[18,16,1120]{2,1,0:T(8,128)(2,1)}, bf16[18,16,1120]{2,1,0:T(8,128)(2,1)S(1)}, u32[]{:S(2)}, u32[]{:S(2)}) collective-permute-start(bf16[18,16,1120]{2,1,0:T(8,128)(2,1)} %bitcast.157), channel_id=1, source_target_pairs={{0,8},{4,12},{8,0},{12,4},{16,24},{20,28},{24,16},{28,20},{1,9},{5... | collective-permute-start | bytes 1935368 | tf_op jit(solution)/shard_map/ppermute | solution.py:31
  475.4 2.2 copy-start.2
  503.4 4.6 copy-start.30
  506.1 6.8 %copy-start.5 = (bf16[64,16,1120]{2,1,0:T(8,128)(2,1)S(1)}, bf16[64,16,1120]{2,1,0:T(8,128)(2,1)}, u32[]{:S(2)}) copy-start(bf16[64,16,1120]{2,1,0:T(8,128)(2,1)} %get-tuple-element.275) | copy-start | bytes 6881284
  506.1 26.1 %collective-permute-start.32 = (bf16[18,16,1120]{2,1,0:T(8,128)(2,1)}, bf16[18,16,1120]{2,1,0:T(8,128)(2,1)S(1)}, u32[]{:S(2)}, u32[]{:S(2)}) collective-permute-start(bf16[18,16,1120]{2,1,0:T(8,128)(2,1)} %bitcast.151), channel_id=1, source_target_pairs={{0,8},{4,12},{8,0},{12,4},{16,24},{20,28},{24,16},{28,20},{1,9},{5... | collective-permute-start | bytes 1935368 | tf_op jit(solution)/shard_map/ppermute | solution.py:31
  507.9 20.9 %collective-permute-start.34 = (bf16[9,16,1120]{2,1,0:T(8,128)(2,1)S(1)}, bf16[9,16,1120]{2,1,0:T(8,128)(2,1)S(1)}, u32[]{:S(2)}, u32[]{:S(2)}) collective-permute-start(bf16[9,16,1120]{2,1,0:T(8,128)(2,1)S(1)} %bitcast.163), channel_id=1, source_target_pairs={{0,16},{4,20},{8,24},{12,28},{16,0},{20,4},{24,8},{28,12},{1,17},{... | collective-permute-start | bytes 967688 | tf_op jit(solution)/shard_map/ppermute | solution.py:31
  512.3 19.9 %collective-permute-start.33 = (f32[40,1120]{1,0:T(8,128)}, f32[40,1120]{1,0:T(8,128)S(1)}, u32[]{:S(2)}, u32[]{:S(2)}) collective-permute-start(f32[40,1120]{1,0:T(8,128)} %get-tuple-element.288), channel_id=1, source_target_pairs={{0,2},{1,3},{2,0},{3,1},{4,6},{5,7},{6,4},{7,5},{8,10},{9,11},{10,... | collective-permute-start | bytes 537608 | tf_op jit(solution)/shard_map/ppermute | solution.py:31
  514.0 47.1 %collective-permute-start.41 = (bf16[32,16,1120]{2,1,0:T(8,128)(2,1)}, bf16[32,16,1120]{2,1,0:T(8,128)(2,1)S(1)}, u32[]{:S(2)}, u32[]{:S(2)}) collective-permute-start(bf16[32,16,1120]{2,1,0:T(8,128)(2,1)} %slice.96), channel_id=1, source_target_pairs={{0,2},{1,3},{2,0},{3,1},{4,6},{5,7},{6,4},{7,5},{8,10},{9,11},{10,... | collective-permute-start | bytes 3440648 | tf_op jit(solution)/shard_map/ppermute | solution.py:31
  515.5 45.7 %collective-permute-start.40 = (bf16[35,16,1120]{2,1,0:T(8,128)(2,1)}, bf16[35,16,1120]{2,1,0:T(8,128)(2,1)}, u32[]{:S(2)}, u32[]{:S(2)}) collective-permute-start(bf16[35,16,1120]{2,1,0:T(8,128)(2,1)} %bitcast.81), channel_id=1, source_target_pairs={{0,4},{4,0},{8,12},{12,8},{16,20},{20,16},{24,28},{28,24},{1,5},{5... | collective-permute-start | bytes 3763208 | tf_op jit(solution)/shard_map/ppermute | solution.py:31
  532.2 4.1 copy-start.12
  533.1 3.3 copy-start.35
  536.3 38.4 %collective-permute-start.39 = (bf16[35,16,1120]{2,1,0:T(8,128)(2,1)}, bf16[35,16,1120]{2,1,0:T(8,128)(2,1)}, u32[]{:S(2)}, u32[]{:S(2)}) collective-permute-start(bf16[35,16,1120]{2,1,0:T(8,128)(2,1)} %bitcast.145), channel_id=1, source_target_pairs={{0,4},{4,0},{8,12},{12,8},{16,20},{20,16},{24,28},{28,24},{1,5},{5... | collective-permute-start | bytes 3763208 | tf_op jit(solution)/shard_map/ppermute | solution.py:31
  536.4 16.8 %collective-permute-start.37 = (bf16[9,16,1120]{2,1,0:T(8,128)(2,1)S(1)}, bf16[9,16,1120]{2,1,0:T(8,128)(2,1)S(1)}, u32[]{:S(2)}, u32[]{:S(2)}) collective-permute-start(bf16[9,16,1120]{2,1,0:T(8,128)(2,1)S(1)} %bitcast.170), channel_id=1, source_target_pairs={{0,16},{4,20},{8,24},{12,28},{16,0},{20,4},{24,8},{28,12},{1,17},{... | collective-permute-start | bytes 967688 | tf_op jit(solution)/shard_map/ppermute | solution.py:31
  554.0 6.1 copy-start
  556.7 23.3 %collective-permute-start.38 = (bf16[18,16,1120]{2,1,0:T(8,128)(2,1)}, bf16[18,16,1120]{2,1,0:T(8,128)(2,1)}, u32[]{:S(2)}, u32[]{:S(2)}) collective-permute-start(bf16[18,16,1120]{2,1,0:T(8,128)(2,1)} %bitcast.154), channel_id=1, source_target_pairs={{0,8},{4,12},{8,0},{12,4},{16,24},{20,28},{24,16},{28,20},{1,9},{5... | collective-permute-start | bytes 1935368 | tf_op jit(solution)/shard_map/ppermute | solution.py:31
  558.5 24.7 %collective-permute-start.36 = (f32[40,1120]{1,0:T(8,128)S(1)}, f32[40,1120]{1,0:T(8,128)S(1)}, u32[]{:S(2)}, u32[]{:S(2)}) collective-permute-start(f32[40,1120]{1,0:T(8,128)S(1)} %add.107), channel_id=1, source_target_pairs={{0,4},{4,0},{8,12},{12,8},{16,20},{20,16},{24,28},{28,24},{1,5},{5... | collective-permute-start | bytes 537608 | tf_op jit(solution)/shard_map/ppermute | solution.py:31
  561.1 29.2 %collective-permute-start.35 = (bf16[32,16,1120]{2,1,0:T(8,128)(2,1)}, bf16[32,16,1120]{2,1,0:T(8,128)(2,1)}, u32[]{:S(2)}, u32[]{:S(2)}) collective-permute-start(bf16[32,16,1120]{2,1,0:T(8,128)(2,1)} %slice.114), channel_id=1, source_target_pairs={{0,2},{1,3},{2,0},{3,1},{4,6},{5,7},{6,4},{7,5},{8,10},{9,11},{10,... | collective-permute-start | bytes 3440648 | tf_op jit(solution)/shard_map/ppermute | solution.py:31
  580.0 3.9 copy-start.6
  583.2 7.0 %collective-permute-start.42 = (f32[40,1120]{1,0:T(8,128)S(1)}, f32[40,1120]{1,0:T(8,128)S(1)}, u32[]{:S(2)}, u32[]{:S(2)}) collective-permute-start(f32[40,1120]{1,0:T(8,128)S(1)} %add.108), channel_id=1, source_target_pairs={{0,8},{4,12},{8,0},{12,4},{16,24},{20,28},{24,16},{28,20},{1,9},{5... | collective-permute-start | bytes 537608 | tf_op jit(solution)/shard_map/ppermute | solution.py:31
  586.0 26.1 %collective-permute-start.44 = (bf16[35,16,1120]{2,1,0:T(8,128)(2,1)}, bf16[35,16,1120]{2,1,0:T(8,128)(2,1)}, u32[]{:S(2)}, u32[]{:S(2)}) collective-permute-start(bf16[35,16,1120]{2,1,0:T(8,128)(2,1)} %bitcast.89), channel_id=1, source_target_pairs={{0,4},{4,0},{8,12},{12,8},{16,20},{20,16},{24,28},{28,24},{1,5},{5... | collective-permute-start | bytes 3763208 | tf_op jit(solution)/shard_map/ppermute | solution.py:31
  590.3 8.2 %collective-permute-start.43 = (f32[40,1120]{1,0:T(8,128)S(1)}, f32[40,1120]{1,0:T(8,128)S(1)}, u32[]{:S(2)}, u32[]{:S(2)}) collective-permute-start(f32[40,1120]{1,0:T(8,128)S(1)} %add.109), channel_id=1, source_target_pairs={{0,16},{4,20},{8,24},{12,28},{16,0},{20,4},{24,8},{28,12},{1,17},{... | collective-permute-start | bytes 537608 | tf_op jit(solution)/shard_map/ppermute | solution.py:31
  (22 other events, 21.8 us)
Sparse Core Ops, SparseCore 0:
  18.7 50.6 all-gather.2
  71.5 55.8 all-gather.4

commit v5 on v4

--- a/solution.py
+++ b/solution.py
@@ -13,7 +13,7 @@
 BLOCK = 256
 META_BLOCKS = 8
 TILE = 16
-UNROLL = 4
+UNROLL = 6
 F32 = jnp.float32
 LOW = jnp.bfloat16
 VMEM_BYTES = 56 * 1024 * 1024

time: 626 us -> 619 us (0.989); the launches traced: 624 us -> 608 us
  Pallas kernels: 216 us -> 319 us
  waiting for transfers between devices: 208 us -> 140 us
  starting transfers between devices: 125 us -> 72.8 us
    pallas_call x40, Pallas kernels: 216 us -> 319 us  [call(): pl.pallas_call(kernel, grid_spec=pltpu.PrefetchScalarGridSpec(num_scalar_...]
    ppermute x45, waiting for transfers between devices: 207 us -> 140 us  [swap(): return lax.ppermute(value, axis, [(i, i ^ bit) for i in range(count)])]
    ppermute x45, starting transfers between devices: 125 us -> 72.7 us  [swap(): return lax.ppermute(value, axis, [(i, i ^ bit) for i in range(count)])]
  transfers between devices with their start and end apart: 47 -> 47, of which waited for: 19 -> 17; matrix products, arithmetic and copies ran while one was open for 6% -> 6% of each run, Pallas kernels for 30% -> 43%
where the time goes in v5:
time: 619 us; the launch traced here: 608 us
  Pallas kernels  319 us (52%)
  waiting for transfers between devices  140 us (23%)
  starting transfers between devices  72.8 us (12%)
  local copies, waits for them, and re-layouts  47.4 us (8%)
  between operations  15.5 us (3%)
  other arithmetic  12.8 us (2%)
    pallas_call x40, Pallas kernels, call(): pl.pallas_call(kernel, grid_spec=pltpu.PrefetchScalarGridSpec(num_scalar_...  319 us
    ppermute x45, waiting for transfers between devices, swap(): return lax.ppermute(value, axis, [(i, i ^ bit) for i in range(count)])  140 us
    ppermute x45, starting transfers between devices, swap(): return lax.ppermute(value, axis, [(i, i ^ bit) for i in range(count)])  72.7 us
    unnamed x78, local copies, waits for them, and re-layouts  19.2 us
  transfers between devices with their start and end apart: 47, of which 17 were waited for; matrix products, arithmetic and copies ran while one was open for 6% of the time, Pallas kernels for 43%

profile of v5, /device:TPU:0, one launch (start us, length us, event | category | flops | bytes accessed | tf_op | source)
XLA Modules:
  0.0 608.0 jit_solution(12714914608193273191)
XLA Ops:
  9.1 2.9 collective-permute-start.2
  32.2 15.7 %collective-permute-done.1.a1 = bf16[32,16,1120]{2,1,0:T(8,128)(2,1)} collective-permute-done((bf16[32,16,1120]{2,1,0:T(8,128)(2,1)}, bf16[32,16,1120]{2,1,0:T(8,128)(2,1)}, u32[]{:S(2)}, u32[]{:S(2)}) %collective-permute-start.1) | collective-permute-done | bytes 1146912 | tf_op jit(solution)/shard_map/ppermute | solution.py:31
  54.1 1.9 concatenate.35.meta
  56.1 11.8 %begin.1 = (f32[2048,1120]{1,0:T(8,128)}, bf16[2048,1120]{1,0:T(8,128)(2,1)}, bf16[2048,840]{1,0:T(8,128)(2,1)}) custom-call(s32[584]{0:T(1024)} %concatenate.35.meta, bf16[32,16,1120]{2,1,0:T(8,128)(2,1)} %copy-done.10, bf16[32,16,1120]{2,1,0:T(8,128)(2,1)} %collective-permute-done.1.a1, bf16[32,16,1120]{2,1,0:T(8,128)(2,1)} %collective-permute-done.a2, ...), custom_call_target="tpu_custom_call" | custom-call | flops 6750000128 | tf_op jit(solution)/shard_map/begin/pallas_call | solution.py:184
  71.3 2.0 slice.88.weight_b.refs_8_
  74.5 9.5 %attend.2 = (bf16[2048,280]{1,0:T(8,128)(2,1)}, bf16[32,64,320]{2,1,0:T(8,128)(2,1)}) custom-call(s32[584]{0:T(1024)} %concatenate.35.meta, bf16[2048,840]{1,0:T(8,128)(2,1)} %get-tuple-element.243.projected), custom_call_target="tpu_custom_call" | custom-call | flops 1800000000 | tf_op jit(solution)/shard_map/attend/pallas_call | solution.py:184
  83.9 13.9 %collective-permute-done.7.refs_8_ = bf16[32,16,1120]{2,1,0:T(8,128)(2,1)} collective-permute-done((bf16[32,16,1120]{2,1,0:T(8,128)(2,1)S(1)}, bf16[32,16,1120]{2,1,0:T(8,128)(2,1)}, u32[]{:S(2)}, u32[]{:S(2)}) %collective-permute-start.7) | collective-permute-done | bytes 1146912 | tf_op jit(solution)/shard_map/ppermute | solution.py:31
  97.8 8.9 %project.1.projected = bf16[2048,840]{1,0:T(8,128)(2,1)} custom-call(s32[584]{0:T(1024)} %concatenate.35.meta, bf16[2048,1120]{1,0:T(8,128)(2,1)} %get-tuple-element.254.normed.refs_1_, bf16[896,1120]{1,0:T(8,128)(2,1)} %bitcast.122, f32[1,840]{1,0:T(1,128)} %fusion.7.bias), custom_call_target="tpu_custom_call" | custom-call | flops 2700000000 | tf_op jit(solution)/shard_map/project/pallas_call | solution.py:184
  106.7 9.7 %attend.3 = (bf16[2048,280]{1,0:T(8,128)(2,1)}, bf16[32,64,320]{2,1,0:T(8,128)(2,1)}) custom-call(s32[584]{0:T(1024)} %concatenate.35.meta, bf16[2048,840]{1,0:T(8,128)(2,1)} %project.1.projected), custom_call_target="tpu_custom_call" | custom-call | flops 1800000000 | tf_op jit(solution)/shard_map/attend/pallas_call | solution.py:184
  116.5 7.1 %out_project.1 = (bf16[1024,1120]{1,0:T(8,128)(2,1)}, bf16[1024,1120]{1,0:T(8,128)(2,1)}) custom-call(s32[584]{0:T(1024)} %concatenate.35.meta, bf16[2048,280]{1,0:T(8,128)(2,1)} %get-tuple-element.255.a.refs_2_, bf16[2048,280]{1,0:T(8,128)(2,1)} %get-tuple-element.234.b.refs_2_, bf16[280,1120]{1,0:T(8,128)(2,1)} %refs_7_.1, ...), custom_call_target="tpu_custom_call" | custom-call | flops 4499999744 | tf_op jit(solution)/shard_map/out_project/pallas_call | solution.py:184
  126.1 7.3 %collective-permute-done.8.refs_10_ = bf16[32,16,1120]{2,1,0:T(8,128)(2,1)S(1)} collective-permute-done((bf16[32,16,1120]{2,1,0:T(8,128)(2,1)}, bf16[32,16,1120]{2,1,0:T(8,128)(2,1)S(1)}, u32[]{:S(2)}, u32[]{:S(2)}) %collective-permute-start.8) | collective-permute-done | bytes 1146912 | tf_op jit(solution)/shard_map/ppermute | solution.py:31
  133.5 18.4 %collective-permute-done.9 = bf16[70,16,1120]{2,1,0:T(8,128)(2,1)} collective-permute-done((bf16[70,16,1120]{2,1,0:T(8,128)(2,1)}, bf16[70,16,1120]{2,1,0:T(8,128)(2,1)}, u32[]{:S(2)}, u32[]{:S(2)}) %collective-permute-start.9) | collective-permute-done | bytes 2508832 | tf_op jit(solution)/shard_map/ppermute | solution.py:31
  153.3 46.9 %mlp.1 = (f32[2048,1120]{1,0:T(8,128)}, bf16[2048,1120]{1,0:T(8,128)(2,1)}, bf16[2048,1120]{1,0:T(8,128)(2,1)}, bf16[2048,1120]{1,0:T(8,128)(2,1)}, bf16[2048,11...) custom-call(s32[584]{0:T(1024)} %concatenate.35.meta, ...), custom_call_target="tpu_custom_call" | custom-call | flops 29250000896 | tf_op jit(solution)/shard_map/mlp/pallas_call | solution.py:184
  201.3 8.8 %weight_grad.6 = bf16[1120,1120]{1,0:T(8,128)(2,1)} custom-call(s32[584]{0:T(1024)} %concatenate.35.meta, bf16[2048,1120]{1,0:T(8,128)(2,1)} %get-tuple-element.220.refs_0_, bf16[2048,1120]{1,0:T(8,128)(2,1)} %get-tuple-element.210.refs_1_), custom_call_target="tpu_custom_call" | custom-call | flops 5849999872 | tf_op jit(solution)/shard_map/weight_grad/pallas_call | solution.py:184
  211.8 8.4 %weight_grad.7 = bf16[1120,1120]{1,0:T(8,128)(2,1)} custom-call(s32[584]{0:T(1024)} %concatenate.35.meta, bf16[2048,1120]{1,0:T(8,128)(2,1)} %get-tuple-element.211.refs_0_, bf16[2048,1120]{1,0:T(8,128)(2,1)} %get-tuple-element.230.refs_1_.refs_5_), custom_call_target="tpu_custom_call" | custom-call | flops 5849999872 | tf_op jit(solution)/shard_map/weight_grad/pallas_call | solution.py:184
  220.5 14.5 %middle_back.1 = (f32[2048,1120]{1,0:T(8,128)}, bf16[2048,1120]{1,0:T(8,128)(2,1)}, bf16[2048,280]{1,0:T(8,128)(2,1)}, bf16[2048,280]{1,0:T(8,128)(2,1)}, f32[8,1120]{1,0:T(8,128)}) custom-call(s32[584]{0:T(1024)} %concatenate.35.meta, bf16[1024,1120]{1,0:T(8,128)(2,1)} %get-tuple-element.203.refs_0_, bf16[1024,1120]{1,0:T(8,128)(2,1)} %get-tuple-element.204.refs_1_, ...), custom_call_target="tpu_custom_call" | custom-call | flops 8099999744 | tf_op jit(solution)/shard_map/middle_back/pallas_call | solution.py:184
  235.1 9.3 %weight_grad.8.own.mine = bf16[1120,1120]{1,0:T(8,128)(2,1)} custom-call(s32[584]{0:T(1024)} %concatenate.35.meta, bf16[2048,1120]{1,0:T(8,128)(2,1)} %get-tuple-element.220.refs_0_, bf16[2048,1120]{1,0:T(8,128)(2,1)} %get-tuple-element.221.refs_1_), custom_call_target="tpu_custom_call" | custom-call | flops 5849999872 | tf_op jit(solution)/shard_map/weight_grad/pallas_call | solution.py:184
  244.4 20.4 %attend_back.2 = (bf16[2048,840]{1,0:T(8,128)(2,1)}, f32[8,280]{1,0:T(8,128)}) custom-call(s32[584]{0:T(1024)} %concatenate.35.meta, bf16[2048,840]{1,0:T(8,128)(2,1)} %project.1.projected, bf16[32,64,320]{2,1,0:T(8,128)(2,1)} %get-tuple-element.224.attend, bf16[2048,280]{1,0:T(8,128)(2,1)} %get-tuple-element.225.context_grad), custom_call_target="tpu_custom_call" | custom-call | flops 13500000256 | tf_op jit(solution)/shard_map/attend_back/pallas_call | solution.py:184
  264.8 4.3 collective-permute-done.16
  270.6 5.4 first_sum.3
  276.0 8.4 %weight_grad.9.own.mine = bf16[1120,1120]{1,0:T(8,128)(2,1)} custom-call(s32[584]{0:T(1024)} %concatenate.35.meta, bf16[2048,1120]{1,0:T(8,128)(2,1)} %get-tuple-element.229.refs_0_, bf16[2048,1120]{1,0:T(8,128)(2,1)} %get-tuple-element.230.refs_1_.refs_5_), custom_call_target="tpu_custom_call" | custom-call | flops 5849999872 | tf_op jit(solution)/shard_map/weight_grad/pallas_call | solution.py:184
  284.4 10.1 %weight_grad.10 = bf16[1120,1120]{1,0:T(8,128)(2,1)} custom-call(s32[584]{0:T(1024)} %concatenate.35.meta, bf16[2048,840]{1,0:T(8,128)(2,1)} %get-tuple-element.232.refs_0_.b, bf16[2048,1120]{1,0:T(8,128)(2,1)} %get-tuple-element.254.normed.refs_1_, bf16[2048,280]{1,0:T(8,128)(2,1)} %get-tuple-element.234.b.refs_2_, ...), custom_call_target="tpu_custom_call" | custom-call | flops 5849999872 | tf_op jit(solution)/shard_map/weight_grad/pallas_call | solution.py:184
  296.3 28.3 %collective-permute-done.17 = bf16[70,16,1120]{2,1,0:T(8,128)(2,1)} collective-permute-done((bf16[70,16,1120]{2,1,0:T(8,128)(2,1)}, bf16[70,16,1120]{2,1,0:T(8,128)(2,1)}, u32[]{:S(2)}, u32[]{:S(2)}) %collective-permute-start.17) | collective-permute-done | bytes 2508832 | tf_op jit(solution)/shard_map/ppermute | solution.py:31
  324.6 5.2 first_sum.4
  330.8 4.3 second_sum.3
  335.1 14.2 %collective-permute-start.20 = (bf16[18,16,1120]{2,1,0:T(8,128)(2,1)}, bf16[18,16,1120]{2,1,0:T(8,128)(2,1)S(1)}, u32[]{:S(2)}, u32[]{:S(2)}) collective-permute-start(bf16[18,16,1120]{2,1,0:T(8,128)(2,1)} %bitcast.159), channel_id=1, source_target_pairs={{0,8},{4,12},{8,0},{12,4},{16,24},{20,28},{24,16},{28,20},{1,9},{5... | collective-permute-start | bytes 1935368 | tf_op jit(solution)/shard_map/ppermute | solution.py:31
  349.3 20.3 %attend_back.3 = (bf16[2048,840]{1,0:T(8,128)(2,1)}, f32[8,280]{1,0:T(8,128)}) custom-call(s32[584]{0:T(1024)} %concatenate.35.meta, bf16[2048,840]{1,0:T(8,128)(2,1)} %get-tuple-element.243.projected, bf16[32,64,320]{2,1,0:T(8,128)(2,1)} %get-tuple-element.244.attend, bf16[2048,280]{1,0:T(8,128)(2,1)} %get-tuple-element.245.context_grad), custom_call_target="tpu_custom_call" | custom-call | flops 13500000256 | tf_op jit(solution)/shard_map/attend_back/pallas_call | solution.py:184
  370.4 3.2 third_sum.3
  374.7 4.4 second_sum.4
  379.1 19.4 %collective-permute-start.22 = (bf16[9,16,1120]{2,1,0:T(8,128)(2,1)S(1)}, bf16[9,16,1120]{2,1,0:T(8,128)(2,1)S(1)}, u32[]{:S(2)}, u32[]{:S(2)}) collective-permute-start(bf16[9,16,1120]{2,1,0:T(8,128)(2,1)S(1)} %bitcast.165), channel_id=1, source_target_pairs={{0,16},{4,20},{8,24},{12,28},{16,0},{20,4},{24,8},{28,12},{1,17},{... | collective-permute-start | bytes 967688 | tf_op jit(solution)/shard_map/ppermute | solution.py:31
  398.5 10.4 %weight_grad.11.own.mine = bf16[1120,1120]{1,0:T(8,128)(2,1)} custom-call(s32[584]{0:T(1024)} %concatenate.35.meta, bf16[2048,840]{1,0:T(8,128)(2,1)} %get-tuple-element.263.refs_0_.a, bf16[2048,1120]{1,0:T(8,128)(2,1)} %get-tuple-element.254.normed.refs_1_, bf16[2048,280]{1,0:T(8,128)(2,1)} %get-tuple-element.255.a.refs_2_, ...), custom_call_target="tpu_custom_call" | custom-call | flops 5849999872 | tf_op jit(solution)/shard_map/weight_grad/pallas_call | solution.py:184
  410.3 5.2 first_sum.5
  416.3 2.7 fourth_sum.3.mine
  418.9 2.9 collective-permute-start.25
  422.6 3.3 third_sum.4
  426.0 11.4 %first_part.1 = (bf16[1024,1120]{1,0:T(8,128)(2,1)}, bf16[1024,1120]{1,0:T(8,128)(2,1)}) custom-call(s32[584]{0:T(1024)} %concatenate.35.meta, bf16[2048,840]{1,0:T(8,128)(2,1)} %get-tuple-element.263.refs_0_.a, bf16[2048,840]{1,0:T(8,128)(2,1)} %get-tuple-element.232.refs_0_.b, bf16[840,1120]{1,0:T(8,128)(2,1)} %bitcast.126, bf16[896,1120]{1,0:T(8,128)(2,1)} %bitcast.123), custom_call_target="tpu_custom_call" | custom-call | flops 6750000128 | tf_op jit(solution)/shard_map/first_part/pallas_call | solution.py:184
  437.9 2.6 collective-permute-done.25
  441.2 2.7 join.6.mine
  443.9 2.3 collective-permute-start.29
  448.4 2.6 fourth_sum.4.mine
  451.0 1.9 collective-permute-start.26
  454.0 4.3 second_sum.5
  461.2 12.5 %start_back.1 = (bf16[64,16,1120]{2,1,0:T(8,128)(2,1)}, f32[8,1120]{1,0:T(8,128)}, f32[32,1120]{1,0:T(8,128)}) custom-call(s32[584]{0:T(1024)} %concatenate.35.meta, bf16[1024,1120]{1,0:T(8,128)(2,1)} %get-tuple-element.271.refs_0_, bf16[1024,1120]{1,0:T(8,128)(2,1)} %get-tuple-element.264.refs_1_, bf16[1024,1120]{1,0:T(8,128)(2,1)} %bitcast.112, ...), custom_call_target="tpu_custom_call" | custom-call | flops 6750000128 | tf_op jit(solution)/shard_map/start_back/pallas_call | solution.py:184
  474.5 3.0 join.7.mine
  477.6 5.5 collective-permute-done.28
  483.9 3.2 third_sum.5
  487.9 2.8 join.8.mine
  490.8 3.1 collective-permute-start.34
  493.9 2.5 vectors.1
  500.8 11.4 %collective-permute-done.34 = bf16[9,16,1120]{2,1,0:T(8,128)(2,1)S(1)} collective-permute-done((bf16[9,16,1120]{2,1,0:T(8,128)(2,1)S(1)}, bf16[9,16,1120]{2,1,0:T(8,128)(2,1)S(1)}, u32[]{:S(2)}, u32[]{:S(2)}) %collective-permute-start.34) | collective-permute-done | bytes 322592 | tf_op jit(solution)/shard_map/ppermute | solution.py:31
  513.0 2.7 fourth_sum.5.mine
  516.6 3.2 join.9.mine
  521.3 3.4 collective-permute-start.37
  524.6 8.7 %finish.1 = bf16[64,16,1120]{2,1,0:T(8,128)(2,1)} custom-call(s32[584]{0:T(1024)} %concatenate.35.meta, f32[2048,1120]{1,0:T(8,128)} %get-tuple-element.294.refs_4_.middle, bf16[1024,1120]{1,0:T(8,128)(2,1)} %get-tuple-element.201.refs_0_, bf16[1024,1120]{1,0:T(8,128)(2,1)} %get-tuple-element.202.refs_1_, bf16[1024,1120]{1,0:T(8,128)(2,1)} %bitcast.120, ...), custom_call_target="tpu_custom_call" | custom-call | flops 4499999744 | tf_op jit(solution)/shard_map/finish/pallas_call | solution.py:184
  533.3 4.8 collective-permute-done.37
  538.8 2.8 join.10.mine
  546.5 5.1 widen_rows.3
  551.6 6.3 %collective-permute-done.39 = bf16[35,16,1120]{2,1,0:T(8,128)(2,1)} collective-permute-done((bf16[35,16,1120]{2,1,0:T(8,128)(2,1)}, bf16[35,16,1120]{2,1,0:T(8,128)(2,1)}, u32[]{:S(2)}, u32[]{:S(2)}) %collective-permute-start.39) | collective-permute-done | bytes 1254432 | tf_op jit(solution)/shard_map/ppermute | solution.py:31
  557.9 5.3 widen_rows.4
  563.2 3.2 join.11.mine
  570.6 3.4 collective-permute-done.42
  577.5 4.7 collective-permute-done.43
  584.8 11.0 %collective-permute-done.44 = bf16[35,16,1120]{2,1,0:T(8,128)(2,1)} collective-permute-done((bf16[35,16,1120]{2,1,0:T(8,128)(2,1)}, bf16[35,16,1120]{2,1,0:T(8,128)(2,1)}, u32[]{:S(2)}, u32[]{:S(2)}) %collective-permute-start.44) | collective-permute-done | bytes 1254432 | tf_op jit(solution)/shard_map/ppermute | solution.py:31
  595.8 5.1 widen_rows.5
  (209 shorter events, 81.6 us)
Async XLA Ops:
  7.2 8.3 %copy-start.3 = (bf16[64,16,1120]{2,1,0:T(8,128)(2,1)S(1)}, bf16[64,16,1120]{2,1,0:T(8,128)(2,1)}, u32[]{:S(2)}) copy-start(bf16[64,16,1120]{2,1,0:T(8,128)(2,1)} %param.14) | copy-start | bytes 6881284
  7.2 90.6 %all-gather.3.cloned.1.call-start = ((), (), s32[]{:S(2)}) async-start(), calls=%async_computation | async-start | bytes 2322432 | tf_op jit(solution)/shard_map/all_gather | solution.py:666
  9.1 9.5 %collective-permute-start.2 = (bf16[7,16,1120]{2,1,0:T(8,128)(2,1)}, bf16[7,16,1120]{2,1,0:T(8,128)(2,1)}, u32[]{:S(2)}, u32[]{:S(2)}) collective-permute-start(bf16[7,16,1120]{2,1,0:T(8,128)(2,1)} %bitcast.11), channel_id=1, source_target_pairs={{0,2},{1,3},{2,0},{3,1},{4,6},{5,7},{6,4},{7,5},{8,10},{9,11},{10,... | collective-permute-start | bytes 752648 | tf_op jit(solution)/shard_map/ppermute | solution.py:31
  15.4 2.6 copy-start.4
  18.2 52.4 %copy-start.9 = (bf16[32,16,1120]{2,1,0:T(8,128)(2,1)}, bf16[32,16,1120]{2,1,0:T(8,128)(2,1)S(1)}, u32[]{:S(2)}) copy-start(bf16[32,16,1120]{2,1,0:T(8,128)(2,1)S(1)} %get-tuple-element.176.refs_7_) | copy-start | bytes 3440644
  18.6 133.3 %all-gather.5.cloned.1.call-start = ((), (), s32[]{:S(2)}) async-start(), calls=%async_computation.1 | async-start | bytes 2985984 | tf_op jit(solution)/shard_map/all_gather | solution.py:666
  18.6 13.5 %collective-permute-start = (bf16[32,16,1120]{2,1,0:T(8,128)(2,1)S(1)}, bf16[32,16,1120]{2,1,0:T(8,128)(2,1)}, u32[]{:S(2)}, u32[]{:S(2)}) collective-permute-start(bf16[32,16,1120]{2,1,0:T(8,128)(2,1)S(1)} %get-tuple-element.330.a0), channel_id=1, source_target_pairs={{0,1},{1,0},{2,3},{3,2},{4,5},{5,4},{6,7},{7,6},{8,9},{9,8},{10,11... | collective-permute-start | bytes 3440648 | tf_op jit(solution)/shard_map/ppermute | solution.py:31
  18.7 29.1 %collective-permute-start.1 = (bf16[32,16,1120]{2,1,0:T(8,128)(2,1)}, bf16[32,16,1120]{2,1,0:T(8,128)(2,1)}, u32[]{:S(2)}, u32[]{:S(2)}) collective-permute-start(bf16[32,16,1120]{2,1,0:T(8,128)(2,1)} %get-tuple-element.329), channel_id=1, source_target_pairs={{0,2},{1,3},{2,0},{3,1},{4,6},{5,7},{6,4},{7,5},{8,10},{9,11},{10,... | collective-permute-start | bytes 3440648 | tf_op jit(solution)/shard_map/ppermute | solution.py:31
  20.5 48.2 %collective-permute-start.5 = (bf16[18,16,1120]{2,1,0:T(8,128)(2,1)}, bf16[18,16,1120]{2,1,0:T(8,128)(2,1)}, u32[]{:S(2)}, u32[]{:S(2)}) collective-permute-start(bf16[18,16,1120]{2,1,0:T(8,128)(2,1)} %bitcast.127), channel_id=1, source_target_pairs={{0,2},{1,3},{2,0},{3,1},{4,6},{5,7},{6,4},{7,5},{8,10},{9,11},{10,... | collective-permute-start | bytes 1935368 | tf_op jit(solution)/shard_map/ppermute | solution.py:31
  20.8 47.9 %collective-permute-start.4 = (bf16[9,16,1120]{2,1,0:T(8,128)(2,1)}, bf16[9,16,1120]{2,1,0:T(8,128)(2,1)}, u32[]{:S(2)}, u32[]{:S(2)}) collective-permute-start(bf16[9,16,1120]{2,1,0:T(8,128)(2,1)} %bitcast.128), channel_id=1, source_target_pairs={{0,2},{1,3},{2,0},{3,1},{4,6},{5,7},{6,4},{7,5},{8,10},{9,11},{10,... | collective-permute-start | bytes 967688 | tf_op jit(solution)/shard_map/ppermute | solution.py:31
  27.4 3.4 copy-start.16
  47.9 8.2 %collective-permute-start.3 = (bf16[32,16,1120]{2,1,0:T(8,128)(2,1)}, bf16[32,16,1120]{2,1,0:T(8,128)(2,1)}, u32[]{:S(2)}, u32[]{:S(2)}) collective-permute-start(bf16[32,16,1120]{2,1,0:T(8,128)(2,1)} %collective-permute-done.1.a1), channel_id=1, source_target_pairs={{0,1},{1,0},{2,3},{3,2},{4,5},{5,4},{6,7},{7,6},{8,9},{9,8},{10,11... | collective-permute-start | bytes 3440648 | tf_op jit(solution)/shard_map/ppermute | solution.py:31
  68.8 29.0 %collective-permute-start.7 = (bf16[32,16,1120]{2,1,0:T(8,128)(2,1)S(1)}, bf16[32,16,1120]{2,1,0:T(8,128)(2,1)}, u32[]{:S(2)}, u32[]{:S(2)}) collective-permute-start(bf16[32,16,1120]{2,1,0:T(8,128)(2,1)S(1)} %get-tuple-element.177), channel_id=1, source_target_pairs={{0,2},{1,3},{2,0},{3,1},{4,6},{5,7},{6,4},{7,5},{8,10},{9,11},{10,... | collective-permute-start | bytes 3440648 | tf_op jit(solution)/shard_map/ppermute | solution.py:31
  70.6 27.2 %collective-permute-start.6 = (bf16[32,16,1120]{2,1,0:T(8,128)(2,1)S(1)}, bf16[32,16,1120]{2,1,0:T(8,128)(2,1)}, u32[]{:S(2)}, u32[]{:S(2)}) collective-permute-start(bf16[32,16,1120]{2,1,0:T(8,128)(2,1)S(1)} %get-tuple-element.176.refs_7_), channel_id=1, source_target_pairs={{0,1},{1,0},{2,3},{3,2},{4,5},{5,4},{6,7},{7,6},{8,9},{9,8},{10,11... | collective-permute-start | bytes 3440648 | tf_op jit(solution)/shard_map/ppermute | solution.py:31
  73.5 78.4 %collective-permute-start.9 = (bf16[70,16,1120]{2,1,0:T(8,128)(2,1)}, bf16[70,16,1120]{2,1,0:T(8,128)(2,1)}, u32[]{:S(2)}, u32[]{:S(2)}) collective-permute-start(bf16[70,16,1120]{2,1,0:T(8,128)(2,1)} %bitcast.130), channel_id=1, source_target_pairs={{0,2},{1,3},{2,0},{3,1},{4,6},{5,7},{6,4},{7,5},{8,10},{9,11},{10,... | collective-permute-start | bytes 7526408 | tf_op jit(solution)/shard_map/ppermute | solution.py:31
  116.5 7.8 %copy-start.14 = (bf16[1120]{0:T(1024)(128)(2,1)S(1)}, bf16[1120]{0:T(1024)(128)(2,1)}, u32[]{:S(2)}) copy-start(bf16[1120]{0:T(1024)(128)(2,1)} %param.25) | copy-start | bytes 6724
  116.5 8.4 %copy-start.13 = (bf16[2,1120]{1,0:T(2,128)(2,1)S(1)}, bf16[2,1120]{1,0:T(2,128)(2,1)}, u32[]{:S(2)}) copy-start(bf16[2,1120]{1,0:T(2,128)(2,1)} %param.23) | copy-start | bytes 13444
  123.6 28.3 %collective-permute-start.10 = (bf16[64,16,1120]{2,1,0:T(8,128)(2,1)}, bf16[64,16,1120]{2,1,0:T(8,128)(2,1)S(1)}, u32[]{:S(2)}, u32[]{:S(2)}) collective-permute-start(bf16[64,16,1120]{2,1,0:T(8,128)(2,1)} %bitcast.140), channel_id=1, source_target_pairs={{0,1},{1,0},{2,3},{3,2},{4,5},{5,4},{6,7},{7,6},{8,9},{9,8},{10,11... | collective-permute-start | bytes 6881288 | tf_op jit(solution)/shard_map/ppermute | solution.py:31
  123.7 28.2 %collective-permute-start.11 = (bf16[64,16,1120]{2,1,0:T(8,128)(2,1)}, bf16[64,16,1120]{2,1,0:T(8,128)(2,1)}, u32[]{:S(2)}, u32[]{:S(2)}) collective-permute-start(bf16[64,16,1120]{2,1,0:T(8,128)(2,1)} %bitcast.141), channel_id=1, source_target_pairs={{0,1},{1,0},{2,3},{3,2},{4,5},{5,4},{6,7},{7,6},{8,9},{9,8},{10,11... | collective-permute-start | bytes 6881288 | tf_op jit(solution)/shard_map/ppermute | solution.py:31
  124.2 9.3 %collective-permute-start.8 = (bf16[32,16,1120]{2,1,0:T(8,128)(2,1)}, bf16[32,16,1120]{2,1,0:T(8,128)(2,1)S(1)}, u32[]{:S(2)}, u32[]{:S(2)}) collective-permute-start(bf16[32,16,1120]{2,1,0:T(8,128)(2,1)} %collective-permute-done.7.refs_8_), channel_id=1, source_target_pairs={{0,1},{1,0},{2,3},{3,2},{4,5},{5,4},{6,7},{7,6},{8,9},{9,8},{10,11... | collective-permute-start | bytes 3440648 | tf_op jit(solution)/shard_map/ppermute | solution.py:31
  133.5 18.5 %copy-start.23 = (bf16[32,16,1120]{2,1,0:T(8,128)(2,1)}, bf16[32,16,1120]{2,1,0:T(8,128)(2,1)S(1)}, u32[]{:S(2)}) copy-start(bf16[32,16,1120]{2,1,0:T(8,128)(2,1)S(1)} %collective-permute-done.8.refs_10_) | copy-start | bytes 3440644
  200.2 20.1 %collective-permute-start.14 = (bf16[64,16,1120]{2,1,0:T(8,128)(2,1)}, bf16[64,16,1120]{2,1,0:T(8,128)(2,1)}, u32[]{:S(2)}, u32[]{:S(2)}) collective-permute-start(bf16[64,16,1120]{2,1,0:T(8,128)(2,1)} %bitcast.138), channel_id=1, source_target_pairs={{0,1},{1,0},{2,3},{3,2},{4,5},{5,4},{6,7},{7,6},{8,9},{9,8},{10,11... | collective-permute-start | bytes 6881288 | tf_op jit(solution)/shard_map/ppermute | solution.py:31
  200.3 20.3 %collective-permute-start.15 = (bf16[64,16,1120]{2,1,0:T(8,128)(2,1)}, bf16[64,16,1120]{2,1,0:T(8,128)(2,1)}, u32[]{:S(2)}, u32[]{:S(2)}) collective-permute-start(bf16[64,16,1120]{2,1,0:T(8,128)(2,1)} %bitcast.139), channel_id=1, source_target_pairs={{0,1},{1,0},{2,3},{3,2},{4,5},{5,4},{6,7},{7,6},{8,9},{9,8},{10,11... | collective-permute-start | bytes 6881288 | tf_op jit(solution)/shard_map/ppermute | solution.py:31
  200.8 34.3 %collective-permute-start.12 = (bf16[64,16,1120]{2,1,0:T(8,128)(2,1)}, bf16[64,16,1120]{2,1,0:T(8,128)(2,1)S(1)}, u32[]{:S(2)}, u32[]{:S(2)}) collective-permute-start(bf16[64,16,1120]{2,1,0:T(8,128)(2,1)} %bitcast.118), channel_id=1, source_target_pairs={{0,1},{1,0},{2,3},{3,2},{4,5},{5,4},{6,7},{7,6},{8,9},{9,8},{10,11... | collective-permute-start | bytes 6881288 | tf_op jit(solution)/shard_map/ppermute | solution.py:31
  200.8 34.3 %collective-permute-start.13 = (bf16[64,16,1120]{2,1,0:T(8,128)(2,1)}, bf16[64,16,1120]{2,1,0:T(8,128)(2,1)S(1)}, u32[]{:S(2)}, u32[]{:S(2)}) collective-permute-start(bf16[64,16,1120]{2,1,0:T(8,128)(2,1)} %bitcast.119), channel_id=1, source_target_pairs={{0,1},{1,0},{2,3},{3,2},{4,5},{5,4},{6,7},{7,6},{8,9},{9,8},{10,11... | collective-permute-start | bytes 6881288 | tf_op jit(solution)/shard_map/ppermute | solution.py:31
  210.1 59.1 %collective-permute-start.16 = (bf16[70,16,1120]{2,1,0:T(8,128)(2,1)}, bf16[70,16,1120]{2,1,0:T(8,128)(2,1)S(1)}, u32[]{:S(2)}, u32[]{:S(2)}) collective-permute-start(bf16[70,16,1120]{2,1,0:T(8,128)(2,1)} %bitcast.137), channel_id=1, source_target_pairs={{0,2},{1,3},{2,0},{3,1},{4,6},{5,7},{6,4},{7,5},{8,10},{9,11},{10,... | collective-permute-start | bytes 7526408 | tf_op jit(solution)/shard_map/ppermute | solution.py:31
  220.2 104.3 %collective-permute-start.17 = (bf16[70,16,1120]{2,1,0:T(8,128)(2,1)}, bf16[70,16,1120]{2,1,0:T(8,128)(2,1)}, u32[]{:S(2)}, u32[]{:S(2)}) collective-permute-start(bf16[70,16,1120]{2,1,0:T(8,128)(2,1)} %bitcast.136), channel_id=1, source_target_pairs={{0,2},{1,3},{2,0},{3,1},{4,6},{5,7},{6,4},{7,5},{8,10},{9,11},{10,... | collective-permute-start | bytes 7526408 | tf_op jit(solution)/shard_map/ppermute | solution.py:31
  235.1 9.3 %copy-start.7 = (bf16[64,16,1120]{2,1,0:T(8,128)(2,1)}, bf16[64,16,1120]{2,1,0:T(8,128)(2,1)S(1)}, u32[]{:S(2)}) copy-start(bf16[64,16,1120]{2,1,0:T(8,128)(2,1)S(1)} %collective-permute-done.12) | copy-start | bytes 6881284
  235.1 9.3 %copy-start.8 = (bf16[64,16,1120]{2,1,0:T(8,128)(2,1)}, bf16[64,16,1120]{2,1,0:T(8,128)(2,1)S(1)}, u32[]{:S(2)}) copy-start(bf16[64,16,1120]{2,1,0:T(8,128)(2,1)S(1)} %collective-permute-done.13) | copy-start | bytes 6881284
  276.0 53.8 %collective-permute-start.19 = (bf16[35,16,1120]{2,1,0:T(8,128)(2,1)}, bf16[35,16,1120]{2,1,0:T(8,128)(2,1)S(1)}, u32[]{:S(2)}, u32[]{:S(2)}) collective-permute-start(bf16[35,16,1120]{2,1,0:T(8,128)(2,1)} %bitcast.149), channel_id=1, source_target_pairs={{0,4},{4,0},{8,12},{12,8},{16,20},{20,16},{24,28},{28,24},{1,5},{5... | collective-permute-start | bytes 3763208 | tf_op jit(solution)/shard_map/ppermute | solution.py:31
  294.5 114.3 %collective-permute-start.23 = (bf16[70,16,1120]{2,1,0:T(8,128)(2,1)}, bf16[70,16,1120]{2,1,0:T(8,128)(2,1)S(1)}, u32[]{:S(2)}, u32[]{:S(2)}) collective-permute-start(bf16[70,16,1120]{2,1,0:T(8,128)(2,1)} %bitcast.135), channel_id=1, source_target_pairs={{0,2},{1,3},{2,0},{3,1},{4,6},{5,7},{6,4},{7,5},{8,10},{9,11},{10,... | collective-permute-start | bytes 7526408 | tf_op jit(solution)/shard_map/ppermute | solution.py:31
  329.7 43.9 %collective-permute-start.18 = (bf16[35,16,1120]{2,1,0:T(8,128)(2,1)}, bf16[35,16,1120]{2,1,0:T(8,128)(2,1)S(1)}, u32[]{:S(2)}, u32[]{:S(2)}) collective-permute-start(bf16[35,16,1120]{2,1,0:T(8,128)(2,1)} %bitcast.147), channel_id=1, source_target_pairs={{0,4},{4,0},{8,12},{12,8},{16,20},{20,16},{24,28},{28,24},{1,5},{5... | collective-permute-start | bytes 3763208 | tf_op jit(solution)/shard_map/ppermute | solution.py:31
  335.1 34.5 %collective-permute-start.20 = (bf16[18,16,1120]{2,1,0:T(8,128)(2,1)}, bf16[18,16,1120]{2,1,0:T(8,128)(2,1)S(1)}, u32[]{:S(2)}, u32[]{:S(2)}) collective-permute-start(bf16[18,16,1120]{2,1,0:T(8,128)(2,1)} %bitcast.159), channel_id=1, source_target_pairs={{0,8},{4,12},{8,0},{12,4},{16,24},{20,28},{24,16},{28,20},{1,9},{5... | collective-permute-start | bytes 1935368 | tf_op jit(solution)/shard_map/ppermute | solution.py:31
  374.7 4.4 copy-start.31
  379.1 36.4 %collective-permute-start.22 = (bf16[9,16,1120]{2,1,0:T(8,128)(2,1)S(1)}, bf16[9,16,1120]{2,1,0:T(8,128)(2,1)S(1)}, u32[]{:S(2)}, u32[]{:S(2)}) collective-permute-start(bf16[9,16,1120]{2,1,0:T(8,128)(2,1)S(1)} %bitcast.165), channel_id=1, source_target_pairs={{0,16},{4,20},{8,24},{12,28},{16,0},{20,4},{24,8},{28,12},{1,17},{... | collective-permute-start | bytes 967688 | tf_op jit(solution)/shard_map/ppermute | solution.py:31
  398.5 23.3 %collective-permute-start.21 = (bf16[18,16,1120]{2,1,0:T(8,128)(2,1)}, bf16[18,16,1120]{2,1,0:T(8,128)(2,1)S(1)}, u32[]{:S(2)}, u32[]{:S(2)}) collective-permute-start(bf16[18,16,1120]{2,1,0:T(8,128)(2,1)} %bitcast.155), channel_id=1, source_target_pairs={{0,8},{4,12},{8,0},{12,4},{16,24},{20,28},{24,16},{28,20},{1,9},{5... | collective-permute-start | bytes 1935368 | tf_op jit(solution)/shard_map/ppermute | solution.py:31
  415.5 37.4 %collective-permute-start.27 = (bf16[35,16,1120]{2,1,0:T(8,128)(2,1)}, bf16[35,16,1120]{2,1,0:T(8,128)(2,1)S(1)}, u32[]{:S(2)}, u32[]{:S(2)}) collective-permute-start(bf16[35,16,1120]{2,1,0:T(8,128)(2,1)} %bitcast.144), channel_id=1, source_target_pairs={{0,4},{4,0},{8,12},{12,8},{16,20},{20,16},{24,28},{28,24},{1,5},{5... | collective-permute-start | bytes 3763208 | tf_op jit(solution)/shard_map/ppermute | solution.py:31
  418.9 21.6 %collective-permute-start.25 = (bf16[9,16,1120]{2,1,0:T(8,128)(2,1)}, bf16[9,16,1120]{2,1,0:T(8,128)(2,1)S(1)}, u32[]{:S(2)}, u32[]{:S(2)}) collective-permute-start(bf16[9,16,1120]{2,1,0:T(8,128)(2,1)} %bitcast.164), channel_id=1, source_target_pairs={{0,16},{4,20},{8,24},{12,28},{16,0},{20,4},{24,8},{28,12},{1,17},{... | collective-permute-start | bytes 967688 | tf_op jit(solution)/shard_map/ppermute | solution.py:31
  425.9 21.7 %collective-permute-start.24 = (bf16[9,16,1120]{2,1,0:T(8,128)(2,1)}, bf16[9,16,1120]{2,1,0:T(8,128)(2,1)S(1)}, u32[]{:S(2)}, u32[]{:S(2)}) collective-permute-start(bf16[9,16,1120]{2,1,0:T(8,128)(2,1)} %bitcast.168), channel_id=1, source_target_pairs={{0,16},{4,20},{8,24},{12,28},{16,0},{20,4},{24,8},{28,12},{1,17},{... | collective-permute-start | bytes 967688 | tf_op jit(solution)/shard_map/ppermute | solution.py:31
  437.4 21.6 %collective-permute-start.30 = (bf16[64,16,1120]{2,1,0:T(8,128)(2,1)}, bf16[64,16,1120]{2,1,0:T(8,128)(2,1)S(1)}, u32[]{:S(2)}, u32[]{:S(2)}) collective-permute-start(bf16[64,16,1120]{2,1,0:T(8,128)(2,1)} %bitcast.110), channel_id=1, source_target_pairs={{0,1},{1,0},{2,3},{3,2},{4,5},{5,4},{6,7},{7,6},{8,9},{9,8},{10,11... | collective-permute-start | bytes 6881288 | tf_op jit(solution)/shard_map/ppermute | solution.py:31
  437.4 21.5 %collective-permute-start.31 = (bf16[64,16,1120]{2,1,0:T(8,128)(2,1)}, bf16[64,16,1120]{2,1,0:T(8,128)(2,1)S(1)}, u32[]{:S(2)}, u32[]{:S(2)}) collective-permute-start(bf16[64,16,1120]{2,1,0:T(8,128)(2,1)} %bitcast.111), channel_id=1, source_target_pairs={{0,1},{1,0},{2,3},{3,2},{4,5},{5,4},{6,7},{7,6},{8,9},{9,8},{10,11... | collective-permute-start | bytes 6881288 | tf_op jit(solution)/shard_map/ppermute | solution.py:31
  443.9 29.7 %collective-permute-start.29 = (bf16[18,16,1120]{2,1,0:T(8,128)(2,1)}, bf16[18,16,1120]{2,1,0:T(8,128)(2,1)S(1)}, u32[]{:S(2)}, u32[]{:S(2)}) collective-permute-start(bf16[18,16,1120]{2,1,0:T(8,128)(2,1)} %bitcast.150), channel_id=1, source_target_pairs={{0,8},{4,12},{8,0},{12,4},{16,24},{20,28},{24,16},{28,20},{1,9},{5... | collective-permute-start | bytes 1935368 | tf_op jit(solution)/shard_map/ppermute | solution.py:31
  451.0 36.2 %collective-permute-start.26 = (bf16[9,16,1120]{2,1,0:T(8,128)(2,1)}, bf16[9,16,1120]{2,1,0:T(8,128)(2,1)S(1)}, u32[]{:S(2)}, u32[]{:S(2)}) collective-permute-start(bf16[9,16,1120]{2,1,0:T(8,128)(2,1)} %bitcast.161), channel_id=1, source_target_pairs={{0,16},{4,20},{8,24},{12,28},{16,0},{20,4},{24,8},{28,12},{1,17},{... | collective-permute-start | bytes 967688 | tf_op jit(solution)/shard_map/ppermute | solution.py:31
  458.3 24.8 %collective-permute-start.28 = (bf16[18,16,1120]{2,1,0:T(8,128)(2,1)}, bf16[18,16,1120]{2,1,0:T(8,128)(2,1)S(1)}, u32[]{:S(2)}, u32[]{:S(2)}) collective-permute-start(bf16[18,16,1120]{2,1,0:T(8,128)(2,1)} %bitcast.157), channel_id=1, source_target_pairs={{0,8},{4,12},{8,0},{12,4},{16,24},{20,28},{24,16},{28,20},{1,9},{5... | collective-permute-start | bytes 1935368 | tf_op jit(solution)/shard_map/ppermute | solution.py:31
  459.0 2.2 copy-start.2
  487.9 2.9 copy-start.30
  490.7 7.3 %copy-start.5 = (bf16[64,16,1120]{2,1,0:T(8,128)(2,1)S(1)}, bf16[64,16,1120]{2,1,0:T(8,128)(2,1)}, u32[]{:S(2)}) copy-start(bf16[64,16,1120]{2,1,0:T(8,128)(2,1)} %get-tuple-element.275) | copy-start | bytes 6881284
  490.7 25.0 %collective-permute-start.32 = (bf16[18,16,1120]{2,1,0:T(8,128)(2,1)}, bf16[18,16,1120]{2,1,0:T(8,128)(2,1)S(1)}, u32[]{:S(2)}, u32[]{:S(2)}) collective-permute-start(bf16[18,16,1120]{2,1,0:T(8,128)(2,1)} %bitcast.151), channel_id=1, source_target_pairs={{0,8},{4,12},{8,0},{12,4},{16,24},{20,28},{24,16},{28,20},{1,9},{5... | collective-permute-start | bytes 1935368 | tf_op jit(solution)/shard_map/ppermute | solution.py:31
  490.8 21.5 %collective-permute-start.34 = (bf16[9,16,1120]{2,1,0:T(8,128)(2,1)S(1)}, bf16[9,16,1120]{2,1,0:T(8,128)(2,1)S(1)}, u32[]{:S(2)}, u32[]{:S(2)}) collective-permute-start(bf16[9,16,1120]{2,1,0:T(8,128)(2,1)S(1)} %bitcast.163), channel_id=1, source_target_pairs={{0,16},{4,20},{8,24},{12,28},{16,0},{20,4},{24,8},{28,12},{1,17},{... | collective-permute-start | bytes 967688 | tf_op jit(solution)/shard_map/ppermute | solution.py:31
  496.4 19.3 %collective-permute-start.33 = (f32[40,1120]{1,0:T(8,128)}, f32[40,1120]{1,0:T(8,128)S(1)}, u32[]{:S(2)}, u32[]{:S(2)}) collective-permute-start(f32[40,1120]{1,0:T(8,128)} %get-tuple-element.288), channel_id=1, source_target_pairs={{0,2},{1,3},{2,0},{3,1},{4,6},{5,7},{6,4},{7,5},{8,10},{9,11},{10,... | collective-permute-start | bytes 537608 | tf_op jit(solution)/shard_map/ppermute | solution.py:31
  499.0 46.0 %collective-permute-start.41 = (bf16[32,16,1120]{2,1,0:T(8,128)(2,1)}, bf16[32,16,1120]{2,1,0:T(8,128)(2,1)S(1)}, u32[]{:S(2)}, u32[]{:S(2)}) collective-permute-start(bf16[32,16,1120]{2,1,0:T(8,128)(2,1)} %slice.96), channel_id=1, source_target_pairs={{0,2},{1,3},{2,0},{3,1},{4,6},{5,7},{6,4},{7,5},{8,10},{9,11},{10,... | collective-permute-start | bytes 3440648 | tf_op jit(solution)/shard_map/ppermute | solution.py:31
  499.5 47.0 %collective-permute-start.40 = (bf16[35,16,1120]{2,1,0:T(8,128)(2,1)}, bf16[35,16,1120]{2,1,0:T(8,128)(2,1)}, u32[]{:S(2)}, u32[]{:S(2)}) collective-permute-start(bf16[35,16,1120]{2,1,0:T(8,128)(2,1)} %bitcast.81), channel_id=1, source_target_pairs={{0,4},{4,0},{8,12},{12,8},{16,20},{20,16},{24,28},{28,24},{1,5},{5... | collective-permute-start | bytes 3763208 | tf_op jit(solution)/shard_map/ppermute | solution.py:31
  515.7 4.1 copy-start.12
  516.6 4.7 copy-start.35
  519.8 38.2 %collective-permute-start.39 = (bf16[35,16,1120]{2,1,0:T(8,128)(2,1)}, bf16[35,16,1120]{2,1,0:T(8,128)(2,1)}, u32[]{:S(2)}, u32[]{:S(2)}) collective-permute-start(bf16[35,16,1120]{2,1,0:T(8,128)(2,1)} %bitcast.145), channel_id=1, source_target_pairs={{0,4},{4,0},{8,12},{12,8},{16,20},{20,16},{24,28},{28,24},{1,5},{5... | collective-permute-start | bytes 3763208 | tf_op jit(solution)/shard_map/ppermute | solution.py:31
  521.3 16.8 %collective-permute-start.37 = (bf16[9,16,1120]{2,1,0:T(8,128)(2,1)S(1)}, bf16[9,16,1120]{2,1,0:T(8,128)(2,1)S(1)}, u32[]{:S(2)}, u32[]{:S(2)}) collective-permute-start(bf16[9,16,1120]{2,1,0:T(8,128)(2,1)S(1)} %bitcast.170), channel_id=1, source_target_pairs={{0,16},{4,20},{8,24},{12,28},{16,0},{20,4},{24,8},{28,12},{1,17},{... | collective-permute-start | bytes 967688 | tf_op jit(solution)/shard_map/ppermute | solution.py:31
  538.8 5.1 copy-start
  541.6 21.7 %collective-permute-start.38 = (bf16[18,16,1120]{2,1,0:T(8,128)(2,1)}, bf16[18,16,1120]{2,1,0:T(8,128)(2,1)}, u32[]{:S(2)}, u32[]{:S(2)}) collective-permute-start(bf16[18,16,1120]{2,1,0:T(8,128)(2,1)} %bitcast.154), channel_id=1, source_target_pairs={{0,8},{4,12},{8,0},{12,4},{16,24},{20,28},{24,16},{28,20},{1,9},{5... | collective-permute-start | bytes 1935368 | tf_op jit(solution)/shard_map/ppermute | solution.py:31
  542.7 23.7 %collective-permute-start.36 = (f32[40,1120]{1,0:T(8,128)S(1)}, f32[40,1120]{1,0:T(8,128)S(1)}, u32[]{:S(2)}, u32[]{:S(2)}) collective-permute-start(f32[40,1120]{1,0:T(8,128)S(1)} %add.107), channel_id=1, source_target_pairs={{0,4},{4,0},{8,12},{12,8},{16,20},{20,16},{24,28},{28,24},{1,5},{5... | collective-permute-start | bytes 537608 | tf_op jit(solution)/shard_map/ppermute | solution.py:31
  545.0 29.1 %collective-permute-start.35 = (bf16[32,16,1120]{2,1,0:T(8,128)(2,1)}, bf16[32,16,1120]{2,1,0:T(8,128)(2,1)}, u32[]{:S(2)}, u32[]{:S(2)}) collective-permute-start(bf16[32,16,1120]{2,1,0:T(8,128)(2,1)} %slice.114), channel_id=1, source_target_pairs={{0,2},{1,3},{2,0},{3,1},{4,6},{5,7},{6,4},{7,5},{8,10},{9,11},{10,... | collective-permute-start | bytes 3440648 | tf_op jit(solution)/shard_map/ppermute | solution.py:31
  563.2 5.0 copy-start.6
  566.5 7.5 %collective-permute-start.42 = (f32[40,1120]{1,0:T(8,128)S(1)}, f32[40,1120]{1,0:T(8,128)S(1)}, u32[]{:S(2)}, u32[]{:S(2)}) collective-permute-start(f32[40,1120]{1,0:T(8,128)S(1)} %add.108), channel_id=1, source_target_pairs={{0,8},{4,12},{8,0},{12,4},{16,24},{20,28},{24,16},{28,20},{1,9},{5... | collective-permute-start | bytes 537608 | tf_op jit(solution)/shard_map/ppermute | solution.py:31
  570.3 25.5 %collective-permute-start.44 = (bf16[35,16,1120]{2,1,0:T(8,128)(2,1)}, bf16[35,16,1120]{2,1,0:T(8,128)(2,1)}, u32[]{:S(2)}, u32[]{:S(2)}) collective-permute-start(bf16[35,16,1120]{2,1,0:T(8,128)(2,1)} %bitcast.89), channel_id=1, source_target_pairs={{0,4},{4,0},{8,12},{12,8},{16,20},{20,16},{24,28},{28,24},{1,5},{5... | collective-permute-start | bytes 3763208 | tf_op jit(solution)/shard_map/ppermute | solution.py:31
  574.0 8.2 %collective-permute-start.43 = (f32[40,1120]{1,0:T(8,128)S(1)}, f32[40,1120]{1,0:T(8,128)S(1)}, u32[]{:S(2)}, u32[]{:S(2)}) collective-permute-start(f32[40,1120]{1,0:T(8,128)S(1)} %add.109), channel_id=1, source_target_pairs={{0,16},{4,20},{8,24},{12,28},{16,0},{20,4},{24,8},{28,12},{1,17},{... | collective-permute-start | bytes 537608 | tf_op jit(solution)/shard_map/ppermute | solution.py:31
  (22 other events, 21.9 us)
Sparse Core Ops, SparseCore 0:
  18.7 50.6 all-gather.2
  71.5 53.9 all-gather.4
